TPU v7x, 32 devices: a whole 2x2x4 slice. The times are simulated.
32 devices in a mesh: dp: 8 (over z, x), seq: 4 (over y, core).
Axes of the slice: x: 2, y: 2, z: 4, core: 2. Of those that a mesh axis runs over, the one named last changes fastest.
Arguments:
- tokens_in: bfloat16 [10240, 1600], P(('dp', 'seq')), may hold values from -6 to 6
- doc_lengths: int32 [8, 2], P('dp'), may hold values from 40 to 1240, as said below
- norm_gains: bfloat16 [4, 1600], P(None, 'dp'), may hold values from 0.5 to 1.5
- w_qkv: bfloat16 [1600, 2240], P('dp', 'seq'), may hold values from -0.15625 to 0.15625
- w_o: bfloat16 [1600, 1600], P('dp', 'seq'), may hold values from -0.15625 to 0.15625
- w_xz: bfloat16 [1600, 6400], P('dp', 'seq'), may hold values from -0.15625 to 0.15625
- w_bcdt: bfloat16 [1600, 82], P('dp'), may hold values from -0.15625 to 0.15625
- conv_w: bfloat16 [4, 3200], P(None, 'dp'), may hold values from -3 to 3
- ssm_rate: float32 [50], replicated, may hold values from 0.0001 to 0.05
- ssm_skip: float32 [50], replicated, may hold values from 0.5 to 1.5
- w_out: bfloat16 [3200, 1600], P('dp', 'seq'), may hold values from -0.109375 to 0.109375
- w_gate_up: bfloat16 [1600, 2, 5504], P('dp', None, 'seq'), may hold values from -0.15625 to 0.15625
- w_down: bfloat16 [1600, 5504], P('dp', 'seq'), may hold values from -0.078125 to 0.078125
- cotangent: bfloat16 [10240, 1600], P(('dp', 'seq')), may hold values from -6 to 6
Outputs:
- mixed_out: bfloat16 [10240, 1600], P(('dp', 'seq'))
- input_grad: bfloat16 [10240, 1600], P(('dp', 'seq'))
- grad_gains: float32 [4, 1600], P(None, 'dp')
- grad_qkv: float32 [1600, 2240], P('dp', 'seq')
- grad_o: float32 [1600, 1600], P('dp', 'seq')
- grad_xz: float32 [1600, 6400], P('dp', 'seq')
- grad_bcdt: float32 [1600, 82], P('dp')
- grad_conv: float32 [4, 3200], P(None, 'dp')
- grad_rate: float32 [50], replicated
- grad_skip: float32 [50], replicated
- grad_out: float32 [3200, 1600], P('dp', 'seq')
- grad_gate_up: float32 [1600, 2, 5504], P('dp', None, 'seq')
- grad_down: float32 [1600, 5504], P('dp', 'seq')
Inputs may be any that keep to these rules, and one draw needn't show every extreme that they name: `doc_lengths`: each row holds a group's two document lengths in the order in which they are packed from the group's first slot. One has 40 to 80 tokens; the other fills the group but for fewer than 40 padding slots at its end, so that it starts in the block of the group's first device and ends in the block of its last. Some group reaches both ends of the range.
All inputs are finite; a program needn't handle non-finite values.
Results may differ from a plain program's by a relative error of at most 0.02.
Values may be sent and summed in bfloat16 or wider, within the bound.
A program may use at most 576 MiB of HBM per device.

v0:
```python
import jax
import jax.numpy as jnp
from jax import lax
from jax.sharding import PartitionSpec as P

D = 1600
HEADS = 25
KV_HEADS = 5
HEAD = 64
INNER = 3200
SSM_HEAD = 64
STATE = 16
CONV = 4
FF = 5504
WINDOW = 1024
SSM_HEADS = 50


NORM_EPS = 1e-05
MASKED = -1e30
HIGHEST = lax.Precision.HIGHEST


def shifted(block, axis, distance):
    devices = range(lax.axis_size(axis))
    route = [(i - distance, i) for i in devices if i - distance in devices]
    return lax.ppermute(block, axis, route)


def carried_in(value, axis, combine, identity):
    count, index = (lax.axis_size(axis), lax.axis_index(axis))
    everything = jax.tree.map(lambda part: lax.all_gather(part, axis), value)
    start = jax.tree.map(
        lambda part, zero: jnp.broadcast_to(jnp.asarray(zero, part.dtype), part.shape),
        value,
        identity,
    )

    def step(k, before):
        reached = k < index
        new = combine(before, jax.tree.map(lambda part: part[k], everything))
        return jax.tree.map(lambda a, b: jnp.where(reached, a, b), new, before)

    return lax.fori_loop(0, count, step, start)


def carried_in_2(value, axis, join, neutral):
    count = lax.axis_size(axis)
    place = lax.axis_index(axis)
    ahead = count - 1 - place
    gathered = jax.tree.map(
        lambda a, kind: lax.all_gather(a.astype(kind), axis),
        value,
        jax.tree.map(lambda a: jnp.bfloat16 if a.dtype == jnp.float32 else a.dtype, value),
    )
    state = jax.tree.map(lambda a, e: jnp.zeros_like(a) + jnp.asarray(e, a.dtype), value, neutral)

    def one(step, state):
        source = count - 1 - step
        return join(
            state,
            jax.tree.map(
                lambda a, own: lax.dynamic_index_in_dim(a, source, 0, False).astype(own.dtype),
                gathered,
                value,
            ),
        )

    return lax.fori_loop(0, ahead, one, state)


def project(left, right):
    return jnp.dot(left, right, preferred_element_type=jnp.float32)


def project_back(grad_rows, right):
    return lax.dot_general(
        grad_rows, right, (((1,), (1,)), ((), ())), preferred_element_type=jnp.float32
    )


def weight_grad(left, grad_rows):
    return lax.dot_general(
        left, grad_rows, (((0,), (0,)), ((), ())), preferred_element_type=jnp.float32
    )


def rms_norm(values, gain):
    return values * lax.rsqrt(jnp.mean(values * values, axis=-1, keepdims=True) + NORM_EPS) * gain


def document_ids(lengths, positions):
    first_end = lengths[0]
    second_end = lengths[0] + lengths[1]
    doc_ids = (positions >= first_end).astype(jnp.int32) + (positions >= second_end).astype(
        jnp.int32
    )
    return (jnp.where(positions < 0, -1, doc_ids), positions < second_end)


def swiglu(gate_up, unit_block):
    row_count = gate_up.shape[0]
    blocks = gate_up.reshape(row_count, -1, 2, unit_block)
    return (jax.nn.silu(blocks[:, :, 0]) * blocks[:, :, 1]).reshape(row_count, -1)


def join_tail(inputs_x, attn_o, ssm_o, gains_full):
    residual = inputs_x + 0.5 * (rms_norm(attn_o, gains_full[1]) + rms_norm(ssm_o, gains_full[2]))
    return (residual, rms_norm(residual, gains_full[3]))


def convolve(raw_x, raw_rim, conv_weight, doc_ids, rim_ids):
    row_count = raw_x.shape[0]
    padded = jnp.concatenate([raw_rim, raw_x], axis=0)
    padded_ids = jnp.concatenate([rim_ids, doc_ids])
    conv_sum = jnp.zeros(raw_x.shape, jnp.float32)
    for tap_index in range(CONV):
        same_doc = (padded_ids[tap_index : tap_index + row_count] == doc_ids).astype(jnp.float32)
        conv_sum = (
            conv_sum
            + conv_weight[tap_index] * padded[tap_index : tap_index + row_count] * same_doc[:, None]
        )
    return jax.nn.silu(conv_sum)


def decay_terms(bcdt_proj, ssm_rate):
    step_size = jax.nn.softplus(bcdt_proj[:, 2 * STATE :])
    decay_log = jnp.cumsum(-step_size * ssm_rate[None, :], axis=0)
    return (step_size, decay_log)


def ssm_summary(conv_act, bcdt_proj, ssm_rate, doc_ids, prev_id):
    row_count = conv_act.shape[0]
    step_size, decay_log = decay_terms(bcdt_proj, ssm_rate)
    heads_x = conv_act.reshape(row_count, SSM_HEADS, SSM_HEAD)
    last_log = decay_log[row_count - 1]
    same_end = (doc_ids == doc_ids[row_count - 1]).astype(jnp.float32)
    end_weights = jnp.exp(last_log[None, :] - decay_log) * step_size * same_end[:, None]
    state_end = jnp.einsum(
        "th,tn,thd->hnd", end_weights, bcdt_proj[:, :STATE], heads_x, precision=HIGHEST
    )
    carry_end = jnp.exp(last_log) * (doc_ids[row_count - 1] == prev_id).astype(jnp.float32)
    return (carry_end, state_end)


def ssm_readout(conv_act, bcdt_proj, ssm_rate, ssm_skip, gate_z, state_in, doc_ids, prev_id):
    row_count = conv_act.shape[0]
    step_size, decay_log = decay_terms(bcdt_proj, ssm_rate)
    heads_x = conv_act.reshape(row_count, SSM_HEADS, SSM_HEAD)
    places = jnp.arange(row_count, dtype=jnp.int32)
    causal = (places[:, None] >= places[None, :]) & (doc_ids[:, None] == doc_ids[None, :])
    log_by_head = jnp.transpose(decay_log)
    log_gap = log_by_head[:, :, None] - log_by_head[:, None, :]
    decays = jnp.where(causal[None], jnp.exp(jnp.where(causal[None], log_gap, 0.0)), 0.0)
    readout_gram = jnp.dot(
        bcdt_proj[:, STATE : 2 * STATE], jnp.transpose(bcdt_proj[:, :STATE]), precision=HIGHEST
    )
    mixing = decays * readout_gram[None] * jnp.transpose(step_size)[:, None, :]
    within = jnp.einsum("hts,shd->thd", mixing, heads_x, precision=HIGHEST)
    carried = jnp.exp(decay_log) * (doc_ids == prev_id).astype(jnp.float32)[:, None]
    from_state = (
        jnp.einsum("tn,hnd->thd", bcdt_proj[:, STATE : 2 * STATE], state_in, precision=HIGHEST)
        * carried[:, :, None]
    )
    ssm_read = within + from_state + ssm_skip[None, :, None] * heads_x
    return ssm_read.reshape(row_count, INNER) * jax.nn.silu(gate_z)


def chain_combine(earlier, later):
    return (earlier[0] * later[0], later[0][:, None, None] * earlier[1] + later[1])


def head_forward(query_head, key_head, value_head, allowed, scale):
    scores = scale * jnp.einsum(
        "gtd,sd->gts", query_head, key_head, preferred_element_type=jnp.float32
    )
    scores = jnp.where(allowed[None], scores, MASKED)
    top_score = jnp.max(scores, axis=-1, keepdims=True)
    expos = jnp.exp(scores - top_score)
    denom = jnp.sum(expos, axis=-1, keepdims=True)
    weights = (expos / denom).astype(jnp.bfloat16)
    mixed = jnp.einsum("gts,sd->gtd", weights, value_head, preferred_element_type=jnp.float32)
    return (mixed, (top_score + jnp.log(denom))[..., 0])


def head_backward(query_head, key_head, value_head, allowed, log_total, d_mixed, scale):
    scores = scale * jnp.einsum(
        "gtd,sd->gts", query_head, key_head, preferred_element_type=jnp.float32
    )
    scores = jnp.where(allowed[None], scores, MASKED)
    probs = jnp.exp(scores - log_total[..., None])
    weights = probs.astype(jnp.bfloat16)
    d_value = jnp.einsum("gts,gtd->sd", weights, d_mixed, preferred_element_type=jnp.float32)
    d_probs = jnp.einsum("gtd,sd->gts", d_mixed, value_head, preferred_element_type=jnp.float32)
    d_scores = probs * (d_probs - jnp.sum(probs * d_probs, axis=-1, keepdims=True))
    d_low = d_scores.astype(jnp.bfloat16)
    d_query = scale * jnp.einsum("gts,sd->gtd", d_low, key_head, preferred_element_type=jnp.float32)
    d_key = scale * jnp.einsum("gts,gtd->sd", d_low, query_head, preferred_element_type=jnp.float32)
    return (d_query, d_key, d_value)


def gather_weights(w_qkv, w_o, w_xz, w_out, w_gate_up, w_down, w_bcdt, conv_w, norm_gains):
    gate_up_flat = w_gate_up.reshape(w_gate_up.shape[0], -1)
    wide = (
        lax.all_gather(w_qkv, "seq", axis=1, tiled=True),
        lax.all_gather(w_o, "seq", axis=1, tiled=True),
        lax.all_gather(w_xz, "seq", axis=1, tiled=True),
        lax.all_gather(w_out, "seq", axis=1, tiled=True),
    )
    full = (
        lax.all_gather(wide[0], "dp", axis=0, tiled=True),
        lax.all_gather(wide[1], "dp", axis=0, tiled=True),
        lax.all_gather(wide[2], "dp", axis=0, tiled=True),
        lax.all_gather(wide[3], "dp", axis=0, tiled=True),
        lax.all_gather(gate_up_flat, "dp", axis=0, tiled=True),
        lax.all_gather(w_down, "dp", axis=0, tiled=True),
        lax.all_gather(w_bcdt, "dp", axis=0, tiled=True),
        lax.all_gather(conv_w, "dp", axis=1, tiled=True),
        lax.all_gather(norm_gains, "dp", axis=1, tiled=True),
    )
    ffn_weights = (full[4], full[5])
    ffn_weights = (
        lax.all_gather(full[4], "seq", axis=1, tiled=True),
        lax.all_gather(full[5], "seq", axis=1, tiled=True),
    )
    return (
        full[0],
        full[1],
        full[2],
        full[3],
        ffn_weights[0],
        ffn_weights[1],
        full[6],
        full[7],
        full[8],
    )


def reduce_seq(first_grad, second_grad):
    return (
        lax.psum_scatter(
            first_grad.astype(jnp.bfloat16), "seq", scatter_dimension=1, tiled=True
        ).astype(jnp.float32),
        lax.psum_scatter(
            second_grad.astype(jnp.bfloat16), "seq", scatter_dimension=1, tiled=True
        ).astype(jnp.float32),
    )


def reduce_dp(first_grad, second_grad):
    return (
        lax.psum_scatter(
            first_grad.astype(jnp.bfloat16), "dp", scatter_dimension=0, tiled=True
        ).astype(jnp.float32),
        lax.psum_scatter(
            second_grad.astype(jnp.bfloat16), "dp", scatter_dimension=0, tiled=True
        ).astype(jnp.float32),
    )


def reduce_pair(first_grad, second_grad):
    summed = reduce_seq(first_grad, second_grad)
    return reduce_dp(summed[0], summed[1])


def on_device(
    tokens_in,
    doc_lengths,
    norm_gains,
    w_qkv,
    w_o,
    w_xz,
    w_bcdt,
    conv_w,
    ssm_rate,
    ssm_skip,
    w_out,
    w_gate_up,
    w_down,
    cotangent,
):
    row_count = tokens_in.shape[0]
    seq_index = lax.axis_index("seq")
    seq_total = lax.axis_size("seq")
    kv_width = KV_HEADS * HEAD
    group_heads = HEADS // KV_HEADS
    scale = HEAD ** (-0.5)
    unit_block = FF // seq_total
    lengths = doc_lengths[0]
    row_offset = seq_index * row_count
    positions = row_offset + jnp.arange(row_count, dtype=jnp.int32)
    doc_ids, live_mask = document_ids(lengths, positions)
    live_col = live_mask.astype(jnp.float32)[:, None]
    prev_id = document_ids(lengths, jnp.reshape(row_offset - 1, (1,)))[0][0]
    full = gather_weights(w_qkv, w_o, w_xz, w_out, w_gate_up, w_down, w_bcdt, conv_w, norm_gains)
    (
        full_qkv,
        full_o,
        full_xz,
        full_out,
        full_gate_up,
        full_down,
        full_bcdt,
        full_conv,
        full_gains,
    ) = full
    gains_full = full_gains.astype(jnp.float32)
    inputs_x = tokens_in.astype(jnp.float32)
    normed, pull_norm = jax.vjp(rms_norm, inputs_x, gains_full[0])
    normed_low = normed.astype(jnp.bfloat16)
    qkv_proj = project(normed_low, full_qkv).astype(jnp.bfloat16)
    xz_proj = project(normed_low, full_xz)
    raw_low = xz_proj[:, :INNER].astype(jnp.bfloat16)
    gate_z = xz_proj[:, INNER:]
    bcdt_proj = project(normed_low, full_bcdt)
    reach = min(seq_total - 1, (WINDOW + row_count - 2) // row_count)
    kv_local = qkv_proj[:, D:]
    rim_rows = raw_low[row_count - (CONV - 1) :].reshape(-1, 2 * kv_width)
    kv_pieces = [kv_local]
    rim_in = None
    for shift_by in range(1, reach + 1):
        packet = jnp.concatenate([kv_local, rim_rows], axis=0) if shift_by == 1 else kv_local
        arrived = shifted(packet, "seq", shift_by)
        kv_pieces.append(arrived[:row_count])
        if shift_by == 1:
            rim_in = arrived[row_count:].reshape(CONV - 1, INNER)
    key_block = jnp.concatenate(kv_pieces, axis=0)
    key_pos = jnp.concatenate([positions - shift_by * row_count for shift_by in range(reach + 1)])
    key_ids = document_ids(lengths, key_pos)[0]
    distance = positions[:, None] - key_pos[None, :]
    allowed = (distance >= 0) & (distance < WINDOW) & (doc_ids[:, None] == key_ids[None, :])
    query_heads = (
        qkv_proj[:, :D].reshape(row_count, KV_HEADS, group_heads, HEAD).transpose(1, 2, 0, 3)
    )
    key_heads = key_block[:, :kv_width].reshape(-1, KV_HEADS, HEAD).transpose(1, 0, 2)
    value_heads = key_block[:, kv_width:].reshape(-1, KV_HEADS, HEAD).transpose(1, 0, 2)
    mixed_heads, log_totals = lax.map(
        lambda operands: head_forward(operands[0], operands[1], operands[2], allowed, scale),
        (query_heads, key_heads, value_heads),
    )
    attended_low = mixed_heads.transpose(2, 0, 1, 3).reshape(row_count, D).astype(jnp.bfloat16)
    attn_o = project(attended_low, full_o)
    rim_pos = row_offset - (CONV - 1) + jnp.arange(CONV - 1, dtype=jnp.int32)
    rim_ids = document_ids(lengths, rim_pos)[0]

    def conv_local(raw_x, raw_rim, conv_weight):
        return convolve(raw_x, raw_rim, conv_weight, doc_ids, rim_ids)

    conv_act, pull_conv = jax.vjp(
        conv_local,
        raw_low.astype(jnp.float32),
        rim_in.astype(jnp.float32),
        full_conv.astype(jnp.float32),
    )

    def summary_local(act_in, proj_in, rate_in):
        return ssm_summary(act_in, proj_in, rate_in, doc_ids, prev_id)

    (carry_end, state_end), pull_summary = jax.vjp(summary_local, conv_act, bcdt_proj, ssm_rate)
    identity = (
        jnp.ones((SSM_HEADS,), jnp.float32),
        jnp.zeros((SSM_HEADS, STATE, SSM_HEAD), jnp.float32),
    )
    prefix = carried_in((carry_end, state_end), "seq", chain_combine, identity)
    state_in = prefix[1]

    def readout_local(act_in, proj_in, rate_in, skip_in, gate_in, state_given):
        return ssm_readout(
            act_in, proj_in, rate_in, skip_in, gate_in, state_given, doc_ids, prev_id
        )

    gated, pull_read = jax.vjp(
        readout_local, conv_act, bcdt_proj, ssm_rate, ssm_skip, gate_z, state_in
    )
    gated_low = gated.astype(jnp.bfloat16)
    ssm_o = project(gated_low, full_out)
    (residual, normed_two), pull_join = jax.vjp(join_tail, inputs_x, attn_o, ssm_o, gains_full)
    normed_two_low = normed_two.astype(jnp.bfloat16)

    def swiglu_local(gate_up):
        return swiglu(gate_up, unit_block)

    ffn_act, pull_swiglu = jax.vjp(swiglu_local, project(normed_two_low, full_gate_up))
    ffn_low = ffn_act.astype(jnp.bfloat16)
    ffn_part = project_back(ffn_low, full_down)
    mixed_out = ((residual + ffn_part) * live_col).astype(jnp.bfloat16)
    full = gather_weights(w_qkv, w_o, w_xz, w_out, w_gate_up, w_down, w_bcdt, conv_w, norm_gains)
    (
        full_qkv,
        full_o,
        full_xz,
        full_out,
        full_gate_up,
        full_down,
        full_bcdt,
        full_conv,
        full_gains,
    ) = full
    d_total = cotangent.astype(jnp.float32) * live_col
    d_ffn = d_total.astype(jnp.bfloat16)
    grad_down_full = weight_grad(d_ffn, ffn_low)
    d_act = project(d_ffn, full_down)
    d_gate_up = pull_swiglu(d_act)[0].astype(jnp.bfloat16)
    grad_gate_up_full = weight_grad(normed_two_low, d_gate_up)
    d_normed_back = project_back(d_gate_up, full_gate_up)
    ffn_grads = reduce_seq(grad_gate_up_full, grad_down_full)
    ffn_grads = reduce_dp(ffn_grads[0], ffn_grads[1])
    grad_gate_up = ffn_grads[0].reshape(ffn_grads[0].shape[0], 2, -1)
    grad_down = ffn_grads[1]
    d_x_tail, d_attn_o, d_ssm_o, d_gains = pull_join((d_total, d_normed_back))
    d_attn_low = d_attn_o.astype(jnp.bfloat16)
    grad_o_full = weight_grad(attended_low, d_attn_low)
    d_attended = project_back(d_attn_low, full_o).astype(jnp.bfloat16)
    d_ssm_low = d_ssm_o.astype(jnp.bfloat16)
    grad_out_full = weight_grad(gated_low, d_ssm_low)
    d_gated = project_back(d_ssm_low, full_out)
    grad_o, grad_out = reduce_pair(grad_o_full, grad_out_full)
    d_mixed_heads = d_attended.reshape(row_count, KV_HEADS, group_heads, HEAD).transpose(1, 2, 0, 3)
    d_query_heads, d_key_heads, d_value_heads = lax.map(
        lambda operands: head_backward(
            operands[0], operands[1], operands[2], allowed, operands[3], operands[4], scale
        ),
        (query_heads, key_heads, value_heads, log_totals, d_mixed_heads),
    )
    d_queries = d_query_heads.transpose(2, 0, 1, 3).reshape(row_count, D)
    d_kv_all = jnp.concatenate(
        [
            d_key_heads.transpose(1, 0, 2).reshape(-1, kv_width),
            d_value_heads.transpose(1, 0, 2).reshape(-1, kv_width),
        ],
        axis=1,
    )
    d_act_one, d_bcdt_one, d_rate_one, d_skip, d_gate_z, d_state_in = pull_read(d_gated)
    back_prefix = carried_in_2((carry_end, d_state_in), "seq", chain_combine, identity)
    grad_end = back_prefix[1]
    d_carry = jnp.sum(grad_end * state_in, axis=(1, 2))
    d_act_two, d_bcdt_two, d_rate_two = pull_summary((d_carry, grad_end))
    d_raw, d_rim, d_conv_w = pull_conv(d_act_one + d_act_two)
    d_rate = d_rate_one + d_rate_two
    d_kv_local = d_kv_all[:row_count]
    rim_back = None
    for shift_by in range(1, reach + 1):
        d_piece = d_kv_all[shift_by * row_count : (shift_by + 1) * row_count]
        packet = (
            jnp.concatenate([d_piece, d_rim.reshape(-1, 2 * kv_width)], axis=0)
            if shift_by == 1
            else d_piece
        )
        arrived = shifted(packet.astype(jnp.bfloat16), "seq", -shift_by).astype(packet.dtype)
        d_kv_local = d_kv_local + arrived[:row_count]
        if shift_by == 1:
            rim_back = arrived[row_count:].reshape(CONV - 1, INNER)
    d_raw = d_raw.at[row_count - (CONV - 1) :].add(rim_back)
    d_xz = jnp.concatenate([d_raw, d_gate_z], axis=1).astype(jnp.bfloat16)
    grad_xz_full = weight_grad(normed_low, d_xz)
    d_normed = project_back(d_xz, full_xz)
    d_bcdt = (d_bcdt_one + d_bcdt_two).astype(jnp.bfloat16)
    grad_bcdt_full = weight_grad(normed_low, d_bcdt)
    d_normed = d_normed + project_back(d_bcdt, full_bcdt)
    d_qkv = jnp.concatenate([d_queries, d_kv_local], axis=1).astype(jnp.bfloat16)
    grad_qkv_full = weight_grad(normed_low, d_qkv)
    d_normed = d_normed + project_back(d_qkv, full_qkv)
    grad_qkv, grad_xz = reduce_pair(grad_qkv_full, grad_xz_full)
    d_x_head, d_gain_first = pull_norm(d_normed)
    input_grad = (d_x_tail + d_x_head).astype(jnp.bfloat16)
    d_gains = d_gains.at[0].add(d_gain_first)
    summed = lax.psum((grad_bcdt_full, d_conv_w, d_gains, d_rate, d_skip), ("dp", "seq"))
    dp_index = lax.axis_index("dp")
    dp_total = lax.axis_size("dp")
    model_rows = D // dp_total
    inner_cols = INNER // dp_total
    grad_bcdt = lax.dynamic_slice_in_dim(summed[0], dp_index * model_rows, model_rows, 0)
    grad_conv = lax.dynamic_slice_in_dim(summed[1], dp_index * inner_cols, inner_cols, 1)
    grad_gains = lax.dynamic_slice_in_dim(summed[2], dp_index * model_rows, model_rows, 1)
    return (
        mixed_out,
        input_grad,
        grad_gains,
        grad_qkv,
        grad_o,
        grad_xz,
        grad_bcdt,
        grad_conv,
        summed[3],
        summed[4],
        grad_out,
        grad_gate_up,
        grad_down,
    )


def solution(mesh):
    placed = (
        P(("dp", "seq"), None),
        P("dp", None),
        P(None, "dp"),
        P("dp", "seq"),
        P("dp", "seq"),
        P("dp", "seq"),
        P("dp", None),
        P(None, "dp"),
        P(),
        P(),
        P("dp", "seq"),
        P("dp", None, "seq"),
        P("dp", "seq"),
        P(("dp", "seq"), None),
    )
    return jax.shard_map(
        on_device,
        mesh=mesh,
        in_specs=placed,
        out_specs=(
            P(("dp", "seq"), None),
            P(("dp", "seq"), None),
            P(None, "dp"),
            P("dp", "seq"),
            P("dp", "seq"),
            P("dp", "seq"),
            P("dp", None),
            P(None, "dp"),
            P(),
            P(),
            P("dp", "seq"),
            P("dp", None, "seq"),
            P("dp", "seq"),
        ),
        check_vma=False,
    )
```

profile of v0, /device:TPU:0, one launch (start us, length us, event | category | flops | bytes accessed | tf_op | source)
XLA Modules:
  0.0 3825.3 jit_solution(17061880375381779816)
XLA Ops:
  27.8 62.4 %all-gather.34.cloned.1.call-done = bf16[1600,1376]{1,0:T(8,128)(2,1)} async-done(((bf16[200,1376]{1,0:T(8,128)(2,1)}), bf16[1600,1376]{1,0:T(8,128)(2,1)}) %all-gather.34.cloned.1.call-update) | async-done | bytes 4403216 | tf_op jit(solution)/shard_map/all_gather | solution.py:216
  90.3 25.5 all-gather.36.cloned.1.call-done
  122.1 15.9 all-gather.28.cloned.1.call-done
  151.6 121.8 %all-gather.32.cloned.1.call-done = bf16[1600,2752]{1,0:T(8,128)(2,1)} async-done(((bf16[200,2752]{1,0:T(8,128)(2,1)}), bf16[1600,2752]{1,0:T(8,128)(2,1)}) %all-gather.32.cloned.1.call-update) | async-done | bytes 8806416 | tf_op jit(solution)/shard_map/all_gather | solution.py:215
  274.1 26.5 all-gather.2
  300.8 30.8 all-gather.5
  331.7 32.5 all-gather.6
  408.6 105.4 %all-gather.40.cloned.1.call-done = bf16[4,1376,1600]{1,2,0:T(8,128)(2,1)} async-done(((bf16[1,1376,1600]{1,2,0:T(8,128)(2,1)}), bf16[4,1376,1600]{1,2,0:T(8,128)(2,1)}) %all-gather.40.cloned.1.call-update) | async-done | bytes 17612816 | tf_op jit(solution)/shard_map/all_gather | solution.py:224
  514.1 23.6 copy.256
  560.3 349.8 %all-gather.24.cloned.1.call-done = bf16[1600,6400]{1,0:T(8,128)(2,1)} async-done(((bf16[200,6400]{1,0:T(8,128)(2,1)}), bf16[1600,6400]{1,0:T(8,128)(2,1)}) %all-gather.24.cloned.1.call-update) | async-done | bytes 20480016 | tf_op jit(solution)/shard_map/all_gather | solution.py:213
  910.1 14.2 fusion.202
  958.6 17.4 all-gather
  987.7 33.3 fusion.81
  1039.8 25.9 all-gather.30.cloned.1.call-done
  1077.4 46.6 %while.59 = (s32[]{:T(128)}, bf16[5,5,320,64]{2,3,1,0:T(8,128)(2,1)}, f32[5,5,320]{2,1,0:T(8,128)}, bf16[5,5,320,64]{2,3,1,0:T(8,128)(2,1)S(1)}, bf16[5,1280,64]...) while((s32[]{:T(128)}, ...), condition=%wide.region_4.5_spmd.clone, body=%wide.region_1.4_spmd.clone.sunk | while | flops 551320000 | bytes 27351416 | solution.py:337
  1124.0 29.4 all-gather.26.cloned.1.call-done
  1161.1 209.7 %all-gather.38.cloned.1.call-done = bf16[4,2752,1600]{1,2,0:T(8,128)(2,1)} async-done(((bf16[1,2752,1600]{1,2,0:T(8,128)(2,1)}), bf16[4,2752,1600]{1,2,0:T(8,128)(2,1)}) %all-gather.38.cloned.1.call-update) | async-done | bytes 35225616 | tf_op jit(solution)/shard_map/all_gather | solution.py:223
  1370.8 45.2 %copy.251 = bf16[4,2752,1600]{2,1,0:T(8,128)(2,1)} copy(bf16[4,2752,1600]{1,2,0:T(8,128)(2,1)} %all-gather.38.cloned.1.call-done) | data formatting | bytes 70451200 | tf_op jit(solution)/shard_map/all_gather | solution.py:223
  1416.1 23.0 fusion.185
  1439.1 21.8 reshape.529
  1460.9 63.0 %slice_reduce_fusion.13 = (f32[320,4,1376]{2,1,0:T(4,128)}, f32[320,4,1376]{2,1,0:T(4,128)}, f32[320,4,1,1376]{3,2,1,0:T(1,128)}, f32[320,4,1,1376]{3,2,1,0:T(1,128)}) fusion(f32[320,4,2,1376]{3,2,1,0:T(2,128)} %reshape.529), kind=kLoop, calls=%fused_computation.337 | loop fusion | bytes 42270720 | tf_op jit(solution)/shard_map/jvp()/slice | solution.py:104
  1523.9 13.0 multiply_multiply_fusion
  1545.7 28.9 copy.259
  1574.6 17.6 convert_element_type.302
  1592.2 24.1 multiply_reduce_fusion.11
  1636.8 74.1 %while.60 = (s32[]{:T(128)}, bf16[5,5,320,64]{2,3,1,0:T(8,128)(2,1)S(1)}, f32[5,1280,64]{1,2,0:T(8,128)}, f32[5,1280,64]{1,2,0:T(8,128)}, bf16[5,5,320,64]{2,3,1...) while((s32[]{:T(128)}, ...), condition=%wide.region_19.21_spmd.clone, body=%wide.region_17.20_spmd.clone.sunk | while | flops 1331792384 | bytes 64930704 | solution.py:419
  1710.9 16.6 multiply_reduce_fusion.4
  1748.1 13.8 all-gather.1
  1766.6 26.7 bitcast_add_fusion.1
  1869.5 26.3 convolution_convert_fusion
  1923.4 14.5 convolution_convert_fusion.2
  1937.9 24.0 copy.296
  1966.9 15.6 convolution_convert_fusion.1
  1982.5 30.4 copy.290
  2025.9 39.3 %fusion.66 = (f32[50,320]{1,0:T(8,128)S(1)}, f32[50,320]{1,0:T(8,128)S(1)}, f32[50,320]{1,0:T(8,128)}, f32[320,320]{1,0:T(8,128)}) fusion(f32[50,320]{1,0:T(8,128)S(1)} %copy-done.69, f32[320,320]{1,0:T(8,128)S(1)} %copy-done.47, f32[50,320]{1,0:T(8,128)S(1)} %copy-done.71, pred[320,320]{1,0:T(8,128)(4,1)S(1)} %copy-done.67, ...), kind=kOutput, calls=%fused_computation.85 | convolution fusion | flops 4008809472 | bytes 9433600 | tf_op jit(solution)/shard_map/transpose(jvp(hts,shd->thd))/dot_general | solution.py:159
  2109.0 16.7 fusion.108
  2137.5 462.1 %all-reduce.37.cloned.1.call-done = bf16[1600,11008]{1,0:T(8,128)(2,1)} async-done(((bf16[1600,11008]{1,0:T(8,128)(2,1)}), bf16[1600,11008]{1,0:T(8,128)(2,1)}) %all-reduce.37.cloned.1.call-update) | async-done | bytes 35225616
  2612.5 133.2 %reduce-scatter.39.cloned.1.call-done = bf16[1376,1600]{1,0:T(8,128)(2,1)} async-done(((bf16[5504,1600]{1,0:T(8,128)(2,1)}), bf16[1376,1600]{1,0:T(8,128)(2,1)}) %reduce-scatter.39.cloned.1.call-update) | async-done | bytes 4403216
  2753.2 150.3 %reduce-scatter.35.cloned.1.call-done = bf16[1600,1600]{1,0:T(8,128)(2,1)} async-done(((bf16[6400,1600]{1,0:T(8,128)(2,1)}), bf16[1600,1600]{1,0:T(8,128)(2,1)}) %reduce-scatter.35.cloned.1.call-update) | async-done | bytes 5120016
  2915.0 14.9 fusion.98
  2929.9 107.4 %all-reduce.33.cloned.1.call-done = f32[1600,82]{0,1:T(8,128)} async-done(((f32[1600,82]{0,1:T(8,128)}), f32[1600,82]{0,1:T(8,128)}) %all-reduce.33.cloned.1.call-update) | async-done | bytes 524816 | tf_op jit(solution)/shard_map/psum | solution.py:467
  3042.2 123.5 %all-reduce.39.cloned.1.call-done = (f32[4,1600]{1,0:T(4,128)}, f32[4,3200]{1,0:T(4,128)}, f32[50]{0:T(128)}, f32[50]{0:T(128)}) async-done(((f32[4,1600]{1,0:T(4,128)}, f32[4,3200]{1,0:T(4,128)}, f32[50]{0:T(128)}, f32[50]{0:T(128)}), (f32[4,1600]{1,0:T(4,128)}, f32[4,3200]{1,0:T(4,128)}, f32[50]{0:T(128)}, f32[50]{0:T(128)})) %all-reduce.39.cloned.1.call-update) | async-done | bytes 77216 | tf_op jit(solution)/shard_map/psum | solution.py:467
  3168.4 67.7 %reduce-scatter.33.cloned.1.call-done = bf16[200,400]{1,0:T(8,128)(2,1)} async-done(((bf16[1600,400]{1,0:T(8,128)(2,1)}), bf16[200,400]{1,0:T(8,128)(2,1)}) %reduce-scatter.33.cloned.1.call-update) | async-done | bytes 160016
  3238.1 96.9 %all-reduce.35.cloned.1.call-done = bf16[1600,560]{0,1:T(8,128)(2,1)} async-done(((bf16[1600,560]{0,1:T(8,128)(2,1)}), bf16[1600,560]{0,1:T(8,128)(2,1)}) %all-reduce.35.cloned.1.call-update) | async-done | bytes 1792016
  3337.2 77.6 %reduce-scatter.37.cloned.1.call-done = bf16[400,400]{1,0:T(8,128)(2,1)} async-done(((bf16[3200,400]{1,0:T(8,128)(2,1)}), bf16[400,400]{1,0:T(8,128)(2,1)}) %reduce-scatter.37.cloned.1.call-update) | async-done | bytes 320016
  3417.0 157.9 %reduce-scatter.31.cloned.1.call-done = bf16[200,2752]{1,0:T(8,128)(2,1)} async-done(((bf16[1600,2752]{1,0:T(8,128)(2,1)}), bf16[200,2752]{1,0:T(8,128)(2,1)}) %reduce-scatter.31.cloned.1.call-update) | async-done | bytes 1100816 | tf_op jit(solution)/shard_map/reduce_scatter | solution.py:252
  3578.9 109.9 %reduce-scatter.43.cloned.1.call-done = bf16[200,1376]{1,0:T(8,128)(2,1)} async-done(((bf16[1600,1376]{1,0:T(8,128)(2,1)}), bf16[200,1376]{1,0:T(8,128)(2,1)}) %reduce-scatter.43.cloned.1.call-update) | async-done | bytes 550416
  3690.9 124.1 %reduce-scatter.41.cloned.1.call-done = bf16[200,1600]{1,0:T(8,128)(2,1)} async-done(((bf16[1600,1600]{1,0:T(8,128)(2,1)}), bf16[200,1600]{1,0:T(8,128)(2,1)}) %reduce-scatter.41.cloned.1.call-update) | async-done | bytes 640016
  (619 shorter events, 602.1 us)
Async XLA Ops:
  7.2 83.0 %all-gather.34.cloned.1.call-start = ((), (), s32[]{:S(2)}) async-start(), calls=%async_computation.16 | async-start | bytes 5068800 | tf_op jit(solution)/shard_map/all_gather | solution.py:216
  7.9 107.8 %all-gather.36.cloned.1.call-start = ((), (), s32[]{:S(2)}) async-start(), calls=%async_computation.22 | async-start | bytes 3328000 | tf_op jit(solution)/shard_map/all_gather | solution.py:207
  8.7 129.3 %all-gather.28.cloned.1.call-start = ((), (), s32[]{:S(2)}) async-start(), calls=%async_computation.13 | async-start | bytes 2048000 | tf_op jit(solution)/shard_map/all_gather | solution.py:208
  10.7 262.8 %all-gather.32.cloned.1.call-start = ((), (), s32[]{:S(2)}) async-start(), calls=%async_computation.15 | async-start | bytes 10137600 | tf_op jit(solution)/shard_map/all_gather | solution.py:215
  14.3 379.1 %all-gather.22.cloned.1.call-start = ((), (), s32[]{:S(2)}) async-start(), calls=%async_computation.10 | async-start | bytes 8294400 | tf_op jit(solution)/shard_map/all_gather | solution.py:211
  27.7 486.3 %all-gather.40.cloned.1.call-start = ((), (), s32[]{:S(2)}) async-start(), calls=%async_computation.24 | async-start | bytes 22528000 | tf_op jit(solution)/shard_map/all_gather | solution.py:224
  90.2 819.9 %all-gather.24.cloned.1.call-start = ((), (), s32[]{:S(2)}) async-start(), calls=%async_computation.11 | async-start | bytes 23040000 | tf_op jit(solution)/shard_map/all_gather | solution.py:213
  122.0 943.6 %all-gather.30.cloned.1.call-start = ((), (), s32[]{:S(2)}) async-start(), calls=%async_computation.14 | async-start | bytes 11980800 | tf_op jit(solution)/shard_map/all_gather | solution.py:214
  141.5 1011.9 %all-gather.26.cloned.1.call-start = ((), (), s32[]{:S(2)}) async-start(), calls=%async_computation.12 | async-start | bytes 5990400 | tf_op jit(solution)/shard_map/all_gather | solution.py:212
  151.6 1219.2 %all-gather.38.cloned.1.call-start = ((), (), s32[]{:S(2)}) async-start(), calls=%async_computation.23 | async-start | bytes 45056000 | tf_op jit(solution)/shard_map/all_gather | solution.py:223
  273.5 91.8 %copy-start.14 = (bf16[320,1600]{1,0:T(8,128)(2,1)S(1)}, bf16[320,1600]{1,0:T(8,128)(2,1)}, u32[]{:S(2)}) copy-start(bf16[320,1600]{1,0:T(8,128)(2,1)} %param.27) | copy-start | bytes 3072004
  273.5 92.8 %copy-start.121 = (f32[50]{0:T(128)S(1)}, f32[50]{0:T(128)}, u32[]{:S(2)}) copy-start(f32[50]{0:T(128)} %param.35) | copy-start | bytes 604
  273.5 94.9 %copy-start.120 = (s32[1,2]{1,0:T(1,128)S(1)}, s32[1,2]{1,0:T(1,128)}, u32[]{:S(2)}) copy-start(s32[1,2]{1,0:T(1,128)} %param.28) | copy-start | bytes 28
  273.5 1853.0 %reduce-scatter.27.cloned.1.call-start = ((), (), s32[]{:S(2)}) async-start(), calls=%async_computation.18 | async-start | bytes 6656000 | tf_op jit(solution)/shard_map/reduce_scatter | solution.py:241
  365.3 544.8 %copy-start.85 = (f32[1600]{0:T(1024)}, f32[1600]{0:T(1024)S(1)}, u32[]{:S(2)}) copy-start(f32[1600]{0:T(1024)S(1)} %get-tuple-element.516) | copy-start | bytes 19204
  366.2 617.3 %copy-start.24 = (f32[320,82]{0,1:T(8,128)}, f32[320,82]{0,1:T(8,128)S(1)}, u32[]{:S(2)}) copy-start(f32[320,82]{0,1:T(8,128)S(1)} %fusion.191) | copy-start | bytes 314884
  366.3 585.2 %copy-start.52 = (f32[320,16]{0,1:T(8,128)}, f32[320,16]{0,1:T(8,128)S(1)}, u32[]{:S(2)}) copy-start(f32[320,16]{0,1:T(8,128)S(1)} %slice.274) | copy-start | bytes 61444
  385.1 152.6 %copy-start.108 = (f32[320]{0:T(512)}, f32[320]{0:T(512)S(1)}, u32[]{:S(2)}) copy-start(f32[320]{0:T(512)S(1)} %fusion.167) | copy-start | bytes 3844
  387.3 547.0 %copy-start.59 = (f32[3200]{0:T(1024)}, f32[3200]{0:T(1024)S(1)}, u32[]{:S(2)}) copy-start(f32[3200]{0:T(1024)S(1)} %get-tuple-element.509) | copy-start | bytes 38404
  391.3 560.2 %copy-start.27 = (f32[320,50]{0,1:T(8,128)}, f32[320,50]{0,1:T(8,128)S(1)}, u32[]{:S(2)}) copy-start(f32[320,50]{0,1:T(8,128)S(1)} %get-tuple-element.623) | copy-start | bytes 192004
  391.3 596.4 %copy-start.40 = (f32[320,50]{0,1:T(8,128)}, f32[320,50]{0,1:T(8,128)S(1)}, u32[]{:S(2)}) copy-start(f32[320,50]{0,1:T(8,128)S(1)} %get-tuple-element.624) | copy-start | bytes 192004
  400.6 626.1 %collective-permute-start.2 = (bf16[320,640]{1,0:T(8,128)(2,1)S(1)}, bf16[320,640]{1,0:T(8,128)(2,1)}, u32[]{:S(2)}, u32[]{:S(2)}) collective-permute-start(bf16[320,640]{1,0:T(8,128)(2,1)S(1)} %slice.254), channel_id=1, source_target_pairs={{0,3},{4,7},{8,11},{12,15},{16,19},{20,23},{24,27},{28,31}} | collective-permute-start | bytes 1228808 | tf_op jit(solution)/shard_map/ppermute | solution.py:27
  403.9 622.9 %collective-permute-start.1 = (bf16[320,640]{1,0:T(8,128)(2,1)S(1)}, bf16[320,640]{1,0:T(8,128)(2,1)}, u32[]{:S(2)}, u32[]{:S(2)}) collective-permute-start(bf16[320,640]{1,0:T(8,128)(2,1)S(1)} %slice.254), channel_id=1, source_target_pairs={{0,2},{1,3},{4,6},{5,7},{8,10},{9,11},{12,14},{13,15},{16,18},{17,... | collective-permute-start | bytes 1228808 | tf_op jit(solution)/shard_map/ppermute | solution.py:27
  550.4 359.7 %copy-start.105 = (f32[320]{0:T(512)S(1)}, f32[320]{0:T(512)}, u32[]{:S(2)}) copy-start(f32[320]{0:T(512)} %copy-done.104) | copy-start | bytes 3844
  926.3 5.8 collective-permute-start
  1158.8 257.2 %copy-start.102 = (f32[320]{0:T(512)}, f32[320]{0:T(512)S(1)}, u32[]{:S(2)}) copy-start(f32[320]{0:T(512)S(1)} %get-tuple-element.634) | copy-start | bytes 3844
  1161.1 455.2 %copy-start.112 = (f32[320]{0:T(512)}, f32[320]{0:T(512)S(1)}, u32[]{:S(2)}) copy-start(f32[320]{0:T(512)S(1)} %fusion.174) | copy-start | bytes 3844
  1161.1 255.0 %copy-start.88 = (f32[1600]{0:T(1024)S(1)}, f32[1600]{0:T(1024)}, u32[]{:S(2)}) copy-start(f32[1600]{0:T(1024)} %get-tuple-element.513) | copy-start | bytes 19204
  1710.9 419.2 %reduce-scatter.25.cloned.1.call-start = ((), (), s32[]{:S(2)}) async-start(), calls=%async_computation.17 | async-start | bytes 9318400 | tf_op jit(solution)/shard_map/reduce_scatter | solution.py:241
  1823.8 4.0 collective-permute-start.3
  1825.3 13.6 collective-permute-start.5
  1826.6 19.7 collective-permute-start.4
  1855.8 274.9 %reduce-scatter.29.cloned.1.call-start = ((), (), s32[]{:S(2)}) async-start(), calls=%async_computation.20 | async-start | bytes 12800000 | tf_op jit(solution)/shard_map/reduce_scatter | solution.py:244
  1867.8 731.9 %all-reduce.37.cloned.1.call-start = ((), (), s32[]{:S(2)}) async-start(), calls=%async_computation.30 | async-start | bytes 70451200
  1895.8 850.0 %reduce-scatter.39.cloned.1.call-start = ((), (), s32[]{:S(2)}) async-start(), calls=%async_computation.28 | async-start | bytes 22896640
  1961.9 941.7 %reduce-scatter.35.cloned.1.call-start = ((), (), s32[]{:S(2)}) async-start(), calls=%async_computation.26 | async-start | bytes 26624000
  2012.9 1024.4 %all-reduce.33.cloned.1.call-start = ((), (), s32[]{:S(2)}) async-start(), calls=%async_computation.19 | async-start | bytes 1171456 | tf_op jit(solution)/shard_map/psum | solution.py:467
  2099.7 1066.0 %all-reduce.39.cloned.1.call-start = ((), (), s32[]{:S(2)}) async-start(), calls=%async_computation.33 | async-start | bytes 157696 | tf_op jit(solution)/shard_map/psum | solution.py:467
  2126.4 1109.7 %reduce-scatter.33.cloned.1.call-start = ((), (), s32[]{:S(2)}) async-start(), calls=%async_computation.25 | async-start | bytes 1843200
  2130.0 1205.0 %all-reduce.35.cloned.1.call-start = ((), (), s32[]{:S(2)}) async-start(), calls=%async_computation.29 | async-start | bytes 3727360
  2130.6 1284.1 %reduce-scatter.37.cloned.1.call-start = ((), (), s32[]{:S(2)}) async-start(), calls=%async_computation.27 | async-start | bytes 3686400
  2136.2 1438.7 %reduce-scatter.31.cloned.1.call-start = ((), (), s32[]{:S(2)}) async-start(), calls=%async_computation.21 | async-start | bytes 10137600 | tf_op jit(solution)/shard_map/reduce_scatter | solution.py:252
  2612.5 1076.3 %reduce-scatter.43.cloned.1.call-start = ((), (), s32[]{:S(2)}) async-start(), calls=%async_computation.32 | async-start | bytes 5068800
  2753.2 1061.8 %reduce-scatter.41.cloned.1.call-start = ((), (), s32[]{:S(2)}) async-start(), calls=%async_computation.31 | async-start | bytes 5990400
  2915.0 124.0 %copy-start.101 = (f32[320]{0:T(512)S(1)}, f32[320]{0:T(512)}, u32[]{:S(2)}) copy-start(f32[320]{0:T(512)} %copy-done.100) | copy-start | bytes 3844
  2915.0 124.0 %copy-start.9 = (f32[320,1600]{1,0:T(8,128)S(1)}, f32[320,1600]{1,0:T(8,128)}, u32[]{:S(2)}) copy-start(f32[320,1600]{1,0:T(8,128)} %copy-done.8) | copy-start | bytes 6144004
  3416.0 401.3 %copy-start.126 = (f32[50]{0:T(128)S(1)}, f32[50]{0:T(128)}, u32[]{:S(2)}) copy-start(f32[50]{0:T(128)} %get-tuple-element.988) | copy-start | bytes 604
  3416.0 401.8 %copy-start.125 = (f32[50]{0:T(128)S(1)}, f32[50]{0:T(128)}, u32[]{:S(2)}) copy-start(f32[50]{0:T(128)} %get-tuple-element.989) | copy-start | bytes 604
  (116 other events, 1694.2 us)
Sparse Core Ops, SparseCore 0:
  10.2 79.9 all-gather.33
  91.7 23.9 all-gather.35
  117.9 20.0 all-gather.27
  140.6 132.8 all-gather.31
  276.1 117.2 all-gather.21
  394.8 119.2 all-gather.39
  515.6 394.4 all-gather.23
  912.8 152.8 all-gather.29
  1067.9 85.4 all-gather.25
  1154.8 215.9 all-gather.37
  1711.0 56.3 reduce-scatter.26
  1855.9 66.4 reduce-scatter.24
  1925.0 87.4 reduce-scatter.28
  2014.9 584.7 all-reduce.36
  2602.3 143.4 reduce-scatter.38
  2748.2 155.2 reduce-scatter.34
  2910.1 127.2 all-reduce.32
  3044.4 121.1 all-reduce.38
  3169.1 66.9 reduce-scatter.32
  3240.0 94.9 all-reduce.34
  3339.0 75.7 reduce-scatter.36
  3418.3 156.6 reduce-scatter.30
  3578.8 109.9 reduce-scatter.42
  3692.5 122.4 reduce-scatter.40
where the time goes:
time: 3840 us; the launch traced here: 3830 us
  waiting for transfers between devices  2580 us (67%)
  matrix products  471 us (12%)
  local copies, waits for them, and re-layouts  437 us (11%)
  other arithmetic  154 us (4%)
  blocking collectives  152 us (4%)
    unnamed x32, waiting for transfers between devices  1220 us
    all_gather x1, waiting for transfers between devices, gather_weights(): lax.all_gather(wide[2], 'dp', axis=0, tiled=True)  350 us
    psum x2, waiting for transfers between devices, on_device(): lax.psum((grad_bcdt_full, d_conv_w, d_gains, d_rate, d_skip), ('dp', 'seq'))  231 us
    all_gather x1, waiting for transfers between devices, gather_weights(): lax.all_gather(full[4], 'seq', axis=1, tiled=True)  210 us
    reduce_scatter x1, waiting for transfers between devices, reduce_dp(): lax.psum_scatter(first_grad.astype(jnp.bfloat16), 'dp', scatter_dimension...  158 us
    unnamed x294, local copies, waits for them, and re-layouts  122 us
    all_gather x1, waiting for transfers between devices, gather_weights(): lax.all_gather(gate_up_flat, 'dp', axis=0, tiled=True)  122 us
    all_gather x1, waiting for transfers between devices, gather_weights(): lax.all_gather(full[5], 'seq', axis=1, tiled=True)  105 us
  transfers between devices with their start and end apart: 30, of which 23 were waited for; matrix products, arithmetic and copies ran while one was open for 18% of the time, Pallas kernels for 0%

commit v1 on v0

v1 whole, which is shorter than its diff:
```python
import jax
import jax.numpy as jnp
from jax import lax
from jax.sharding import PartitionSpec as P

D = 1600
HEADS = 25
KV_HEADS = 5
HEAD = 64
INNER = 3200
SSM_HEAD = 64
STATE = 16
CONV = 4
FF = 5504
WINDOW = 1024
SSM_HEADS = 50

NORM_EPS = 1e-05
MASKED = -1e30
LOW = jnp.bfloat16
FULL = jnp.float32

SEQ = 4
GROUP_HEADS = HEADS // KV_HEADS
QW = GROUP_HEADS * HEAD
LOCAL_HEADS = 13
LOCAL_CH = LOCAL_HEADS * SSM_HEAD
CHUNK = 128
UNITS = FF // SEQ
UNITS_PAD = 1408
BCDT_PAD = 128
OUT_AT, O_AT, O5_AT, OUT_WIDTH = 0, 896, 1280, 1600
FIRST_HEAD = tuple((SSM_HEADS * s // 2 + 1) // 2 for s in range(SEQ))
HEAD_COUNT = tuple(b - a for a, b in zip(FIRST_HEAD, FIRST_HEAD[1:] + (SSM_HEADS,)))


def swap(value, axis, bit):
    return lax.ppermute(value, axis, [(i, i ^ bit) for i in range(lax.axis_size(axis))])


def hop(value, step, senders):
    return lax.ppermute(
        value, "dp", [(2 * z + x, 2 * (z + step) + x) for z in senders for x in (0, 1)]
    )


def place(blocks):
    stacked = jnp.zeros((len(blocks),) + blocks[0][1].shape, blocks[0][1].dtype)
    for index, block in blocks:
        stacked = lax.dynamic_update_index_in_dim(stacked, block, index, 0)
    return stacked


def gather_seq(block):
    me = lax.axis_index("seq")
    far = swap(block, "seq", 2)
    near = swap(block, "seq", 1)
    near_far = swap(far, "seq", 1)
    return place([(me, block), (me ^ 1, near), (me ^ 2, far), (me ^ 3, near_far)])


def scatter_seq(rows, out_dtype):
    me = lax.axis_index("seq")
    core, far = me % 2, me // 2
    by_core = rows.reshape((2, 2) + rows.shape[1:])
    give = lax.dynamic_index_in_dim(by_core, 1 - core, 1, False)
    keep = lax.dynamic_index_in_dim(by_core, core, 1, False)
    got = swap(give, "seq", 1)
    give_far = (
        lax.dynamic_index_in_dim(keep, 1 - far, 0, False).astype(FULL)
        + lax.dynamic_index_in_dim(got, 1 - far, 0, False).astype(FULL)
    ).astype(LOW)
    got_far = swap(give_far, "seq", 2)
    return (
        lax.dynamic_index_in_dim(keep, far, 0, False).astype(FULL)
        + lax.dynamic_index_in_dim(got, far, 0, False).astype(FULL)
        + got_far.astype(FULL)
    ).astype(out_dtype)


def gather_dp(block):
    count = lax.axis_size("dp")
    if count != 8:
        return lax.all_gather(block, "dp", axis=0)
    line = count // 2
    me = lax.axis_index("dp")
    z, x = me // 2, me % 2
    up, down = [block], [block]
    for k in range(1, line):
        up.append(hop(up[-1], 1, range(k - 1, line - 1)))
        down.append(hop(down[-1], -1, range(1, line - k + 1)))
    placed = []
    for j in range(line):
        held = block if j == 0 else jnp.where(z + j < line, down[j], up[line - j])
        other = swap(held, "dp", 1)
        at = 2 * lax.rem(z + j, line)
        placed += [(at + x, held), (at + 1 - x, other)]
    return place(placed)


def scatter_dp(parts):
    count = lax.axis_size("dp")
    parts = parts.astype(LOW)
    if count != 8:
        summed = lax.psum_scatter(parts, "dp", scatter_dimension=0)
        return lax.optimization_barrier(summed).astype(FULL)
    line = count // 2
    me = lax.axis_index("dp")
    z, x = me // 2, me % 2
    grid = parts.reshape((line, 2) + parts.shape[1:])
    got = swap(lax.dynamic_index_in_dim(grid, 1 - x, 1, False), "dp", 1)
    part = lax.dynamic_index_in_dim(grid, x, 1, False).astype(FULL) + got.astype(FULL)
    part = part.astype(LOW)

    def own(t):
        return lax.dynamic_index_in_dim(part, jnp.clip(t, 0, line - 1), 0, False).astype(FULL)

    up = down = None
    for k in range(1, line):
        send_up, send_down = own(line - k + z), own(z - (line - k))
        if k > 1:
            send_up, send_down = send_up + up.astype(FULL), send_down + down.astype(FULL)
        up = hop(send_up.astype(LOW), 1, range(0, k))
        down = hop(send_down.astype(LOW), -1, range(line - k, line))
    return own(z) + up.astype(FULL) + down.astype(FULL)


def sum_all(value):
    for axis in ("seq", "dp"):
        bit = 1
        while bit < lax.axis_size(axis):
            value = value + swap(value, axis, bit)
            bit *= 2
    return value


def mm(left, right):
    return jnp.dot(left, right, preferred_element_type=FULL)


def mm_nt(left, right):
    return lax.dot_general(left, right, (((1,), (1,)), ((), ())), preferred_element_type=FULL)


def mm_tn(left, right):
    return lax.dot_general(left, right, (((0,), (0,)), ((), ())), preferred_element_type=FULL)


def rms_norm(values, gain):
    return values * lax.rsqrt(jnp.mean(values * values, axis=-1, keepdims=True) + NORM_EPS) * gain


def join_tail(inputs_x, attn_o, ssm_o, gains):
    residual = inputs_x + 0.5 * (rms_norm(attn_o, gains[1]) + rms_norm(ssm_o, gains[2]))
    return (residual, rms_norm(residual, gains[3]))


def document_ids(lengths, positions):
    first_end = lengths[0]
    second_end = lengths[0] + lengths[1]
    return (positions >= first_end).astype(jnp.int32) + (positions >= second_end).astype(jnp.int32)


def convolve(raw_x, conv_weight, doc_ids):
    row_count = raw_x.shape[0]
    padded = jnp.pad(raw_x, ((CONV - 1, 0), (0, 0)))
    padded_ids = jnp.pad(doc_ids, (CONV - 1, 0), constant_values=-1)
    conv_sum = jnp.zeros(raw_x.shape, FULL)
    for tap in range(CONV):
        same = (padded_ids[tap : tap + row_count] == doc_ids).astype(FULL)
        conv_sum = conv_sum + conv_weight[tap] * padded[tap : tap + row_count] * same[:, None]
    return jax.nn.silu(conv_sum)


def allowed_block(row_ids, row_pos, key_ids, key_pos):
    distance = row_pos[:, None] - key_pos[None, :]
    return (distance >= 0) & (distance < WINDOW) & (row_ids[:, None] == key_ids[None, :])


def head_forward(q, k, v, allowed):
    scale = HEAD ** (-0.5)
    scores = scale * jnp.einsum("gtd,sd->gts", q, k, preferred_element_type=FULL)
    scores = jnp.where(allowed[None], scores, MASKED)
    top = jnp.max(scores, axis=-1, keepdims=True)
    expos = jnp.exp(scores - top)
    denom = jnp.sum(expos, axis=-1, keepdims=True)
    weights = (expos / denom).astype(LOW)
    mixed = jnp.einsum("gts,sd->gtd", weights, v, preferred_element_type=FULL)
    return mixed, top + jnp.log(denom)


def head_backward(q, k, v, allowed, log_total, d_mixed):
    scale = HEAD ** (-0.5)
    scores = scale * jnp.einsum("gtd,sd->gts", q, k, preferred_element_type=FULL)
    probs = jnp.where(allowed[None], jnp.exp(scores - log_total), 0.0)
    d_v = jnp.einsum("gts,gtd->sd", probs.astype(LOW), d_mixed, preferred_element_type=FULL)
    d_probs = jnp.einsum("gtd,sd->gts", d_mixed, v, preferred_element_type=FULL)
    d_scores = probs * (d_probs - jnp.sum(probs * d_probs, axis=-1, keepdims=True))
    d_low = d_scores.astype(LOW)
    d_q = scale * jnp.einsum("gts,sd->gtd", d_low, k, preferred_element_type=FULL)
    d_k = scale * jnp.einsum("gts,gtd->sd", d_low, q, preferred_element_type=FULL)
    return d_q, d_k, d_v


def to_heads(block):
    return block.reshape(block.shape[0], GROUP_HEADS, HEAD).transpose(1, 0, 2)


def from_heads(block):
    return block.transpose(1, 0, 2).reshape(block.shape[1], QW)


def attention_steps(rows, seq_index, doc_ids):
    positions = jnp.arange(doc_ids.shape[0], dtype=jnp.int32)
    steps = []
    for t in range(SEQ + 1):
        last = t == SEQ
        extent = (SEQ if last else t + 1) * rows
        at = seq_index * rows if last else t * rows
        allowed = allowed_block(
            lax.dynamic_slice_in_dim(doc_ids, at, rows),
            lax.dynamic_slice_in_dim(positions, at, rows),
            doc_ids[:extent],
            positions[:extent],
        )
        steps.append((t, 1 if last else 0, extent, allowed))
    return steps


def attention_forward(queries, kv, steps, rows):
    out, logs = [], []
    for t, which, extent, allowed in steps:
        k = kv[:extent, which * 128 : which * 128 + 64]
        v = kv[:extent, which * 128 + 64 : which * 128 + 128]
        mixed, log_total = head_forward(to_heads(queries[t * rows : (t + 1) * rows]), k, v, allowed)
        out.append(from_heads(mixed).astype(LOW))
        logs.append(log_total)
    return jnp.concatenate(out), logs


def attention_backward(queries, kv, logs, d_out, steps, rows):
    d_q = []
    d_k = [jnp.zeros((kv.shape[0], HEAD), FULL) for _ in range(2)]
    d_v = [jnp.zeros((kv.shape[0], HEAD), FULL) for _ in range(2)]
    for (t, which, extent, allowed), log_total in zip(steps, logs):
        k = kv[:extent, which * 128 : which * 128 + 64]
        v = kv[:extent, which * 128 + 64 : which * 128 + 128]
        part = slice(t * rows, (t + 1) * rows)
        q_one, k_one, v_one = head_backward(
            to_heads(queries[part]), k, v, allowed, log_total, to_heads(d_out[part])
        )
        d_q.append(from_heads(q_one))
        d_k[which] = d_k[which].at[:extent].add(k_one)
        d_v[which] = d_v[which].at[:extent].add(v_one)
    d_kv = jnp.concatenate([d_k[0], d_v[0], d_k[1], d_v[1]], axis=1)
    return jnp.concatenate(d_q).astype(LOW), d_kv.astype(LOW)


def ssm_group(conv_act, bcdt, rate, skip, gate_z, doc_ids):
    total = conv_act.shape[0]
    chunks = total // CHUNK
    heads = rate.shape[0]
    low = lambda v: v.astype(LOW)
    ein = lambda spec, *v: jnp.einsum(spec, *v, preferred_element_type=FULL)
    ids = doc_ids.reshape(chunks, CHUNK)
    ids_prev = jnp.concatenate([jnp.full((1,), -1, jnp.int32), ids[:-1, -1]])
    step = jax.nn.softplus(bcdt[:, 2 * STATE : 2 * STATE + heads]).reshape(chunks, CHUNK, heads)
    b_in = bcdt[:, :STATE].reshape(chunks, CHUNK, STATE)
    c_in = bcdt[:, STATE : 2 * STATE].reshape(chunks, CHUNK, STATE)
    x = conv_act.reshape(chunks, CHUNK, heads, SSM_HEAD)
    log = jnp.cumsum(-step * rate, axis=1)
    places = jnp.arange(CHUNK, dtype=jnp.int32)
    causal = (places[:, None] >= places[None, :])[None] & (ids[:, :, None] == ids[:, None, :])
    log_h = log.transpose(0, 2, 1)
    gap = log_h[:, :, :, None] - log_h[:, :, None, :]
    decays = jnp.where(causal[:, None], jnp.exp(jnp.where(causal[:, None], gap, 0.0)), 0.0)
    gram = ein("ctn,csn->cts", low(c_in), low(b_in))
    mixing = decays * gram[:, None]
    step_x = low(x * step[..., None])
    within = ein("chts,cshd->cthd", low(mixing), step_x)
    last = log[:, -1]
    ends = jnp.exp(last[:, None] - log) * (ids == ids[:, -1:]).astype(FULL)[..., None]
    state_end = ein("cshd,csn->chnd", low(x * (step * ends)[..., None]), low(b_in))
    carry = jnp.exp(last) * (ids[:, -1] == ids_prev).astype(FULL)[:, None]
    state = jnp.zeros(state_end.shape[1:], FULL)
    states = []
    for c in range(chunks):
        states.append(state)
        state = carry[c][:, None, None] * state + state_end[c]
    states = jnp.stack(states)
    reach = jnp.exp(log) * (ids == ids_prev[:, None]).astype(FULL)[..., None]
    from_state = ein("ctn,chnd->cthd", low(c_in), low(states)) * reach[..., None]
    read = within + from_state + skip[:, None] * x
    return read.reshape(total, heads * SSM_HEAD) * jax.nn.silu(gate_z)


def pick(options, seq_index):
    return lax.select_n(seq_index, *options)


def own_cut(values, seq_index, axis, unit):
    cuts = []
    for first, count in zip(FIRST_HEAD, HEAD_COUNT):
        cut = lax.slice_in_dim(values, first * unit, (first + count) * unit, axis=axis)
        pads = [(0, 0)] * values.ndim
        pads[axis] = (0, (LOCAL_HEADS - count) * unit)
        cuts.append(jnp.pad(cut, pads))
    return pick(cuts, seq_index)


def own_spread(values, seq_index, unit):
    spreads = []
    for first, count in zip(FIRST_HEAD, HEAD_COUNT):
        pads = [(0, 0)] * (values.ndim - 1) + [(first * unit, (SSM_HEADS - first - count) * unit)]
        spreads.append(jnp.pad(values[..., : count * unit], pads))
    return pick(spreads, seq_index)


def channel_cut(wide, seq_index, axis):
    return own_cut(wide, seq_index, axis, SSM_HEAD)


def bcdt_cut(w_bcdt, seq_index):
    first = pick([jnp.int32(h) for h in FIRST_HEAD], seq_index)
    count = pick([jnp.int32(c) for c in HEAD_COUNT], seq_index)
    source = jnp.arange(w_bcdt.shape[1], dtype=jnp.int32)[:, None]
    target = jnp.arange(BCDT_PAD, dtype=jnp.int32)[None]
    shared = (target < 2 * STATE) & (source == target)
    steps = (target >= 2 * STATE) & (target < 2 * STATE + count) & (source == target + first)
    return mm(w_bcdt, (shared | steps).astype(LOW)).astype(LOW)


def wide_of(gathered):
    return gathered.transpose(1, 0, 2).reshape(gathered.shape[1], -1)


def on_device(
    tokens_in,
    doc_lengths,
    norm_gains,
    w_qkv,
    w_o,
    w_xz,
    w_bcdt,
    conv_w,
    ssm_rate,
    ssm_skip,
    w_out,
    w_gate_up,
    w_down,
    cotangent,
):
    rows = tokens_in.shape[0]
    group = rows * SEQ
    s = lax.axis_index("seq")
    dp_index = lax.axis_index("dp")
    dp_total = lax.axis_size("dp")
    block_rows = w_qkv.shape[0]
    kv_width = KV_HEADS * HEAD
    lengths = doc_lengths[0]
    doc_ids = document_ids(lengths, jnp.arange(group, dtype=jnp.int32))
    live = (jnp.arange(rows, dtype=jnp.int32) + s * rows < lengths[0] + lengths[1]).astype(FULL)[:, None]

    gains_block = norm_gains.shape[1]
    conv_block = conv_w.shape[1]
    width = -(-max(conv_block, gains_block) // 128) * 128
    small = jnp.concatenate(
        [
            jnp.pad(conv_w, ((0, 4), (0, width - conv_block))),
            jnp.pad(norm_gains, ((0, 4), (0, width - gains_block))),
        ]
    )
    small = gather_dp(small)
    full_conv = small[:, :4, :conv_block].transpose(1, 0, 2).reshape(4, INNER).astype(FULL)
    gains = small[:, 8:12, :gains_block].transpose(1, 0, 2).reshape(4, D).astype(FULL)

    tokens_group = gather_seq(tokens_in).reshape(group, D)
    qkv_wide = wide_of(gather_seq(w_qkv))
    q_at = lambda h: lax.dynamic_slice_in_dim(qkv_wide, h * QW, QW, 1)
    kv_at = lambda h: [
        lax.dynamic_slice_in_dim(qkv_wide, D + h * HEAD, HEAD, 1),
        lax.dynamic_slice_in_dim(qkv_wide, D + kv_width + h * HEAD, HEAD, 1),
    ]
    qkv_packet = jnp.concatenate(kv_at(s) + kv_at(KV_HEADS - 1) + [q_at(s), q_at(KV_HEADS - 1)], axis=1)
    full_qkv = gather_dp(qkv_packet).reshape(D, -1)

    xz_wide = wide_of(gather_seq(w_xz))
    bcdt_own = bcdt_cut(w_bcdt, s)
    xz_packet = jnp.concatenate(
        [
            channel_cut(xz_wide[:, :INNER], s, 1),
            channel_cut(xz_wide[:, INNER:], s, 1),
            bcdt_own,
        ],
        axis=1,
    )
    full_xz = gather_dp(xz_packet).reshape(D, -1)

    out_block = w_out.shape[0]
    out_cols = gather_dp(jnp.concatenate([w_o, w_out], axis=0))
    o_cols = out_cols[:, :block_rows].reshape(D, -1)
    mamba_cols = out_cols[:, block_rows:].reshape(INNER, -1)

    def rows_for(peer):
        return jnp.concatenate(
            [
                jnp.pad(channel_cut(mamba_cols, peer, 0).T, ((0, 0), (0, O_AT - LOCAL_CH))),
                jnp.pad(
                    lax.dynamic_slice_in_dim(o_cols, peer * QW, QW, 0).T, ((0, 0), (0, O5_AT - O_AT - QW))
                ),
                o_cols[(KV_HEADS - 1) * QW :].T,
            ],
            axis=1,
        )

    out_t = place(
        [(s, rows_for(s))] + [(s ^ bit, swap(rows_for(s ^ bit), "seq", bit)) for bit in (1, 2, 3)]
    ).reshape(D, OUT_WIDTH)
    w_out_t = out_t[:, :LOCAL_CH]
    w_o_t = out_t[:, O_AT : O_AT + QW]
    w_o5_t = out_t[:, O5_AT:]

    gate_up_packet = jnp.pad(w_gate_up, ((0, 0), (0, 0), (0, UNITS_PAD - UNITS))).reshape(block_rows, -1)
    full_gate_up = gather_dp(gate_up_packet).reshape(D, -1)
    full_down = gather_dp(jnp.pad(w_down, ((0, 0), (0, UNITS_PAD - UNITS)))).reshape(D, -1)

    d_total = cotangent.astype(FULL) * live
    d_ffn_group = gather_seq(d_total.astype(LOW)).reshape(group, D)

    own = lambda a: lax.dynamic_slice_in_dim(a, s * rows, rows, 0)
    normed = rms_norm(tokens_group.astype(FULL), gains[0]).astype(LOW)
    normed_own = own(normed)
    kvq = mm(normed, full_qkv[:, : 256 + QW]).astype(LOW)
    q_last = mm(normed_own, full_qkv[:, 256 + QW :]).astype(LOW)
    queries = jnp.concatenate([kvq[:, 256:], q_last])
    kv = kvq[:, :256]
    steps = attention_steps(rows, s, doc_ids)
    attended, logs = attention_forward(queries, kv, steps, rows)
    attn_part = mm_nt(attended[:group], w_o_t).astype(LOW)
    attn_o = scatter_seq(attn_part.reshape(SEQ, rows, D), FULL) + mm_nt(attended[group:], w_o5_t)

    xzb = mm(normed, full_xz)
    raw_x = xzb[:, :LOCAL_CH].astype(LOW)
    gate_z = xzb[:, LOCAL_CH : 2 * LOCAL_CH]
    bcdt = xzb[:, 2 * LOCAL_CH :]
    conv_own = channel_cut(full_conv, s, 1)
    rate = own_cut(ssm_rate, s, 0, 1)
    skip = own_cut(ssm_skip, s, 0, 1)
    conv_act, pull_conv = jax.vjp(
        lambda a, w: convolve(a, w, doc_ids), raw_x.astype(FULL), conv_own
    )
    gated, pull_ssm = jax.vjp(
        lambda *v: ssm_group(*v, doc_ids), conv_act, bcdt, rate, skip, gate_z
    )
    gated = gated.astype(LOW)
    ssm_part = mm_nt(gated, w_out_t).astype(LOW)
    ssm_o = scatter_seq(ssm_part.reshape(SEQ, rows, D), FULL)

    inputs_x = tokens_in.astype(FULL)
    (residual, normed_two), pull_join = jax.vjp(join_tail, inputs_x, attn_o, ssm_o, gains)
    normed_two = gather_seq(normed_two.astype(LOW)).reshape(group, D)
    gate_up = mm(normed_two, full_gate_up)
    ffn_gate, ffn_up = gate_up[:, :UNITS_PAD], gate_up[:, UNITS_PAD:]
    ffn_act = (jax.nn.silu(ffn_gate) * ffn_up).astype(LOW)
    ffn_part = mm_nt(ffn_act, full_down).astype(LOW)
    ffn_own = scatter_seq(ffn_part.reshape(SEQ, rows, D), FULL)
    mixed_out = ((residual + ffn_own) * live).astype(LOW)

    d_act = mm(d_ffn_group, full_down)
    sig = jax.nn.sigmoid(ffn_gate)
    d_gate = d_act * ffn_up * (sig * (1.0 + ffn_gate * (1.0 - sig)))
    d_up = d_act * ffn_gate * sig
    d_gate_up = jnp.concatenate([d_gate.astype(LOW), d_up.astype(LOW)], axis=1)
    d_two_part = mm_nt(d_gate_up, full_gate_up).astype(LOW)
    d_normed_two = scatter_seq(d_two_part.reshape(SEQ, rows, D), FULL)
    grad_gate_up_sum = scatter_dp(mm_tn(normed_two, d_gate_up).reshape(dp_total, block_rows, -1))
    grad_down_sum = scatter_dp(mm_tn(d_ffn_group, ffn_act).reshape(dp_total, block_rows, -1))
    grad_gate_up = grad_gate_up_sum.reshape(block_rows, 2, UNITS_PAD)[:, :, :UNITS]
    grad_down = grad_down_sum[:, :UNITS]

    d_x_tail, d_attn_o, d_ssm_o, d_gains = pull_join((d_total, d_normed_two))
    d_attn_own = d_attn_o.astype(LOW)
    d_attn = gather_seq(d_attn_own).reshape(group, D)
    d_ssm = gather_seq(d_ssm_o.astype(LOW)).reshape(group, D)
    d_gated = mm(d_ssm, w_out_t)
    d_attended = jnp.concatenate([mm(d_attn, w_o_t), mm(d_attn_own, w_o5_t)]).astype(LOW)

    def padded(a, width):
        return jnp.pad(a.astype(LOW), ((0, 0), (0, width - a.shape[1])))

    grad_out_t = jnp.concatenate(
        [
            padded(mm_tn(d_ssm, gated), O_AT),
            padded(mm_tn(d_attn, attended[:group]), O5_AT - O_AT),
            mm_tn(d_attn_own, attended[group:]).astype(LOW),
        ],
        axis=1,
    ).reshape(SEQ, D // SEQ, OUT_WIDTH)
    cut_for = lambda peer: lax.dynamic_index_in_dim(grad_out_t, peer, 0, False)
    arrived = place([(s, cut_for(s))] + [(s ^ bit, swap(cut_for(s ^ bit), "seq", bit)) for bit in (1, 2, 3)])
    arrived = arrived.transpose(0, 2, 1)
    grad_o_cols = jnp.concatenate(
        [arrived[j, O_AT : O_AT + QW] for j in range(SEQ)]
        + [jnp.sum(arrived[:, O5_AT:].astype(FULL), axis=0).astype(LOW)]
    )
    grad_mamba_cols = jnp.concatenate(
        [arrived[j, : HEAD_COUNT[j] * SSM_HEAD] for j in range(SEQ)]
    )
    grad_out_sum = scatter_dp(
        jnp.concatenate(
            [
                grad_o_cols.reshape(dp_total, block_rows, -1),
                grad_mamba_cols.reshape(dp_total, out_block, -1),
            ],
            axis=1,
        )
    )
    grad_o, grad_out = grad_out_sum[:block_rows], grad_out_sum[block_rows:]

    d_act_conv, d_bcdt, d_rate, d_skip, d_gate_z = pull_ssm(d_gated)
    d_raw, d_conv = pull_conv(d_act_conv)
    d_xzb = jnp.concatenate([d_raw, d_gate_z, d_bcdt], axis=1).astype(LOW)
    grad_xz_part = scatter_dp(mm_tn(normed, d_xzb).reshape(dp_total, block_rows, -1))
    xz_all = gather_seq(grad_xz_part.astype(LOW)).astype(FULL)
    x_cols = [xz_all[j, :, : HEAD_COUNT[j] * SSM_HEAD] for j in range(SEQ)]
    z_cols = [xz_all[j, :, LOCAL_CH : LOCAL_CH + HEAD_COUNT[j] * SSM_HEAD] for j in range(SEQ)]
    xz_width = w_xz.shape[1]
    grad_xz = lax.dynamic_slice_in_dim(jnp.concatenate(x_cols + z_cols, axis=1), s * xz_width, xz_width, 1)
    bc_at = 2 * LOCAL_CH
    grad_bcdt = jnp.concatenate(
        [jnp.sum(xz_all[:, :, bc_at : bc_at + 2 * STATE], axis=0)]
        + [xz_all[j, :, bc_at + 2 * STATE : bc_at + 2 * STATE + HEAD_COUNT[j]] for j in range(SEQ)],
        axis=1,
    )

    d_queries, d_kv = attention_backward(queries, kv, logs, d_attended, steps, rows)
    d_kvq = jnp.concatenate([d_kv, d_queries[:group]], axis=1)
    d_q_last = d_queries[group:]
    grad_qkv_part = scatter_dp(
        jnp.concatenate(
            [mm_tn(normed, d_kvq).astype(LOW), mm_tn(normed_own, d_q_last).astype(LOW)], axis=1
        ).reshape(dp_total, block_rows, -1)
    )
    qkv_all = gather_seq(grad_qkv_part.astype(LOW)).astype(FULL)
    col = lambda j, at, width: qkv_all[j, :, at : at + width]
    last = lambda at, width: jnp.sum(qkv_all[:, :, at : at + width], axis=0)
    grad_qkv_wide = jnp.concatenate(
        [col(j, 256, QW) for j in range(SEQ)]
        + [last(256 + QW, QW)]
        + [col(j, 0, HEAD) for j in range(SEQ)]
        + [last(128, HEAD)]
        + [col(j, HEAD, HEAD) for j in range(SEQ)]
        + [last(128 + HEAD, HEAD)],
        axis=1,
    )
    qkv_width = w_qkv.shape[1]
    grad_qkv = lax.dynamic_slice_in_dim(grad_qkv_wide, s * qkv_width, qkv_width, 1)

    d_normed_part = mm_nt(d_xzb, full_xz) + mm_nt(d_kvq, full_qkv[:, : 256 + QW])
    d_normed = scatter_seq(d_normed_part.astype(LOW).reshape(SEQ, rows, D), FULL)
    d_normed = d_normed + mm_nt(d_q_last, full_qkv[:, 256 + QW :])
    _, pull_norm = jax.vjp(rms_norm, inputs_x, gains[0])
    d_x_head, d_gain_first = pull_norm(d_normed)
    input_grad = (d_x_tail + d_x_head).astype(LOW)
    d_gains = d_gains.at[0].add(d_gain_first)

    d_rate = own_spread(d_rate, s, 1)
    d_skip = own_spread(d_skip, s, 1)
    d_conv = own_spread(d_conv, s, SSM_HEAD)
    flat = jnp.concatenate([d_conv.reshape(-1), d_gains.reshape(-1), d_rate, d_skip])
    size = flat.shape[0]
    flat = jnp.pad(flat, (0, -size % 1024)).reshape(-1, 128)
    flat = sum_all(flat).reshape(-1)[:size]
    conv_sum = flat[: CONV * INNER].reshape(CONV, INNER)
    gain_sum = flat[CONV * INNER : CONV * INNER + 4 * D].reshape(4, D)
    grad_conv = lax.dynamic_slice_in_dim(conv_sum, dp_index * conv_block, conv_block, 1)
    grad_gains = lax.dynamic_slice_in_dim(gain_sum, dp_index * gains_block, gains_block, 1)
    grad_rate = flat[size - 2 * SSM_HEADS : size - SSM_HEADS]
    grad_skip = flat[size - SSM_HEADS :]
    return (
        mixed_out,
        input_grad,
        grad_gains,
        grad_qkv,
        grad_o,
        grad_xz,
        grad_bcdt,
        grad_conv,
        grad_rate,
        grad_skip,
        grad_out,
        grad_gate_up,
        grad_down,
    )


def solution(mesh):
    placed = (
        P(("dp", "seq"), None),
        P("dp", None),
        P(None, "dp"),
        P("dp", "seq"),
        P("dp", "seq"),
        P("dp", "seq"),
        P("dp", None),
        P(None, "dp"),
        P(),
        P(),
        P("dp", "seq"),
        P("dp", None, "seq"),
        P("dp", "seq"),
        P(("dp", "seq"), None),
    )
    return jax.shard_map(
        on_device,
        mesh=mesh,
        in_specs=placed,
        out_specs=(
            P(("dp", "seq"), None),
            P(("dp", "seq"), None),
            P(None, "dp"),
            P("dp", "seq"),
            P("dp", "seq"),
            P("dp", "seq"),
            P("dp", None),
            P(None, "dp"),
            P(),
            P(),
            P("dp", "seq"),
            P("dp", None, "seq"),
            P("dp", "seq"),
        ),
        check_vma=False,
    )
```

time: 3840 us -> 1980 us (0.52)
  waiting for transfers between devices: 2580 us -> 323 us
  local copies, waits for them, and re-layouts: 437 us -> 753 us
  starting transfers between devices: 12.4 us -> 238 us
  other arithmetic: 154 us -> 312 us
  matrix products: 471 us -> 314 us
  blocking collectives: 152 us -> 0 us
    unnamed x32 -> x0, waiting for transfers between devices: 1220 us -> none
    all_gather x10 -> x0, waiting for transfers between devices: 947 us -> none  [the longest x1 350 us: gather_weights(): lax.all_gather(wide[2], 'dp', axis=0, tiled=True)]
    dynamic_update_slice x0 -> x72, local copies, waits for them, and re-layouts: none -> 354 us  [place(): stacked = lax.dynamic_update_index_in_dim(stacked, block, index, 0)]
    ppermute x6 -> x143, waiting for transfers between devices: 18.3 us -> 323 us  [the longest x77 215 us: swap(): lax.ppermute(value, axis, [(i, i ^ bit) for i in range(lax.axis_size(axis...]
    psum x2 -> x0, waiting for transfers between devices: 231 us -> none  [on_device(): lax.psum((grad_bcdt_full, d_conv_w, d_gains, d_rate, d_skip), ('dp', 'seq'))]
    ppermute x6 -> x143, starting transfers between devices: 11.4 us -> 238 us  [the longest x66 174 us: hop(): lax.ppermute(value, 'dp', [(2 * z + x, 2 * (z + step) + x) for z in sende...]
    reduce_scatter x4 -> x0, waiting for transfers between devices: 158 us -> none  [the longest x1 158 us: reduce_dp(): lax.psum_scatter(first_grad.astype(jnp.bfloat16), 'dp', scatter_dimension...]
    dot_general x68 -> x67, matrix products: 471 us -> 314 us  [the longest x9 70.3 us: mm(): return jnp.dot(left, right, preferred_element_type=FULL)]
  transfers between devices with their start and end apart: 30 -> 143, of which waited for: 23 -> 34; matrix products, arithmetic and copies ran while one was open for 18% -> 66% of each run, Pallas kernels for 0% -> 0%
where the time goes in v1:
time: 1980 us; the launch traced here: 1950 us
  local copies, waits for them, and re-layouts  753 us (38%)
  waiting for transfers between devices  323 us (16%)
  matrix products  314 us (16%)
  other arithmetic  312 us (16%)
  starting transfers between devices  238 us (12%)
    dynamic_update_slice x72, local copies, waits for them, and re-layouts, place(): stacked = lax.dynamic_update_index_in_dim(stacked, block, index, 0)  354 us
    ppermute x77, waiting for transfers between devices, swap(): lax.ppermute(value, axis, [(i, i ^ bit) for i in range(lax.axis_size(axis...  215 us
    ppermute x66, starting transfers between devices, hop(): lax.ppermute(value, 'dp', [(2 * z + x, 2 * (z + step) + x) for z in sende...  174 us
    ppermute x66, waiting for transfers between devices, hop(): lax.ppermute(value, 'dp', [(2 * z + x, 2 * (z + step) + x) for z in sende...  108 us
    dot_general x9, matrix products, mm(): return jnp.dot(left, right, preferred_element_type=FULL)  70.3 us
    dot_general x8, matrix products, mm_nt(): lax.dot_general(left, right, (((1,), (1,)), ((), ())), preferred_element_...  69.3 us
    ppermute x77, starting transfers between devices, swap(): lax.ppermute(value, axis, [(i, i ^ bit) for i in range(lax.axis_size(axis...  63.4 us
    dot_general x8, matrix products, mm_tn(): lax.dot_general(left, right, (((0,), (0,)), ((), ())), preferred_element_...  60.2 us
  transfers between devices with their start and end apart: 143, of which 34 were waited for; matrix products, arithmetic and copies ran while one was open for 66% of the time, Pallas kernels for 0%

profile of v1, /device:TPU:0, one launch (start us, length us, event | category | flops | bytes accessed | tf_op | source)
XLA Modules:
  0.0 1948.2 jit_solution(1271765553289084285)
XLA Ops:
  85.7 19.7 %dynamic_update_slice.312 = bf16[8,600,400]{1,0,2:T(8,128)(2,1)} dynamic-update-slice(bf16[8,600,400]{1,0,2:T(8,128)(2,1)} %broadcast_in_dim.591, bf16[1,600,400]{1,0,2:T(2,128)(2,1)S(1)} %copy.592, s32[]{:T(128)S(6)} %select_n.804, s32[]{:T(128)} %constant.1113.clone.1, s32[]{:T(128)} %constant.1113.clone.1) | dynamic-update-slice | bytes 960004 | tf_op jit(solution)/shard_map/jit(dynamic_update_index_in_dim)/dynamic_update_slice | solution.py:50
  106.2 19.4 dynamic_update_slice.324
  167.1 10.2 dynamic_update_slice.301
  177.4 10.2 dynamic_update_slice.302
  190.2 10.2 dynamic_update_slice.303
  215.5 19.8 %dynamic_update_slice.313 = bf16[8,600,400]{1,0,2:T(8,128)(2,1)} dynamic-update-slice(bf16[8,600,400]{1,0,2:T(8,128)(2,1)} %dynamic_update_slice.312, bf16[1,600,400]{1,0,2:T(2,128)(2,1)} %copy.593, s32[]{:T(128)S(6)} %select_n.805, s32[]{:T(128)} %constant.1113.clone.1, s32[]{:T(128)} %constant.1113.clone.1) | dynamic-update-slice | bytes 960004 | tf_op jit(solution)/shard_map/jit(dynamic_update_index_in_dim)/dynamic_update_slice | solution.py:50
  249.4 19.4 dynamic_update_slice.325
  268.8 19.4 dynamic_update_slice.326
  316.8 12.6 collective-permute-done.82
  338.9 19.4 dynamic_update_slice.327
  396.9 19.9 %dynamic_update_slice.314 = bf16[8,600,400]{1,0,2:T(8,128)(2,1)} dynamic-update-slice(bf16[8,600,400]{1,0,2:T(8,128)(2,1)} %dynamic_update_slice.313, bf16[1,600,400]{1,0,2:T(2,128)(2,1)S(1)} %copy.594, s32[]{:T(128)S(6)} %select_n.808, s32[]{:T(128)} %constant.1113.clone.1, s32[]{:T(128)} %constant.1113.clone.1) | dynamic-update-slice | bytes 960004 | tf_op jit(solution)/shard_map/jit(dynamic_update_index_in_dim)/dynamic_update_slice | solution.py:50
  422.9 14.8 collective-permute-done.21
  453.3 19.8 %dynamic_update_slice.315 = bf16[8,600,400]{1,0,2:T(8,128)(2,1)} dynamic-update-slice(bf16[8,600,400]{1,0,2:T(8,128)(2,1)} %dynamic_update_slice.314, bf16[1,600,400]{1,0,2:T(2,128)(2,1)} %copy.595, s32[]{:T(128)S(6)} %select_n.809, s32[]{:T(128)} %constant.1113.clone.1, s32[]{:T(128)} %constant.1113.clone.1) | dynamic-update-slice | bytes 960004 | tf_op jit(solution)/shard_map/jit(dynamic_update_index_in_dim)/dynamic_update_slice | solution.py:50
  473.1 19.7 %dynamic_update_slice.316 = bf16[8,600,400]{1,0,2:T(8,128)(2,1)} dynamic-update-slice(bf16[8,600,400]{1,0,2:T(8,128)(2,1)} %dynamic_update_slice.315, bf16[1,600,400]{1,0,2:T(2,128)(2,1)S(1)} %copy-done.80, s32[]{:T(128)S(6)} %select_n.812, s32[]{:T(128)} %constant.1113.clone.1, s32[]{:T(128)} %constant.1113.clone.1) | dynamic-update-slice | bytes 960004 | tf_op jit(solution)/shard_map/jit(dynamic_update_index_in_dim)/dynamic_update_slice | solution.py:50
  492.8 19.8 %dynamic_update_slice.317 = bf16[8,600,400]{1,0,2:T(8,128)(2,1)} dynamic-update-slice(bf16[8,600,400]{1,0,2:T(8,128)(2,1)} %dynamic_update_slice.316, bf16[1,600,400]{1,0,2:T(2,128)(2,1)S(1)} %copy.597, s32[]{:T(128)S(6)} %select_n.813, s32[]{:T(128)} %constant.1113.clone.1, s32[]{:T(128)} %constant.1113.clone.1) | dynamic-update-slice | bytes 960004 | tf_op jit(solution)/shard_map/jit(dynamic_update_index_in_dim)/dynamic_update_slice | solution.py:50
  512.6 19.8 %dynamic_update_slice.318 = bf16[8,600,400]{1,0,2:T(8,128)(2,1)} dynamic-update-slice(bf16[8,600,400]{1,0,2:T(8,128)(2,1)} %dynamic_update_slice.317, bf16[1,600,400]{1,0,2:T(2,128)(2,1)} %copy.598, s32[]{:T(128)S(6)} %select_n.816, s32[]{:T(128)} %constant.1113.clone.1, s32[]{:T(128)} %constant.1113.clone.1) | dynamic-update-slice | bytes 960004 | tf_op jit(solution)/shard_map/jit(dynamic_update_index_in_dim)/dynamic_update_slice | solution.py:50
  532.4 19.7 %dynamic_update_slice.319 = bf16[8,600,400]{1,0,2:T(8,128)(2,1)} dynamic-update-slice(bf16[8,600,400]{1,0,2:T(8,128)(2,1)} %dynamic_update_slice.318, bf16[1,600,400]{1,0,2:T(2,128)(2,1)S(1)} %copy-done.81, s32[]{:T(128)S(6)} %select_n.817, s32[]{:T(128)} %constant.1113.clone.1, s32[]{:T(128)} %constant.1113.clone.1) | dynamic-update-slice | bytes 960004 | tf_op jit(solution)/shard_map/jit(dynamic_update_index_in_dim)/dynamic_update_slice | solution.py:50
  617.3 13.8 collective-permute-start.46
  701.1 18.8 collective-permute-done.60
  722.5 12.8 collective-permute-done.50
  789.0 12.0 collective-permute-done.64
  802.6 21.8 %collective-permute-done.53 = bf16[200,1792]{1,0:T(8,128)(2,1)S(1)} collective-permute-done((bf16[200,1792]{1,0:T(8,128)(2,1)S(1)}, bf16[200,1792]{1,0:T(8,128)(2,1)S(1)}, u32[]{:S(2)}, u32[]{:S(2)}) %collective-permute-start.53) | collective-permute-done | bytes 716832 | tf_op jit(solution)/shard_map/ppermute | solution.py:38
  825.4 13.1 fusion.385
  843.4 23.3 %fusion.386 = f32[10,128,13]{2,0,1:T(8,128)S(1)} fusion(f32[10,128,13]{2,0,1:T(8,128)S(1)} %copy.609), kind=kOutput, calls=%fused_computation.844 | output fusion | flops 2113280 | bytes 133120 | tf_op jit(solution)/shard_map/jvp(jit(cumsum))/reduce_window_sum | solution.py:271
  960.1 21.5 %collective-permute-done.66 = bf16[200,2816]{1,0:T(8,128)(2,1)S(1)} collective-permute-done((bf16[200,2816]{1,0:T(8,128)(2,1)S(1)}, bf16[200,2816]{1,0:T(8,128)(2,1)S(1)}, u32[]{:S(2)}, u32[]{:S(2)}) %collective-permute-start.66) | collective-permute-done | bytes 1126432 | tf_op jit(solution)/shard_map/ppermute | solution.py:38
  988.7 19.5 %collective-permute-done.55 = bf16[320,1600]{1,0:T(8,128)(2,1)S(1)} collective-permute-done((bf16[320,1600]{1,0:T(8,128)(2,1)S(1)}, bf16[320,1600]{1,0:T(8,128)(2,1)S(1)}, u32[]{:S(2)}, u32[]{:S(2)}) %collective-permute-start.55) | collective-permute-done | bytes 1024032 | tf_op jit(solution)/shard_map/ppermute | solution.py:38
  1017.5 21.6 %collective-permute-done.57 = bf16[320,1600]{1,0:T(8,128)(2,1)S(1)} collective-permute-done((bf16[320,1600]{1,0:T(8,128)(2,1)S(1)}, bf16[320,1600]{1,0:T(8,128)(2,1)S(1)}, u32[]{:S(2)}, u32[]{:S(2)}) %collective-permute-start.57) | collective-permute-done | bytes 1024032 | tf_op jit(solution)/shard_map/ppermute | solution.py:38
  1042.0 16.4 fusion.390
  1058.4 16.1 multiply_convert_fusion.6
  1103.7 17.0 convolution_convert_fusion.3
  1159.0 17.3 fusion.14
  1226.2 16.2 collective-permute-start.139
  1254.7 25.0 %collective-permute-done.129 = bf16[4,200,2816]{2,1,0:T(8,128)(2,1)} collective-permute-done((bf16[4,200,2816]{2,1,0:T(8,128)(2,1)}, bf16[4,200,2816]{2,1,0:T(8,128)(2,1)}, u32[]{:S(2)}, u32[]{:S(2)}) %collective-permute-start.129) | collective-permute-done | bytes 4505632 | tf_op jit(solution)/shard_map/ppermute | solution.py:38
  1296.0 11.8 multiply_reduce_fusion.4
  1320.0 13.9 fusion.13
  1342.2 10.4 multiply_reduce_fusion.9
  1457.8 23.3 %fusion.387 = f32[10,128,13]{2,0,1:T(8,128)S(1)} fusion(f32[10,128,13]{2,0,1:T(8,128)S(1)} %copy.652), kind=kOutput, calls=%fused_computation.845 | output fusion | flops 2113280 | bytes 133120 | tf_op jit(solution)/shard_map/transpose(jvp(jit(cumsum)))/reduce_window_sum | solution.py:271
  1501.2 12.4 multiply_reduce_fusion.7
  1534.7 10.7 convolution_convert_fusion.5
  1551.6 13.6 fusion.21
  1580.0 14.5 fusion.9
  1619.4 21.7 %collective-permute-done.111 = bf16[400,1600]{1,0:T(8,128)(2,1)S(1)} collective-permute-done((bf16[400,1600]{1,0:T(8,128)(2,1)}, bf16[400,1600]{1,0:T(8,128)(2,1)S(1)}, u32[]{:S(2)}, u32[]{:S(2)}) %collective-permute-start.111) | collective-permute-done | bytes 1280032 | tf_op jit(solution)/shard_map/ppermute | solution.py:38
  1650.7 10.9 concatenate.134
  1695.7 19.7 %dynamic-slice_maximum_fusion = (bf16[4,1,600,400]{2,1,0,3:T(2,128)(2,1)S(1)}, f32[4,1,600,400]{2,1,0,3:T(1,128)}) fusion(s32[]{:T(128)S(6)} %select_n.965, bf16[4,2,200,400]{2,1,0,3:T(2,128)(2,1)S(1)} %copy-done.56, bf16[4,2,400,400]{2,1,0,3:T(2,128)(2,1)S(1)} %concatenate.134, s32[]{:T(128)S(6)} %select_n.964), kind=kLoop, calls=%fused_computation.114 | loop fusion | flops 7680000 | bytes 9600008 | tf_op jit(solution)/shard_map/concatenate | solution.py:510
  1740.5 13.8 collective-permute-done.102
  1805.0 14.4 collective-permute-start.98
  1830.8 11.3 collective-permute-done.121
  1894.0 20.0 %collective-permute-done.135 = bf16[200,2816]{1,0:T(8,128)(2,1)S(1)} collective-permute-done((bf16[200,2816]{1,0:T(8,128)(2,1)}, bf16[200,2816]{1,0:T(8,128)(2,1)S(1)}, u32[]{:S(2)}, u32[]{:S(2)}) %collective-permute-start.135) | collective-permute-done | bytes 1126432 | tf_op jit(solution)/shard_map/ppermute | solution.py:42
  (1428 shorter events, 1138.2 us)
Async XLA Ops:
  2.1 123.5 %collective-permute-start.3 = (bf16[16,512]{1,0:T(8,128)(2,1)}, bf16[16,512]{1,0:T(8,128)(2,1)}, u32[]{:S(2)}, u32[]{:S(2)}) collective-permute-start(bf16[16,512]{1,0:T(8,128)(2,1)} %get-tuple-element.505), channel_id=1, source_target_pairs={{0,4},{4,0},{8,12},{12,8},{16,20},{20,16},{24,28},{28,24},{1,5},{5... | collective-permute-start | bytes 49160 | tf_op jit(solution)/shard_map/ppermute | solution.py:38
  10.4 152.0 %collective-permute-start.13 = (bf16[200,560]{1,0:T(8,128)(2,1)}, bf16[200,560]{1,0:T(8,128)(2,1)}, u32[]{:S(2)}, u32[]{:S(2)}) collective-permute-start(bf16[200,560]{1,0:T(8,128)(2,1)} %param.47), channel_id=1, source_target_pairs={{0,1},{1,0},{2,3},{3,2},{4,5},{5,4},{6,7},{7,6},{8,9},{9,8},{10,11... | collective-permute-start | bytes 672008 | tf_op jit(solution)/shard_map/ppermute | solution.py:38
  57.8 73.3 %collective-permute-start.10 = (bf16[16,512]{1,0:T(8,128)(2,1)}, bf16[16,512]{1,0:T(8,128)(2,1)}, u32[]{:S(2)}, u32[]{:S(2)}) collective-permute-start(bf16[16,512]{1,0:T(8,128)(2,1)} %broadcast_select_fusion.16), channel_id=1, source_target_pairs={{0,4},{4,0},{8,12},{12,8},{16,20},{20,16},{24,28},{28,24},{1,5},{5... | collective-permute-start | bytes 49160 | tf_op jit(solution)/shard_map/ppermute | solution.py:38
  60.6 75.4 %collective-permute-start.8 = (bf16[16,512]{1,0:T(8,128)(2,1)S(1)}, bf16[16,512]{1,0:T(8,128)(2,1)}, u32[]{:S(2)}, u32[]{:S(2)}) collective-permute-start(bf16[16,512]{1,0:T(8,128)(2,1)S(1)} %broadcast_select_fusion.17), channel_id=1, source_target_pairs={{0,4},{4,0},{8,12},{12,8},{16,20},{20,16},{24,28},{28,24},{1,5},{5... | collective-permute-start | bytes 49160 | tf_op jit(solution)/shard_map/ppermute | solution.py:38
  64.6 77.0 %collective-permute-start.12 = (bf16[16,512]{1,0:T(8,128)(2,1)}, bf16[16,512]{1,0:T(8,128)(2,1)}, u32[]{:S(2)}, u32[]{:S(2)}) collective-permute-start(bf16[16,512]{1,0:T(8,128)(2,1)} %broadcast_select_fusion.15), channel_id=1, source_target_pairs={{0,4},{4,0},{8,12},{12,8},{16,20},{20,16},{24,28},{28,24},{1,5},{5... | collective-permute-start | bytes 49160 | tf_op jit(solution)/shard_map/ppermute | solution.py:38
  131.0 72.1 %collective-permute-start.26 = (bf16[600,400]{0,1:T(8,128)(2,1)}, bf16[600,400]{0,1:T(8,128)(2,1)}, u32[]{:S(2)}, u32[]{:S(2)}) collective-permute-start(bf16[600,400]{0,1:T(8,128)(2,1)} %pad_maximum_fusion.8), channel_id=1, source_target_pairs={{0,4},{4,0},{8,12},{12,8},{16,20},{20,16},{24,28},{28,24},{1,5},{5... | collective-permute-start | bytes 1440008 | tf_op jit(solution)/shard_map/ppermute | solution.py:38
  136.0 73.2 %collective-permute-start.28 = (bf16[600,400]{0,1:T(8,128)(2,1)}, bf16[600,400]{0,1:T(8,128)(2,1)}, u32[]{:S(2)}, u32[]{:S(2)}) collective-permute-start(bf16[600,400]{0,1:T(8,128)(2,1)} %pad_maximum_fusion.8), channel_id=1, source_target_pairs={{0,8},{4,12},{8,16},{12,20},{16,24},{20,28},{1,9},{5,13},{9,17},{1... | collective-permute-start | bytes 1440008 | tf_op jit(solution)/shard_map/ppermute | solution.py:42
  141.5 93.8 %collective-permute-start.27 = (bf16[600,400]{0,1:T(8,128)(2,1)}, bf16[600,400]{0,1:T(8,128)(2,1)}, u32[]{:S(2)}, u32[]{:S(2)}) collective-permute-start(bf16[600,400]{0,1:T(8,128)(2,1)} %pad_maximum_fusion.8), channel_id=1, source_target_pairs={{8,0},{12,4},{16,8},{20,12},{24,16},{28,20},{9,1},{13,5},{17,9},{2... | collective-permute-start | bytes 1440008 | tf_op jit(solution)/shard_map/ppermute | solution.py:42
  162.4 76.0 %collective-permute-start.41 = (bf16[200,1600]{1,0:T(8,128)(2,1)}, bf16[200,1600]{1,0:T(8,128)(2,1)}, u32[]{:S(2)}, u32[]{:S(2)}) collective-permute-start(bf16[200,1600]{1,0:T(8,128)(2,1)} %param.49), channel_id=1, source_target_pairs={{0,1},{1,0},{2,3},{3,2},{4,5},{5,4},{6,7},{7,6},{8,9},{9,8},{10,11... | collective-permute-start | bytes 1920008 | tf_op jit(solution)/shard_map/ppermute | solution.py:38
  187.6 52.2 %collective-permute-start.42 = (bf16[200,1600]{1,0:T(8,128)(2,1)}, bf16[200,1600]{1,0:T(8,128)(2,1)}, u32[]{:S(2)}, u32[]{:S(2)}) collective-permute-start(bf16[200,1600]{1,0:T(8,128)(2,1)} %param.49), channel_id=1, source_target_pairs={{0,2},{1,3},{2,0},{3,1},{4,6},{5,7},{6,4},{7,5},{8,10},{9,11},{10,... | collective-permute-start | bytes 1920008 | tf_op jit(solution)/shard_map/ppermute | solution.py:38
  209.2 94.3 %collective-permute-start = (bf16[320,1600]{1,0:T(8,128)(2,1)}, bf16[320,1600]{1,0:T(8,128)(2,1)}, u32[]{:S(2)}, u32[]{:S(2)}) collective-permute-start(bf16[320,1600]{1,0:T(8,128)(2,1)} %param.44), channel_id=1, source_target_pairs={{0,1},{1,0},{2,3},{3,2},{4,5},{5,4},{6,7},{7,6},{8,9},{9,8},{10,11... | collective-permute-start | bytes 3072008 | tf_op jit(solution)/shard_map/ppermute | solution.py:38
  235.3 70.9 %collective-permute-start.1 = (bf16[320,1600]{1,0:T(8,128)(2,1)}, bf16[320,1600]{1,0:T(8,128)(2,1)}, u32[]{:S(2)}, u32[]{:S(2)}) collective-permute-start(bf16[320,1600]{1,0:T(8,128)(2,1)} %param.44), channel_id=1, source_target_pairs={{0,2},{1,3},{2,0},{3,1},{4,6},{5,7},{6,4},{7,5},{8,10},{9,11},{10,... | collective-permute-start | bytes 3072008 | tf_op jit(solution)/shard_map/ppermute | solution.py:38
  236.9 51.4 %collective-permute-start.16 = (bf16[200,896]{1,0:T(8,128)(2,1)}, bf16[200,896]{1,0:T(8,128)(2,1)}, u32[]{:S(2)}, u32[]{:S(2)}) collective-permute-start(bf16[200,896]{1,0:T(8,128)(2,1)} %concatenate.113), channel_id=1, source_target_pairs={{0,4},{4,0},{8,12},{12,8},{16,20},{20,16},{24,28},{28,24},{1,5},{5... | collective-permute-start | bytes 1075208 | tf_op jit(solution)/shard_map/ppermute | solution.py:38
  238.4 59.0 %collective-permute-start.29 = (bf16[600,400]{0,1:T(8,128)(2,1)}, bf16[600,400]{0,1:T(8,128)(2,1)}, u32[]{:S(2)}, u32[]{:S(2)}) collective-permute-start(bf16[600,400]{0,1:T(8,128)(2,1)} %collective-permute-done.28), channel_id=1, source_target_pairs={{8,16},{12,20},{16,24},{20,28},{9,17},{13,21},{17,25},{21,29},{10,... | collective-permute-start | bytes 1440008 | tf_op jit(solution)/shard_map/ppermute | solution.py:42
  239.8 58.8 %collective-permute-start.32 = (bf16[600,400]{0,1:T(8,128)(2,1)}, bf16[600,400]{0,1:T(8,128)(2,1)}, u32[]{:S(2)}, u32[]{:S(2)}) collective-permute-start(bf16[600,400]{0,1:T(8,128)(2,1)} %collective-permute-done.27), channel_id=1, source_target_pairs={{8,0},{12,4},{16,8},{20,12},{9,1},{13,5},{17,9},{21,13},{10,2},{14... | collective-permute-start | bytes 1440008 | tf_op jit(solution)/shard_map/ppermute | solution.py:42
  297.4 84.4 %collective-permute-start.70 = (bf16[200,1408]{1,0:T(8,128)(2,1)}, bf16[200,1408]{1,0:T(8,128)(2,1)}, u32[]{:S(2)}, u32[]{:S(2)}) collective-permute-start(bf16[200,1408]{1,0:T(8,128)(2,1)} %pad.309), channel_id=1, source_target_pairs={{8,0},{12,4},{16,8},{20,12},{24,16},{28,20},{9,1},{13,5},{17,9},{2... | collective-permute-start | bytes 1689608 | tf_op jit(solution)/shard_map/ppermute | solution.py:42
  315.6 76.2 %collective-permute-start.17 = (bf16[200,896]{1,0:T(8,128)(2,1)}, bf16[200,896]{1,0:T(8,128)(2,1)}, u32[]{:S(2)}, u32[]{:S(2)}) collective-permute-start(bf16[200,896]{1,0:T(8,128)(2,1)} %concatenate.113), channel_id=1, source_target_pairs={{8,0},{12,4},{16,8},{20,12},{24,16},{28,20},{9,1},{13,5},{17,9},{2... | collective-permute-start | bytes 1075208 | tf_op jit(solution)/shard_map/ppermute | solution.py:42
  381.7 305.2 %collective-permute-start.61 = (bf16[200,2816]{1,0:T(8,128)(2,1)}, bf16[200,2816]{1,0:T(8,128)(2,1)}, u32[]{:S(2)}, u32[]{:S(2)}) collective-permute-start(bf16[200,2816]{1,0:T(8,128)(2,1)} %bitcast.452), channel_id=1, source_target_pairs={{0,8},{4,12},{8,16},{12,20},{16,24},{20,28},{1,9},{5,13},{9,17},{1... | collective-permute-start | bytes 3379208 | tf_op jit(solution)/shard_map/ppermute | solution.py:42
  391.7 246.2 %collective-permute-start.75 = (bf16[200,1408]{1,0:T(8,128)(2,1)}, bf16[200,1408]{1,0:T(8,128)(2,1)}, u32[]{:S(2)}, u32[]{:S(2)}) collective-permute-start(bf16[200,1408]{1,0:T(8,128)(2,1)} %collective-permute-done.70), channel_id=1, source_target_pairs={{8,0},{12,4},{16,8},{20,12},{9,1},{13,5},{17,9},{21,13},{10,2},{14... | collective-permute-start | bytes 1689608 | tf_op jit(solution)/shard_map/ppermute | solution.py:42
  393.0 47.0 %collective-permute-start.22 = (bf16[200,896]{1,0:T(8,128)(2,1)}, bf16[200,896]{1,0:T(8,128)(2,1)}, u32[]{:S(2)}, u32[]{:S(2)}) collective-permute-start(bf16[200,896]{1,0:T(8,128)(2,1)} %collective-permute-done.17), channel_id=1, source_target_pairs={{8,0},{12,4},{16,8},{20,12},{9,1},{13,5},{17,9},{21,13},{10,2},{14... | collective-permute-start | bytes 1075208 | tf_op jit(solution)/shard_map/ppermute | solution.py:42
  440.0 141.9 %collective-permute-start.2 = (bf16[320,1600]{1,0:T(8,128)(2,1)}, bf16[320,1600]{1,0:T(8,128)(2,1)}, u32[]{:S(2)}, u32[]{:S(2)}) collective-permute-start(bf16[320,1600]{1,0:T(8,128)(2,1)} %collective-permute-done.1), channel_id=1, source_target_pairs={{0,1},{1,0},{2,3},{3,2},{4,5},{5,4},{6,7},{7,6},{8,9},{9,8},{10,11... | collective-permute-start | bytes 3072008 | tf_op jit(solution)/shard_map/ppermute | solution.py:38
  442.0 164.5 %collective-permute-start.83 = (bf16[320,1600]{1,0:T(8,128)(2,1)}, bf16[320,1600]{1,0:T(8,128)(2,1)}, u32[]{:S(2)}, u32[]{:S(2)}) collective-permute-start(bf16[320,1600]{1,0:T(8,128)(2,1)} %collective-permute-done.82), channel_id=1, source_target_pairs={{0,1},{1,0},{2,3},{3,2},{4,5},{5,4},{6,7},{7,6},{8,9},{9,8},{10,11... | collective-permute-start | bytes 3072008 | tf_op jit(solution)/shard_map/ppermute | solution.py:38
  450.0 128.2 %collective-permute-start.44 = (bf16[200,1792]{1,0:T(8,128)(2,1)}, bf16[200,1792]{1,0:T(8,128)(2,1)}, u32[]{:S(2)}, u32[]{:S(2)}) collective-permute-start(bf16[200,1792]{1,0:T(8,128)(2,1)} %concatenate.120), channel_id=1, source_target_pairs={{0,4},{4,0},{8,12},{12,8},{16,20},{20,16},{24,28},{28,24},{1,5},{5... | collective-permute-start | bytes 2150408 | tf_op jit(solution)/shard_map/ppermute | solution.py:38
  578.2 54.7 %collective-permute-start.24 = (bf16[200,896]{1,0:T(8,128)(2,1)}, bf16[200,896]{1,0:T(8,128)(2,1)}, u32[]{:S(2)}, u32[]{:S(2)}) collective-permute-start(bf16[200,896]{1,0:T(8,128)(2,1)} %collective-permute-done.22), channel_id=1, source_target_pairs={{8,0},{12,4},{9,1},{13,5},{10,2},{14,6},{11,3},{15,7}} | collective-permute-start | bytes 1075208 | tf_op jit(solution)/shard_map/ppermute | solution.py:42
  582.0 54.1 %collective-permute-start.74 = (bf16[200,1408]{1,0:T(8,128)(2,1)}, bf16[200,1408]{1,0:T(8,128)(2,1)}, u32[]{:S(2)}, u32[]{:S(2)}) collective-permute-start(bf16[200,1408]{1,0:T(8,128)(2,1)} %get-tuple-element.331), channel_id=1, source_target_pairs={{0,4},{4,0},{8,12},{12,8},{16,20},{20,16},{24,28},{28,24},{1,5},{5... | collective-permute-start | bytes 1689608 | tf_op jit(solution)/shard_map/ppermute | solution.py:38
  632.9 55.5 %collective-permute-start.45 = (bf16[200,1792]{1,0:T(8,128)(2,1)}, bf16[200,1792]{1,0:T(8,128)(2,1)S(1)}, u32[]{:S(2)}, u32[]{:S(2)}) collective-permute-start(bf16[200,1792]{1,0:T(8,128)(2,1)} %concatenate.120), channel_id=1, source_target_pairs={{8,0},{12,4},{16,8},{20,12},{24,16},{28,20},{9,1},{13,5},{17,9},{2... | collective-permute-start | bytes 2150408 | tf_op jit(solution)/shard_map/ppermute | solution.py:42
  636.0 57.9 %collective-permute-start.36 = (bf16[400,1600]{1,0:T(8,128)(2,1)}, bf16[400,1600]{1,0:T(8,128)(2,1)}, u32[]{:S(2)}, u32[]{:S(2)}) collective-permute-start(bf16[400,1600]{1,0:T(8,128)(2,1)} %get-tuple-element.471), channel_id=1, source_target_pairs={{0,1},{1,0},{2,3},{3,2},{4,5},{5,4},{6,7},{7,6},{8,9},{9,8},{10,11... | collective-permute-start | bytes 3840008 | tf_op jit(solution)/shard_map/ppermute | solution.py:38
  642.7 52.7 %collective-permute-start.37 = (bf16[400,1600]{1,0:T(8,128)(2,1)S(1)}, bf16[400,1600]{1,0:T(8,128)(2,1)}, u32[]{:S(2)}, u32[]{:S(2)}) collective-permute-start(bf16[400,1600]{1,0:T(8,128)(2,1)S(1)} %get-tuple-element.472), channel_id=1, source_target_pairs={{0,2},{1,3},{2,0},{3,1},{4,6},{5,7},{6,4},{7,5},{8,10},{9,11},{10,... | collective-permute-start | bytes 3840008 | tf_op jit(solution)/shard_map/ppermute | solution.py:38
  719.9 235.6 %collective-permute-start.77 = (bf16[200,1408]{1,0:T(8,128)(2,1)}, bf16[200,1408]{1,0:T(8,128)(2,1)}, u32[]{:S(2)}, u32[]{:S(2)}) collective-permute-start(bf16[200,1408]{1,0:T(8,128)(2,1)} %collective-permute-done.75), channel_id=1, source_target_pairs={{8,0},{12,4},{9,1},{13,5},{10,2},{14,6},{11,3},{15,7}} | collective-permute-start | bytes 1689608 | tf_op jit(solution)/shard_map/ppermute | solution.py:42
  721.2 50.3 %collective-permute-start.65 = (bf16[200,2816]{1,0:T(8,128)(2,1)}, bf16[200,2816]{1,0:T(8,128)(2,1)}, u32[]{:S(2)}, u32[]{:S(2)}) collective-permute-start(bf16[200,2816]{1,0:T(8,128)(2,1)} %collective-permute-done.60), channel_id=1, source_target_pairs={{8,0},{12,4},{16,8},{20,12},{9,1},{13,5},{17,9},{21,13},{10,2},{14... | collective-permute-start | bytes 3379208 | tf_op jit(solution)/shard_map/ppermute | solution.py:42
  736.0 50.8 %collective-permute-start.52 = (bf16[200,1792]{1,0:T(8,128)(2,1)}, bf16[200,1792]{1,0:T(8,128)(2,1)}, u32[]{:S(2)}, u32[]{:S(2)}) collective-permute-start(bf16[200,1792]{1,0:T(8,128)(2,1)} %collective-permute-done.50), channel_id=1, source_target_pairs={{8,0},{12,4},{9,1},{13,5},{10,2},{14,6},{11,3},{15,7}} | collective-permute-start | bytes 2150408 | tf_op jit(solution)/shard_map/ppermute | solution.py:42
  771.5 182.5 %collective-permute-start.76 = (bf16[200,1408]{1,0:T(8,128)(2,1)}, bf16[200,1408]{1,0:T(8,128)(2,1)}, u32[]{:S(2)}, u32[]{:S(2)}) collective-permute-start(bf16[200,1408]{1,0:T(8,128)(2,1)} %get-tuple-element.329), channel_id=1, source_target_pairs={{0,4},{4,0},{8,12},{12,8},{16,20},{20,16},{24,28},{28,24},{1,5},{5... | collective-permute-start | bytes 1689608 | tf_op jit(solution)/shard_map/ppermute | solution.py:38
  776.9 206.2 %collective-permute-start.67 = (bf16[200,2816]{1,0:T(8,128)(2,1)}, bf16[200,2816]{1,0:T(8,128)(2,1)}, u32[]{:S(2)}, u32[]{:S(2)}) collective-permute-start(bf16[200,2816]{1,0:T(8,128)(2,1)} %collective-permute-done.65), channel_id=1, source_target_pairs={{8,0},{12,4},{9,1},{13,5},{10,2},{14,6},{11,3},{15,7}} | collective-permute-start | bytes 3379208 | tf_op jit(solution)/shard_map/ppermute | solution.py:42
  786.9 171.6 %collective-permute-start.39 = (bf16[2,320,1600]{2,1,0:T(8,128)(2,1)}, bf16[2,320,1600]{2,1,0:T(8,128)(2,1)}, u32[]{:S(2)}, u32[]{:S(2)}) collective-permute-start(bf16[2,320,1600]{2,1,0:T(8,128)(2,1)} %dynamic-slice_bitcast_fusion.7), channel_id=1, source_target_pairs={{0,1},{1,0},{2,3},{3,2},{4,5},{5,4},{6,7},{7,6},{8,9},{9,8},{10,11... | collective-permute-start | bytes 6144008 | tf_op jit(solution)/shard_map/ppermute | solution.py:38
  956.8 56.7 %collective-permute-start.78 = (bf16[200,1408]{1,0:T(8,128)(2,1)S(1)}, bf16[200,1408]{1,0:T(8,128)(2,1)S(1)}, u32[]{:S(2)}, u32[]{:S(2)}) collective-permute-start(bf16[200,1408]{1,0:T(8,128)(2,1)S(1)} %get-tuple-element.327), channel_id=1, source_target_pairs={{0,4},{4,0},{8,12},{12,8},{16,20},{20,16},{24,28},{28,24},{1,5},{5... | collective-permute-start | bytes 1689608 | tf_op jit(solution)/shard_map/ppermute | solution.py:38
  1093.0 56.8 %collective-permute-start.136 = (bf16[4,200,1408]{2,1,0:T(8,128)(2,1)}, bf16[4,200,1408]{2,1,0:T(8,128)(2,1)}, u32[]{:S(2)}, u32[]{:S(2)}) collective-permute-start(bf16[4,200,1408]{2,1,0:T(8,128)(2,1)} %dynamic-slice_bitcast_fusion.2), channel_id=1, source_target_pairs={{0,4},{4,0},{8,12},{12,8},{16,20},{20,16},{24,28},{28,24},{1,5},{5... | collective-permute-start | bytes 6758408 | tf_op jit(solution)/shard_map/ppermute | solution.py:38
  1181.1 98.6 %collective-permute-start.129 = (bf16[4,200,2816]{2,1,0:T(8,128)(2,1)}, bf16[4,200,2816]{2,1,0:T(8,128)(2,1)}, u32[]{:S(2)}, u32[]{:S(2)}) collective-permute-start(bf16[4,200,2816]{2,1,0:T(8,128)(2,1)} %dynamic-slice_bitcast_fusion), channel_id=1, source_target_pairs={{0,4},{4,0},{8,12},{12,8},{16,20},{20,16},{24,28},{28,24},{1,5},{5... | collective-permute-start | bytes 13516808 | tf_op jit(solution)/shard_map/ppermute | solution.py:38
  1226.2 62.4 %collective-permute-start.139 = (bf16[200,1408]{1,0:T(8,128)(2,1)S(1)}, bf16[200,1408]{1,0:T(8,128)(2,1)}, u32[]{:S(2)}, u32[]{:S(2)}) collective-permute-start(bf16[200,1408]{1,0:T(8,128)(2,1)S(1)} %get-tuple-element.432), channel_id=1, source_target_pairs={{0,8},{4,12},{8,16},{12,20},{16,24},{20,28},{1,9},{5,13},{9,17},{1... | collective-permute-start | bytes 1689608 | tf_op jit(solution)/shard_map/ppermute | solution.py:42
  1244.7 46.0 %collective-permute-start.142 = (bf16[200,1408]{1,0:T(8,128)(2,1)}, bf16[200,1408]{1,0:T(8,128)(2,1)}, u32[]{:S(2)}, u32[]{:S(2)}) collective-permute-start(bf16[200,1408]{1,0:T(8,128)(2,1)} %fusion.219), channel_id=1, source_target_pairs={{8,0},{12,4},{16,8},{20,12},{24,16},{28,20},{9,1},{13,5},{17,9},{2... | collective-permute-start | bytes 1689608 | tf_op jit(solution)/shard_map/ppermute | solution.py:42
  1286.1 324.0 %collective-permute-start.130 = (bf16[200,2816]{1,0:T(8,128)(2,1)}, bf16[200,2816]{1,0:T(8,128)(2,1)}, u32[]{:S(2)}, u32[]{:S(2)}) collective-permute-start(bf16[200,2816]{1,0:T(8,128)(2,1)} %get-tuple-element.400), channel_id=1, source_target_pairs={{0,8},{4,12},{1,9},{5,13},{2,10},{6,14},{3,11},{7,15}} | collective-permute-start | bytes 3379208 | tf_op jit(solution)/shard_map/ppermute | solution.py:42
  1288.7 397.3 %collective-permute-start.133 = (bf16[200,2816]{1,0:T(8,128)(2,1)}, bf16[200,2816]{1,0:T(8,128)(2,1)}, u32[]{:S(2)}, u32[]{:S(2)}) collective-permute-start(bf16[200,2816]{1,0:T(8,128)(2,1)} %get-tuple-element.401), channel_id=1, source_target_pairs={{24,16},{28,20},{25,17},{29,21},{26,18},{30,22},{27,19},{31,23}} | collective-permute-start | bytes 3379208 | tf_op jit(solution)/shard_map/ppermute | solution.py:42
  1550.1 185.2 %collective-permute-start.119 = (bf16[4,200,1792]{2,1,0:T(8,128)(2,1)}, bf16[4,200,1792]{2,1,0:T(8,128)(2,1)}, u32[]{:S(2)}, u32[]{:S(2)}) collective-permute-start(bf16[4,200,1792]{2,1,0:T(8,128)(2,1)} %dynamic-slice_bitcast_fusion.1), channel_id=1, source_target_pairs={{0,4},{4,0},{8,12},{12,8},{16,20},{20,16},{24,28},{28,24},{1,5},{5... | collective-permute-start | bytes 8601608 | tf_op jit(solution)/shard_map/ppermute | solution.py:38
  1613.2 48.4 %collective-permute-start.99 = (bf16[4,200,896]{2,1,0:T(8,128)(2,1)}, bf16[4,200,896]{2,1,0:T(8,128)(2,1)}, u32[]{:S(2)}, u32[]{:S(2)}) collective-permute-start(bf16[4,200,896]{2,1,0:T(8,128)(2,1)} %dynamic-slice_bitcast_fusion.8), channel_id=1, source_target_pairs={{0,4},{4,0},{8,12},{12,8},{16,20},{20,16},{24,28},{28,24},{1,5},{5... | collective-permute-start | bytes 4300808 | tf_op jit(solution)/shard_map/ppermute | solution.py:38
  1616.5 102.1 %collective-permute-start.92 = (bf16[2,320,1600]{2,1,0:T(8,128)(2,1)}, bf16[2,320,1600]{2,1,0:T(8,128)(2,1)}, u32[]{:S(2)}, u32[]{:S(2)}) collective-permute-start(bf16[2,320,1600]{2,1,0:T(8,128)(2,1)} %dynamic-slice_bitcast_fusion.3), channel_id=1, source_target_pairs={{0,1},{1,0},{2,3},{3,2},{4,5},{5,4},{6,7},{7,6},{8,9},{9,8},{10,11... | collective-permute-start | bytes 6144008 | tf_op jit(solution)/shard_map/ppermute | solution.py:38
  1641.0 46.3 %collective-permute-start.131 = (bf16[200,2816]{1,0:T(8,128)(2,1)}, bf16[200,2816]{1,0:T(8,128)(2,1)}, u32[]{:S(2)}, u32[]{:S(2)}) collective-permute-start(bf16[200,2816]{1,0:T(8,128)(2,1)} %fusion.107), channel_id=1, source_target_pairs={{0,8},{4,12},{8,16},{12,20},{1,9},{5,13},{9,17},{13,21},{2,10},{6,... | collective-permute-start | bytes 3379208 | tf_op jit(solution)/shard_map/ppermute | solution.py:42
  1717.8 56.5 %collective-permute-start.112 = (bf16[4,600,400]{1,0,2:T(4,128)(2,1)}, bf16[4,600,400]{1,0,2:T(4,128)(2,1)}, u32[]{:S(2)}, u32[]{:S(2)}) collective-permute-start(bf16[4,600,400]{1,0,2:T(4,128)(2,1)} %copy.661), channel_id=1, source_target_pairs={{0,4},{4,0},{8,12},{12,8},{16,20},{20,16},{24,28},{28,24},{1,5},{5... | collective-permute-start | bytes 5760008 | tf_op jit(solution)/shard_map/ppermute | solution.py:38
  1718.6 173.8 %collective-permute-start.132 = (bf16[200,2816]{1,0:T(8,128)(2,1)}, bf16[200,2816]{1,0:T(8,128)(2,1)}, u32[]{:S(2)}, u32[]{:S(2)}) collective-permute-start(bf16[200,2816]{1,0:T(8,128)(2,1)} %get-tuple-element.398), channel_id=1, source_target_pairs={{0,8},{4,12},{8,16},{12,20},{16,24},{20,28},{1,9},{5,13},{9,17},{1... | collective-permute-start | bytes 3379208 | tf_op jit(solution)/shard_map/ppermute | solution.py:42
  1754.3 69.0 %collective-permute-start.120 = (bf16[200,1792]{1,0:T(8,128)(2,1)}, bf16[200,1792]{1,0:T(8,128)(2,1)}, u32[]{:S(2)}, u32[]{:S(2)}) collective-permute-start(bf16[200,1792]{1,0:T(8,128)(2,1)} %get-tuple-element.410), channel_id=1, source_target_pairs={{0,8},{4,12},{1,9},{5,13},{2,10},{6,14},{3,11},{7,15}} | collective-permute-start | bytes 2150408 | tf_op jit(solution)/shard_map/ppermute | solution.py:42
  (426 other events, 7933.8 us)

commit v2 on v1

--- a/solution.py
+++ b/solution.py
@@ -1,6 +1,8 @@
 import jax
 import jax.numpy as jnp
 from jax import lax
+from jax.experimental import pallas as pl
+from jax.experimental.pallas import tpu as pltpu
 from jax.sharding import PartitionSpec as P
 
 D = 1600
@@ -38,17 +40,47 @@
     return lax.ppermute(value, axis, [(i, i ^ bit) for i in range(lax.axis_size(axis))])
 
 
-def hop(value, step, senders):
-    return lax.ppermute(
-        value, "dp", [(2 * z + x, 2 * (z + step) + x) for z in senders for x in (0, 1)]
-    )
+def place_kernel(count, index_ref, *refs):
+    blocks, stacked, held, in_sems, out_sems = refs[:count], *refs[count:]
+    loads = [
+        pltpu.make_async_copy(block, held.at[i], in_sems.at[i]) for i, block in enumerate(blocks)
+    ]
+    stores = [
+        pltpu.make_async_copy(held.at[i], stacked.at[index_ref[i]], out_sems.at[i])
+        for i in range(count)
+    ]
+    for load in loads:
+        load.start()
+    for load, store in zip(loads, stores):
+        load.wait()
+        store.start()
+    for store in stores:
+        store.wait()
 
 
 def place(blocks):
-    stacked = jnp.zeros((len(blocks),) + blocks[0][1].shape, blocks[0][1].dtype)
-    for index, block in blocks:
-        stacked = lax.dynamic_update_index_in_dim(stacked, block, index, 0)
-    return stacked
+    count = len(blocks)
+    block = blocks[0][1]
+    anywhere = pl.BlockSpec(memory_space=pl.ANY)
+    return pl.pallas_call(
+        lambda *refs: place_kernel(count, *refs),
+        out_shape=jax.ShapeDtypeStruct((count,) + block.shape, block.dtype),
+        grid_spec=pltpu.PrefetchScalarGridSpec(
+            num_scalar_prefetch=1,
+            grid=(1,),
+            in_specs=[anywhere] * count,
+            out_specs=anywhere,
+            scratch_shapes=[
+                pltpu.VMEM((count,) + block.shape, block.dtype),
+                pltpu.SemaphoreType.DMA((count,)),
+                pltpu.SemaphoreType.DMA((count,)),
+            ],
+        ),
+        compiler_params=pltpu.CompilerParams(vmem_limit_bytes=32 << 20),
+        cost_estimate=pl.CostEstimate(
+            flops=0, bytes_accessed=2 * count * block.size * block.dtype.itemsize, transcendentals=0
+        ),
+    )(jnp.stack([jnp.asarray(i, jnp.int32) for i, _ in blocks]), *[b for _, b in blocks])
 
 
 def gather_seq(block):
@@ -78,51 +110,237 @@
     ).astype(out_dtype)
 
 
-def gather_dp(block):
-    count = lax.axis_size("dp")
-    if count != 8:
-        return lax.all_gather(block, "dp", axis=0)
-    line = count // 2
+def line_place():
     me = lax.axis_index("dp")
-    z, x = me // 2, me % 2
-    up, down = [block], [block]
-    for k in range(1, line):
-        up.append(hop(up[-1], 1, range(k - 1, line - 1)))
-        down.append(hop(down[-1], -1, range(1, line - k + 1)))
-    placed = []
-    for j in range(line):
-        held = block if j == 0 else jnp.where(z + j < line, down[j], up[line - j])
-        other = swap(held, "dp", 1)
-        at = 2 * lax.rem(z + j, line)
-        placed += [(at + x, held), (at + 1 - x, other)]
-    return place(placed)
-
-
-def scatter_dp(parts):
-    count = lax.axis_size("dp")
-    parts = parts.astype(LOW)
-    if count != 8:
-        summed = lax.psum_scatter(parts, "dp", scatter_dimension=0)
-        return lax.optimization_barrier(summed).astype(FULL)
-    line = count // 2
-    me = lax.axis_index("dp")
-    z, x = me // 2, me % 2
-    grid = parts.reshape((line, 2) + parts.shape[1:])
-    got = swap(lax.dynamic_index_in_dim(grid, 1 - x, 1, False), "dp", 1)
-    part = lax.dynamic_index_in_dim(grid, x, 1, False).astype(FULL) + got.astype(FULL)
-    part = part.astype(LOW)
-
-    def own(t):
-        return lax.dynamic_index_in_dim(part, jnp.clip(t, 0, line - 1), 0, False).astype(FULL)
-
-    up = down = None
-    for k in range(1, line):
-        send_up, send_down = own(line - k + z), own(z - (line - k))
-        if k > 1:
-            send_up, send_down = send_up + up.astype(FULL), send_down + down.astype(FULL)
-        up = hop(send_up.astype(LOW), 1, range(0, k))
-        down = hop(send_down.astype(LOW), -1, range(line - k, line))
-    return own(z) + up.astype(FULL) + down.astype(FULL)
+    return lax.axis_size("dp") // 2, me // 2, lax.rem(me, 2)
+
+
+def greet(line, z, x):
+    barrier = pltpu.get_barrier_semaphore()
+
+    def signal(target):
+        pl.semaphore_signal(
+            barrier, inc=1, device_id={"dp": target}, device_id_type=pl.DeviceIdType.MESH
+        )
+
+    signal(2 * z + 1 - x)
+    pl.when(z > 0)(lambda: signal(2 * (z - 1) + x))
+    pl.when(z < line - 1)(lambda: signal(2 * (z + 1) + x))
+    pl.semaphore_wait(
+        barrier, 1 + (z > 0).astype(jnp.int32) + (z < line - 1).astype(jnp.int32)
+    )
+
+
+def gather_kernel(count, line, *refs):
+    packets, outs = refs[:count], refs[count : 2 * count]
+    own_sem, up_sem, down_sem, line_sem, give_sem, got_sem = refs[2 * count :]
+    _, z, x = line_place()
+    greet(line, z, x)
+
+    def copy(src, i, zb, send_sem, recv_sem, target):
+        return pltpu.make_async_remote_copy(
+            src_ref=src,
+            dst_ref=outs[i].at[2 * zb + x],
+            send_sem=send_sem.at[i, zb],
+            recv_sem=recv_sem.at[i, zb],
+            device_id={"dp": target},
+            device_id_type=pl.DeviceIdType.MESH,
+        )
+
+    up_to = lambda src, i, zb: copy(src, i, zb, up_sem, line_sem, 2 * (z + 1) + x)
+    down_to = lambda src, i, zb: copy(src, i, zb, down_sem, line_sem, 2 * (z - 1) + x)
+    give = lambda src, i, zb: copy(src, i, zb, give_sem, got_sem, 2 * z + 1 - x)
+    held = lambda i, zb: outs[i].at[2 * zb + x]
+    own = lambda i: pltpu.make_async_copy(packets[i], held(i, z), own_sem.at[i])
+
+    for turn in range(count + line - 1):
+        for i in range(count):
+            far = turn - i
+            if far == 0:
+                own(i).start()
+                give(packets[i], i, z).start()
+                pl.when(z < line - 1)(lambda: up_to(packets[i], i, z).start())
+                pl.when(z > 0)(lambda: down_to(packets[i], i, z).start())
+            elif 0 < far < line:
+
+                @pl.when(z - far >= 0)
+                def _():
+                    zb = z - far
+                    up_to(held(i, zb), i, zb).wait_recv()
+                    pl.when(z < line - 1)(lambda: up_to(held(i, zb), i, zb).start())
+                    give(held(i, zb), i, zb).start()
+
+                @pl.when(z + far < line)
+                def _():
+                    zb = z + far
+                    down_to(held(i, zb), i, zb).wait_recv()
+                    pl.when(z > 0)(lambda: down_to(held(i, zb), i, zb).start())
+                    give(held(i, zb), i, zb).start()
+
+    for i in range(count):
+        own(i).wait()
+        for zb in range(line):
+            give(held(i, zb), i, zb).wait()
+            pl.when((zb <= z) & (z < line - 1))(lambda: up_to(held(i, zb), i, zb).wait_send())
+            pl.when((zb >= z) & (z > 0))(lambda: down_to(held(i, zb), i, zb).wait_send())
+
+
+def gather_dp(packets, collective_id):
+    total = lax.axis_size("dp")
+    if total != 8:
+        return [lax.all_gather(packet, "dp", axis=0) for packet in packets]
+    count, line = len(packets), total // 2
+    sems = lambda *shape: pltpu.SemaphoreType.DMA(shape)
+    return pl.pallas_call(
+        lambda *refs: gather_kernel(count, line, *refs),
+        out_shape=[jax.ShapeDtypeStruct((total,) + p.shape, p.dtype) for p in packets],
+        in_specs=[pl.BlockSpec(memory_space=pltpu.VMEM)] * count,
+        out_specs=[pl.BlockSpec(memory_space=pl.ANY)] * count,
+        scratch_shapes=[sems(count)] + [sems(count, line) for _ in range(5)],
+        compiler_params=pltpu.CompilerParams(
+            collective_id=collective_id, has_side_effects=True, vmem_limit_bytes=32 << 20
+        ),
+        cost_estimate=pl.CostEstimate(
+            flops=0,
+            bytes_accessed=2 * total * sum(p.size * p.dtype.itemsize for p in packets),
+            transcendentals=0,
+        ),
+    )(*packets)
+
+
+def add_columns(total, parts):
+    width = total.shape[-1]
+    step = 128 if width % 256 else 256
+
+    def columns(c):
+        at = pl.ds(pl.multiple_of(c * step, step), step)
+        total[:, at] = sum(part[:, at].astype(FULL) for part in parts).astype(total.dtype)
+
+    pl.loop(0, width // step)(columns)
+    if width % step:
+        at = slice(width // step * step, width)
+        total[:, at] = sum(part[:, at].astype(FULL) for part in parts).astype(total.dtype)
+
+
+def scatter_kernel(count, line, *refs):
+    parts, outs = refs[:count], refs[count : 2 * count]
+    own_refs, near_refs, line_refs = (
+        refs[2 * count : 3 * count],
+        refs[3 * count : 4 * count],
+        refs[4 * count : 5 * count],
+    )
+    load_sem, give_sem, got_sem, send_sem, line_sem = refs[5 * count :]
+    _, z, x = line_place()
+    greet(line, z, x)
+    order = [t for pair in zip(range(line - 1, -1, -1), range(line)) for t in pair][:line]
+    remote = lambda src, dst, send, recv, target: pltpu.make_async_remote_copy(
+        src_ref=src,
+        dst_ref=dst,
+        send_sem=send,
+        recv_sem=recv,
+        device_id={"dp": target},
+        device_id_type=pl.DeviceIdType.MESH,
+    )
+    give = lambda i, t: remote(
+        parts[i].at[2 * t + 1 - x],
+        near_refs[i].at[t],
+        give_sem.at[i, t],
+        got_sem.at[i, t],
+        2 * z + 1 - x,
+    )
+    load = lambda i, t: pltpu.make_async_copy(
+        parts[i].at[2 * t + x], own_refs[i].at[t], load_sem.at[i, t]
+    )
+    along = lambda i, t, slot, target: remote(
+        own_refs[i].at[t], line_refs[i].at[slot], send_sem.at[i, t], line_sem.at[i, slot], target
+    )
+    for i in range(count):
+        for t in order:
+            load(i, t).start()
+            give(i, t).start()
+    for i in range(count):
+        own, near, held = own_refs[i], near_refs[i], line_refs[i]
+        for t in order:
+            load(i, t).wait()
+            give(i, t).wait_recv()
+
+            @pl.when((t > z) & (z > 0) | (t < z) & (z < line - 1))
+            def _():
+                along(i, t, t, 0).wait_recv()
+                add_columns(own.at[t], (own.at[t], near.at[t], held.at[t]))
+
+            @pl.when((t > z) & (z == 0) | (t < z) & (z == line - 1))
+            def _():
+                add_columns(own.at[t], (own.at[t], near.at[t]))
+
+            pl.when(t > z)(lambda: along(i, t, t, 2 * (z + 1) + x).start())
+            pl.when(t == z - 1)(lambda: along(i, t, line, 2 * (z - 1) + x).start())
+            pl.when(t < z - 1)(lambda: along(i, t, t, 2 * (z - 1) + x).start())
+    for i in range(count):
+        own, near, held = own_refs[i], near_refs[i], line_refs[i]
+        pl.when(z > 0)(lambda: along(i, z, z, 0).wait_recv())
+        pl.when(z < line - 1)(lambda: along(i, z, line, 0).wait_recv())
+        for t in range(line):
+
+            @pl.when(t == z)
+            def _():
+                terms = [own.at[t], near.at[t]]
+                terms += [held.at[t]] if t > 0 else []
+                terms += [held.at[line]] if t < line - 1 else []
+                add_columns(outs[i], terms)
+
+            pl.when(t != z)(lambda: along(i, t, t, 0).wait_send())
+            give(i, t).wait_send()
+
+
+def scatter_dp(parts, collective_id):
+    parts = [p.astype(LOW) for p in parts]
+    total = lax.axis_size("dp")
+    if total != 8:
+        sums = [lax.psum_scatter(p, "dp", scatter_dimension=0) for p in parts]
+        return [lax.optimization_barrier(p).astype(FULL) for p in sums]
+    count, line = len(parts), total // 2
+    sems = lambda *shape: pltpu.SemaphoreType.DMA(shape)
+    return pl.pallas_call(
+        lambda *refs: scatter_kernel(count, line, *refs),
+        out_shape=[jax.ShapeDtypeStruct(p.shape[1:], FULL) for p in parts],
+        in_specs=[pl.BlockSpec(memory_space=pl.ANY)] * count,
+        out_specs=[pl.BlockSpec(memory_space=pltpu.VMEM)] * count,
+        scratch_shapes=[pltpu.VMEM((line,) + p.shape[1:], LOW) for p in parts]
+        + [pltpu.VMEM((line,) + p.shape[1:], LOW) for p in parts]
+        + [pltpu.VMEM((line + 1,) + p.shape[1:], LOW) for p in parts]
+        + [sems(count, line) for _ in range(4)]
+        + [sems(count, line + 1)],
+        compiler_params=pltpu.CompilerParams(
+            collective_id=collective_id, has_side_effects=True, vmem_limit_bytes=56 << 20
+        ),
+        cost_estimate=pl.CostEstimate(
+            flops=0, bytes_accessed=sum(p.size * 2 for p in parts), transcendentals=0
+        ),
+    )(*parts)
+
+
+def gather_dp_apart(packet):
+    return lax.all_gather(packet, "dp", axis=0)
+
+
+def scatter_dp_apart(parts):
+    summed = lax.psum_scatter(parts.astype(LOW), "dp", scatter_dimension=0)
+    return lax.optimization_barrier(summed).astype(FULL)
+
+
+def trade_halves(first, last):
+    me = lax.axis_index("seq")
+    one = lax.ppermute(jnp.where(me == 0, last, first), "seq", [(0, 1), (1, 2), (2, 0)])
+    two = lax.ppermute(jnp.where(me == 3, first, last), "seq", [(1, 3), (2, 1), (3, 2)])
+    return pick([first, one, one, two], me), pick([one, two, two, last], me)
+
+
+def trade_back(x_part, z_part):
+    me = lax.axis_index("seq")
+    one = lax.ppermute(jnp.where(me == 0, z_part, x_part), "seq", [(1, 0), (2, 1), (0, 2)])
+    two = lax.ppermute(jnp.where(me == 3, x_part, z_part), "seq", [(3, 1), (1, 2), (2, 3)])
+    return pick([x_part, one, one, two], me), pick([one, two, two, z_part], me)
 
 
 def sum_all(value):
@@ -268,8 +486,9 @@
     b_in = bcdt[:, :STATE].reshape(chunks, CHUNK, STATE)
     c_in = bcdt[:, STATE : 2 * STATE].reshape(chunks, CHUNK, STATE)
     x = conv_act.reshape(chunks, CHUNK, heads, SSM_HEAD)
-    log = jnp.cumsum(-step * rate, axis=1)
     places = jnp.arange(CHUNK, dtype=jnp.int32)
+    before = (places[:, None] >= places[None, :]).astype(FULL)
+    log = jnp.einsum("ts,csh->cth", before, -step * rate, precision=lax.Precision.HIGHEST)
     causal = (places[:, None] >= places[None, :])[None] & (ids[:, :, None] == ids[:, None, :])
     log_h = log.transpose(0, 2, 1)
     gap = log_h[:, :, :, None] - log_h[:, :, None, :]
@@ -370,7 +589,7 @@
             jnp.pad(norm_gains, ((0, 4), (0, width - gains_block))),
         ]
     )
-    small = gather_dp(small)
+    (small,) = gather_dp([small], 0)
     full_conv = small[:, :4, :conv_block].transpose(1, 0, 2).reshape(4, INNER).astype(FULL)
     gains = small[:, 8:12, :gains_block].transpose(1, 0, 2).reshape(4, D).astype(FULL)
 
@@ -382,22 +601,23 @@
         lax.dynamic_slice_in_dim(qkv_wide, D + kv_width + h * HEAD, HEAD, 1),
     ]
     qkv_packet = jnp.concatenate(kv_at(s) + kv_at(KV_HEADS - 1) + [q_at(s), q_at(KV_HEADS - 1)], axis=1)
-    full_qkv = gather_dp(qkv_packet).reshape(D, -1)
-
-    xz_wide = wide_of(gather_seq(w_xz))
     bcdt_own = bcdt_cut(w_bcdt, s)
+    x_part, z_part = trade_halves(
+        w_xz[:, :LOCAL_CH], jnp.pad(w_xz[:, LOCAL_CH:], ((0, 0), (0, 2 * LOCAL_CH - w_xz.shape[1])))
+    )
     xz_packet = jnp.concatenate(
         [
-            channel_cut(xz_wide[:, :INNER], s, 1),
-            channel_cut(xz_wide[:, INNER:], s, 1),
+            x_part,
+            z_part,
             bcdt_own,
         ],
         axis=1,
     )
-    full_xz = gather_dp(xz_packet).reshape(D, -1)
-
     out_block = w_out.shape[0]
-    out_cols = gather_dp(jnp.concatenate([w_o, w_out], axis=0))
+    out_packet = jnp.concatenate([w_o, w_out], axis=0)
+    full_qkv, full_xz, out_cols = gather_dp([qkv_packet, xz_packet, out_packet], 1)
+    full_qkv = full_qkv.reshape(D, -1)
+    full_xz = full_xz.reshape(D, -1)
     o_cols = out_cols[:, :block_rows].reshape(D, -1)
     mamba_cols = out_cols[:, block_rows:].reshape(INNER, -1)
 
@@ -421,8 +641,8 @@
     w_o5_t = out_t[:, O5_AT:]
 
     gate_up_packet = jnp.pad(w_gate_up, ((0, 0), (0, 0), (0, UNITS_PAD - UNITS))).reshape(block_rows, -1)
-    full_gate_up = gather_dp(gate_up_packet).reshape(D, -1)
-    full_down = gather_dp(jnp.pad(w_down, ((0, 0), (0, UNITS_PAD - UNITS)))).reshape(D, -1)
+    full_gate_up = gather_dp_apart(gate_up_packet).reshape(D, -1)
+    full_down = gather_dp_apart(jnp.pad(w_down, ((0, 0), (0, UNITS_PAD - UNITS)))).reshape(D, -1)
 
     d_total = cotangent.astype(FULL) * live
     d_ffn_group = gather_seq(d_total.astype(LOW)).reshape(group, D)
@@ -473,8 +693,8 @@
     d_gate_up = jnp.concatenate([d_gate.astype(LOW), d_up.astype(LOW)], axis=1)
     d_two_part = mm_nt(d_gate_up, full_gate_up).astype(LOW)
     d_normed_two = scatter_seq(d_two_part.reshape(SEQ, rows, D), FULL)
-    grad_gate_up_sum = scatter_dp(mm_tn(normed_two, d_gate_up).reshape(dp_total, block_rows, -1))
-    grad_down_sum = scatter_dp(mm_tn(d_ffn_group, ffn_act).reshape(dp_total, block_rows, -1))
+    grad_gate_up_sum = scatter_dp_apart(mm_tn(normed_two, d_gate_up).reshape(dp_total, block_rows, -1))
+    grad_down_sum = scatter_dp_apart(mm_tn(d_ffn_group, ffn_act).reshape(dp_total, block_rows, -1))
     grad_gate_up = grad_gate_up_sum.reshape(block_rows, 2, UNITS_PAD)[:, :, :UNITS]
     grad_down = grad_down_sum[:, :UNITS]
 
@@ -506,51 +726,48 @@
     grad_mamba_cols = jnp.concatenate(
         [arrived[j, : HEAD_COUNT[j] * SSM_HEAD] for j in range(SEQ)]
     )
-    grad_out_sum = scatter_dp(
-        jnp.concatenate(
-            [
-                grad_o_cols.reshape(dp_total, block_rows, -1),
-                grad_mamba_cols.reshape(dp_total, out_block, -1),
-            ],
-            axis=1,
-        )
-    )
-    grad_o, grad_out = grad_out_sum[:block_rows], grad_out_sum[block_rows:]
+    grad_out_part = jnp.concatenate(
+        [
+            grad_o_cols.reshape(dp_total, block_rows, -1),
+            grad_mamba_cols.reshape(dp_total, out_block, -1),
+        ],
+        axis=1,
+    )
 
     d_act_conv, d_bcdt, d_rate, d_skip, d_gate_z = pull_ssm(d_gated)
     d_raw, d_conv = pull_conv(d_act_conv)
     d_xzb = jnp.concatenate([d_raw, d_gate_z, d_bcdt], axis=1).astype(LOW)
-    grad_xz_part = scatter_dp(mm_tn(normed, d_xzb).reshape(dp_total, block_rows, -1))
-    xz_all = gather_seq(grad_xz_part.astype(LOW)).astype(FULL)
-    x_cols = [xz_all[j, :, : HEAD_COUNT[j] * SSM_HEAD] for j in range(SEQ)]
-    z_cols = [xz_all[j, :, LOCAL_CH : LOCAL_CH + HEAD_COUNT[j] * SSM_HEAD] for j in range(SEQ)]
-    xz_width = w_xz.shape[1]
-    grad_xz = lax.dynamic_slice_in_dim(jnp.concatenate(x_cols + z_cols, axis=1), s * xz_width, xz_width, 1)
-    bc_at = 2 * LOCAL_CH
-    grad_bcdt = jnp.concatenate(
-        [jnp.sum(xz_all[:, :, bc_at : bc_at + 2 * STATE], axis=0)]
-        + [xz_all[j, :, bc_at + 2 * STATE : bc_at + 2 * STATE + HEAD_COUNT[j]] for j in range(SEQ)],
-        axis=1,
-    )
+    grad_xz_part = mm_tn(normed, d_xzb).astype(LOW).reshape(dp_total, block_rows, -1)
 
     d_queries, d_kv = attention_backward(queries, kv, logs, d_attended, steps, rows)
     d_kvq = jnp.concatenate([d_kv, d_queries[:group]], axis=1)
     d_q_last = d_queries[group:]
-    grad_qkv_part = scatter_dp(
-        jnp.concatenate(
-            [mm_tn(normed, d_kvq).astype(LOW), mm_tn(normed_own, d_q_last).astype(LOW)], axis=1
-        ).reshape(dp_total, block_rows, -1)
-    )
-    qkv_all = gather_seq(grad_qkv_part.astype(LOW)).astype(FULL)
+    grad_qkv_part = jnp.concatenate(
+        [mm_tn(normed, d_kvq).astype(LOW), mm_tn(normed_own, d_q_last).astype(LOW)], axis=1
+    ).reshape(dp_total, block_rows, -1)
+    grad_out_sum, grad_xz_sum, grad_qkv_sum = scatter_dp(
+        [grad_out_part, grad_xz_part, grad_qkv_part], 2
+    )
+    grad_o, grad_out = grad_out_sum[:block_rows], grad_out_sum[block_rows:]
+    grad_xz_sum = grad_xz_sum.astype(LOW)
+    first, last = trade_back(grad_xz_sum[:, :LOCAL_CH], grad_xz_sum[:, LOCAL_CH : 2 * LOCAL_CH])
+    grad_xz = jnp.concatenate([first, last], axis=1)[:, : w_xz.shape[1]].astype(FULL)
+    bcdt_all = gather_seq(grad_xz_sum[:, 2 * LOCAL_CH :]).astype(FULL)
+    grad_bcdt = jnp.concatenate(
+        [jnp.sum(bcdt_all[:, :, : 2 * STATE], axis=0)]
+        + [bcdt_all[j, :, 2 * STATE : 2 * STATE + HEAD_COUNT[j]] for j in range(SEQ)],
+        axis=1,
+    )
+    qkv_all = gather_seq(grad_qkv_sum.astype(LOW)).astype(FULL)
     col = lambda j, at, width: qkv_all[j, :, at : at + width]
-    last = lambda at, width: jnp.sum(qkv_all[:, :, at : at + width], axis=0)
+    shared = lambda at, width: jnp.sum(qkv_all[:, :, at : at + width], axis=0)
     grad_qkv_wide = jnp.concatenate(
         [col(j, 256, QW) for j in range(SEQ)]
-        + [last(256 + QW, QW)]
+        + [shared(256 + QW, QW)]
         + [col(j, 0, HEAD) for j in range(SEQ)]
-        + [last(128, HEAD)]
+        + [shared(128, HEAD)]
         + [col(j, HEAD, HEAD) for j in range(SEQ)]
-        + [last(128 + HEAD, HEAD)],
+        + [shared(128 + HEAD, HEAD)],
         axis=1,
     )
     qkv_width = w_qkv.shape[1]

time: 1980 us -> 1460 us (0.74); the launches traced: 1950 us -> 1450 us
  local copies, waits for them, and re-layouts: 753 us -> 274 us
  Pallas kernels: 0 us -> 407 us
  starting transfers between devices: 238 us -> 38.5 us
  other arithmetic: 312 us -> 189 us
  waiting for transfers between devices: 323 us -> 201 us
    pallas_call x0 -> x13, Pallas kernels: none -> 407 us  [the longest x2 220 us: gather_dp(): pl.pallas_call(lambda *refs: gather_kernel(count, line, *refs), out_shape...]
    dynamic_update_slice x72 -> x0, local copies, waits for them, and re-layouts: 354 us -> none  [place(): stacked = lax.dynamic_update_index_in_dim(stacked, block, index, 0)]
    ppermute x66 -> x4, starting transfers between devices: 174 us -> 7.6 us  [the longest x1 2.54 us: trade_halves(): lax.ppermute(jnp.where(me == 0, last, first), 'seq', [(0, 1), (1, 2), (2,...]
    ppermute x66 -> x4, waiting for transfers between devices: 108 us -> 3.44 us  [the longest x1 3.43 us: trade_back(): lax.ppermute(jnp.where(me == 0, z_part, x_part), 'seq', [(1, 0), (2, 1),...]
    broadcast_in_dim x39 -> x0, local copies, waits for them, and re-layouts: 58.6 us -> none  [the longest x29 46.5 us: place(): stacked = lax.dynamic_update_index_in_dim(stacked, block, index, 0)]
    convert_element_type x24 -> x8, other arithmetic: 48 us -> 4.43 us  [the longest x1 1.57 us: on_device(): grad_xz_sum = grad_xz_sum.astype(LOW)]
    another operation x4 -> x3, other arithmetic: 52.7 us -> 10.4 us  [the longest x2 46.6 us: ssm_group(): log = jnp.cumsum(-step * rate, axis=1)]
    ppermute x77 -> x45, starting transfers between devices: 63.4 us -> 30.6 us  [swap(): lax.ppermute(value, axis, [(i, i ^ bit) for i in range(lax.axis_size(axis...]
  transfers between devices with their start and end apart: 143 -> 53, of which waited for: 34 -> 17; matrix products, arithmetic and copies ran while one was open for 66% -> 49% of each run, Pallas kernels for 0% -> 28%
where the time goes in v2:
time: 1460 us; the launch traced here: 1450 us
  Pallas kernels  407 us (28%)
  matrix products  324 us (22%)
  local copies, waits for them, and re-layouts  274 us (19%)
  waiting for transfers between devices  201 us (14%)
  other arithmetic  189 us (13%)
  starting transfers between devices  38.5 us (3%)
  between operations  18.8 us (1%)
    pallas_call x2, Pallas kernels, gather_dp(): pl.pallas_call(lambda *refs: gather_kernel(count, line, *refs), out_shape...  220 us
    ppermute x45, waiting for transfers between devices, swap(): lax.ppermute(value, axis, [(i, i ^ bit) for i in range(lax.axis_size(axis...  197 us
    pallas_call x1, Pallas kernels, scatter_dp(): pl.pallas_call(lambda *refs: scatter_kernel(count, line, *refs), out_shap...  165 us
    dot_general x9, matrix products, mm(): return jnp.dot(left, right, preferred_element_type=FULL)  68.5 us
    dot_general x8, matrix products, mm_nt(): lax.dot_general(left, right, (((1,), (1,)), ((), ())), preferred_element_...  63.6 us
    dot_general x8, matrix products, mm_tn(): lax.dot_general(left, right, (((0,), (0,)), ((), ())), preferred_element_...  57.5 us
    dot_general x12, matrix products, ssm_group(): ein = lambda spec, *v: jnp.einsum(spec, *v, preferred_element_type=FULL)  50.3 us
    unnamed x505, local copies, waits for them, and re-layouts  49.3 us
  transfers between devices with their start and end apart: 53, of which 17 were waited for; matrix products, arithmetic and copies ran while one was open for 49% of the time, Pallas kernels for 28%

profile of v2, /device:TPU:0, one launch (start us, length us, event | category | flops | bytes accessed | tf_op | source)
XLA Modules:
  0.0 1451.8 jit_solution(7621784572268830042)
XLA Ops:
  29.7 16.0 %shard_map.258 = bf16[8,16,512]{2,1,0:T(8,128)(2,1)S(1)} custom-call(bf16[16,512]{1,0:T(8,128)(2,1)S(1)} %fusion.286.refs_0_), custom_call_target="tpu_custom_call" | custom-call | bytes 262144 | tf_op jit(solution)/shard_map/pallas_call | solution.py:194
  69.7 204.3 %shard_map.260 = (bf16[8,200,896]{2,1,0:T(8,128)(2,1)S(1)}, bf16[8,200,1792]{2,1,0:T(8,128)(2,1)S(1)}, bf16[8,600,400]{2,1,0:T(8,128)(2,1)S(1)}) custom-call(bf16[200,896]{1,0:T(8,128)(2,1)S(1)} %concatenate.108.refs_0_, bf16[200,1792]{1,0:T(8,128)(2,1)S(1)} %concatenate.109.refs_1_, bf16[600,400]{1,0:T(8,128)(2,1)S(1)} %pad_maximum_fusion.10.refs_2_), custom_call_target="tpu_custom_call" | custom-call | bytes 24883200 | tf_op jit(solution)/shard_map/pallas_call | solution.py:194
  316.0 21.3 %collective-permute-done.10.refs_4_ = bf16[400,1600]{1,0:T(8,128)(2,1)} collective-permute-done((bf16[400,1600]{1,0:T(8,128)(2,1)}, bf16[400,1600]{1,0:T(8,128)(2,1)}, u32[]{:S(2)}, u32[]{:S(2)}) %collective-permute-start.10) | collective-permute-done | bytes 1280032 | tf_op jit(solution)/shard_map/ppermute | solution.py:40
  337.3 28.3 %collective-permute-done.9.refs_3_ = bf16[400,1600]{1,0:T(8,128)(2,1)} collective-permute-done((bf16[400,1600]{1,0:T(8,128)(2,1)}, bf16[400,1600]{1,0:T(8,128)(2,1)}, u32[]{:S(2)}, u32[]{:S(2)}) %collective-permute-start.9) | collective-permute-done | bytes 1280032 | tf_op jit(solution)/shard_map/ppermute | solution.py:40
  409.3 6.8 copy.505
  422.9 10.0 fusion.350
  445.0 8.6 reshape.1326
  453.6 8.9 copy.509
  478.6 8.4 copy.584
  487.0 9.4 reshape.1327
  503.1 8.5 convolution_convert_fusion.2
  511.5 6.8 copy.520
  541.7 29.7 %collective-permute-done.12 = bf16[320,1600]{1,0:T(8,128)(2,1)S(1)} collective-permute-done((bf16[320,1600]{1,0:T(8,128)(2,1)S(1)}, bf16[320,1600]{1,0:T(8,128)(2,1)S(1)}, u32[]{:S(2)}, u32[]{:S(2)}) %collective-permute-start.12) | collective-permute-done | bytes 1024032 | tf_op jit(solution)/shard_map/ppermute | solution.py:40
  574.1 19.3 %collective-permute-done.14 = bf16[320,1600]{1,0:T(8,128)(2,1)S(1)} collective-permute-done((bf16[320,1600]{1,0:T(8,128)(2,1)S(1)}, bf16[320,1600]{1,0:T(8,128)(2,1)S(1)}, u32[]{:S(2)}, u32[]{:S(2)}) %collective-permute-start.14) | collective-permute-done | bytes 1024032 | tf_op jit(solution)/shard_map/ppermute | solution.py:40
  597.9 24.0 %collective-permute-done.16.refs_3_ = bf16[320,1600]{1,0:T(8,128)(2,1)} collective-permute-done((bf16[320,1600]{1,0:T(8,128)(2,1)S(1)}, bf16[320,1600]{1,0:T(8,128)(2,1)}, u32[]{:S(2)}, u32[]{:S(2)}) %collective-permute-start.16) | collective-permute-done | bytes 1024032 | tf_op jit(solution)/shard_map/ppermute | solution.py:40
  625.8 7.0 copy.555
  637.6 19.4 %fusion.353 = f32[1280,2816]{1,0:T(8,128)} fusion(bf16[1280,1600]{1,0:T(8,128)(2,1)} %bitcast.693, bf16[1600,2816]{1,0:T(8,128)(2,1)} %bitcast.828), kind=kOutput, calls=%fused_computation.674 | convolution fusion | flops 11534336000 | bytes 27525120 | tf_op jit(solution)/shard_map/dot_general | solution.py:356
  657.0 17.1 %multiply_convert_fusion.5 = (bf16[1280,1408]{1,0:T(8,128)(2,1)}, bf16[1280,1408]{1,0:T(8,128)(2,1)}, bf16[1280,1408]{1,0:T(8,128)(2,1)S(1)}) fusion(f32[1280,2816]{1,0:T(8,128)} %fusion.353, bf16[1280,1600]{1,0:T(8,128)(2,1)} %bitcast.696, bf16[1600,1408]{1,0:T(8,128)(2,1)} %all-gather.6.cloned.1.call-done), kind=kOutput, calls=%fused_computation.43 | convolution fusion | flops 5796003840 | bytes 33832960 | tf_op jit(solution)/shard_map/dot_general | solution.py:356
  675.9 8.2 convolution_convert_fusion.1
  684.1 6.8 copy.521
  694.7 10.3 convolution_convert_fusion.5
  705.1 17.7 %convolution_convert_fusion.4 = bf16[1280,1600]{0,1:T(8,128)(2,1)} fusion(bf16[1600,2816]{1,0:T(8,128)(2,1)} %bitcast.829, bf16[1280,1408]{1,0:T(8,128)(2,1)} %get-tuple-element.337, bf16[1280,1408]{1,0:T(8,128)(2,1)} %get-tuple-element.336), kind=kOutput, calls=%fused_computation.38 | convolution fusion | flops 11550801920 | bytes 20316160 | tf_op jit(solution)/shard_map/dot_general | solution.py:360
  722.8 6.9 copy.522
  743.6 7.2 copy.554
  750.8 11.9 collective-permute-done.19
  762.7 22.2 %collective-permute-done.24 = bf16[320,1600]{1,0:T(8,128)(2,1)} collective-permute-done((bf16[320,1600]{1,0:T(8,128)(2,1)}, bf16[320,1600]{1,0:T(8,128)(2,1)}, u32[]{:S(2)}, u32[]{:S(2)}) %collective-permute-start.24) | collective-permute-done | bytes 1024032 | tf_op jit(solution)/shard_map/ppermute | solution.py:40
  798.5 14.3 fusion.15
  825.2 9.3 multiply_reduce_fusion.1
  834.5 9.3 collective-permute-done.26.refs_3_
  865.4 11.0 multiply_reduce_fusion.4
  882.0 6.5 reshape.1235
  888.6 14.1 fusion.14
  907.6 9.4 multiply_reduce_fusion.2
  917.1 16.6 %multiply_convert_fusion.2 = (bf16[5,320,1280]{2,1,0:T(8,128)(2,1)}, bf16[5,320,1280]{2,1,0:T(8,128)(2,1)}) fusion(f32[5,320,1280]{2,1,0:T(8,128)} %get-tuple-element.471, f32[5,320,1280]{2,1,0:T(8,128)} %copy-done.14, f32[5,320]{1,0:T(8,128)S(1)} %get-tuple-element.470, f32[5,320]{1,0:T(8,128)S(1)} %log_add_fusion, ...), kind=kLoop, calls=%fused_computation.21 | loop fusion | flops 24576000 | bytes 41804800 | tf_op jit(solution)/shard_map/convert_element_type | solution.py:417
  985.4 6.9 convolution_convert_fusion.7
  995.5 13.4 fusion.21
  1008.9 9.5 copy.550
  1035.0 11.2 multiply_reduce_fusion.9
  1066.6 8.4 copy.585
  1075.0 9.5 reshape.1328
  1088.8 11.6 multiply_reduce_fusion.7
  1106.1 8.1 fusion.28
  1114.2 8.6 concatenate.119
  1128.5 11.4 fusion.10
  1139.9 6.8 copy.549
  1154.4 12.8 convolution_convert_fusion
  1191.4 164.9 %shard_map.267 = (f32[600,400]{1,0:T(8,128)}, f32[200,1792]{1,0:T(8,128)}, f32[200,896]{1,0:T(8,128)}) custom-call(bf16[8,600,400]{2,1,0:T(8,128)(2,1)} %pad_maximum_fusion.1.refs_0_, bf16[8,200,1792]{2,1,0:T(8,128)(2,1)} %bitcast.765, bf16[8,200,896]{2,1,0:T(8,128)(2,1)} %bitcast.758), custom_call_target="tpu_custom_call" | custom-call | bytes 12441600 | tf_op jit(solution)/shard_map/pallas_call | solution.py:304
  1388.9 16.1 %collective-permute-done.32 = bf16[320,1600]{1,0:T(8,128)(2,1)S(1)} collective-permute-done((bf16[320,1600]{1,0:T(8,128)(2,1)S(1)}, bf16[320,1600]{1,0:T(8,128)(2,1)S(1)}, u32[]{:S(2)}, u32[]{:S(2)}) %collective-permute-start.32) | collective-permute-done | bytes 1024032 | tf_op jit(solution)/shard_map/ppermute | solution.py:40
  (905 shorter events, 497.9 us)
Async XLA Ops:
  7.2 630.4 %all-gather.4.cloned.1.call-start = ((), (), s32[]{:S(2)}) async-start(), calls=%async_computation.2 | async-start | bytes 10137600 | tf_op jit(solution)/shard_map/all_gather | solution.py:324
  7.2 50.4 %collective-permute-start.4 = (bf16[200,560]{1,0:T(8,128)(2,1)}, bf16[200,560]{1,0:T(8,128)(2,1)S(1)}, u32[]{:S(2)}, u32[]{:S(2)}) collective-permute-start(bf16[200,560]{1,0:T(8,128)(2,1)} %refs_1_.3), channel_id=1, source_target_pairs={{0,2},{1,3},{2,0},{3,1},{4,6},{5,7},{6,4},{7,5},{8,10},{9,11},{10,... | collective-permute-start | bytes 672008 | tf_op jit(solution)/shard_map/ppermute | solution.py:40
  10.3 51.7 %collective-permute-start.3 = (bf16[200,560]{1,0:T(8,128)(2,1)}, bf16[200,560]{1,0:T(8,128)(2,1)S(1)}, u32[]{:S(2)}, u32[]{:S(2)}) collective-permute-start(bf16[200,560]{1,0:T(8,128)(2,1)} %refs_1_.3), channel_id=1, source_target_pairs={{0,1},{1,0},{2,3},{3,2},{4,5},{5,4},{6,7},{7,6},{8,9},{9,8},{10,11... | collective-permute-start | bytes 672008 | tf_op jit(solution)/shard_map/ppermute | solution.py:40
  13.6 44.1 %collective-permute-start.6 = (bf16[200,832]{1,0:T(8,128)(2,1)}, bf16[200,832]{1,0:T(8,128)(2,1)}, u32[]{:S(2)}, u32[]{:S(2)}) collective-permute-start(bf16[200,832]{1,0:T(8,128)(2,1)} %get-tuple-element.398), channel_id=1, source_target_pairs={{0,1},{1,2},{2,0},{4,5},{5,6},{6,4},{8,9},{9,10},{10,8},{12,13},{1... | collective-permute-start | bytes 998408 | tf_op jit(solution)/shard_map/ppermute | solution.py:334
  16.1 42.0 %collective-permute-start.7 = (bf16[200,832]{1,0:T(8,128)(2,1)}, bf16[200,832]{1,0:T(8,128)(2,1)}, u32[]{:S(2)}, u32[]{:S(2)}) collective-permute-start(bf16[200,832]{1,0:T(8,128)(2,1)} %get-tuple-element.397), channel_id=1, source_target_pairs={{1,3},{2,1},{3,2},{5,7},{6,5},{7,6},{9,11},{10,9},{11,10},{13,15},... | collective-permute-start | bytes 998408 | tf_op jit(solution)/shard_map/ppermute | solution.py:335
  17.5 291.3 %collective-permute-start.1 = (bf16[320,1600]{1,0:T(8,128)(2,1)}, bf16[320,1600]{1,0:T(8,128)(2,1)}, u32[]{:S(2)}, u32[]{:S(2)}) collective-permute-start(bf16[320,1600]{1,0:T(8,128)(2,1)} %refs_1_.2), channel_id=1, source_target_pairs={{0,2},{1,3},{2,0},{3,1},{4,6},{5,7},{6,4},{7,5},{8,10},{9,11},{10,... | collective-permute-start | bytes 3072008 | tf_op jit(solution)/shard_map/ppermute | solution.py:40
  23.7 633.3 %all-gather.6.cloned.1.call-start = ((), (), s32[]{:S(2)}) async-start(), calls=%async_computation.4 | async-start | bytes 5068800 | tf_op jit(solution)/shard_map/all_gather | solution.py:324
  57.7 313.3 %collective-permute-start = (bf16[320,1600]{1,0:T(8,128)(2,1)S(1)}, bf16[320,1600]{1,0:T(8,128)(2,1)}, u32[]{:S(2)}, u32[]{:S(2)}) collective-permute-start(bf16[320,1600]{1,0:T(8,128)(2,1)S(1)} %copy-done.6), channel_id=1, source_target_pairs={{0,1},{1,0},{2,3},{3,2},{4,5},{5,4},{6,7},{7,6},{8,9},{9,8},{10,11... | collective-permute-start | bytes 3072008 | tf_op jit(solution)/shard_map/ppermute | solution.py:40
  305.5 31.8 %collective-permute-start.10 = (bf16[400,1600]{1,0:T(8,128)(2,1)}, bf16[400,1600]{1,0:T(8,128)(2,1)}, u32[]{:S(2)}, u32[]{:S(2)}) collective-permute-start(bf16[400,1600]{1,0:T(8,128)(2,1)} %get-tuple-element.417), channel_id=1, source_target_pairs={{0,3},{1,2},{2,1},{3,0},{4,7},{5,6},{6,5},{7,4},{8,11},{9,10},{10,... | collective-permute-start | bytes 3840008 | tf_op jit(solution)/shard_map/ppermute | solution.py:40
  305.5 31.8 %collective-permute-start.8 = (bf16[400,1600]{1,0:T(8,128)(2,1)}, bf16[400,1600]{1,0:T(8,128)(2,1)}, u32[]{:S(2)}, u32[]{:S(2)}) collective-permute-start(bf16[400,1600]{1,0:T(8,128)(2,1)} %get-tuple-element.418), channel_id=1, source_target_pairs={{0,1},{1,0},{2,3},{3,2},{4,5},{5,4},{6,7},{7,6},{8,9},{9,8},{10,11... | collective-permute-start | bytes 3840008 | tf_op jit(solution)/shard_map/ppermute | solution.py:40
  306.9 58.7 %collective-permute-start.9 = (bf16[400,1600]{1,0:T(8,128)(2,1)}, bf16[400,1600]{1,0:T(8,128)(2,1)}, u32[]{:S(2)}, u32[]{:S(2)}) collective-permute-start(bf16[400,1600]{1,0:T(8,128)(2,1)} %get-tuple-element.419), channel_id=1, source_target_pairs={{0,2},{1,3},{2,0},{3,1},{4,6},{5,7},{6,4},{7,5},{8,10},{9,11},{10,... | collective-permute-start | bytes 3840008 | tf_op jit(solution)/shard_map/ppermute | solution.py:40
  308.9 62.0 %collective-permute-start.2 = (bf16[320,1600]{1,0:T(8,128)(2,1)}, bf16[320,1600]{1,0:T(8,128)(2,1)S(1)}, u32[]{:S(2)}, u32[]{:S(2)}) collective-permute-start(bf16[320,1600]{1,0:T(8,128)(2,1)} %collective-permute-done.1.refs_3_), channel_id=1, source_target_pairs={{0,1},{1,0},{2,3},{3,2},{4,5},{5,4},{6,7},{7,6},{8,9},{9,8},{10,11... | collective-permute-start | bytes 3072008 | tf_op jit(solution)/shard_map/ppermute | solution.py:40
  419.4 113.3 %collective-permute-start.11 = (bf16[2,320,1600]{2,1,0:T(8,128)(2,1)}, bf16[2,320,1600]{2,1,0:T(8,128)(2,1)}, u32[]{:S(2)}, u32[]{:S(2)}) collective-permute-start(bf16[2,320,1600]{2,1,0:T(8,128)(2,1)} %dynamic-slice_bitcast_fusion.4), channel_id=1, source_target_pairs={{0,1},{1,0},{2,3},{3,2},{4,5},{5,4},{6,7},{7,6},{8,9},{9,8},{10,11... | collective-permute-start | bytes 6144008 | tf_op jit(solution)/shard_map/ppermute | solution.py:40
  521.6 14.9 %collective-permute-start.13 = (bf16[2,320,1600]{2,1,0:T(8,128)(2,1)}, bf16[2,320,1600]{2,1,0:T(8,128)(2,1)}, u32[]{:S(2)}, u32[]{:S(2)}) collective-permute-start(bf16[2,320,1600]{2,1,0:T(8,128)(2,1)} %dynamic-slice_bitcast_fusion.3), channel_id=1, source_target_pairs={{0,1},{1,0},{2,3},{3,2},{4,5},{5,4},{6,7},{7,6},{8,9},{9,8},{10,11... | collective-permute-start | bytes 6144008 | tf_op jit(solution)/shard_map/ppermute | solution.py:40
  522.2 75.2 %collective-permute-start.21 = (bf16[320,1600]{1,0:T(8,128)(2,1)S(1)}, bf16[320,1600]{1,0:T(8,128)(2,1)S(1)}, u32[]{:S(2)}, u32[]{:S(2)}) collective-permute-start(bf16[320,1600]{1,0:T(8,128)(2,1)S(1)} %fusion.125.refs_1_), channel_id=1, source_target_pairs={{0,2},{1,3},{2,0},{3,1},{4,6},{5,7},{6,4},{7,5},{8,10},{9,11},{10,... | collective-permute-start | bytes 3072008 | tf_op jit(solution)/shard_map/ppermute | solution.py:40
  523.3 914.8 %reduce-scatter.7.cloned.1.call-start = ((), (), s32[]{:S(2)}) async-start(), calls=%async_computation.5 | async-start | bytes 5068800
  534.6 36.9 %collective-permute-start.12 = (bf16[320,1600]{1,0:T(8,128)(2,1)S(1)}, bf16[320,1600]{1,0:T(8,128)(2,1)S(1)}, u32[]{:S(2)}, u32[]{:S(2)}) collective-permute-start(bf16[320,1600]{1,0:T(8,128)(2,1)S(1)} %fusion.122), channel_id=1, source_target_pairs={{0,2},{1,3},{2,0},{3,1},{4,6},{5,7},{6,4},{7,5},{8,10},{9,11},{10,... | collective-permute-start | bytes 3072008 | tf_op jit(solution)/shard_map/ppermute | solution.py:40
  538.0 55.4 %collective-permute-start.14 = (bf16[320,1600]{1,0:T(8,128)(2,1)S(1)}, bf16[320,1600]{1,0:T(8,128)(2,1)S(1)}, u32[]{:S(2)}, u32[]{:S(2)}) collective-permute-start(bf16[320,1600]{1,0:T(8,128)(2,1)S(1)} %fusion.120), channel_id=1, source_target_pairs={{0,2},{1,3},{2,0},{3,1},{4,6},{5,7},{6,4},{7,5},{8,10},{9,11},{10,... | collective-permute-start | bytes 3072008 | tf_op jit(solution)/shard_map/ppermute | solution.py:40
  596.9 25.0 %collective-permute-start.16 = (bf16[320,1600]{1,0:T(8,128)(2,1)S(1)}, bf16[320,1600]{1,0:T(8,128)(2,1)}, u32[]{:S(2)}, u32[]{:S(2)}) collective-permute-start(bf16[320,1600]{1,0:T(8,128)(2,1)S(1)} %multiply_convert_fusion.15.refs_1_), channel_id=1, source_target_pairs={{0,2},{1,3},{2,0},{3,1},{4,6},{5,7},{6,4},{7,5},{8,10},{9,11},{10,... | collective-permute-start | bytes 3072008 | tf_op jit(solution)/shard_map/ppermute | solution.py:40
  597.4 24.5 %collective-permute-start.20 = (bf16[320,1600]{1,0:T(8,128)(2,1)S(1)}, bf16[320,1600]{1,0:T(8,128)(2,1)S(1)}, u32[]{:S(2)}, u32[]{:S(2)}) collective-permute-start(bf16[320,1600]{1,0:T(8,128)(2,1)S(1)} %fusion.125.refs_1_), channel_id=1, source_target_pairs={{0,1},{1,0},{2,3},{3,2},{4,5},{5,4},{6,7},{7,6},{8,9},{9,8},{10,11... | collective-permute-start | bytes 3072008 | tf_op jit(solution)/shard_map/ppermute | solution.py:40
  597.4 24.5 %collective-permute-start.22 = (bf16[320,1600]{1,0:T(8,128)(2,1)S(1)}, bf16[320,1600]{1,0:T(8,128)(2,1)S(1)}, u32[]{:S(2)}, u32[]{:S(2)}) collective-permute-start(bf16[320,1600]{1,0:T(8,128)(2,1)S(1)} %collective-permute-done.21.refs_3_), channel_id=1, source_target_pairs={{0,1},{1,0},{2,3},{3,2},{4,5},{5,4},{6,7},{7,6},{8,9},{9,8},{10,11... | collective-permute-start | bytes 3072008 | tf_op jit(solution)/shard_map/ppermute | solution.py:40
  597.9 35.0 %collective-permute-start.15 = (bf16[320,1600]{1,0:T(8,128)(2,1)S(1)}, bf16[320,1600]{1,0:T(8,128)(2,1)}, u32[]{:S(2)}, u32[]{:S(2)}) collective-permute-start(bf16[320,1600]{1,0:T(8,128)(2,1)S(1)} %multiply_convert_fusion.15.refs_1_), channel_id=1, source_target_pairs={{0,1},{1,0},{2,3},{3,2},{4,5},{5,4},{6,7},{7,6},{8,9},{9,8},{10,11... | collective-permute-start | bytes 3072008 | tf_op jit(solution)/shard_map/ppermute | solution.py:40
  621.9 11.0 collective-permute-start.17
  694.2 38.9 %collective-permute-start.18 = (bf16[2,320,1600]{2,1,0:T(8,128)(2,1)}, bf16[2,320,1600]{2,1,0:T(8,128)(2,1)}, u32[]{:S(2)}, u32[]{:S(2)}) collective-permute-start(bf16[2,320,1600]{2,1,0:T(8,128)(2,1)} %dynamic-slice_bitcast_fusion.2), channel_id=1, source_target_pairs={{0,1},{1,0},{2,3},{3,2},{4,5},{5,4},{6,7},{7,6},{8,9},{9,8},{10,11... | collective-permute-start | bytes 6144008 | tf_op jit(solution)/shard_map/ppermute | solution.py:40
  705.0 735.3 %reduce-scatter.5.cloned.1.call-start = ((), (), s32[]{:S(2)}) async-start(), calls=%async_computation.3 | async-start | bytes 10137600 | tf_op jit(solution)/shard_map/reduce_scatter | solution.py:328
  736.0 26.6 %collective-permute-start.19 = (bf16[320,1600]{1,0:T(8,128)(2,1)}, bf16[320,1600]{1,0:T(8,128)(2,1)}, u32[]{:S(2)}, u32[]{:S(2)}) collective-permute-start(bf16[320,1600]{1,0:T(8,128)(2,1)} %fusion.115), channel_id=1, source_target_pairs={{0,2},{1,3},{2,0},{3,1},{4,6},{5,7},{6,4},{7,5},{8,10},{9,11},{10,... | collective-permute-start | bytes 3072008 | tf_op jit(solution)/shard_map/ppermute | solution.py:40
  740.7 44.2 %collective-permute-start.24 = (bf16[320,1600]{1,0:T(8,128)(2,1)}, bf16[320,1600]{1,0:T(8,128)(2,1)}, u32[]{:S(2)}, u32[]{:S(2)}) collective-permute-start(bf16[320,1600]{1,0:T(8,128)(2,1)} %fusion.113), channel_id=1, source_target_pairs={{0,2},{1,3},{2,0},{3,1},{4,6},{5,7},{6,4},{7,5},{8,10},{9,11},{10,... | collective-permute-start | bytes 3072008 | tf_op jit(solution)/shard_map/ppermute | solution.py:40
  795.8 26.4 %collective-permute-start.29 = (bf16[320,1600]{1,0:T(8,128)(2,1)S(1)}, bf16[320,1600]{1,0:T(8,128)(2,1)S(1)}, u32[]{:S(2)}, u32[]{:S(2)}) collective-permute-start(bf16[320,1600]{1,0:T(8,128)(2,1)S(1)} %get-tuple-element.382.refs_1_), channel_id=1, source_target_pairs={{0,2},{1,3},{2,0},{3,1},{4,6},{5,7},{6,4},{7,5},{8,10},{9,11},{10,... | collective-permute-start | bytes 3072008 | tf_op jit(solution)/shard_map/ppermute | solution.py:40
  812.8 31.0 %collective-permute-start.28 = (bf16[320,1600]{1,0:T(8,128)(2,1)S(1)}, bf16[320,1600]{1,0:T(8,128)(2,1)S(1)}, u32[]{:S(2)}, u32[]{:S(2)}) collective-permute-start(bf16[320,1600]{1,0:T(8,128)(2,1)S(1)} %get-tuple-element.382.refs_1_), channel_id=1, source_target_pairs={{0,1},{1,0},{2,3},{3,2},{4,5},{5,4},{6,7},{7,6},{8,9},{9,8},{10,11... | collective-permute-start | bytes 3072008 | tf_op jit(solution)/shard_map/ppermute | solution.py:40
  812.8 30.9 %collective-permute-start.26 = (bf16[320,1600]{1,0:T(8,128)(2,1)S(1)}, bf16[320,1600]{1,0:T(8,128)(2,1)S(1)}, u32[]{:S(2)}, u32[]{:S(2)}) collective-permute-start(bf16[320,1600]{1,0:T(8,128)(2,1)S(1)} %get-tuple-element.381.refs_1_), channel_id=1, source_target_pairs={{0,2},{1,3},{2,0},{3,1},{4,6},{5,7},{6,4},{7,5},{8,10},{9,11},{10,... | collective-permute-start | bytes 3072008 | tf_op jit(solution)/shard_map/ppermute | solution.py:40
  813.8 44.0 %collective-permute-start.25 = (bf16[320,1600]{1,0:T(8,128)(2,1)S(1)}, bf16[320,1600]{1,0:T(8,128)(2,1)S(1)}, u32[]{:S(2)}, u32[]{:S(2)}) collective-permute-start(bf16[320,1600]{1,0:T(8,128)(2,1)S(1)} %get-tuple-element.381.refs_1_), channel_id=1, source_target_pairs={{0,1},{1,0},{2,3},{3,2},{4,5},{5,4},{6,7},{7,6},{8,9},{9,8},{10,11... | collective-permute-start | bytes 3072008 | tf_op jit(solution)/shard_map/ppermute | solution.py:40
  822.2 21.6 %collective-permute-start.30 = (bf16[320,1600]{1,0:T(8,128)(2,1)S(1)}, bf16[320,1600]{1,0:T(8,128)(2,1)S(1)}, u32[]{:S(2)}, u32[]{:S(2)}) collective-permute-start(bf16[320,1600]{1,0:T(8,128)(2,1)S(1)} %collective-permute-done.29.refs_3_), channel_id=1, source_target_pairs={{0,1},{1,0},{2,3},{3,2},{4,5},{5,4},{6,7},{7,6},{8,9},{9,8},{10,11... | collective-permute-start | bytes 3072008 | tf_op jit(solution)/shard_map/ppermute | solution.py:40
  843.7 14.1 collective-permute-start.27
  1023.2 144.0 %collective-permute-start.38 = (bf16[400,1600]{1,0:T(8,128)(2,1)}, bf16[400,1600]{1,0:T(8,128)(2,1)S(1)}, u32[]{:S(2)}, u32[]{:S(2)}) collective-permute-start(bf16[400,1600]{1,0:T(8,128)(2,1)} %get-tuple-element.352), channel_id=1, source_target_pairs={{0,1},{1,0},{2,3},{3,2},{4,5},{5,4},{6,7},{7,6},{8,9},{9,8},{10,11... | collective-permute-start | bytes 3840008 | tf_op jit(solution)/shard_map/ppermute | solution.py:40
  1023.7 143.5 %collective-permute-start.39 = (bf16[400,1600]{1,0:T(8,128)(2,1)}, bf16[400,1600]{1,0:T(8,128)(2,1)}, u32[]{:S(2)}, u32[]{:S(2)}) collective-permute-start(bf16[400,1600]{1,0:T(8,128)(2,1)} %get-tuple-element.351), channel_id=1, source_target_pairs={{0,2},{1,3},{2,0},{3,1},{4,6},{5,7},{6,4},{7,5},{8,10},{9,11},{10,... | collective-permute-start | bytes 3840008 | tf_op jit(solution)/shard_map/ppermute | solution.py:40
  1024.5 142.7 %collective-permute-start.40 = (bf16[400,1600]{1,0:T(8,128)(2,1)}, bf16[400,1600]{1,0:T(8,128)(2,1)}, u32[]{:S(2)}, u32[]{:S(2)}) collective-permute-start(bf16[400,1600]{1,0:T(8,128)(2,1)} %get-tuple-element.350), channel_id=1, source_target_pairs={{0,3},{1,2},{2,1},{3,0},{4,7},{5,6},{6,5},{7,4},{8,11},{9,10},{10,... | collective-permute-start | bytes 3840008 | tf_op jit(solution)/shard_map/ppermute | solution.py:40
  1149.9 225.8 %collective-permute-start.31 = (bf16[2,320,1600]{2,1,0:T(8,128)(2,1)}, bf16[2,320,1600]{2,1,0:T(8,128)(2,1)}, u32[]{:S(2)}, u32[]{:S(2)}) collective-permute-start(bf16[2,320,1600]{2,1,0:T(8,128)(2,1)} %dynamic-slice_bitcast_fusion), channel_id=1, source_target_pairs={{0,1},{1,0},{2,3},{3,2},{4,5},{5,4},{6,7},{7,6},{8,9},{9,8},{10,11... | collective-permute-start | bytes 6144008 | tf_op jit(solution)/shard_map/ppermute | solution.py:40
  1357.9 4.6 collective-permute-start.47
  1361.1 6.4 collective-permute-start.46
  1362.5 7.3 collective-permute-start.48
  1363.4 11.2 collective-permute-start.42
  1365.5 18.6 %collective-permute-start.41 = (bf16[200,896]{1,0:T(8,128)(2,1)S(1)}, bf16[200,896]{1,0:T(8,128)(2,1)S(1)}, u32[]{:S(2)}, u32[]{:S(2)}) collective-permute-start(bf16[200,896]{1,0:T(8,128)(2,1)S(1)} %convert_element_type.766.refs_1_), channel_id=1, source_target_pairs={{0,1},{1,0},{2,3},{3,2},{4,5},{5,4},{6,7},{7,6},{8,9},{9,8},{10,11... | collective-permute-start | bytes 1075208 | tf_op jit(solution)/shard_map/ppermute | solution.py:40
  1367.5 14.2 collective-permute-start.44
  1369.8 11.9 collective-permute-start.45
  1374.7 9.4 collective-permute-start.43
  1377.5 27.5 %collective-permute-start.32 = (bf16[320,1600]{1,0:T(8,128)(2,1)S(1)}, bf16[320,1600]{1,0:T(8,128)(2,1)S(1)}, u32[]{:S(2)}, u32[]{:S(2)}) collective-permute-start(bf16[320,1600]{1,0:T(8,128)(2,1)S(1)} %fusion.110), channel_id=1, source_target_pairs={{0,2},{1,3},{2,0},{3,1},{4,6},{5,7},{6,4},{7,5},{8,10},{9,11},{10,... | collective-permute-start | bytes 3072008 | tf_op jit(solution)/shard_map/ppermute | solution.py:40
  1413.1 7.6 collective-permute-start.34
  1430.7 5.4 collective-permute-start.37
  (252 other events, 4461.8 us)
Sparse Core Ops, SparseCore 0:
  23.8 196.6 all-gather.3
  523.5 75.4 all-gather.5
  705.1 107.8 reduce-scatter.6
  816.3 156.7 reduce-scatter.4

commit v3 on v2

v3 whole, which is shorter than its diff:
```python
import jax
import jax.numpy as jnp
from jax import lax
from jax.experimental import pallas as pl
from jax.experimental.pallas import tpu as pltpu
from jax.sharding import PartitionSpec as P

D = 1600
HEADS = 25
KV_HEADS = 5
HEAD = 64
INNER = 3200
SSM_HEAD = 64
STATE = 16
CONV = 4
FF = 5504
WINDOW = 1024
SSM_HEADS = 50

NORM_EPS = 1e-05
MASKED = -1e30
LOW = jnp.bfloat16
FULL = jnp.float32

SEQ = 4
GROUP_HEADS = HEADS // KV_HEADS
QW = GROUP_HEADS * HEAD
LOCAL_HEADS = 13
LOCAL_CH = LOCAL_HEADS * SSM_HEAD
CHUNK = 128
UNITS = FF // SEQ
UNITS_PAD = 1408
BCDT_PAD = 128
OUT_AT, O_AT, O5_AT, OUT_WIDTH = 0, 896, 1280, 1600
FIRST_HEAD = tuple((SSM_HEADS * s // 2 + 1) // 2 for s in range(SEQ))
HEAD_COUNT = tuple(b - a for a, b in zip(FIRST_HEAD, FIRST_HEAD[1:] + (SSM_HEADS,)))


def swap(value, axis, bit):
    return lax.ppermute(value, axis, [(i, i ^ bit) for i in range(lax.axis_size(axis))])


def place_kernel(count, index_ref, *refs):
    blocks, stacked, held, in_sems, out_sems = refs[:count], *refs[count:]
    loads = [
        pltpu.make_async_copy(block, held.at[i], in_sems.at[i]) for i, block in enumerate(blocks)
    ]
    stores = [
        pltpu.make_async_copy(held.at[i], stacked.at[index_ref[i]], out_sems.at[i])
        for i in range(count)
    ]
    for load in loads:
        load.start()
    for load, store in zip(loads, stores):
        load.wait()
        store.start()
    for store in stores:
        store.wait()


def place(blocks):
    count = len(blocks)
    block = blocks[0][1]
    anywhere = pl.BlockSpec(memory_space=pl.ANY)
    return pl.pallas_call(
        lambda *refs: place_kernel(count, *refs),
        out_shape=jax.ShapeDtypeStruct((count,) + block.shape, block.dtype),
        grid_spec=pltpu.PrefetchScalarGridSpec(
            num_scalar_prefetch=1,
            grid=(1,),
            in_specs=[anywhere] * count,
            out_specs=anywhere,
            scratch_shapes=[
                pltpu.VMEM((count,) + block.shape, block.dtype),
                pltpu.SemaphoreType.DMA((count,)),
                pltpu.SemaphoreType.DMA((count,)),
            ],
        ),
        compiler_params=pltpu.CompilerParams(vmem_limit_bytes=32 << 20),
        cost_estimate=pl.CostEstimate(
            flops=0, bytes_accessed=2 * count * block.size * block.dtype.itemsize, transcendentals=0
        ),
    )(jnp.stack([jnp.asarray(i, jnp.int32) for i, _ in blocks]), *[b for _, b in blocks])


def seq_order():
    me = lax.axis_index("seq")
    return [me, me ^ 1, me ^ 2, me ^ 3]


def seq_arrivals(block):
    far = swap(block, "seq", 2)
    return [block, swap(block, "seq", 1), far, swap(far, "seq", 1)]


def gather_seq(block):
    return place(list(zip(seq_order(), seq_arrivals(block))))


def scatter_begin(part):
    core = lax.axis_index("seq") % 2
    by_core = part.astype(LOW).reshape((2, 2, part.shape[0] // SEQ) + part.shape[1:])
    give = lax.dynamic_index_in_dim(by_core, 1 - core, 1, False)
    keep = lax.dynamic_index_in_dim(by_core, core, 1, False)
    return keep, swap(give, "seq", 1)


def scatter_far(keep, got):
    far = lax.axis_index("seq") // 2
    at = lambda a, i: lax.dynamic_index_in_dim(a, i, 0, False).astype(FULL)
    give_far = (at(keep, 1 - far) + at(got, 1 - far)).astype(LOW)
    return at(keep, far) + at(got, far), swap(give_far, "seq", 2)


def scatter_end(held, got_far):
    return held + got_far.astype(FULL)


def after(values, done):
    return lax.optimization_barrier((values, done))[0]


def line_place():
    me = lax.axis_index("dp")
    return lax.axis_size("dp") // 2, me // 2, lax.rem(me, 2)


def greet(line, z, x):
    barrier = pltpu.get_barrier_semaphore()

    def signal(target):
        pl.semaphore_signal(
            barrier, inc=1, device_id={"dp": target}, device_id_type=pl.DeviceIdType.MESH
        )

    signal(2 * z + 1 - x)
    pl.when(z > 0)(lambda: signal(2 * (z - 1) + x))
    pl.when(z < line - 1)(lambda: signal(2 * (z + 1) + x))
    pl.semaphore_wait(
        barrier, 1 + (z > 0).astype(jnp.int32) + (z < line - 1).astype(jnp.int32)
    )


def gather_kernel(count, line, *refs):
    packets, outs = refs[:count], refs[count : 2 * count]
    own_sem, up_sem, down_sem, line_sem, give_sem, got_sem = refs[2 * count :]
    _, z, x = line_place()
    greet(line, z, x)

    def copy(src, i, zb, send_sem, recv_sem, target):
        return pltpu.make_async_remote_copy(
            src_ref=src,
            dst_ref=outs[i].at[2 * zb + x],
            send_sem=send_sem.at[i, zb],
            recv_sem=recv_sem.at[i, zb],
            device_id={"dp": target},
            device_id_type=pl.DeviceIdType.MESH,
        )

    up_to = lambda src, i, zb: copy(src, i, zb, up_sem, line_sem, 2 * (z + 1) + x)
    down_to = lambda src, i, zb: copy(src, i, zb, down_sem, line_sem, 2 * (z - 1) + x)
    give = lambda src, i, zb: copy(src, i, zb, give_sem, got_sem, 2 * z + 1 - x)
    held = lambda i, zb: outs[i].at[2 * zb + x]
    own = lambda i: pltpu.make_async_copy(packets[i], held(i, z), own_sem.at[i])

    for turn in range(count + line - 1):
        for i in range(count):
            far = turn - i
            if far == 0:
                own(i).start()
                give(packets[i], i, z).start()
                pl.when(z < line - 1)(lambda: up_to(packets[i], i, z).start())
                pl.when(z > 0)(lambda: down_to(packets[i], i, z).start())
            elif 0 < far < line:

                @pl.when(z - far >= 0)
                def _():
                    zb = z - far
                    up_to(held(i, zb), i, zb).wait_recv()
                    pl.when(z < line - 1)(lambda: up_to(held(i, zb), i, zb).start())
                    give(held(i, zb), i, zb).start()

                @pl.when(z + far < line)
                def _():
                    zb = z + far
                    down_to(held(i, zb), i, zb).wait_recv()
                    pl.when(z > 0)(lambda: down_to(held(i, zb), i, zb).start())
                    give(held(i, zb), i, zb).start()

    for i in range(count):
        own(i).wait()
        for zb in range(line):
            give(held(i, zb), i, zb).wait()
            pl.when((zb <= z) & (z < line - 1))(lambda: up_to(held(i, zb), i, zb).wait_send())
            pl.when((zb >= z) & (z > 0))(lambda: down_to(held(i, zb), i, zb).wait_send())


def gather_dp(packets, collective_id):
    total = lax.axis_size("dp")
    if total != 8:
        return [lax.all_gather(packet, "dp", axis=0) for packet in packets]
    count, line = len(packets), total // 2
    sems = lambda *shape: pltpu.SemaphoreType.DMA(shape)
    return pl.pallas_call(
        lambda *refs: gather_kernel(count, line, *refs),
        out_shape=[jax.ShapeDtypeStruct((total,) + p.shape, p.dtype) for p in packets],
        in_specs=[pl.BlockSpec(memory_space=pltpu.VMEM)] * count,
        out_specs=[pl.BlockSpec(memory_space=pl.ANY)] * count,
        scratch_shapes=[sems(count)] + [sems(count, line) for _ in range(5)],
        compiler_params=pltpu.CompilerParams(
            collective_id=collective_id, has_side_effects=True, vmem_limit_bytes=32 << 20
        ),
        cost_estimate=pl.CostEstimate(
            flops=0,
            bytes_accessed=2 * total * sum(p.size * p.dtype.itemsize for p in packets),
            transcendentals=0,
        ),
    )(*packets)


def add_columns(total, parts):
    width = total.shape[-1]
    step = 128 if width % 256 else 256

    def columns(c):
        at = pl.ds(pl.multiple_of(c * step, step), step)
        total[:, at] = sum(part[:, at].astype(FULL) for part in parts).astype(total.dtype)

    pl.loop(0, width // step)(columns)
    if width % step:
        at = slice(width // step * step, width)
        total[:, at] = sum(part[:, at].astype(FULL) for part in parts).astype(total.dtype)


def scatter_kernel(count, line, *refs):
    parts, outs = refs[:count], refs[count : 2 * count]
    own_refs, near_refs, line_refs = (
        refs[2 * count : 3 * count],
        refs[3 * count : 4 * count],
        refs[4 * count : 5 * count],
    )
    load_sem, give_sem, got_sem, send_sem, line_sem = refs[5 * count :]
    _, z, x = line_place()
    greet(line, z, x)
    order = [t for pair in zip(range(line - 1, -1, -1), range(line)) for t in pair][:line]
    remote = lambda src, dst, send, recv, target: pltpu.make_async_remote_copy(
        src_ref=src,
        dst_ref=dst,
        send_sem=send,
        recv_sem=recv,
        device_id={"dp": target},
        device_id_type=pl.DeviceIdType.MESH,
    )
    give = lambda i, t: remote(
        parts[i].at[2 * t + 1 - x],
        near_refs[i].at[t],
        give_sem.at[i, t],
        got_sem.at[i, t],
        2 * z + 1 - x,
    )
    load = lambda i, t: pltpu.make_async_copy(
        parts[i].at[2 * t + x], own_refs[i].at[t], load_sem.at[i, t]
    )
    along = lambda i, t, slot, target: remote(
        own_refs[i].at[t], line_refs[i].at[slot], send_sem.at[i, t], line_sem.at[i, slot], target
    )
    for i in range(count):
        for t in order:
            load(i, t).start()
            give(i, t).start()
    for i in range(count):
        own, near, held = own_refs[i], near_refs[i], line_refs[i]
        for t in order:
            load(i, t).wait()
            give(i, t).wait_recv()

            @pl.when((t > z) & (z > 0) | (t < z) & (z < line - 1))
            def _():
                along(i, t, t, 0).wait_recv()
                add_columns(own.at[t], (own.at[t], near.at[t], held.at[t]))

            @pl.when((t > z) & (z == 0) | (t < z) & (z == line - 1))
            def _():
                add_columns(own.at[t], (own.at[t], near.at[t]))

            pl.when(t > z)(lambda: along(i, t, t, 2 * (z + 1) + x).start())
            pl.when(t == z - 1)(lambda: along(i, t, line, 2 * (z - 1) + x).start())
            pl.when(t < z - 1)(lambda: along(i, t, t, 2 * (z - 1) + x).start())
    for i in range(count):
        own, near, held = own_refs[i], near_refs[i], line_refs[i]
        pl.when(z > 0)(lambda: along(i, z, z, 0).wait_recv())
        pl.when(z < line - 1)(lambda: along(i, z, line, 0).wait_recv())
        for t in range(line):

            @pl.when(t == z)
            def _():
                terms = [own.at[t], near.at[t]]
                terms += [held.at[t]] if t > 0 else []
                terms += [held.at[line]] if t < line - 1 else []
                add_columns(outs[i], terms)

            pl.when(t != z)(lambda: along(i, t, t, 0).wait_send())
            give(i, t).wait_send()


def scatter_dp(parts, collective_id):
    total = lax.axis_size("dp")
    if total != 8:
        sums = [lax.psum_scatter(p, "dp", scatter_dimension=0) for p in parts]
        return [lax.optimization_barrier(p).astype(FULL) for p in sums]
    count, line = len(parts), total // 2
    sems = lambda *shape: pltpu.SemaphoreType.DMA(shape)
    return pl.pallas_call(
        lambda *refs: scatter_kernel(count, line, *refs),
        out_shape=[jax.ShapeDtypeStruct(p.shape[1:], FULL) for p in parts],
        in_specs=[pl.BlockSpec(memory_space=pl.ANY)] * count,
        out_specs=[pl.BlockSpec(memory_space=pltpu.VMEM)] * count,
        scratch_shapes=[pltpu.VMEM((line,) + p.shape[1:], p.dtype) for p in parts]
        + [pltpu.VMEM((line,) + p.shape[1:], p.dtype) for p in parts]
        + [pltpu.VMEM((line + 1,) + p.shape[1:], p.dtype) for p in parts]
        + [sems(count, line) for _ in range(4)]
        + [sems(count, line + 1)],
        compiler_params=pltpu.CompilerParams(
            collective_id=collective_id, has_side_effects=True, vmem_limit_bytes=56 << 20
        ),
        cost_estimate=pl.CostEstimate(
            flops=0, bytes_accessed=sum(p.size * 2 for p in parts), transcendentals=0
        ),
    )(*parts)


def gather_dp_apart(packet):
    return lax.all_gather(packet, "dp", axis=0, tiled=True)


def scatter_dp_apart(parts):
    summed = lax.psum_scatter(parts.astype(LOW), "dp", scatter_dimension=0, tiled=True)
    return lax.optimization_barrier(summed).astype(FULL)


def trade_halves(first, last):
    me = lax.axis_index("seq")
    one = lax.ppermute(jnp.where(me == 0, last, first), "seq", [(0, 1), (1, 2), (2, 0)])
    two = lax.ppermute(jnp.where(me == 3, first, last), "seq", [(1, 3), (2, 1), (3, 2)])
    return pick([first, one, one, two], me), pick([one, two, two, last], me)


def trade_back(x_part, z_part):
    me = lax.axis_index("seq")
    one = lax.ppermute(jnp.where(me == 0, z_part, x_part), "seq", [(1, 0), (2, 1), (0, 2)])
    two = lax.ppermute(jnp.where(me == 3, x_part, z_part), "seq", [(3, 1), (1, 2), (2, 3)])
    return pick([x_part, one, one, two], me), pick([one, two, two, z_part], me)


def mm(left, right):
    return jnp.dot(left, right, preferred_element_type=FULL)


def mm_nt(left, right):
    return lax.dot_general(left, right, (((1,), (1,)), ((), ())), preferred_element_type=FULL)


def mm_tn(left, right):
    return lax.dot_general(left, right, (((0,), (0,)), ((), ())), preferred_element_type=FULL)


def rms_norm(values, gain):
    return values * lax.rsqrt(jnp.mean(values * values, axis=-1, keepdims=True) + NORM_EPS) * gain


def join_tail(inputs_x, attn_o, ssm_o, gains):
    residual = inputs_x + 0.5 * (rms_norm(attn_o, gains[1]) + rms_norm(ssm_o, gains[2]))
    return (residual, rms_norm(residual, gains[3]))


STEP_AT = 2 * STATE
WIDE = 896
PAIRS = WIDE // 128
XZB = 1792


def dot_any(left, right, contract):
    return lax.dot_general(
        left, right, ((contract[:1], contract[1:]), ((), ())), preferred_element_type=FULL
    )


def low_dot(left, right, contract):
    return dot_any(left.astype(LOW), right.astype(LOW), contract)


def iota(shape, axis):
    return lax.broadcasted_iota(jnp.int32, shape, axis)


def pair_spread(values):
    rows = values.shape[0]
    low_half = iota((rows, 128), 1) < SSM_HEAD
    tiles = []
    for p in range(PAIRS):
        one = values[:, STEP_AT + 2 * p : STEP_AT + 2 * p + 1]
        two = values[:, STEP_AT + 2 * p + 1 : STEP_AT + 2 * p + 2]
        tiles.append(
            jnp.where(
                low_half,
                jnp.broadcast_to(one, (rows, 128)),
                jnp.broadcast_to(two, (rows, 128)),
            )
        )
    return jnp.concatenate(tiles, axis=1)


def halves(tile):
    low_half = iota(tile.shape, 1) < SSM_HEAD
    zero = jnp.zeros_like(tile)
    return jnp.concatenate([jnp.where(low_half, tile, zero), jnp.where(low_half, zero, tile)], axis=0)


def mamba_chunk(c, lengths_ref, xzb_ref, tail_ref, conv_ref, rate_ref, pad_ref):
    first_end = lengths_ref[0, 0]
    second_end = first_end + lengths_ref[0, 1]
    doc_of = lambda pos: (pos >= first_end).astype(jnp.int32) + (pos >= second_end).astype(jnp.int32)
    base = c * CHUNK
    square = (CHUNK, CHUNK)
    row, lane = iota(square, 0), iota(square, 1)
    doc_row = doc_of(base + row)
    doc_lane = doc_of(base + lane)
    before = jnp.where(c > 0, doc_of(base - 1), -1)
    end = doc_of(base + CHUNK - 1)
    causal = (row >= lane) & (doc_row == doc_lane)
    channel = iota((CHUNK, WIDE), 1) < LOCAL_CH

    raw = jnp.where(channel, xzb_ref[:, :WIDE], 0.0).astype(LOW).astype(FULL)
    gate = pltpu.roll(xzb_ref[:, LOCAL_CH - 64 :], XZB - LOCAL_CH, 1)[:, :WIDE]
    gate = jnp.where(channel, gate, 0.0)
    pad_ref[0:8] = tail_ref[:, :WIDE].astype(LOW).astype(FULL)
    pad_ref[8 : 8 + CHUNK] = raw
    taps = []
    pos = base + iota((CHUNK, 1), 0)
    conv = jnp.zeros((CHUNK, WIDE), FULL)
    for k in range(CONV):
        back = CONV - 1 - k
        same = (doc_of(pos) == doc_of(pos - back)) & (pos >= back)
        shifted = jnp.where(same, pad_ref[8 - back : 8 - back + CHUNK], 0.0)
        taps.append(shifted)
        conv = conv + conv_ref[k : k + 1] * shifted
    conv_sig = jax.nn.sigmoid(conv)
    act = conv * conv_sig

    bc = xzb_ref[:, 2 * LOCAL_CH :]
    b_in = jnp.where(lane < STATE, bc, 0.0)
    c_at = jnp.where((lane >= STATE) & (lane < 2 * STATE), bc, 0.0)
    c_in = pltpu.roll(c_at, CHUNK - STATE, 1)
    step = jnp.maximum(bc, 0.0) + jnp.log(1.0 + jnp.exp(-jnp.abs(bc)))
    lower = (row >= lane).astype(FULL)
    log = lax.dot_general(
        lower,
        -step * rate_ref[0:1],
        (((1,), (0,)), ((), ())),
        precision=lax.Precision.HIGHEST,
        preferred_element_type=FULL,
    )
    last = log[CHUNK - 1 : CHUNK]
    ends = jnp.where(doc_row == end, jnp.exp(last - log), 0.0)
    reach = jnp.where(doc_row == before, jnp.exp(log), 0.0)
    carry = jnp.where(end == before, jnp.exp(last), 0.0)
    gram = low_dot(c_in, b_in, (1, 1))
    log_t = log.T

    def decays(h):
        gap = log[:, STEP_AT + h : STEP_AT + h + 1] - log_t[STEP_AT + h : STEP_AT + h + 1]
        return jnp.exp(jnp.where(causal, gap, MASKED))

    step_wide = pair_spread(step)
    return dict(
        row=row, lane=lane, pos=pos, doc_of=doc_of, gate=gate, taps=taps, conv=conv, conv_sig=conv_sig,
        act=act, bc=bc, b_in=b_in, c_in=c_in, c_at=c_at, step=step, ends=ends, reach=reach,
        carry=carry, gram=gram, decays=decays, step_wide=step_wide, moved=act * step_wide,
    )


def mamba_forward_kernel(
    lengths_ref, xzb_ref, tail_ref, conv_ref, rate_ref, skip_ref, gated_ref, read_ref, states_ref, pad_ref, state_ref
):
    c = pl.program_id(0)

    @pl.when(c == 0)
    def _():
        state_ref[...] = jnp.zeros_like(state_ref)

    v = mamba_chunk(c, lengths_ref, xzb_ref, tail_ref, conv_ref, rate_ref, pad_ref)
    states_ref[0] = state_ref[STATE : 2 * STATE]
    moved = v["moved"]
    from_state = low_dot(v["c_at"], state_ref[...], (1, 0)) * pair_spread(v["reach"])
    tiles = []
    for p in range(PAIRS):
        mixing = jnp.concatenate(
            [(v["decays"](2 * p + j) * v["gram"]).astype(LOW) for j in range(2)], axis=1
        )
        tiles.append(dot_any(mixing, halves(moved[:, 128 * p : 128 * p + 128].astype(LOW)), (1, 0)))
    read = jnp.concatenate(tiles, axis=1) + from_state + skip_ref[0:1] * v["act"]
    read_ref[...] = read.astype(LOW)
    gated_ref[...] = (read * v["gate"] * jax.nn.sigmoid(v["gate"])).astype(LOW)
    added = low_dot(v["b_in"], moved * pair_spread(v["ends"]), (0, 0))[:STATE]
    state_ref[STATE : 2 * STATE] = pair_spread(v["carry"]) * state_ref[STATE : 2 * STATE] + added


def mamba_backward_kernel(
    lengths_ref, xzb_ref, tail_ref, conv_ref, rate_ref, skip_ref, states_ref, read_ref, d_gated_ref,
    d_xzb_ref, d_chan_ref, d_rate_ref, pad_ref, state_ref, d_state_ref, d_pad_ref,
):
    g = pl.program_id(0)
    c = pl.num_programs(0) - 1 - g

    @pl.when(g == 0)
    def _():
        state_ref[...] = jnp.zeros_like(state_ref)
        d_state_ref[...] = jnp.zeros_like(d_state_ref)
        d_pad_ref[...] = jnp.zeros_like(d_pad_ref)
        d_chan_ref[...] = jnp.zeros_like(d_chan_ref)
        d_rate_ref[...] = jnp.zeros_like(d_rate_ref)

    v = mamba_chunk(c, lengths_ref, xzb_ref, tail_ref, conv_ref, rate_ref, pad_ref)
    row, lane, act, moved, gate = v["row"], v["lane"], v["act"], v["moved"], v["gate"]
    state_ref[STATE : 2 * STATE] = states_ref[0]
    by_head = (iota((WIDE, 128), 0) // SSM_HEAD + STEP_AT == iota((WIDE, 128), 1)).astype(LOW)
    head_sum = lambda wide: dot_any(wide.astype(LOW), by_head, (1, 0))

    d_gated = d_gated_ref[...].astype(FULL)
    gate_sig = jax.nn.sigmoid(gate)
    d_read = d_gated * gate * gate_sig
    d_gate = d_gated * read_ref[...].astype(FULL) * gate_sig * (1.0 + gate * (1.0 - gate_sig))
    d_chan_ref[CONV : CONV + 1] += jnp.sum(d_read * act, axis=0, keepdims=True)
    d_act = skip_ref[0:1] * d_read

    d_log = jnp.zeros_like(v["gram"])
    d_log_t = jnp.zeros_like(v["gram"])
    d_gram = jnp.zeros_like(v["gram"])
    tiles = []
    for p in range(PAIRS):
        at = slice(128 * p, 128 * p + 128)
        d_pair = halves(d_read[:, at].astype(LOW))
        d_mixing = dot_any(d_pair, moved[:, at].astype(LOW), (1, 1))
        mixings = []
        for j in range(2):
            h = 2 * p + j
            decay = v["decays"](h)
            mixing = decay * v["gram"]
            d_one = d_mixing[CHUNK * j : CHUNK * (j + 1)]
            d_gram = d_gram + d_one * decay
            d_gap = d_one * mixing
            mixings.append(mixing.astype(LOW))
            d_log = d_log + jnp.where(lane == STEP_AT + h, jnp.sum(d_gap, axis=1, keepdims=True), 0.0)
            d_log_t = d_log_t + jnp.where(row == STEP_AT + h, jnp.sum(d_gap, axis=0, keepdims=True), 0.0)
        tiles.append(dot_any(jnp.concatenate(mixings, axis=0), d_pair, (0, 0)))
    d_moved = jnp.concatenate(tiles, axis=1)
    d_log = d_log - d_log_t.T

    d_product = d_read * pair_spread(v["reach"])
    state_low = state_ref[...].astype(LOW)
    product = dot_any(v["c_at"].astype(LOW), state_low, (1, 0))
    d_log = d_log + head_sum(d_product * product)
    d_c = low_dot(d_product, state_low, (1, 1)) + low_dot(d_gram, pltpu.roll(v["b_in"], STATE, 1), (1, 0))
    d_state_in = low_dot(v["c_at"], d_product, (0, 0))[STATE : 2 * STATE]

    d_state = d_state_ref[...]
    d_state_low = d_state.astype(LOW)
    ends_wide = pair_spread(v["ends"])
    d_put = dot_any(v["b_in"].astype(LOW), d_state_low, (1, 0)) * ends_wide
    d_b = low_dot(moved * ends_wide, d_state_low, (1, 1)) + low_dot(d_gram, v["c_in"], (0, 0))
    d_moved = d_moved + d_put
    d_ends = head_sum(d_put * moved)
    carry_wide = pair_spread(v["carry"])
    d_carry = head_sum(
        jnp.broadcast_to(
            jnp.sum(d_state[:STATE] * states_ref[0], axis=0, keepdims=True) * carry_wide, (16, WIDE)
        )
    )[0:1]
    d_last = jnp.sum(d_ends, axis=0, keepdims=True) + d_carry
    d_log = d_log - d_ends + jnp.where(row == CHUNK - 1, d_last, 0.0)
    d_state_ref[:STATE] = d_state_in + carry_wide * d_state[:STATE]

    d_act = d_act + d_moved * v["step_wide"]
    d_rate_step = lax.dot_general(
        (row >= lane).astype(FULL),
        d_log,
        (((0,), (0,)), ((), ())),
        precision=lax.Precision.HIGHEST,
        preferred_element_type=FULL,
    )
    d_step = head_sum(d_moved * act) - rate_ref[0:1] * d_rate_step
    d_rate_ref[0:1] += jnp.sum(-v["step"] * d_rate_step, axis=0, keepdims=True)
    is_step = (lane >= STEP_AT) & (lane < STEP_AT + LOCAL_HEADS)
    d_bc = d_b + d_c + jnp.where(is_step, d_step * jax.nn.sigmoid(v["bc"]), 0.0)

    d_conv = d_act * v["conv_sig"] * (1.0 + v["conv"] * (1.0 - v["conv_sig"]))
    d_pad_ref[0:CHUNK] = d_conv
    d_raw = jnp.zeros_like(d_conv)
    for k in range(CONV):
        ahead = CONV - 1 - k
        d_chan_ref[k : k + 1] += jnp.sum(d_conv * v["taps"][k], axis=0, keepdims=True)
        same = v["doc_of"](v["pos"]) == v["doc_of"](v["pos"] + ahead)
        d_raw = d_raw + conv_ref[k : k + 1] * jnp.where(same, d_pad_ref[ahead : ahead + CHUNK], 0.0)
    d_pad_ref[CHUNK : CHUNK + 8] = d_conv[0:8]

    moved_gate = pltpu.roll(jnp.concatenate([d_gate, jnp.zeros_like(row).astype(FULL)], axis=1), 64, 1)
    d_xzb_ref[:, : LOCAL_CH - 64] = d_raw[:, : LOCAL_CH - 64].astype(LOW)
    d_xzb_ref[:, LOCAL_CH - 64 : LOCAL_CH + 64] = (
        d_raw[:, LOCAL_CH - 64 :] + moved_gate[:, :128]
    ).astype(LOW)
    d_xzb_ref[:, LOCAL_CH + 64 : 2 * LOCAL_CH] = moved_gate[:, 128:WIDE].astype(LOW)
    d_xzb_ref[:, 2 * LOCAL_CH :] = d_bc.astype(LOW)


def mamba_specs(chunk_of):
    tail = lambda g: (jnp.maximum(chunk_of(g) * (CHUNK // 8) - 1, 0), 0)
    fixed = lambda shape: pl.BlockSpec(shape, lambda g: (0,) * len(shape))
    return [
        pl.BlockSpec(memory_space=pltpu.SMEM),
        pl.BlockSpec((CHUNK, XZB), lambda g: (chunk_of(g), 0)),
        pl.BlockSpec((8, XZB), tail),
        fixed((8, WIDE)),
        fixed((8, 128)),
        fixed((8, WIDE)),
    ]


def mamba_forward(lengths, xzb, conv_rows, rate_row, skip_row):
    total = xzb.shape[0]
    chunks = total // CHUNK
    by_chunk = lambda width: pl.BlockSpec((CHUNK, width), lambda g: (g, 0))
    return pl.pallas_call(
        mamba_forward_kernel,
        grid=(chunks,),
        in_specs=mamba_specs(lambda g: g),
        out_specs=[by_chunk(WIDE), by_chunk(WIDE), pl.BlockSpec((1, STATE, WIDE), lambda g: (g, 0, 0))],
        out_shape=[
            jax.ShapeDtypeStruct((total, WIDE), LOW),
            jax.ShapeDtypeStruct((total, WIDE), LOW),
            jax.ShapeDtypeStruct((chunks, STATE, WIDE), FULL),
        ],
        scratch_shapes=[pltpu.VMEM((8 + CHUNK, WIDE), FULL), pltpu.VMEM((CHUNK, WIDE), FULL)],
        compiler_params=pltpu.CompilerParams(vmem_limit_bytes=32 << 20),
        cost_estimate=pl.CostEstimate(flops=2 * 10**9, bytes_accessed=16 << 20, transcendentals=10**7),
    )(lengths, xzb, xzb, conv_rows, rate_row, skip_row)


def mamba_backward(lengths, xzb, conv_rows, rate_row, skip_row, states, read, d_gated):
    total = xzb.shape[0]
    chunks = total // CHUNK
    chunk_of = lambda g: chunks - 1 - g
    by_chunk = lambda width: pl.BlockSpec((CHUNK, width), lambda g: (chunk_of(g), 0))
    return pl.pallas_call(
        mamba_backward_kernel,
        grid=(chunks,),
        in_specs=mamba_specs(chunk_of)
        + [pl.BlockSpec((1, STATE, WIDE), lambda g: (chunk_of(g), 0, 0)), by_chunk(WIDE), by_chunk(WIDE)],
        out_specs=[
            by_chunk(XZB),
            pl.BlockSpec((8, WIDE), lambda g: (0, 0)),
            pl.BlockSpec((8, 128), lambda g: (0, 0)),
        ],
        out_shape=[
            jax.ShapeDtypeStruct((total, XZB), LOW),
            jax.ShapeDtypeStruct((8, WIDE), FULL),
            jax.ShapeDtypeStruct((8, 128), FULL),
        ],
        scratch_shapes=[
            pltpu.VMEM((8 + CHUNK, WIDE), FULL),
            pltpu.VMEM((CHUNK, WIDE), FULL),
            pltpu.VMEM((CHUNK, WIDE), FULL),
            pltpu.VMEM((8 + CHUNK, WIDE), FULL),
        ],
        compiler_params=pltpu.CompilerParams(vmem_limit_bytes=32 << 20),
        cost_estimate=pl.CostEstimate(flops=5 * 10**9, bytes_accessed=24 << 20, transcendentals=10**7),
    )(lengths, xzb, xzb, conv_rows, rate_row, skip_row, states, read, d_gated)


def head_under(h, at, value):
    row, lane = iota((QW, 128), 0), iota((QW, 128), 1)
    inside = (lane >= at) & (lane < at + HEAD) & (row == h * HEAD + lane - at)
    return jnp.where(inside, value, 0.0).astype(LOW)


def row_block(t):
    return jnp.where(t < SEQ, t, lax.axis_index("seq"))


def allowed_keys(lengths_ref, block, rows, extent):
    first_end = lengths_ref[0, 0]
    second_end = first_end + lengths_ref[0, 1]
    row = block * rows + iota((rows, 1), 0)
    start = jnp.where(row >= second_end, second_end, jnp.where(row >= first_end, first_end, 0))
    least = jnp.maximum(start, row - (WINDOW - 1))
    key = iota((rows, extent), 1)
    return (key >= least) & (key <= row)


def for_extent(block, rows, run):
    for e in range(SEQ):
        pl.when(block == e)(lambda e=e: run((e + 1) * rows))


def attention_forward_kernel(lengths_ref, q_ref, kv_ref, out_ref, log_ref):
    t, h = pl.program_id(0), pl.program_id(1)
    rows = q_ref.shape[0]
    block = row_block(t)

    def run(extent):
        q = dot_any(q_ref[...], head_under(h, 0, HEAD ** (-0.5)), (1, 0)).astype(LOW)
        kv = kv_ref[:extent]
        scores = dot_any(q, kv, (1, 1))
        scores = jnp.where(allowed_keys(lengths_ref, block, rows, extent), scores, MASKED)
        top = jnp.max(scores, axis=1, keepdims=True)
        expos = jnp.exp(scores - top)
        denom = jnp.sum(expos, axis=1, keepdims=True)
        mixed = dot_any((expos * (1.0 / denom)).astype(LOW), kv, (1, 0)).astype(LOW)
        out = dot_any(mixed, head_under(h, HEAD, 1.0), (1, 1)).astype(LOW)
        log = jnp.where(iota((rows, 128), 1) == h, top + jnp.log(denom), 0.0)

        @pl.when(h == 0)
        def _():
            out_ref[...] = out
            log_ref[...] = log

        @pl.when(h > 0)
        def _():
            out_ref[...] += out
            log_ref[...] += log

    for_extent(block, rows, run)


def attention_backward_kernel(
    lengths_ref, q_ref, kv_ref, out_ref, log_ref, d_out_ref, d_q_ref, d_kv_ref, sum_ref
):
    t, h = pl.program_id(0), pl.program_id(1)
    rows = q_ref.shape[0]
    block = row_block(t)

    @pl.when((h == 0) & ((t == 0) | (t == SEQ)))
    def _():
        sum_ref[...] = jnp.zeros_like(sum_ref)

    def run(extent):
        under_q = head_under(h, 0, HEAD ** (-0.5))
        q = dot_any(q_ref[...], under_q, (1, 0)).astype(LOW)
        d_out = dot_any(d_out_ref[...], head_under(h, HEAD, 1.0), (1, 0)).astype(LOW)
        log = jnp.sum(jnp.where(iota((rows, 128), 1) == h, log_ref[...], 0.0), axis=1, keepdims=True)
        own = iota((rows, QW), 1) // HEAD == h
        product = d_out_ref[...].astype(FULL) * out_ref[...].astype(FULL)
        d_total = jnp.sum(jnp.where(own, product, 0.0), axis=1, keepdims=True)
        kv = kv_ref[:extent]
        scores = dot_any(q, kv, (1, 1))
        allowed = allowed_keys(lengths_ref, block, rows, extent)
        probs = jnp.exp(jnp.where(allowed, scores - log, MASKED))
        d_probs = dot_any(d_out, kv, (1, 1))
        d_scores = (probs * (d_probs - d_total)).astype(LOW)
        sum_ref[:extent] += dot_any(probs.astype(LOW), d_out, (0, 0)) + dot_any(d_scores, q, (0, 0))
        d_q = dot_any(dot_any(d_scores, kv, (1, 0)).astype(LOW), under_q, (1, 1)).astype(LOW)

        @pl.when(h == 0)
        def _():
            d_q_ref[...] = d_q

        @pl.when(h > 0)
        def _():
            d_q_ref[...] += d_q

    for_extent(block, rows, run)

    @pl.when((h == GROUP_HEADS - 1) & (t >= SEQ - 1))
    def _():
        d_kv_ref[...] = sum_ref[...].astype(LOW)


def attention_specs(rows, group):
    by_step = lambda width: pl.BlockSpec((rows, width), lambda t, h: (t, 0))
    kv_block = pl.BlockSpec((group, 128), lambda t, h: (0, t // SEQ))
    return by_step, kv_block


def attention_forward(lengths, queries, kv, rows):
    by_step, kv_block = attention_specs(rows, kv.shape[0])
    return pl.pallas_call(
        attention_forward_kernel,
        grid=(SEQ + 1, GROUP_HEADS),
        in_specs=[pl.BlockSpec(memory_space=pltpu.SMEM), by_step(QW), kv_block],
        out_specs=[by_step(QW), by_step(128)],
        out_shape=[
            jax.ShapeDtypeStruct(queries.shape, LOW),
            jax.ShapeDtypeStruct((queries.shape[0], 128), FULL),
        ],
        compiler_params=pltpu.CompilerParams(vmem_limit_bytes=32 << 20),
        cost_estimate=pl.CostEstimate(flops=3 * 10**9, bytes_accessed=4 << 20, transcendentals=8 * 10**6),
    )(lengths, queries, kv)


def attention_backward(lengths, queries, kv, out, logs, d_out, rows):
    group = kv.shape[0]
    by_step, kv_block = attention_specs(rows, group)
    return pl.pallas_call(
        attention_backward_kernel,
        grid=(SEQ + 1, GROUP_HEADS),
        in_specs=[pl.BlockSpec(memory_space=pltpu.SMEM), by_step(QW), kv_block]
        + [by_step(QW), by_step(128), by_step(QW)],
        out_specs=[by_step(QW), kv_block],
        out_shape=[jax.ShapeDtypeStruct(queries.shape, LOW), jax.ShapeDtypeStruct(kv.shape, LOW)],
        scratch_shapes=[pltpu.VMEM((group, 128), FULL)],
        compiler_params=pltpu.CompilerParams(vmem_limit_bytes=32 << 20),
        cost_estimate=pl.CostEstimate(flops=8 * 10**9, bytes_accessed=8 << 20, transcendentals=8 * 10**6),
    )(lengths, queries, kv, out, logs, d_out)


def pick(options, seq_index):
    return lax.select_n(seq_index, *options)


def own_cut(values, seq_index, axis, unit):
    cuts = []
    for first, count in zip(FIRST_HEAD, HEAD_COUNT):
        cut = lax.slice_in_dim(values, first * unit, (first + count) * unit, axis=axis)
        pads = [(0, 0)] * values.ndim
        pads[axis] = (0, (LOCAL_HEADS - count) * unit)
        cuts.append(jnp.pad(cut, pads))
    return pick(cuts, seq_index)


def own_spread(values, seq_index, unit):
    spreads = []
    for first, count in zip(FIRST_HEAD, HEAD_COUNT):
        pads = [(0, 0)] * (values.ndim - 1) + [(first * unit, (SSM_HEADS - first - count) * unit)]
        spreads.append(jnp.pad(values[..., : count * unit], pads))
    return pick(spreads, seq_index)


def channel_cut(wide, seq_index, axis):
    return own_cut(wide, seq_index, axis, SSM_HEAD)


def bcdt_cut(w_bcdt, seq_index):
    first = pick([jnp.int32(h) for h in FIRST_HEAD], seq_index)
    count = pick([jnp.int32(c) for c in HEAD_COUNT], seq_index)
    source = jnp.arange(w_bcdt.shape[1], dtype=jnp.int32)[:, None]
    target = jnp.arange(BCDT_PAD, dtype=jnp.int32)[None]
    shared = (target < 2 * STATE) & (source == target)
    steps = (target >= 2 * STATE) & (target < 2 * STATE + count) & (source == target + first)
    return mm(w_bcdt, (shared | steps).astype(LOW)).astype(LOW)


def wide_of(arrivals):
    me = lax.axis_index("seq")
    return jnp.concatenate([pick(arrivals, me ^ j) for j in range(SEQ)], axis=1)


def on_device(
    tokens_in,
    doc_lengths,
    norm_gains,
    w_qkv,
    w_o,
    w_xz,
    w_bcdt,
    conv_w,
    ssm_rate,
    ssm_skip,
    w_out,
    w_gate_up,
    w_down,
    cotangent,
):
    rows = tokens_in.shape[0]
    group = rows * SEQ
    s = lax.axis_index("seq")
    dp_index = lax.axis_index("dp")
    dp_total = lax.axis_size("dp")
    block_rows = w_qkv.shape[0]
    kv_width = KV_HEADS * HEAD
    lengths = doc_lengths[0]
    live = (jnp.arange(rows, dtype=jnp.int32) + s * rows < lengths[0] + lengths[1]).astype(FULL)[:, None]

    gains_block = norm_gains.shape[1]
    conv_block = conv_w.shape[1]
    width = -(-max(conv_block, gains_block) // 128) * 128
    small = jnp.concatenate(
        [
            jnp.pad(conv_w, ((0, 4), (0, width - conv_block))),
            jnp.pad(norm_gains, ((0, 4), (0, width - gains_block))),
        ]
    )
    out_block = w_out.shape[0]
    out_packet = jnp.concatenate([w_o, w_out], axis=0)
    qkv_shards = seq_arrivals(w_qkv)
    x_part, z_part = trade_halves(
        w_xz[:, :LOCAL_CH], jnp.pad(w_xz[:, LOCAL_CH:], ((0, 0), (0, 2 * LOCAL_CH - w_xz.shape[1])))
    )
    token_blocks = seq_arrivals(tokens_in)
    small, out_cols = gather_dp([small, out_packet], 0)
    small, out_cols, qkv_shards, x_part, z_part, token_blocks = lax.optimization_barrier(
        (small, out_cols, qkv_shards, x_part, z_part, token_blocks)
    )
    full_conv = small[:, :4, :conv_block].transpose(1, 0, 2).reshape(4, INNER).astype(FULL)
    gains = small[:, 8:12, :gains_block].transpose(1, 0, 2).reshape(4, D).astype(FULL)
    tokens_group = place(list(zip(seq_order(), token_blocks))).reshape(group, D)
    normed = rms_norm(tokens_group.astype(FULL), gains[0]).astype(LOW)
    qkv_wide = wide_of(qkv_shards)
    q_at = lambda h: lax.dynamic_slice_in_dim(qkv_wide, h * QW, QW, 1)
    kv_at = lambda h: [
        lax.dynamic_slice_in_dim(qkv_wide, D + h * HEAD, HEAD, 1),
        lax.dynamic_slice_in_dim(qkv_wide, D + kv_width + h * HEAD, HEAD, 1),
    ]
    qkv_packet = jnp.concatenate(kv_at(s) + kv_at(KV_HEADS - 1) + [q_at(s), q_at(KV_HEADS - 1)], axis=1)
    xz_packet = jnp.concatenate([x_part, z_part, bcdt_cut(w_bcdt, s)], axis=1)
    full_qkv, full_xz = gather_dp([qkv_packet, xz_packet], 1)
    gate_up_packet = jnp.pad(w_gate_up, ((0, 0), (0, 0), (0, UNITS_PAD - UNITS))).reshape(block_rows, -1)
    down_packet = jnp.pad(w_down, ((0, 0), (0, UNITS_PAD - UNITS)))
    full_qkv, full_xz, out_cols, gate_up_packet, down_packet = lax.optimization_barrier(
        (full_qkv, full_xz, out_cols, gate_up_packet, down_packet)
    )
    full_qkv = full_qkv.reshape(D, -1)
    full_xz = full_xz.reshape(D, -1)
    full_gate_up = gather_dp_apart(gate_up_packet)
    full_down = gather_dp_apart(down_packet)

    d_total = cotangent.astype(FULL) * live
    d_ffn_group = gather_seq(d_total.astype(LOW)).reshape(group, D)

    own = lambda a: lax.dynamic_slice_in_dim(a, s * rows, rows, 0)
    normed_own = own(normed)
    kvq = mm(normed, full_qkv[:, : 256 + QW]).astype(LOW)
    q_last = mm(normed_own, full_qkv[:, 256 + QW :]).astype(LOW)
    queries = jnp.concatenate([kvq[:, 256:], q_last])
    kv = kvq[:, :256]
    attended, logs = attention_forward(doc_lengths, queries, kv, rows)
    o_cols = out_cols[:, :block_rows].reshape(D, -1)
    mamba_cols = out_cols[:, block_rows:].reshape(INNER, -1)

    def rows_for(peer):
        cut = channel_cut(mamba_cols, peer, 0)
        heads = lax.dynamic_slice_in_dim(o_cols, peer * QW, QW, 0)
        spare = lambda n: jnp.zeros((n, cut.shape[1]), LOW)
        return jnp.concatenate(
            [cut, spare(O_AT - LOCAL_CH), heads, spare(O5_AT - O_AT - QW), o_cols[(KV_HEADS - 1) * QW :]]
        )

    out_pieces = [rows_for(s)] + [swap(rows_for(s ^ bit), "seq", bit) for bit in (1, 2, 3)]
    out_rows = lax.optimization_barrier(wide_of(after(out_pieces, attended)))
    w_out_rows = out_rows[:WIDE]
    w_o_rows = out_rows[O_AT : O_AT + QW]
    w_o5_rows = out_rows[O5_AT:]
    attn_part = mm(attended[:group], w_o_rows).astype(LOW)
    normed_now, attn_part = lax.optimization_barrier((normed, attn_part))
    attn_keep, attn_got = scatter_begin(attn_part)

    xzb = mm(normed_now, full_xz)
    attn_held, attn_far = scatter_far(attn_keep, after(attn_got, xzb))
    conv_rows = jnp.pad(channel_cut(full_conv, s, 1), ((0, 4), (0, WIDE - LOCAL_CH)))
    rate_row = jnp.pad(own_cut(ssm_rate, s, 0, 1), (STEP_AT, 128 - STEP_AT - LOCAL_HEADS))
    rate_row = jnp.broadcast_to(rate_row, (8, 128))
    skip_row = jnp.pad(jnp.repeat(own_cut(ssm_skip, s, 0, 1), SSM_HEAD), (0, WIDE - LOCAL_CH))
    skip_row = jnp.broadcast_to(skip_row, (8, WIDE))
    mamba_in = (doc_lengths, xzb, conv_rows, rate_row, skip_row)
    gated, read, states = mamba_forward(*mamba_in)
    ssm_held, ssm_far = scatter_far(*scatter_begin(mm(gated, w_out_rows)))
    attn_o = scatter_end(attn_held, after(attn_far, gated)) + mm(attended[group:], w_o5_rows)
    ssm_o = scatter_end(ssm_held, ssm_far)

    inputs_x = tokens_in.astype(FULL)
    (residual, normed_two), pull_join = jax.vjp(join_tail, inputs_x, attn_o, ssm_o, gains)
    normed_two = gather_seq(normed_two.astype(LOW)).reshape(group, D)
    gate_up = mm(normed_two, full_gate_up)
    ffn_gate, ffn_up = gate_up[:, :UNITS_PAD], gate_up[:, UNITS_PAD:]
    ffn_act = (jax.nn.silu(ffn_gate) * ffn_up).astype(LOW)

    d_act = mm(d_ffn_group, full_down)
    sig = jax.nn.sigmoid(ffn_gate)
    d_gate = d_act * ffn_up * (sig * (1.0 + ffn_gate * (1.0 - sig)))
    d_up = d_act * ffn_gate * sig
    d_gate_up = jnp.concatenate([d_gate.astype(LOW), d_up.astype(LOW)], axis=1)
    two_keep, two_got = scatter_begin(mm_nt(d_gate_up, full_gate_up))
    grad_down_part = mm_tn(d_ffn_group, ffn_act).astype(LOW)
    two_held, two_far = scatter_far(two_keep, after(two_got, grad_down_part))
    grad_gate_up_part = mm_tn(normed_two, d_gate_up).astype(LOW)
    d_normed_two = scatter_end(two_held, after(two_far, grad_gate_up_part))
    grad_gate_up_sum = scatter_dp_apart(grad_gate_up_part)
    grad_down_sum = scatter_dp_apart(grad_down_part)
    grad_gate_up = grad_gate_up_sum.reshape(block_rows, 2, UNITS_PAD)[:, :, :UNITS]
    grad_down = grad_down_sum[:, :UNITS]

    d_x_tail, d_attn_o, d_ssm_o, d_gains = pull_join((d_total, d_normed_two))
    ssm_arrivals = seq_arrivals(d_ssm_o.astype(LOW))
    ffn_part = mm_nt(ffn_act, full_down).astype(LOW)
    ssm_arrivals = after(ssm_arrivals, ffn_part)
    d_attn_own = after(d_attn_o.astype(LOW), ssm_arrivals[2])
    attn_arrivals = seq_arrivals(d_attn_own)
    d_ssm = place(list(zip(seq_order(), ssm_arrivals))).reshape(group, D)
    d_gated = mm_nt(d_ssm, w_out_rows).astype(LOW)

    def send_columns(grad):
        width = D // SEQ
        blocks = [grad[:, width * j : width * (j + 1)] for j in range(SEQ)]
        return [pick(blocks, s)] + [swap(pick(blocks, s ^ bit), "seq", bit) for bit in (1, 2, 3)]

    mamba_pieces = send_columns(mm_tn(gated, d_ssm).astype(LOW))
    d_xzb, d_chan, d_rate = mamba_backward(*mamba_in, states, read, d_gated)
    mamba_pieces, attn_arrivals = after((mamba_pieces, attn_arrivals), d_xzb)
    arrived = place(list(zip(seq_order(), mamba_pieces)))
    grad_out = scatter_dp_apart(
        jnp.concatenate([arrived[j, : HEAD_COUNT[j] * SSM_HEAD] for j in range(SEQ)])
    )

    d_attn = place(list(zip(seq_order(), attn_arrivals))).reshape(group, D)
    d_attended = jnp.concatenate([mm_nt(d_attn, w_o_rows), mm_nt(d_attn_own, w_o5_rows)]).astype(LOW)
    head_pieces = send_columns(
        jnp.concatenate([mm_tn(attended[:group], d_attn), mm_tn(attended[group:], d_attn_own)]).astype(LOW)
    )
    ffn_held, ffn_far = scatter_far(*scatter_begin(ffn_part))
    ffn_own = scatter_end(ffn_held, after(ffn_far, d_xzb))
    mixed_out = ((residual + ffn_own) * live).astype(LOW)
    d_conv = d_chan[:CONV, :LOCAL_CH]
    d_skip = jnp.sum(d_chan[CONV, :LOCAL_CH].reshape(LOCAL_HEADS, SSM_HEAD), axis=1)
    d_rate = d_rate[0, STEP_AT : STEP_AT + LOCAL_HEADS]
    grad_xz_part = mm_tn(normed, d_xzb).astype(LOW).reshape(dp_total, block_rows, -1)

    d_queries, d_kv = attention_backward(doc_lengths, queries, kv, attended, logs, d_attended, rows)
    arrived = place(list(zip(seq_order(), after(head_pieces, d_queries))))
    grad_o_part = jnp.concatenate(
        [arrived[j, :QW] for j in range(SEQ)] + [jnp.sum(arrived[:, QW:].astype(FULL), axis=0).astype(LOW)]
    ).reshape(dp_total, block_rows, -1)
    d_kvq = jnp.concatenate([d_kv, d_queries[:group]], axis=1)
    d_q_last = d_queries[group:]
    grad_qkv_part = jnp.concatenate(
        [mm_tn(normed, d_kvq).astype(LOW), mm_tn(normed_own, d_q_last).astype(LOW)], axis=1
    ).reshape(dp_total, block_rows, -1)
    d_normed_part = mm_nt(d_xzb, full_xz) + mm_nt(d_kvq, full_qkv[:, : 256 + QW])
    d_normed_own = mm_nt(d_q_last, full_qkv[:, 256 + QW :])

    tokens_wide = tokens_group.astype(FULL)
    unit = tokens_wide * lax.rsqrt(jnp.mean(tokens_wide * tokens_wide, axis=-1, keepdims=True) + NORM_EPS)
    d_gain_first = jnp.sum(d_normed_part * unit, axis=0) + jnp.sum(d_normed_own * own(unit), axis=0)
    d_gains = d_gains.at[0].add(d_gain_first)
    by_dp = lambda a: a.reshape(a.shape[0], dp_total, -1).transpose(1, 0, 2)
    d_heads = jnp.concatenate([own_spread(d_rate, s, 1), own_spread(d_skip, s, 1)])[None]
    small_part = jnp.concatenate(
        [
            jnp.pad(by_dp(own_spread(d_conv, s, SSM_HEAD)), ((0, 0), (0, 0), (0, width - conv_block))),
            jnp.pad(by_dp(d_gains), ((0, 0), (0, 0), (0, width - gains_block))),
            jnp.broadcast_to(
                jnp.pad(d_heads, ((0, 7), (0, width - d_heads.shape[1])))[None], (dp_total, 8, width)
            ),
        ],
        axis=1,
    )
    normed_keep, normed_got = scatter_begin(d_normed_part)
    normed_held, normed_far = scatter_far(normed_keep, after(normed_got, grad_qkv_part))
    grad_xz_part, normed_held = lax.optimization_barrier((grad_xz_part, normed_held))
    grad_o, grad_xz_sum, grad_qkv_sum, small_sum = scatter_dp(
        [grad_o_part, grad_xz_part, grad_qkv_part, small_part], 2
    )
    normed_far = after(normed_far, small_sum)
    small_sum = small_sum + swap(small_sum, "seq", 1)
    small_sum = small_sum + swap(small_sum, "seq", 2)
    grad_xz_sum = grad_xz_sum.astype(LOW)
    first, last = trade_back(grad_xz_sum[:, :LOCAL_CH], grad_xz_sum[:, LOCAL_CH : 2 * LOCAL_CH])
    grad_xz = jnp.concatenate([first, last], axis=1)[:, : w_xz.shape[1]].astype(FULL)
    both_all = gather_seq(jnp.concatenate([grad_qkv_sum.astype(LOW), grad_xz_sum[:, 2 * LOCAL_CH :]], axis=1))
    bcdt_all = both_all[:, :, grad_qkv_sum.shape[1] :].astype(FULL)
    grad_bcdt = jnp.concatenate(
        [jnp.sum(bcdt_all[:, :, : 2 * STATE], axis=0)]
        + [bcdt_all[j, :, 2 * STATE : 2 * STATE + HEAD_COUNT[j]] for j in range(SEQ)],
        axis=1,
    )
    qkv_all = both_all[:, :, : grad_qkv_sum.shape[1]].astype(FULL)
    col = lambda j, at, width: qkv_all[j, :, at : at + width]
    shared = lambda at, width: jnp.sum(qkv_all[:, :, at : at + width], axis=0)
    grad_qkv_wide = jnp.concatenate(
        [col(j, 256, QW) for j in range(SEQ)]
        + [shared(256 + QW, QW)]
        + [col(j, 0, HEAD) for j in range(SEQ)]
        + [shared(128, HEAD)]
        + [col(j, HEAD, HEAD) for j in range(SEQ)]
        + [shared(128 + HEAD, HEAD)],
        axis=1,
    )
    qkv_width = w_qkv.shape[1]
    grad_qkv = lax.dynamic_slice_in_dim(grad_qkv_wide, s * qkv_width, qkv_width, 1)

    d_normed = scatter_end(normed_held, normed_far) + d_normed_own
    d_unit = d_normed * gains[0]
    scale = lax.rsqrt(jnp.mean(inputs_x * inputs_x, axis=-1, keepdims=True) + NORM_EPS)
    d_x_head = scale * (
        d_unit - inputs_x * scale * scale * jnp.mean(d_unit * inputs_x, axis=-1, keepdims=True)
    )
    input_grad = (d_x_tail + d_x_head).astype(LOW)
    grad_conv = small_sum[:CONV, :conv_block]
    grad_gains = small_sum[CONV : CONV + 4, :gains_block]
    grad_rate = small_sum[8, :SSM_HEADS]
    grad_skip = small_sum[8, SSM_HEADS : 2 * SSM_HEADS]
    return (
        mixed_out,
        input_grad,
        grad_gains,
        grad_qkv,
        grad_o,
        grad_xz,
        grad_bcdt,
        grad_conv,
        grad_rate,
        grad_skip,
        grad_out,
        grad_gate_up,
        grad_down,
    )


def solution(mesh):
    placed = (
        P(("dp", "seq"), None),
        P("dp", None),
        P(None, "dp"),
        P("dp", "seq"),
        P("dp", "seq"),
        P("dp", "seq"),
        P("dp", None),
        P(None, "dp"),
        P(),
        P(),
        P("dp", "seq"),
        P("dp", None, "seq"),
        P("dp", "seq"),
        P(("dp", "seq"), None),
    )
    return jax.shard_map(
        on_device,
        mesh=mesh,
        in_specs=placed,
        out_specs=(
            P(("dp", "seq"), None),
            P(("dp", "seq"), None),
            P(None, "dp"),
            P("dp", "seq"),
            P("dp", "seq"),
            P("dp", "seq"),
            P("dp", None),
            P(None, "dp"),
            P(),
            P(),
            P("dp", "seq"),
            P("dp", None, "seq"),
            P("dp", "seq"),
        ),
        check_vma=False,
    )
```

time: 1460 us -> 1190 us (0.82)
  matrix products: 324 us -> 186 us
  other arithmetic: 189 us -> 101 us
  local copies, waits for them, and re-layouts: 274 us -> 196 us
  Pallas kernels: 407 us -> 472 us
  waiting for transfers between devices: 201 us -> 172 us
    pallas_call x0 -> x4, Pallas kernels: none -> 148 us  [the longest x1 54.3 us: mamba_backward(): pl.pallas_call(mamba_backward_kernel, grid=(chunks,), in_specs=mamba_spec...]
    dot_general x44 -> x0, matrix products: 134 us -> none  [the longest x12 50.3 us: ssm_group(): ein = lambda spec, *v: jnp.einsum(spec, *v, preferred_element_type=FULL)]
    pallas_call x2, Pallas kernels: 220 us -> 158 us  [gather_dp(): pl.pallas_call(lambda *refs: gather_kernel(count, line, *refs), out_shape...]
    reshape x17 -> x5, local copies, waits for them, and re-layouts: 62.2 us -> 0.33 us  [the longest x4 0.26 us: on_device(): by_dp = lambda a: a.reshape(a.shape[0], dp_total, -1).transpose(1, 0, 2)]
    ppermute x45 -> x42, waiting for transfers between devices: 197 us -> 172 us  [swap(): lax.ppermute(value, axis, [(i, i ^ bit) for i in range(lax.axis_size(axis...]
    select_n x7 -> x15, other arithmetic: 5.74 us -> 27.2 us  [pick(): return lax.select_n(seq_index, *options)]
    convert_element_type x18 -> x11, other arithmetic: 42.8 us -> 24 us  [the longest x5 16.2 us: scatter_far(): give_far = (at(keep, 1 - far) + at(got, 1 - far)).astype(LOW)]
    reduce_sum x11 -> x4, other arithmetic: 23.8 us -> 5.92 us  [the longest x1 2.94 us: on_device(): jnp.sum(d_normed_own * own(unit), axis=0)]
  transfers between devices with their start and end apart: 53 -> 51, of which waited for: 17 -> 14; matrix products, arithmetic and copies ran while one was open for 49% -> 33% of each run, Pallas kernels for 28% -> 32%
where the time goes in v3:
time: 1190 us
  Pallas kernels  472 us (40%)
  local copies, waits for them, and re-layouts  196 us (16%)
  matrix products  186 us (16%)
  waiting for transfers between devices  172 us (14%)
  other arithmetic  101 us (8%)
  starting transfers between devices  41.7 us (4%)
  between operations  17.2 us (1%)
    ppermute x42, waiting for transfers between devices, swap(): lax.ppermute(value, axis, [(i, i ^ bit) for i in range(lax.axis_size(axis...  172 us
    pallas_call x2, Pallas kernels, gather_dp(): pl.pallas_call(lambda *refs: gather_kernel(count, line, *refs), out_shape...  158 us
    pallas_call x1, Pallas kernels, scatter_dp(): pl.pallas_call(lambda *refs: scatter_kernel(count, line, *refs), out_shap...  150 us
    dot_general x9, matrix products, mm(): return jnp.dot(left, right, preferred_element_type=FULL)  70.1 us
    dot_general x8, matrix products, mm_nt(): lax.dot_general(left, right, (((1,), (1,)), ((), ())), preferred_element_...  59 us
    dot_general x8, matrix products, mm_tn(): lax.dot_general(left, right, (((0,), (0,)), ((), ())), preferred_element_...  56.8 us
    pallas_call x1, Pallas kernels, mamba_backward(): pl.pallas_call(mamba_backward_kernel, grid=(chunks,), in_specs=mamba_spec...  54.3 us
    unnamed x224, local copies, waits for them, and re-layouts  49.5 us
  transfers between devices with their start and end apart: 51, of which 14 were waited for; matrix products, arithmetic and copies ran while one was open for 33% of the time, Pallas kernels for 32%

profile of v3, /device:TPU:0, one launch (start us, length us, event | category | flops | bytes accessed | tf_op | source)
XLA Modules:
  0.0 1186.2 jit_solution(5031562301564882521)
XLA Ops:
  15.0 4.2 collective-permute-start.3
  23.4 11.4 collective-permute-done.6.refs_3_
  35.9 62.1 %shard_map.237 = (bf16[8,16,512]{2,1,0:T(8,128)(2,1)S(1)}, bf16[8,600,400]{2,1,0:T(8,128)(2,1)S(1)}) custom-call(bf16[16,512]{1,0:T(8,128)(2,1)S(1)} %fusion.66.refs_0_, bf16[600,400]{1,0:T(8,128)(2,1)S(1)} %pad_maximum_fusion.13.refs_1_), custom_call_target="tpu_custom_call" | custom-call | bytes 7942144 | tf_op jit(solution)/shard_map/pallas_call | solution.py:204
  116.0 96.1 %shard_map.239 = (bf16[8,200,896]{2,1,0:T(8,128)(2,1)S(1)}, bf16[8,200,1792]{2,1,0:T(8,128)(2,1)S(1)}) custom-call(bf16[200,896]{1,0:T(8,128)(2,1)S(1)} %concatenate.79.refs_0_, bf16[200,1792]{1,0:T(8,128)(2,1)S(1)} %concatenate.80.refs_1_), custom_call_target="tpu_custom_call" | custom-call | bytes 17203200 | tf_op jit(solution)/shard_map/pallas_call | solution.py:204
  230.4 7.4 copy.103
  237.8 6.2 multiply_convert_fusion
  295.6 35.7 %shard_map.240 = (bf16[1600,320]{1,0:T(8,128)(2,1)S(1)}, f32[1600,128]{1,0:T(8,128)S(1)}) custom-call(s32[1,2]{1,0:T(1,128)S(1)} %copy-done.36, bf16[1600,320]{1,0:T(8,128)(2,1)S(1)} %pad_maximum_fusion.7.q_ref, bf16[1280,256]{1,0:T(8,128)(2,1)S(1)} %slice.453.kv_ref), custom_call_target="tpu_custom_call" | custom-call | flops 3000000000 | bytes 4194304 | tf_op jit(solution)/shard_map/pallas_call | solution.py:785
  331.4 7.3 collective-permute-done.10
  342.2 4.5 pad_maximum_fusion.1
  346.7 5.5 convolution_convert_fusion.5
  352.2 6.8 copy.115
  362.6 12.6 %fusion.90.xzb_ref.tail_ref = f32[1280,1792]{1,0:T(8,128)S(1)} fusion(bf16[1280,1600]{0,1:T(8,128)(2,1)} %copy-done.58, bf16[1600,1792]{1,0:T(8,128)(2,1)} %bitcast.237), kind=kOutput, calls=%fused_computation.287 | convolution fusion | flops 7340032000 | bytes 19005440 | tf_op jit(solution)/shard_map/dot_general | solution.py:356
  375.2 18.3 %shard_map.241 = (bf16[1280,896]{1,0:T(8,128)(2,1)S(1)}, bf16[1280,896]{1,0:T(8,128)(2,1)S(1)}, f32[10,16,896]{2,1,0:T(8,128)S(1)}) custom-call(s32[1,2]{1,0:T(1,128)S(1)} %copy-done.36, f32[1280,1792]{1,0:T(8,128)S(1)} %fusion.90.xzb_ref.tail_ref, f32[1280,1792]{1,0:T(8,128)S(1)} %fusion.90.xzb_ref.tail_ref, f32[8,896]{1,0:T(8,128)S(1)} %pad.141.conv_ref, ...), custom_call_target="tpu_custom_call" | custom-call | flops 2000000000 | bytes 16777216 | tf_op jit(solution)/shard_map/pallas_call | solution.py:632
  397.2 6.0 convolution_convert_fusion.4
  403.1 6.8 copy.117
  426.0 17.4 %collective-permute-done.12 = bf16[320,1600]{1,0:T(8,128)(2,1)} collective-permute-done((bf16[320,1600]{1,0:T(8,128)(2,1)}, bf16[320,1600]{1,0:T(8,128)(2,1)}, u32[]{:S(2)}, u32[]{:S(2)}) %collective-permute-start.12) | collective-permute-done | bytes 1024032 | tf_op jit(solution)/shard_map/ppermute | solution.py:40
  445.9 20.3 %collective-permute-done.14 = bf16[320,1600]{1,0:T(8,128)(2,1)} collective-permute-done((bf16[320,1600]{1,0:T(8,128)(2,1)}, bf16[320,1600]{1,0:T(8,128)(2,1)}, u32[]{:S(2)}, u32[]{:S(2)}) %collective-permute-start.14) | collective-permute-done | bytes 1024032 | tf_op jit(solution)/shard_map/ppermute | solution.py:40
  471.9 17.0 %collective-permute-done.21.refs_3_ = bf16[320,1600]{1,0:T(8,128)(2,1)S(1)} collective-permute-done((bf16[320,1600]{1,0:T(8,128)(2,1)S(1)}, bf16[320,1600]{1,0:T(8,128)(2,1)S(1)}, u32[]{:S(2)}, u32[]{:S(2)}) %collective-permute-start.21) | collective-permute-done | bytes 1024032 | tf_op jit(solution)/shard_map/ppermute | solution.py:40
  489.5 21.7 %collective-permute-done.16.refs_3_ = bf16[320,1600]{1,0:T(8,128)(2,1)S(1)} collective-permute-done((bf16[320,1600]{1,0:T(8,128)(2,1)S(1)}, bf16[320,1600]{1,0:T(8,128)(2,1)S(1)}, u32[]{:S(2)}, u32[]{:S(2)}) %collective-permute-start.16) | collective-permute-done | bytes 1024032 | tf_op jit(solution)/shard_map/ppermute | solution.py:40
  518.3 19.4 %fusion.91 = f32[1280,2816]{1,0:T(8,128)} fusion(bf16[1280,1600]{1,0:T(8,128)(2,1)} %bitcast.225, bf16[1600,2816]{1,0:T(8,128)(2,1)} %all-gather.3.cloned.1.call-done), kind=kOutput, calls=%fused_computation.288 | convolution fusion | flops 11534336000 | bytes 27525120 | tf_op jit(solution)/shard_map/dot_general | solution.py:356
  537.7 16.5 %multiply_convert_fusion.2 = (bf16[1280,1408]{1,0:T(8,128)(2,1)S(1)}, bf16[1280,1408]{1,0:T(8,128)(2,1)S(1)}, bf16[1280,1408]{1,0:T(8,128)(2,1)}) fusion(f32[1280,2816]{1,0:T(8,128)} %fusion.91, bf16[1280,1600]{1,0:T(8,128)(2,1)} %bitcast.223, bf16[1600,1408]{1,0:T(8,128)(2,1)} %all-gather.5.cloned.1.call-done), kind=kOutput, calls=%fused_computation.13 | convolution fusion | flops 5796003840 | bytes 33832960 | tf_op jit(solution)/shard_map/dot_general | solution.py:356
  557.3 13.4 %convolution_convert_fusion.6 = bf16[1280,1600]{0,1:T(8,128)(2,1)} fusion(bf16[1600,2816]{1,0:T(8,128)(2,1)S(1)} %copy-done.86, bf16[1280,1408]{1,0:T(8,128)(2,1)S(1)} %get-tuple-element.216, bf16[1280,1408]{1,0:T(8,128)(2,1)S(1)} %get-tuple-element.215), kind=kOutput, calls=%fused_computation.10 | convolution fusion | flops 11550801920 | bytes 20316160 | tf_op jit(solution)/shard_map/dot_general | solution.py:360
  570.7 6.8 copy.119
  581.3 10.3 convolution_convert_fusion.2
  596.6 19.0 %convolution_convert_fusion = bf16[1600,2816]{1,0:T(8,128)(2,1)} fusion(bf16[1280,1600]{1,0:T(8,128)(2,1)} %bitcast.226, bf16[1280,1408]{1,0:T(8,128)(2,1)} %copy-done.88, bf16[1280,1408]{1,0:T(8,128)(2,1)} %copy-done.87), kind=kOutput, calls=%fused_computation | convolution fusion | flops 11553259520 | bytes 20316160 | tf_op jit(solution)/shard_map/dot_general | solution.py:364
  615.7 4.9 collective-permute-done.24
  623.8 4.3 multiply_reduce_fusion.4
  631.3 23.0 %collective-permute-done.26.refs_3_ = bf16[320,1600]{1,0:T(8,128)(2,1)S(1)} collective-permute-done((bf16[320,1600]{1,0:T(8,128)(2,1)S(1)}, bf16[320,1600]{1,0:T(8,128)(2,1)S(1)}, u32[]{:S(2)}, u32[]{:S(2)}) %collective-permute-start.26) | collective-permute-done | bytes 1024032 | tf_op jit(solution)/shard_map/ppermute | solution.py:40
  654.3 8.3 convolution_convert_fusion.3
  666.0 4.5 convolution_convert_fusion.8
  674.8 4.4 select_select_fusion.5
  689.0 8.4 convolution_convert_fusion.7.d_gated_ref
  697.4 54.3 %shard_map.245 = (bf16[1280,1792]{1,0:T(8,128)(2,1)S(1)}, f32[8,896]{1,0:T(8,128)S(1)}, f32[8,128]{1,0:T(8,128)S(1)}) custom-call(s32[1,2]{1,0:T(1,128)S(1)} %copy-done.36, f32[1280,1792]{1,0:T(8,128)S(1)} %bitcast.222, f32[1280,1792]{1,0:T(8,128)S(1)} %bitcast.222, f32[8,896]{1,0:T(8,128)S(1)} %copy-done.33, f32[8,128]{1,0:T(8,128)S(1)} %broadcast_in_dim.16.rate_ref, ...), custom_call_target="tpu_custom_call" | custom-call | flops 5000000000 | bytes 25165824 | tf_op jit(solution)/shard_map/pallas_call | solution.py:653
  769.3 7.1 copy.118
  779.4 4.5 collective-permute-done.18
  791.1 20.5 %collective-permute-done.19 = bf16[320,1600]{1,0:T(8,128)(2,1)} collective-permute-done((bf16[320,1600]{1,0:T(8,128)(2,1)S(1)}, bf16[320,1600]{1,0:T(8,128)(2,1)}, u32[]{:S(2)}, u32[]{:S(2)}) %collective-permute-start.19) | collective-permute-done | bytes 1024032 | tf_op jit(solution)/shard_map/ppermute | solution.py:40
  817.7 11.0 convolution_convert_fusion.1
  841.5 40.0 %shard_map.247 = (bf16[1600,320]{1,0:T(8,128)(2,1)S(1)}, bf16[1280,256]{1,0:T(8,128)(2,1)S(1)}) custom-call(s32[1,2]{1,0:T(1,128)S(1)} %copy-done.36, bf16[1600,320]{1,0:T(8,128)(2,1)S(1)} %copy-done.17, bf16[1280,256]{1,0:T(8,128)(2,1)S(1)} %copy-done.25, bf16[1600,320]{1,0:T(8,128)(2,1)S(1)} %copy-done.31, f32[1600,128]{1,0:T(8,128)S(1)} %copy-done.44, ...), custom_call_target="tpu_custom_call" | custom-call | flops 8000000000 | bytes 8388608 | tf_op jit(solution)/shard_map/pallas_call | solution.py:802
  888.4 5.3 collective-permute-start.38
  896.0 5.2 convolution_convert_fusion.10
  903.1 5.3 copy.127
  922.5 5.4 fusion.26
  927.9 13.3 %multiply_reduce_fusion.1 = (f32[1600]{0:T(1024)S(1)}, bf16[1280,1600]{0,1:T(8,128)(2,1)}) fusion(f32[1280,1600]{0,1:T(8,128)} %get-tuple-element.214, f32[1280,1600]{0,1:T(8,128)S(1)} %fusion.26, bf16[1280,1792]{1,0:T(8,128)(2,1)S(1)} %bitcast.242, bf16[1600,1792]{1,0:T(8,128)(2,1)} %bitcast.238), kind=kOutput, calls=%fused_computation.3 | convolution fusion | flops 7348222464 | bytes 30808320 | tf_op jit(solution)/shard_map/dot_general | solution.py:360
  941.2 6.9 copy.126
  962.0 5.5 fusion.12
  967.5 150.0 %shard_map.249 = (f32[200,400]{1,0:T(8,128)}, f32[200,1792]{1,0:T(8,128)}, f32[200,896]{1,0:T(8,128)}, f32[16,512]{1,0:T(8,128)}) custom-call(bf16[8,200,400]{2,1,0:T(8,128)(2,1)} %bitcast.267, bf16[8,200,1792]{2,1,0:T(8,128)(2,1)} %bitcast.264, bf16[8,200,896]{2,1,0:T(8,128)(2,1)} %bitcast.260, f32[8,16,512]{2,1,0:T(8,128)} %fusion.50.refs_3_), custom_call_target="tpu_custom_call" | custom-call | bytes 10012672 | tf_op jit(solution)/shard_map/pallas_call | solution.py:313
  1128.0 12.8 %collective-permute-done.40 = f32[16,512]{1,0:T(8,128)S(1)} collective-permute-done((f32[16,512]{1,0:T(8,128)S(1)}, f32[16,512]{1,0:T(8,128)S(1)}, u32[]{:S(2)}, u32[]{:S(2)}) %collective-permute-start.40) | collective-permute-done | bytes 32800 | tf_op jit(solution)/shard_map/ppermute | solution.py:40
  1158.2 7.8 collective-permute-done.35
  (511 shorter events, 303.6 us)
Async XLA Ops:
  7.2 511.1 %all-gather.3.cloned.1.call-start = ((), (), s32[]{:S(2)}) async-start(), calls=%async_computation.3 | async-start | bytes 10137600 | tf_op jit(solution)/shard_map/all_gather | solution.py:333
  7.2 27.6 %collective-permute-start.6 = (bf16[320,1600]{1,0:T(8,128)(2,1)}, bf16[320,1600]{1,0:T(8,128)(2,1)S(1)}, u32[]{:S(2)}, u32[]{:S(2)}) collective-permute-start(bf16[320,1600]{1,0:T(8,128)(2,1)} %refs_1_), channel_id=1, source_target_pairs={{0,2},{1,3},{2,0},{3,1},{4,6},{5,7},{6,4},{7,5},{8,10},{9,11},{10,... | collective-permute-start | bytes 3072008 | tf_op jit(solution)/shard_map/ppermute | solution.py:40
  10.3 93.6 %collective-permute-start.5 = (bf16[320,1600]{1,0:T(8,128)(2,1)}, bf16[320,1600]{1,0:T(8,128)(2,1)S(1)}, u32[]{:S(2)}, u32[]{:S(2)}) collective-permute-start(bf16[320,1600]{1,0:T(8,128)(2,1)} %refs_1_), channel_id=1, source_target_pairs={{0,1},{1,0},{2,3},{3,2},{4,5},{5,4},{6,7},{7,6},{8,9},{9,8},{10,11... | collective-permute-start | bytes 3072008 | tf_op jit(solution)/shard_map/ppermute | solution.py:40
  10.3 90.9 %collective-permute-start.1 = (bf16[200,560]{1,0:T(8,128)(2,1)}, bf16[200,560]{1,0:T(8,128)(2,1)}, u32[]{:S(2)}, u32[]{:S(2)}) collective-permute-start(bf16[200,560]{1,0:T(8,128)(2,1)} %param.19), channel_id=1, source_target_pairs={{0,2},{1,3},{2,0},{3,1},{4,6},{5,7},{6,4},{7,5},{8,10},{9,11},{10,... | collective-permute-start | bytes 672008 | tf_op jit(solution)/shard_map/ppermute | solution.py:40
  13.6 87.6 %collective-permute-start.4 = (bf16[200,832]{1,0:T(8,128)(2,1)}, bf16[200,832]{1,0:T(8,128)(2,1)}, u32[]{:S(2)}, u32[]{:S(2)}) collective-permute-start(bf16[200,832]{1,0:T(8,128)(2,1)} %get-tuple-element.269), channel_id=1, source_target_pairs={{1,3},{2,1},{3,2},{5,7},{6,5},{7,6},{9,11},{10,9},{11,10},{13,15},... | collective-permute-start | bytes 998408 | tf_op jit(solution)/shard_map/ppermute | solution.py:344
  15.0 86.7 %collective-permute-start.3 = (bf16[200,832]{1,0:T(8,128)(2,1)}, bf16[200,832]{1,0:T(8,128)(2,1)}, u32[]{:S(2)}, u32[]{:S(2)}) collective-permute-start(bf16[200,832]{1,0:T(8,128)(2,1)} %get-tuple-element.270), channel_id=1, source_target_pairs={{0,1},{1,2},{2,0},{4,5},{5,6},{6,4},{8,9},{9,10},{10,8},{12,13},{1... | collective-permute-start | bytes 998408 | tf_op jit(solution)/shard_map/ppermute | solution.py:343
  34.8 69.1 %collective-permute-start.7 = (bf16[320,1600]{1,0:T(8,128)(2,1)S(1)}, bf16[320,1600]{1,0:T(8,128)(2,1)S(1)}, u32[]{:S(2)}, u32[]{:S(2)}) collective-permute-start(bf16[320,1600]{1,0:T(8,128)(2,1)S(1)} %collective-permute-done.6.refs_3_), channel_id=1, source_target_pairs={{0,1},{1,0},{2,3},{3,2},{4,5},{5,4},{6,7},{7,6},{8,9},{9,8},{10,11... | collective-permute-start | bytes 3072008 | tf_op jit(solution)/shard_map/ppermute | solution.py:40
  216.4 321.3 %all-gather.5.cloned.1.call-start = ((), (), s32[]{:S(2)}) async-start(), calls=%async_computation.4 | async-start | bytes 5068800 | tf_op jit(solution)/shard_map/all_gather | solution.py:333
  274.3 57.1 %collective-permute-start.8 = (bf16[1600,400]{0,1:T(8,128)(2,1)}, bf16[1600,400]{0,1:T(8,128)(2,1)}, u32[]{:S(2)}, u32[]{:S(2)}) collective-permute-start(bf16[1600,400]{0,1:T(8,128)(2,1)} %concatenate.83), channel_id=1, source_target_pairs={{0,1},{1,0},{2,3},{3,2},{4,5},{5,4},{6,7},{7,6},{8,9},{9,8},{10,11... | collective-permute-start | bytes 3840008 | tf_op jit(solution)/shard_map/ppermute | solution.py:40
  277.5 53.9 %collective-permute-start.9 = (bf16[1600,400]{0,1:T(8,128)(2,1)}, bf16[1600,400]{0,1:T(8,128)(2,1)}, u32[]{:S(2)}, u32[]{:S(2)}) collective-permute-start(bf16[1600,400]{0,1:T(8,128)(2,1)} %concatenate.84), channel_id=1, source_target_pairs={{0,2},{1,3},{2,0},{3,1},{4,6},{5,7},{6,4},{7,5},{8,10},{9,11},{10,... | collective-permute-start | bytes 3840008 | tf_op jit(solution)/shard_map/ppermute | solution.py:40
  283.4 55.4 %collective-permute-start.10 = (bf16[1600,400]{0,1:T(8,128)(2,1)}, bf16[1600,400]{0,1:T(8,128)(2,1)}, u32[]{:S(2)}, u32[]{:S(2)}) collective-permute-start(bf16[1600,400]{0,1:T(8,128)(2,1)} %concatenate.85), channel_id=1, source_target_pairs={{0,3},{1,2},{2,1},{3,0},{4,7},{5,6},{6,5},{7,4},{8,11},{9,10},{10,... | collective-permute-start | bytes 3840008 | tf_op jit(solution)/shard_map/ppermute | solution.py:40
  362.3 51.7 %collective-permute-start.11 = (bf16[2,320,1600]{2,1,0:T(8,128)(2,1)}, bf16[2,320,1600]{2,1,0:T(8,128)(2,1)}, u32[]{:S(2)}, u32[]{:S(2)}) collective-permute-start(bf16[2,320,1600]{2,1,0:T(8,128)(2,1)} %dynamic-slice_bitcast_fusion.4), channel_id=1, source_target_pairs={{0,1},{1,0},{2,3},{3,2},{4,5},{5,4},{6,7},{7,6},{8,9},{9,8},{10,11... | collective-permute-start | bytes 6144008 | tf_op jit(solution)/shard_map/ppermute | solution.py:40
  411.7 6.6 collective-permute-start.13
  413.9 548.1 %reduce-scatter.10.cloned.1.call-start = ((), (), s32[]{:S(2)}) async-start(), calls=%async_computation.7 | async-start | bytes 5068800
  416.8 26.7 %collective-permute-start.12 = (bf16[320,1600]{1,0:T(8,128)(2,1)}, bf16[320,1600]{1,0:T(8,128)(2,1)}, u32[]{:S(2)}, u32[]{:S(2)}) collective-permute-start(bf16[320,1600]{1,0:T(8,128)(2,1)} %fusion.22), channel_id=1, source_target_pairs={{0,2},{1,3},{2,0},{3,1},{4,6},{5,7},{6,4},{7,5},{8,10},{9,11},{10,... | collective-permute-start | bytes 3072008 | tf_op jit(solution)/shard_map/ppermute | solution.py:40
  421.1 45.1 %collective-permute-start.14 = (bf16[320,1600]{1,0:T(8,128)(2,1)}, bf16[320,1600]{1,0:T(8,128)(2,1)}, u32[]{:S(2)}, u32[]{:S(2)}) collective-permute-start(bf16[320,1600]{1,0:T(8,128)(2,1)} %fusion.20), channel_id=1, source_target_pairs={{0,2},{1,3},{2,0},{3,1},{4,6},{5,7},{6,4},{7,5},{8,10},{9,11},{10,... | collective-permute-start | bytes 3072008 | tf_op jit(solution)/shard_map/ppermute | solution.py:40
  421.8 67.1 %collective-permute-start.21 = (bf16[320,1600]{1,0:T(8,128)(2,1)S(1)}, bf16[320,1600]{1,0:T(8,128)(2,1)S(1)}, u32[]{:S(2)}, u32[]{:S(2)}) collective-permute-start(bf16[320,1600]{1,0:T(8,128)(2,1)S(1)} %fusion.25.refs_1_), channel_id=1, source_target_pairs={{0,2},{1,3},{2,0},{3,1},{4,6},{5,7},{6,4},{7,5},{8,10},{9,11},{10,... | collective-permute-start | bytes 3072008 | tf_op jit(solution)/shard_map/ppermute | solution.py:40
  470.3 40.9 %collective-permute-start.16 = (bf16[320,1600]{1,0:T(8,128)(2,1)S(1)}, bf16[320,1600]{1,0:T(8,128)(2,1)S(1)}, u32[]{:S(2)}, u32[]{:S(2)}) collective-permute-start(bf16[320,1600]{1,0:T(8,128)(2,1)S(1)} %multiply_convert_fusion.4.refs_1_), channel_id=1, source_target_pairs={{0,2},{1,3},{2,0},{3,1},{4,6},{5,7},{6,4},{7,5},{8,10},{9,11},{10,... | collective-permute-start | bytes 3072008 | tf_op jit(solution)/shard_map/ppermute | solution.py:40
  471.9 39.2 %collective-permute-start.20 = (bf16[320,1600]{1,0:T(8,128)(2,1)S(1)}, bf16[320,1600]{1,0:T(8,128)(2,1)S(1)}, u32[]{:S(2)}, u32[]{:S(2)}) collective-permute-start(bf16[320,1600]{1,0:T(8,128)(2,1)S(1)} %fusion.25.refs_1_), channel_id=1, source_target_pairs={{0,1},{1,0},{2,3},{3,2},{4,5},{5,4},{6,7},{7,6},{8,9},{9,8},{10,11... | collective-permute-start | bytes 3072008 | tf_op jit(solution)/shard_map/ppermute | solution.py:40
  488.9 22.2 %collective-permute-start.22 = (bf16[320,1600]{1,0:T(8,128)(2,1)S(1)}, bf16[320,1600]{1,0:T(8,128)(2,1)S(1)}, u32[]{:S(2)}, u32[]{:S(2)}) collective-permute-start(bf16[320,1600]{1,0:T(8,128)(2,1)S(1)} %collective-permute-done.21.refs_3_), channel_id=1, source_target_pairs={{0,1},{1,0},{2,3},{3,2},{4,5},{5,4},{6,7},{7,6},{8,9},{9,8},{10,11... | collective-permute-start | bytes 3072008 | tf_op jit(solution)/shard_map/ppermute | solution.py:40
  488.9 26.0 %collective-permute-start.15 = (bf16[320,1600]{1,0:T(8,128)(2,1)S(1)}, bf16[320,1600]{1,0:T(8,128)(2,1)S(1)}, u32[]{:S(2)}, u32[]{:S(2)}) collective-permute-start(bf16[320,1600]{1,0:T(8,128)(2,1)S(1)} %multiply_convert_fusion.4.refs_1_), channel_id=1, source_target_pairs={{0,1},{1,0},{2,3},{3,2},{4,5},{5,4},{6,7},{7,6},{8,9},{9,8},{10,11... | collective-permute-start | bytes 3072008 | tf_op jit(solution)/shard_map/ppermute | solution.py:40
  511.1 3.8 collective-permute-start.17
  580.7 10.9 collective-permute-start.23
  594.9 25.7 %collective-permute-start.24 = (bf16[320,1600]{1,0:T(8,128)(2,1)}, bf16[320,1600]{1,0:T(8,128)(2,1)}, u32[]{:S(2)}, u32[]{:S(2)}) collective-permute-start(bf16[320,1600]{1,0:T(8,128)(2,1)} %fusion.13), channel_id=1, source_target_pairs={{0,2},{1,3},{2,0},{3,1},{4,6},{5,7},{6,4},{7,5},{8,10},{9,11},{10,... | collective-permute-start | bytes 3072008 | tf_op jit(solution)/shard_map/ppermute | solution.py:40
  615.6 556.3 %reduce-scatter.6.cloned.1.call-start = ((), (), s32[]{:S(2)}) async-start(), calls=%async_computation.5 | async-start | bytes 3686400 | tf_op jit(solution)/shard_map/reduce_scatter | solution.py:337
  629.5 24.7 %collective-permute-start.26 = (bf16[320,1600]{1,0:T(8,128)(2,1)S(1)}, bf16[320,1600]{1,0:T(8,128)(2,1)S(1)}, u32[]{:S(2)}, u32[]{:S(2)}) collective-permute-start(bf16[320,1600]{1,0:T(8,128)(2,1)S(1)} %get-tuple-element.127.refs_1_), channel_id=1, source_target_pairs={{0,2},{1,3},{2,0},{3,1},{4,6},{5,7},{6,4},{7,5},{8,10},{9,11},{10,... | collective-permute-start | bytes 3072008 | tf_op jit(solution)/shard_map/ppermute | solution.py:40
  631.3 31.3 %collective-permute-start.25 = (bf16[320,1600]{1,0:T(8,128)(2,1)S(1)}, bf16[320,1600]{1,0:T(8,128)(2,1)S(1)}, u32[]{:S(2)}, u32[]{:S(2)}) collective-permute-start(bf16[320,1600]{1,0:T(8,128)(2,1)S(1)} %get-tuple-element.127.refs_1_), channel_id=1, source_target_pairs={{0,1},{1,0},{2,3},{3,2},{4,5},{5,4},{6,7},{7,6},{8,9},{9,8},{10,11... | collective-permute-start | bytes 3072008 | tf_op jit(solution)/shard_map/ppermute | solution.py:40
  654.3 8.3 collective-permute-start.27
  662.6 26.4 %collective-permute-start.32 = (bf16[320,1600]{1,0:T(8,128)(2,1)S(1)}, bf16[320,1600]{1,0:T(8,128)(2,1)S(1)}, u32[]{:S(2)}, u32[]{:S(2)}) collective-permute-start(bf16[320,1600]{1,0:T(8,128)(2,1)S(1)} %get-tuple-element.135.refs_1_), channel_id=1, source_target_pairs={{0,2},{1,3},{2,0},{3,1},{4,6},{5,7},{6,4},{7,5},{8,10},{9,11},{10,... | collective-permute-start | bytes 3072008 | tf_op jit(solution)/shard_map/ppermute | solution.py:40
  664.4 89.5 %collective-permute-start.31 = (bf16[320,1600]{1,0:T(8,128)(2,1)S(1)}, bf16[320,1600]{1,0:T(8,128)(2,1)}, u32[]{:S(2)}, u32[]{:S(2)}) collective-permute-start(bf16[320,1600]{1,0:T(8,128)(2,1)S(1)} %get-tuple-element.135.refs_1_), channel_id=1, source_target_pairs={{0,1},{1,0},{2,3},{3,2},{4,5},{5,4},{6,7},{7,6},{8,9},{9,8},{10,11... | collective-permute-start | bytes 3072008 | tf_op jit(solution)/shard_map/ppermute | solution.py:40
  684.0 69.8 %collective-permute-start.28 = (bf16[896,400]{0,1:T(8,128)(2,1)}, bf16[896,400]{0,1:T(8,128)(2,1)S(1)}, u32[]{:S(2)}, u32[]{:S(2)}) collective-permute-start(bf16[896,400]{0,1:T(8,128)(2,1)} %copy.121), channel_id=1, source_target_pairs={{0,1},{1,0},{2,3},{3,2},{4,5},{5,4},{6,7},{7,6},{8,9},{9,8},{10,11... | collective-permute-start | bytes 2150408 | tf_op jit(solution)/shard_map/ppermute | solution.py:40
  684.4 69.4 %collective-permute-start.29 = (bf16[896,400]{0,1:T(8,128)(2,1)}, bf16[896,400]{0,1:T(8,128)(2,1)S(1)}, u32[]{:S(2)}, u32[]{:S(2)}) collective-permute-start(bf16[896,400]{0,1:T(8,128)(2,1)} %copy.122), channel_id=1, source_target_pairs={{0,2},{1,3},{2,0},{3,1},{4,6},{5,7},{6,4},{7,5},{8,10},{9,11},{10,... | collective-permute-start | bytes 2150408 | tf_op jit(solution)/shard_map/ppermute | solution.py:40
  684.7 69.1 %collective-permute-start.30 = (bf16[896,400]{0,1:T(8,128)(2,1)}, bf16[896,400]{0,1:T(8,128)(2,1)S(1)}, u32[]{:S(2)}, u32[]{:S(2)}) collective-permute-start(bf16[896,400]{0,1:T(8,128)(2,1)} %copy.123), channel_id=1, source_target_pairs={{0,3},{1,2},{2,1},{3,0},{4,7},{5,6},{6,5},{7,4},{8,11},{9,10},{10,... | collective-permute-start | bytes 2150408 | tf_op jit(solution)/shard_map/ppermute | solution.py:40
  689.0 64.9 %collective-permute-start.33 = (bf16[320,1600]{1,0:T(8,128)(2,1)S(1)}, bf16[320,1600]{1,0:T(8,128)(2,1)S(1)}, u32[]{:S(2)}, u32[]{:S(2)}) collective-permute-start(bf16[320,1600]{1,0:T(8,128)(2,1)S(1)} %collective-permute-done.32.refs_3_), channel_id=1, source_target_pairs={{0,1},{1,0},{2,3},{3,2},{4,5},{5,4},{6,7},{7,6},{8,9},{9,8},{10,11... | collective-permute-start | bytes 3072008 | tf_op jit(solution)/shard_map/ppermute | solution.py:40
  769.2 404.7 %reduce-scatter.8.cloned.1.call-start = ((), (), s32[]{:S(2)}) async-start(), calls=%async_computation.6 | async-start | bytes 10137600 | tf_op jit(solution)/shard_map/reduce_scatter | solution.py:337
  779.4 4.5 collective-permute-start.18
  785.8 25.7 %collective-permute-start.19 = (bf16[320,1600]{1,0:T(8,128)(2,1)S(1)}, bf16[320,1600]{1,0:T(8,128)(2,1)}, u32[]{:S(2)}, u32[]{:S(2)}) collective-permute-start(bf16[320,1600]{1,0:T(8,128)(2,1)S(1)} %fusion.15), channel_id=1, source_target_pairs={{0,2},{1,3},{2,0},{3,1},{4,6},{5,7},{6,4},{7,5},{8,10},{9,11},{10,... | collective-permute-start | bytes 3072008 | tf_op jit(solution)/shard_map/ppermute | solution.py:40
  888.4 67.0 %collective-permute-start.38 = (bf16[640,400]{0,1:T(8,128)(2,1)}, bf16[640,400]{0,1:T(8,128)(2,1)}, u32[]{:S(2)}, u32[]{:S(2)}) collective-permute-start(bf16[640,400]{0,1:T(8,128)(2,1)} %copy.130), channel_id=1, source_target_pairs={{0,3},{1,2},{2,1},{3,0},{4,7},{5,6},{6,5},{7,4},{8,11},{9,10},{10,... | collective-permute-start | bytes 1536008 | tf_op jit(solution)/shard_map/ppermute | solution.py:40
  914.7 40.7 %collective-permute-start.36 = (bf16[640,400]{0,1:T(8,128)(2,1)}, bf16[640,400]{0,1:T(8,128)(2,1)}, u32[]{:S(2)}, u32[]{:S(2)}) collective-permute-start(bf16[640,400]{0,1:T(8,128)(2,1)} %copy.128), channel_id=1, source_target_pairs={{0,1},{1,0},{2,3},{3,2},{4,5},{5,4},{6,7},{7,6},{8,9},{9,8},{10,11... | collective-permute-start | bytes 1536008 | tf_op jit(solution)/shard_map/ppermute | solution.py:40
  914.7 40.7 %collective-permute-start.37 = (bf16[640,400]{0,1:T(8,128)(2,1)S(1)}, bf16[640,400]{0,1:T(8,128)(2,1)}, u32[]{:S(2)}, u32[]{:S(2)}) collective-permute-start(bf16[640,400]{0,1:T(8,128)(2,1)S(1)} %copy.129), channel_id=1, source_target_pairs={{0,2},{1,3},{2,0},{3,1},{4,6},{5,7},{6,4},{7,5},{8,10},{9,11},{10,... | collective-permute-start | bytes 1536008 | tf_op jit(solution)/shard_map/ppermute | solution.py:40
  951.4 10.6 collective-permute-start.34
  1118.7 6.5 collective-permute-start.39
  1120.6 22.5 %collective-permute-start.42 = (bf16[200,1024]{1,0:T(8,128)(2,1)S(1)}, bf16[200,1024]{1,0:T(8,128)(2,1)S(1)}, u32[]{:S(2)}, u32[]{:S(2)}) collective-permute-start(bf16[200,1024]{1,0:T(8,128)(2,1)S(1)} %pad_maximum_fusion.14.refs_1_), channel_id=1, source_target_pairs={{0,2},{1,3},{2,0},{3,1},{4,6},{5,7},{6,4},{7,5},{8,10},{9,11},{10,... | collective-permute-start | bytes 1228808 | tf_op jit(solution)/shard_map/ppermute | solution.py:40
  1121.0 22.0 %collective-permute-start.44 = (bf16[200,832]{1,0:T(8,128)(2,1)S(1)}, bf16[200,832]{1,0:T(8,128)(2,1)S(1)}, u32[]{:S(2)}, u32[]{:S(2)}) collective-permute-start(bf16[200,832]{1,0:T(8,128)(2,1)S(1)} %get-tuple-element.273), channel_id=1, source_target_pairs={{1,0},{2,1},{0,2},{5,4},{6,5},{4,6},{9,8},{10,9},{8,10},{13,12},{1... | collective-permute-start | bytes 998408 | tf_op jit(solution)/shard_map/ppermute | solution.py:350
  1124.6 18.5 %collective-permute-start.45 = (bf16[200,832]{1,0:T(8,128)(2,1)S(1)}, bf16[200,832]{1,0:T(8,128)(2,1)S(1)}, u32[]{:S(2)}, u32[]{:S(2)}) collective-permute-start(bf16[200,832]{1,0:T(8,128)(2,1)S(1)} %get-tuple-element.274), channel_id=1, source_target_pairs={{3,1},{1,2},{2,3},{7,5},{5,6},{6,7},{11,9},{9,10},{10,11},{15,13},... | collective-permute-start | bytes 998408 | tf_op jit(solution)/shard_map/ppermute | solution.py:351
  1125.3 15.6 %collective-permute-start.40 = (f32[16,512]{1,0:T(8,128)S(1)}, f32[16,512]{1,0:T(8,128)S(1)}, u32[]{:S(2)}, u32[]{:S(2)}) collective-permute-start(f32[16,512]{1,0:T(8,128)S(1)} %add.429), channel_id=1, source_target_pairs={{0,2},{1,3},{2,0},{3,1},{4,6},{5,7},{6,4},{7,5},{8,10},{9,11},{10,... | collective-permute-start | bytes 98312 | tf_op jit(solution)/shard_map/ppermute | solution.py:40
  1127.9 16.7 %collective-permute-start.41 = (bf16[200,1024]{1,0:T(8,128)(2,1)S(1)}, bf16[200,1024]{1,0:T(8,128)(2,1)S(1)}, u32[]{:S(2)}, u32[]{:S(2)}) collective-permute-start(bf16[200,1024]{1,0:T(8,128)(2,1)S(1)} %pad_maximum_fusion.14.refs_1_), channel_id=1, source_target_pairs={{0,1},{1,0},{2,3},{3,2},{4,5},{5,4},{6,7},{7,6},{8,9},{9,8},{10,11... | collective-permute-start | bytes 1228808 | tf_op jit(solution)/shard_map/ppermute | solution.py:40
  1140.9 25.1 %collective-permute-start.35 = (bf16[320,1600]{1,0:T(8,128)(2,1)}, bf16[320,1600]{1,0:T(8,128)(2,1)}, u32[]{:S(2)}, u32[]{:S(2)}) collective-permute-start(bf16[320,1600]{1,0:T(8,128)(2,1)} %get-tuple-element.220), channel_id=1, source_target_pairs={{0,2},{1,3},{2,0},{3,1},{4,6},{5,7},{6,4},{7,5},{8,10},{9,11},{10,... | collective-permute-start | bytes 3072008 | tf_op jit(solution)/shard_map/ppermute | solution.py:40
  (108 other events, 1546.3 us)
Sparse Core Ops, SparseCore 0:
  216.5 132.8 all-gather.2
  414.0 76.0 all-gather.4
  615.8 108.7 reduce-scatter.9
  769.3 74.7 reduce-scatter.5
  847.9 168.7 reduce-scatter.7

commit v4 on v3

--- a/solution.py
+++ b/solution.py
@@ -2,6 +2,7 @@
 import jax.numpy as jnp
 from jax import lax
 from jax.experimental import pallas as pl
+from jax.experimental.layout import Layout, with_layout_constraint
 from jax.experimental.pallas import tpu as pltpu
 from jax.sharding import PartitionSpec as P
 
@@ -88,9 +89,12 @@
     return [me, me ^ 1, me ^ 2, me ^ 3]
 
 
-def seq_arrivals(block):
-    far = swap(block, "seq", 2)
-    return [block, swap(block, "seq", 1), far, swap(far, "seq", 1)]
+def seq_arrivals(block, beside=None):
+    far, near = swap(block, "seq", 2), swap(block, "seq", 1)
+    if beside is not None:
+        far, beside = meet(far, beside)
+    blocks = [block, near, far, swap(far, "seq", 1)]
+    return blocks if beside is None else (blocks, beside)
 
 
 def gather_seq(block):
@@ -99,7 +103,8 @@
 
 def scatter_begin(part):
     core = lax.axis_index("seq") % 2
-    by_core = part.astype(LOW).reshape((2, 2, part.shape[0] // SEQ) + part.shape[1:])
+    part = with_layout_constraint(part.astype(LOW), Layout((0, 1)))
+    by_core = part.reshape((2, 2, part.shape[0] // SEQ) + part.shape[1:])
     give = lax.dynamic_index_in_dim(by_core, 1 - core, 1, False)
     keep = lax.dynamic_index_in_dim(by_core, core, 1, False)
     return keep, swap(give, "seq", 1)
@@ -116,6 +121,24 @@
     return held + got_far.astype(FULL)
 
 
+def relative_begin(part):
+    part = with_layout_constraint(part.astype(LOW), Layout((0, 1)))
+    rows = part.shape[0] // SEQ
+    block = lambda k: part[rows * k : rows * (k + 1)]
+    got = swap(jnp.concatenate([block(1), block(3)]), "seq", 1)
+    return (block(0), block(2)), got
+
+
+def relative_far(keep, got):
+    rows = got.shape[0] // 2
+    add = lambda k: keep[k].astype(FULL) + got[rows * k : rows * (k + 1)].astype(FULL)
+    return add(0), swap(add(1).astype(LOW), "seq", 2)
+
+
+def meet(one, two):
+    return lax.optimization_barrier((one, two))
+
+
 def after(values, done):
     return lax.optimization_barrier((values, done))[0]
 
@@ -141,16 +164,29 @@
     )
 
 
-def gather_kernel(count, line, *refs):
-    packets, outs = refs[:count], refs[count : 2 * count]
-    own_sem, up_sem, down_sem, line_sem, give_sem, got_sem = refs[2 * count :]
+def pieces_of(arrays, axis):
+    pieces = []
+    for i, array in enumerate(arrays):
+        rows = array.shape[axis]
+        count = 1 if rows < 64 else 3 if rows < 256 else 4
+        size = rows // count // 16 * 16 if count > 1 else rows
+        for k in range(count):
+            pieces.append((i, pl.ds(k * size, size if k < count - 1 else rows - k * size)))
+    return pieces
+
+
+def gather_phases(pieces, line, refs):
+    packets = pieces[-1][0] + 1
+    sources, outs = refs[:packets], refs[packets : 2 * packets]
+    own_sem, up_sem, down_sem, line_sem, give_sem, got_sem = refs[2 * packets :]
     _, z, x = line_place()
-    greet(line, z, x)
+    held = lambda i, zb: outs[pieces[i][0]].at[2 * zb + x, pieces[i][1]]
+    mine = lambda i: sources[pieces[i][0]].at[pieces[i][1]]
 
     def copy(src, i, zb, send_sem, recv_sem, target):
         return pltpu.make_async_remote_copy(
             src_ref=src,
-            dst_ref=outs[i].at[2 * zb + x],
+            dst_ref=held(i, zb),
             send_sem=send_sem.at[i, zb],
             recv_sem=recv_sem.at[i, zb],
             device_id={"dp": target},
@@ -160,17 +196,18 @@
     up_to = lambda src, i, zb: copy(src, i, zb, up_sem, line_sem, 2 * (z + 1) + x)
     down_to = lambda src, i, zb: copy(src, i, zb, down_sem, line_sem, 2 * (z - 1) + x)
     give = lambda src, i, zb: copy(src, i, zb, give_sem, got_sem, 2 * z + 1 - x)
-    held = lambda i, zb: outs[i].at[2 * zb + x]
-    own = lambda i: pltpu.make_async_copy(packets[i], held(i, z), own_sem.at[i])
-
-    for turn in range(count + line - 1):
-        for i in range(count):
+    own = lambda i: pltpu.make_async_copy(mine(i), held(i, z), own_sem.at[i])
+
+    def take_turn(turn):
+        if turn == 0:
+            greet(line, z, x)
+        for i in range(len(pieces)):
             far = turn - i
             if far == 0:
+                pl.when(z < line - 1)(lambda: up_to(mine(i), i, z).start())
+                pl.when(z > 0)(lambda: down_to(mine(i), i, z).start())
+                give(mine(i), i, z).start()
                 own(i).start()
-                give(packets[i], i, z).start()
-                pl.when(z < line - 1)(lambda: up_to(packets[i], i, z).start())
-                pl.when(z > 0)(lambda: down_to(packets[i], i, z).start())
             elif 0 < far < line:
 
                 @pl.when(z - far >= 0)
@@ -187,26 +224,44 @@
                     pl.when(z > 0)(lambda: down_to(held(i, zb), i, zb).start())
                     give(held(i, zb), i, zb).start()
 
-    for i in range(count):
-        own(i).wait()
-        for zb in range(line):
-            give(held(i, zb), i, zb).wait()
-            pl.when((zb <= z) & (z < line - 1))(lambda: up_to(held(i, zb), i, zb).wait_send())
-            pl.when((zb >= z) & (z > 0))(lambda: down_to(held(i, zb), i, zb).wait_send())
+    def finish():
+        for i in range(len(pieces)):
+            own(i).wait()
+            for zb in range(line):
+                give(held(i, zb), i, zb).wait()
+                pl.when((zb <= z) & (z < line - 1))(lambda: up_to(held(i, zb), i, zb).wait_send())
+                pl.when((zb >= z) & (z > 0))(lambda: down_to(held(i, zb), i, zb).wait_send())
+
+    turns = len(pieces) + line - 1
+    return [lambda turn=turn: take_turn(turn) for turn in range(turns)] + [finish]
+
+
+def gather_kernel(pieces, line, *refs):
+    for phase in gather_phases(pieces, line, refs):
+        phase()
+
+
+def gather_scratch(pieces, line):
+    count = len(pieces)
+    sems = lambda *shape: pltpu.SemaphoreType.DMA(shape)
+    return [sems(count)] + [sems(count, line) for _ in range(5)]
+
+
+def gather_shapes(packets):
+    return [jax.ShapeDtypeStruct((lax.axis_size("dp"),) + p.shape, p.dtype) for p in packets]
 
 
 def gather_dp(packets, collective_id):
     total = lax.axis_size("dp")
     if total != 8:
         return [lax.all_gather(packet, "dp", axis=0) for packet in packets]
-    count, line = len(packets), total // 2
-    sems = lambda *shape: pltpu.SemaphoreType.DMA(shape)
+    pieces, line = pieces_of(packets, 0), total // 2
     return pl.pallas_call(
-        lambda *refs: gather_kernel(count, line, *refs),
-        out_shape=[jax.ShapeDtypeStruct((total,) + p.shape, p.dtype) for p in packets],
-        in_specs=[pl.BlockSpec(memory_space=pltpu.VMEM)] * count,
-        out_specs=[pl.BlockSpec(memory_space=pl.ANY)] * count,
-        scratch_shapes=[sems(count)] + [sems(count, line) for _ in range(5)],
+        lambda *refs: gather_kernel(pieces, line, *refs),
+        out_shape=gather_shapes(packets),
+        in_specs=[pl.BlockSpec(memory_space=pltpu.VMEM)] * len(packets),
+        out_specs=[pl.BlockSpec(memory_space=pl.ANY)] * len(packets),
+        scratch_shapes=gather_scratch(pieces, line),
         compiler_params=pltpu.CompilerParams(
             collective_id=collective_id, has_side_effects=True, vmem_limit_bytes=32 << 20
         ),
@@ -232,7 +287,8 @@
         total[:, at] = sum(part[:, at].astype(FULL) for part in parts).astype(total.dtype)
 
 
-def scatter_kernel(count, line, *refs):
+def scatter_phases(pieces, line, refs):
+    count = pieces[-1][0] + 1
     parts, outs = refs[:count], refs[count : 2 * count]
     own_refs, near_refs, line_refs = (
         refs[2 * count : 3 * count],
@@ -241,8 +297,8 @@
     )
     load_sem, give_sem, got_sem, send_sem, line_sem = refs[5 * count :]
     _, z, x = line_place()
-    greet(line, z, x)
     order = [t for pair in zip(range(line - 1, -1, -1), range(line)) for t in pair][:line]
+    at = lambda arrays, i, t: arrays[pieces[i][0]].at[t, pieces[i][1]]
     remote = lambda src, dst, send, recv, target: pltpu.make_async_remote_copy(
         src_ref=src,
         dst_ref=dst,
@@ -252,55 +308,88 @@
         device_id_type=pl.DeviceIdType.MESH,
     )
     give = lambda i, t: remote(
-        parts[i].at[2 * t + 1 - x],
-        near_refs[i].at[t],
+        at(parts, i, 2 * t + 1 - x),
+        at(near_refs, i, t),
         give_sem.at[i, t],
         got_sem.at[i, t],
         2 * z + 1 - x,
     )
     load = lambda i, t: pltpu.make_async_copy(
-        parts[i].at[2 * t + x], own_refs[i].at[t], load_sem.at[i, t]
+        at(parts, i, 2 * t + x), at(own_refs, i, t), load_sem.at[i, t]
     )
     along = lambda i, t, slot, target: remote(
-        own_refs[i].at[t], line_refs[i].at[slot], send_sem.at[i, t], line_sem.at[i, slot], target
-    )
-    for i in range(count):
-        for t in order:
-            load(i, t).start()
-            give(i, t).start()
-    for i in range(count):
-        own, near, held = own_refs[i], near_refs[i], line_refs[i]
-        for t in order:
-            load(i, t).wait()
-            give(i, t).wait_recv()
-
-            @pl.when((t > z) & (z > 0) | (t < z) & (z < line - 1))
+        at(own_refs, i, t), at(line_refs, i, slot), send_sem.at[i, t], line_sem.at[i, slot], target
+    )
+    def views(i):
+        return [lambda t, arrays=arrays: at(arrays, i, t) for arrays in (own_refs, near_refs, line_refs)]
+
+    def start():
+        greet(line, z, x)
+        for i in range(len(pieces)):
+            for t in order:
+                load(i, t).start()
+                give(i, t).start()
+
+    def pass_on(i, t, zz):
+        own, near, held = views(i)
+        load(i, t).wait()
+        give(i, t).wait_recv()
+        terms = [own(t), near(t)]
+        if 0 < zz < t or t < zz < line - 1:
+            along(i, t, t, 0).wait_recv()
+            terms.append(held(t))
+        add_columns(own(t), terms)
+        step = 1 if t > zz else -1
+        along(i, t, line if t == zz - 1 else t, 2 * (zz + step) + x).start()
+
+    def take_round(r):
+        for zz in range(line):
+
+            @pl.when(z == zz)
             def _():
-                along(i, t, t, 0).wait_recv()
-                add_columns(own.at[t], (own.at[t], near.at[t], held.at[t]))
-
-            @pl.when((t > z) & (z == 0) | (t < z) & (z == line - 1))
-            def _():
-                add_columns(own.at[t], (own.at[t], near.at[t]))
-
-            pl.when(t > z)(lambda: along(i, t, t, 2 * (z + 1) + x).start())
-            pl.when(t == z - 1)(lambda: along(i, t, line, 2 * (z - 1) + x).start())
-            pl.when(t < z - 1)(lambda: along(i, t, t, 2 * (z - 1) + x).start())
-    for i in range(count):
-        own, near, held = own_refs[i], near_refs[i], line_refs[i]
-        pl.when(z > 0)(lambda: along(i, z, z, 0).wait_recv())
-        pl.when(z < line - 1)(lambda: along(i, z, line, 0).wait_recv())
-        for t in range(line):
-
-            @pl.when(t == z)
-            def _():
-                terms = [own.at[t], near.at[t]]
-                terms += [held.at[t]] if t > 0 else []
-                terms += [held.at[line]] if t < line - 1 else []
-                add_columns(outs[i], terms)
-
-            pl.when(t != z)(lambda: along(i, t, t, 0).wait_send())
-            give(i, t).wait_send()
+                up, down = r - zz, r - (line - 1 - zz)
+                for t in range(line - 1, zz, -1):
+                    if 0 <= up < len(pieces):
+                        pass_on(up, t, zz)
+                for t in range(zz):
+                    if 0 <= down < len(pieces):
+                        pass_on(down, t, zz)
+
+    def finish():
+        for i in range(len(pieces)):
+            own, near, held = views(i)
+            for t in range(line):
+
+                @pl.when(t == z)
+                def _():
+                    load(i, t).wait()
+                    give(i, t).wait_recv()
+                    terms = [own(t), near(t)]
+                    if t > 0:
+                        along(i, t, t, 0).wait_recv()
+                        terms.append(held(t))
+                    if t < line - 1:
+                        along(i, t, line, 0).wait_recv()
+                        terms.append(held(line))
+                    add_columns(outs[pieces[i][0]].at[pieces[i][1]], terms)
+
+                pl.when(t != z)(lambda: along(i, t, t, 0).wait_send())
+                give(i, t).wait_send()
+
+    rounds = len(pieces) + line - 2
+    return [start] + [lambda r=r: take_round(r) for r in range(rounds)] + [finish]
+
+
+def scatter_kernel(pieces, line, *refs):
+    for phase in scatter_phases(pieces, line, refs):
+        phase()
+
+
+def scatter_scratch(parts, pieces, line):
+    count = len(pieces)
+    sems = lambda *shape: pltpu.SemaphoreType.DMA(shape)
+    buffers = [pltpu.VMEM((n,) + p.shape[1:], p.dtype) for n in (line, line, line + 1) for p in parts]
+    return buffers + [sems(count, line) for _ in range(4)] + [sems(count, line + 1)]
 
 
 def scatter_dp(parts, collective_id):
@@ -308,18 +397,13 @@
     if total != 8:
         sums = [lax.psum_scatter(p, "dp", scatter_dimension=0) for p in parts]
         return [lax.optimization_barrier(p).astype(FULL) for p in sums]
-    count, line = len(parts), total // 2
-    sems = lambda *shape: pltpu.SemaphoreType.DMA(shape)
+    pieces, line = pieces_of(parts, 1), total // 2
     return pl.pallas_call(
-        lambda *refs: scatter_kernel(count, line, *refs),
+        lambda *refs: scatter_kernel(pieces, line, *refs),
         out_shape=[jax.ShapeDtypeStruct(p.shape[1:], FULL) for p in parts],
-        in_specs=[pl.BlockSpec(memory_space=pl.ANY)] * count,
-        out_specs=[pl.BlockSpec(memory_space=pltpu.VMEM)] * count,
-        scratch_shapes=[pltpu.VMEM((line,) + p.shape[1:], p.dtype) for p in parts]
-        + [pltpu.VMEM((line,) + p.shape[1:], p.dtype) for p in parts]
-        + [pltpu.VMEM((line + 1,) + p.shape[1:], p.dtype) for p in parts]
-        + [sems(count, line) for _ in range(4)]
-        + [sems(count, line + 1)],
+        in_specs=[pl.BlockSpec(memory_space=pl.ANY)] * len(parts),
+        out_specs=[pl.BlockSpec(memory_space=pltpu.VMEM)] * len(parts),
+        scratch_shapes=scatter_scratch(parts, pieces, line),
         compiler_params=pltpu.CompilerParams(
             collective_id=collective_id, has_side_effects=True, vmem_limit_bytes=56 << 20
         ),
@@ -366,6 +450,24 @@
 
 def rms_norm(values, gain):
     return values * lax.rsqrt(jnp.mean(values * values, axis=-1, keepdims=True) + NORM_EPS) * gain
+
+
+def norm_rows_kernel(values_ref, gain_ref, out_ref):
+    out_ref[...] = rms_norm(values_ref[...].astype(FULL), gain_ref[0:1]).astype(LOW)
+
+
+def norm_rows(values, gain):
+    rows, width = values.shape
+    block = rows // SEQ
+    by_block = pl.BlockSpec((block, width), lambda i: (i, 0))
+    return pl.pallas_call(
+        norm_rows_kernel,
+        grid=(SEQ,),
+        in_specs=[by_block, pl.BlockSpec((8, width), lambda i: (0, 0))],
+        out_specs=by_block,
+        out_shape=jax.ShapeDtypeStruct(values.shape, LOW),
+        cost_estimate=pl.CostEstimate(flops=4 * values.size, bytes_accessed=4 * values.size, transcendentals=rows),
+    )(values, jnp.broadcast_to(gain, (8, width)))
 
 
 def join_tail(inputs_x, attn_o, ssm_o, gains):
@@ -641,7 +743,7 @@
         ],
         scratch_shapes=[pltpu.VMEM((8 + CHUNK, WIDE), FULL), pltpu.VMEM((CHUNK, WIDE), FULL)],
         compiler_params=pltpu.CompilerParams(vmem_limit_bytes=32 << 20),
-        cost_estimate=pl.CostEstimate(flops=2 * 10**9, bytes_accessed=16 << 20, transcendentals=10**7),
+        cost_estimate=pl.CostEstimate(flops=2 * 10**10, bytes_accessed=16 << 20, transcendentals=10**7),
     )(lengths, xzb, xzb, conv_rows, rate_row, skip_row)
 
 
@@ -672,7 +774,7 @@
             pltpu.VMEM((8 + CHUNK, WIDE), FULL),
         ],
         compiler_params=pltpu.CompilerParams(vmem_limit_bytes=32 << 20),
-        cost_estimate=pl.CostEstimate(flops=5 * 10**9, bytes_accessed=24 << 20, transcendentals=10**7),
+        cost_estimate=pl.CostEstimate(flops=6 * 10**10, bytes_accessed=24 << 20, transcendentals=10**7),
     )(lengths, xzb, xzb, conv_rows, rate_row, skip_row, states, read, d_gated)
 
 
@@ -792,24 +894,52 @@
             jax.ShapeDtypeStruct((queries.shape[0], 128), FULL),
         ],
         compiler_params=pltpu.CompilerParams(vmem_limit_bytes=32 << 20),
-        cost_estimate=pl.CostEstimate(flops=3 * 10**9, bytes_accessed=4 << 20, transcendentals=8 * 10**6),
+        cost_estimate=pl.CostEstimate(flops=4 * 10**10, bytes_accessed=4 << 20, transcendentals=8 * 10**6),
     )(lengths, queries, kv)
 
 
-def attention_backward(lengths, queries, kv, out, logs, d_out, rows):
+def attention_backward(lengths, queries, kv, out, logs, d_out, rows, parts, collective_id):
     group = kv.shape[0]
     by_step, kv_block = attention_specs(rows, group)
-    return pl.pallas_call(
-        attention_backward_kernel,
+    total = lax.axis_size("dp")
+    beside = parts if total == 8 else []
+    count, line = len(beside), total // 2
+    pieces = pieces_of(beside, 1)
+
+    def kernel(*refs):
+        own_in, parts_in = refs[:6], refs[6 : 6 + count]
+        own_out, sums_out = refs[6 + count : 8 + count], refs[8 + count : 8 + 2 * count]
+        sum_ref, transfer = refs[8 + 2 * count], refs[9 + 2 * count :]
+        step = pl.program_id(0) * GROUP_HEADS + pl.program_id(1)
+        steps = (SEQ + 1) * GROUP_HEADS
+        phases = scatter_phases(pieces, line, parts_in + sums_out + transfer) if count else []
+        spots = [min(13 * k, steps - 1) for k in range(len(phases))]
+        for phase, spot in zip(phases, spots):
+            if spot < steps - 1:
+                pl.when(step == spot)(phase)
+        attention_backward_kernel(*own_in, *own_out, sum_ref)
+        for phase, spot in zip(phases, spots):
+            if spot == steps - 1:
+                pl.when(step == spot)(phase)
+
+    found = pl.pallas_call(
+        kernel,
         grid=(SEQ + 1, GROUP_HEADS),
         in_specs=[pl.BlockSpec(memory_space=pltpu.SMEM), by_step(QW), kv_block]
-        + [by_step(QW), by_step(128), by_step(QW)],
-        out_specs=[by_step(QW), kv_block],
-        out_shape=[jax.ShapeDtypeStruct(queries.shape, LOW), jax.ShapeDtypeStruct(kv.shape, LOW)],
-        scratch_shapes=[pltpu.VMEM((group, 128), FULL)],
-        compiler_params=pltpu.CompilerParams(vmem_limit_bytes=32 << 20),
-        cost_estimate=pl.CostEstimate(flops=8 * 10**9, bytes_accessed=8 << 20, transcendentals=8 * 10**6),
-    )(lengths, queries, kv, out, logs, d_out)
+        + [by_step(QW), by_step(128), by_step(QW)]
+        + [pl.BlockSpec(memory_space=pl.ANY)] * count,
+        out_specs=[by_step(QW), kv_block] + [pl.BlockSpec(memory_space=pltpu.VMEM)] * count,
+        out_shape=[jax.ShapeDtypeStruct(queries.shape, LOW), jax.ShapeDtypeStruct(kv.shape, LOW)]
+        + [jax.ShapeDtypeStruct(p.shape[1:], FULL) for p in beside],
+        scratch_shapes=[pltpu.VMEM((group, 128), FULL)]
+        + (scatter_scratch(beside, pieces, line) if count else []),
+        compiler_params=pltpu.CompilerParams(
+            vmem_limit_bytes=56 << 20,
+            **(dict(collective_id=collective_id, has_side_effects=True) if count else {}),
+        ),
+        cost_estimate=pl.CostEstimate(flops=10**11, bytes_accessed=8 << 20, transcendentals=8 * 10**6),
+    )(lengths, queries, kv, out, logs, d_out, *beside)
+    return found[0], found[1], list(found[2:]) if count else scatter_dp(parts, collective_id)
 
 
 def pick(options, seq_index):
@@ -902,7 +1032,7 @@
     full_conv = small[:, :4, :conv_block].transpose(1, 0, 2).reshape(4, INNER).astype(FULL)
     gains = small[:, 8:12, :gains_block].transpose(1, 0, 2).reshape(4, D).astype(FULL)
     tokens_group = place(list(zip(seq_order(), token_blocks))).reshape(group, D)
-    normed = rms_norm(tokens_group.astype(FULL), gains[0]).astype(LOW)
+    normed = norm_rows(tokens_group, gains[0])
     qkv_wide = wide_of(qkv_shards)
     q_at = lambda h: lax.dynamic_slice_in_dim(qkv_wide, h * QW, QW, 1)
     kv_at = lambda h: [
@@ -914,16 +1044,18 @@
     full_qkv, full_xz = gather_dp([qkv_packet, xz_packet], 1)
     gate_up_packet = jnp.pad(w_gate_up, ((0, 0), (0, 0), (0, UNITS_PAD - UNITS))).reshape(block_rows, -1)
     down_packet = jnp.pad(w_down, ((0, 0), (0, UNITS_PAD - UNITS)))
-    full_qkv, full_xz, out_cols, gate_up_packet, down_packet = lax.optimization_barrier(
-        (full_qkv, full_xz, out_cols, gate_up_packet, down_packet)
-    )
+    d_total = cotangent.astype(FULL) * live
+    d_ffn = d_total.astype(LOW)
+    d_ffn_far, d_ffn_near = swap(d_ffn, "seq", 2), swap(d_ffn, "seq", 1)
+    full_qkv, full_xz, out_cols, gate_up_packet, down_packet, d_ffn_far, d_ffn_near = lax.optimization_barrier(
+        (full_qkv, full_xz, out_cols, gate_up_packet, down_packet, d_ffn_far, d_ffn_near)
+    )
+    d_ffn_group = jnp.concatenate([d_ffn, d_ffn_near, d_ffn_far, swap(d_ffn_far, "seq", 1)])
     full_qkv = full_qkv.reshape(D, -1)
     full_xz = full_xz.reshape(D, -1)
     full_gate_up = gather_dp_apart(gate_up_packet)
     full_down = gather_dp_apart(down_packet)
 
-    d_total = cotangent.astype(FULL) * live
-    d_ffn_group = gather_seq(d_total.astype(LOW)).reshape(group, D)
 
     own = lambda a: lax.dynamic_slice_in_dim(a, s * rows, rows, 0)
     normed_own = own(normed)
@@ -954,6 +1086,7 @@
 
     xzb = mm(normed_now, full_xz)
     attn_held, attn_far = scatter_far(attn_keep, after(attn_got, xzb))
+    xzb, attn_held = lax.optimization_barrier((xzb, attn_held))
     conv_rows = jnp.pad(channel_cut(full_conv, s, 1), ((0, 4), (0, WIDE - LOCAL_CH)))
     rate_row = jnp.pad(own_cut(ssm_rate, s, 0, 1), (STEP_AT, 128 - STEP_AT - LOCAL_HEADS))
     rate_row = jnp.broadcast_to(rate_row, (8, 128))
@@ -961,69 +1094,81 @@
     skip_row = jnp.broadcast_to(skip_row, (8, WIDE))
     mamba_in = (doc_lengths, xzb, conv_rows, rate_row, skip_row)
     gated, read, states = mamba_forward(*mamba_in)
+    gated, attn_far = meet(gated, attn_far)
     ssm_held, ssm_far = scatter_far(*scatter_begin(mm(gated, w_out_rows)))
-    attn_o = scatter_end(attn_held, after(attn_far, gated)) + mm(attended[group:], w_o5_rows)
+    attn_o = scatter_end(attn_held, attn_far) + mm(attended[group:], w_o5_rows)
     ssm_o = scatter_end(ssm_held, ssm_far)
 
     inputs_x = tokens_in.astype(FULL)
     (residual, normed_two), pull_join = jax.vjp(join_tail, inputs_x, attn_o, ssm_o, gains)
-    normed_two = gather_seq(normed_two.astype(LOW)).reshape(group, D)
+    normed_two, d_act = seq_arrivals(normed_two.astype(LOW), mm(d_ffn_group, full_down))
+    normed_two = jnp.concatenate(normed_two)
     gate_up = mm(normed_two, full_gate_up)
     ffn_gate, ffn_up = gate_up[:, :UNITS_PAD], gate_up[:, UNITS_PAD:]
     ffn_act = (jax.nn.silu(ffn_gate) * ffn_up).astype(LOW)
 
-    d_act = mm(d_ffn_group, full_down)
     sig = jax.nn.sigmoid(ffn_gate)
     d_gate = d_act * ffn_up * (sig * (1.0 + ffn_gate * (1.0 - sig)))
     d_up = d_act * ffn_gate * sig
     d_gate_up = jnp.concatenate([d_gate.astype(LOW), d_up.astype(LOW)], axis=1)
-    two_keep, two_got = scatter_begin(mm_nt(d_gate_up, full_gate_up))
-    grad_down_part = mm_tn(d_ffn_group, ffn_act).astype(LOW)
-    two_held, two_far = scatter_far(two_keep, after(two_got, grad_down_part))
-    grad_gate_up_part = mm_tn(normed_two, d_gate_up).astype(LOW)
-    d_normed_two = scatter_end(two_held, after(two_far, grad_gate_up_part))
+    two_keep, two_got = relative_begin(mm_nt(d_gate_up, full_gate_up))
+    two_got, grad_down_part = meet(two_got, mm_tn(d_ffn_group, ffn_act).astype(LOW))
+    two_held, two_far = relative_far(two_keep, two_got)
+    two_far, grad_gate_up_part = meet(two_far, mm_tn(normed_two, d_gate_up).astype(LOW))
+    d_normed_two = scatter_end(two_held, two_far)
     grad_gate_up_sum = scatter_dp_apart(grad_gate_up_part)
     grad_down_sum = scatter_dp_apart(grad_down_part)
     grad_gate_up = grad_gate_up_sum.reshape(block_rows, 2, UNITS_PAD)[:, :, :UNITS]
     grad_down = grad_down_sum[:, :UNITS]
 
     d_x_tail, d_attn_o, d_ssm_o, d_gains = pull_join((d_total, d_normed_two))
-    ssm_arrivals = seq_arrivals(d_ssm_o.astype(LOW))
-    ffn_part = mm_nt(ffn_act, full_down).astype(LOW)
-    ssm_arrivals = after(ssm_arrivals, ffn_part)
+    ssm_arrivals, ffn_part = seq_arrivals(d_ssm_o.astype(LOW), mm_nt(ffn_act, full_down).astype(LOW))
     d_attn_own = after(d_attn_o.astype(LOW), ssm_arrivals[2])
-    attn_arrivals = seq_arrivals(d_attn_own)
+    attn_near, attn_away = swap(d_attn_own, "seq", 1), swap(d_attn_own, "seq", 2)
     d_ssm = place(list(zip(seq_order(), ssm_arrivals))).reshape(group, D)
     d_gated = mm_nt(d_ssm, w_out_rows).astype(LOW)
 
     def send_columns(grad):
         width = D // SEQ
         blocks = [grad[:, width * j : width * (j + 1)] for j in range(SEQ)]
-        return [pick(blocks, s)] + [swap(pick(blocks, s ^ bit), "seq", bit) for bit in (1, 2, 3)]
-
-    mamba_pieces = send_columns(mm_tn(gated, d_ssm).astype(LOW))
+        return [with_layout_constraint(pick(blocks, s ^ k), Layout((0, 1))) for k in range(SEQ)]
+
+    def trade(blocks):
+        return blocks[:1] + [swap(blocks[bit], "seq", bit) for bit in (1, 2, 3)]
+
+    mamba_blocks, d_gated = meet(send_columns(mm_tn(gated, d_ssm).astype(LOW)), d_gated)
+    mamba_pieces = trade(mamba_blocks)
+    (mamba_pieces[1], attn_near), d_gated = meet((mamba_pieces[1], attn_near), d_gated)
     d_xzb, d_chan, d_rate = mamba_backward(*mamba_in, states, read, d_gated)
-    mamba_pieces, attn_arrivals = after((mamba_pieces, attn_arrivals), d_xzb)
+    (mamba_pieces[2:], attn_away), d_xzb = meet((mamba_pieces[2:], attn_away), d_xzb)
+    ffn_keep, ffn_got = relative_begin(ffn_part)
+    attn_arrivals = [d_attn_own, attn_near, attn_away, swap(attn_away, "seq", 1)]
     arrived = place(list(zip(seq_order(), mamba_pieces)))
-    grad_out = scatter_dp_apart(
-        jnp.concatenate([arrived[j, : HEAD_COUNT[j] * SSM_HEAD] for j in range(SEQ)])
-    )
+    grad_out_part = jnp.concatenate(
+        [arrived[j, : HEAD_COUNT[j] * SSM_HEAD] for j in range(SEQ)]
+    ).reshape(dp_total, out_block, -1)
 
     d_attn = place(list(zip(seq_order(), attn_arrivals))).reshape(group, D)
     d_attended = jnp.concatenate([mm_nt(d_attn, w_o_rows), mm_nt(d_attn_own, w_o5_rows)]).astype(LOW)
-    head_pieces = send_columns(
+    head_blocks = send_columns(
         jnp.concatenate([mm_tn(attended[:group], d_attn), mm_tn(attended[group:], d_attn_own)]).astype(LOW)
     )
-    ffn_held, ffn_far = scatter_far(*scatter_begin(ffn_part))
-    ffn_own = scatter_end(ffn_held, after(ffn_far, d_xzb))
-    mixed_out = ((residual + ffn_own) * live).astype(LOW)
+    head_blocks, d_attended = meet(head_blocks, d_attended)
+    head_pieces = trade(head_blocks)
+    ffn_got, d_attended = meet(ffn_got, d_attended)
+    ffn_held, ffn_far = relative_far(ffn_keep, ffn_got)
+    ffn_held, d_attended = meet(ffn_held, d_attended)
     d_conv = d_chan[:CONV, :LOCAL_CH]
     d_skip = jnp.sum(d_chan[CONV, :LOCAL_CH].reshape(LOCAL_HEADS, SSM_HEAD), axis=1)
     d_rate = d_rate[0, STEP_AT : STEP_AT + LOCAL_HEADS]
     grad_xz_part = mm_tn(normed, d_xzb).astype(LOW).reshape(dp_total, block_rows, -1)
 
-    d_queries, d_kv = attention_backward(doc_lengths, queries, kv, attended, logs, d_attended, rows)
-    arrived = place(list(zip(seq_order(), after(head_pieces, d_queries))))
+    d_queries, d_kv, (grad_xz_sum, grad_out) = attention_backward(
+        doc_lengths, queries, kv, attended, logs, d_attended, rows, [grad_xz_part, grad_out_part], 3
+    )
+    (head_pieces, ffn_far), d_queries = meet((head_pieces, ffn_far), d_queries)
+    mixed_out = ((residual + scatter_end(ffn_held, ffn_far)) * live).astype(LOW)
+    arrived = place(list(zip(seq_order(), head_pieces)))
     grad_o_part = jnp.concatenate(
         [arrived[j, :QW] for j in range(SEQ)] + [jnp.sum(arrived[:, QW:].astype(FULL), axis=0).astype(LOW)]
     ).reshape(dp_total, block_rows, -1)
@@ -1052,12 +1197,11 @@
         axis=1,
     )
     normed_keep, normed_got = scatter_begin(d_normed_part)
-    normed_held, normed_far = scatter_far(normed_keep, after(normed_got, grad_qkv_part))
-    grad_xz_part, normed_held = lax.optimization_barrier((grad_xz_part, normed_held))
-    grad_o, grad_xz_sum, grad_qkv_sum, small_sum = scatter_dp(
-        [grad_o_part, grad_xz_part, grad_qkv_part, small_part], 2
-    )
-    normed_far = after(normed_far, small_sum)
+    normed_got, grad_qkv_part = meet(normed_got, grad_qkv_part)
+    normed_held, normed_far = scatter_far(normed_keep, normed_got)
+    grad_o_part, normed_held = meet(grad_o_part, normed_held)
+    grad_qkv_sum, grad_o, small_sum = scatter_dp([grad_qkv_part, grad_o_part, small_part], 2)
+    normed_far, small_sum = meet(normed_far, small_sum)
     small_sum = small_sum + swap(small_sum, "seq", 1)
     small_sum = small_sum + swap(small_sum, "seq", 2)
     grad_xz_sum = grad_xz_sum.astype(LOW)

time: 1190 us -> 1100 us (0.924)
  waiting for transfers between devices: 172 us -> 102 us
  local copies, waits for them, and re-layouts: 196 us -> 164 us
  matrix products: 186 us -> 198 us
    ppermute x42, waiting for transfers between devices: 172 us -> 97.9 us  [swap(): lax.ppermute(value, axis, [(i, i ^ bit) for i in range(lax.axis_size(axis...]
    convert_element_type x5 -> x0, local copies, waits for them, and re-layouts: 35 us -> none  [the longest x3 20.5 us: scatter_begin(): part.astype(LOW).reshape((2, 2, part.shape[0] // SEQ) + part.shape[1:])]
    optimization_barrier x7 -> x14, local copies, waits for them, and re-layouts: 16.1 us -> 26 us  [meet(): return lax.optimization_barrier((one, two))]
    unnamed x224 -> x261, local copies, waits for them, and re-layouts: 49.5 us -> 59.3 us
    pallas_call x4 -> x5, Pallas kernels: 348 us -> 344 us  [the longest x2 160 us: gather_dp(): pl.pallas_call(lambda *refs: gather_kernel(pieces, line, *refs), out_shap...]
  transfers between devices with their start and end apart: 51 -> 50, of which waited for: 14 -> 12; matrix products, arithmetic and copies ran while one was open for 33% -> 33% of each run, Pallas kernels for 32% -> 43%
where the time goes in v4:
time: 1100 us; the launch traced here: 1090 us
  Pallas kernels  468 us (43%)
  matrix products  198 us (18%)
  local copies, waits for them, and re-layouts  164 us (15%)
  waiting for transfers between devices  102 us (9%)
  other arithmetic  99.4 us (9%)
  starting transfers between devices  41.8 us (4%)
  between operations  17.5 us (2%)
    pallas_call x2, Pallas kernels, gather_dp(): pl.pallas_call(lambda *refs: gather_kernel(pieces, line, *refs), out_shap...  160 us
    pallas_call x1, Pallas kernels, attention_backward(): pl.pallas_call(kernel, grid=(SEQ + 1, GROUP_HEADS), in_specs=[pl.BlockSpe...  113 us
    ppermute x42, waiting for transfers between devices, swap(): lax.ppermute(value, axis, [(i, i ^ bit) for i in range(lax.axis_size(axis...  97.9 us
    dot_general x8, matrix products, mm_nt(): lax.dot_general(left, right, (((1,), (1,)), ((), ())), preferred_element_...  67.6 us
    dot_general x9, matrix products, mm(): return jnp.dot(left, right, preferred_element_type=FULL)  67.2 us
    pallas_call x1, Pallas kernels, scatter_dp(): pl.pallas_call(lambda *refs: scatter_kernel(pieces, line, *refs), out_sha...  65.5 us
    dot_general x8, matrix products, mm_tn(): lax.dot_general(left, right, (((0,), (0,)), ((), ())), preferred_element_...  62.8 us
    unnamed x261, local copies, waits for them, and re-layouts  59.3 us
  transfers between devices with their start and end apart: 50, of which 12 were waited for; matrix products, arithmetic and copies ran while one was open for 33% of the time, Pallas kernels for 43%

profile of v4, /device:TPU:0, one launch (start us, length us, event | category | flops | bytes accessed | tf_op | source)
XLA Modules:
  0.0 1089.3 jit_solution(15696013105693822594)
XLA Ops:
  19.9 14.9 %collective-permute-done.6.refs_3_ = bf16[320,1600]{1,0:T(8,128)(2,1)S(1)} collective-permute-done((bf16[320,1600]{1,0:T(8,128)(2,1)}, bf16[320,1600]{1,0:T(8,128)(2,1)S(1)}, u32[]{:S(2)}, u32[]{:S(2)}) %collective-permute-start.6) | collective-permute-done | bytes 1024032 | tf_op jit(solution)/shard_map/ppermute | solution.py:41
  35.0 5.0 collective-permute-done.1
  49.8 62.5 %shard_map.237 = (bf16[8,16,512]{2,1,0:T(8,128)(2,1)S(1)}, bf16[8,600,400]{2,1,0:T(8,128)(2,1)S(1)}) custom-call(bf16[16,512]{1,0:T(8,128)(2,1)S(1)} %fusion.59.refs_0_, bf16[600,400]{1,0:T(8,128)(2,1)S(1)} %pad_maximum_fusion.21.refs_1_), custom_call_target="tpu_custom_call" | custom-call | bytes 7942144 | tf_op jit(solution)/shard_map/pallas_call | solution.py:259
  129.4 97.8 %shard_map.240 = (bf16[8,200,896]{2,1,0:T(8,128)(2,1)S(1)}, bf16[8,200,1792]{2,1,0:T(8,128)(2,1)S(1)}) custom-call(bf16[200,896]{1,0:T(8,128)(2,1)S(1)} %concatenate.91.refs_0_, bf16[200,1792]{1,0:T(8,128)(2,1)S(1)} %concatenate.92.refs_1_), custom_call_target="tpu_custom_call" | custom-call | bytes 17203200 | tf_op jit(solution)/shard_map/pallas_call | solution.py:259
  239.8 5.5 shard_map.239
  245.3 6.7 convolution_convert_fusion.9
  293.2 36.2 %shard_map.241 = (bf16[1600,320]{1,0:T(8,128)(2,1)S(1)}, f32[1600,128]{1,0:T(8,128)S(1)}) custom-call(s32[1,2]{1,0:T(1,128)S(1)} %copy-done.24, bf16[1600,320]{1,0:T(8,128)(2,1)S(1)} %pad_maximum_fusion.11.q_ref.refs_1_, bf16[1280,256]{1,0:T(8,128)(2,1)S(1)} %slice.501.kv_ref.refs_2_), custom_call_target="tpu_custom_call" | custom-call | flops 40000000000 | bytes 4194304 | tf_op jit(solution)/shard_map/pallas_call | solution.py:887
  338.8 4.2 select_select_fusion.3
  343.0 4.7 pad_maximum_fusion.1
  347.7 3.9 convolution_convert_fusion.6
  353.3 10.3 fusion.87.xzb_ref.tail_ref
  369.3 18.3 %shard_map.242 = (bf16[1280,896]{1,0:T(8,128)(2,1)S(1)}, bf16[1280,896]{1,0:T(8,128)(2,1)S(1)}, f32[10,16,896]{2,1,0:T(8,128)S(1)}) custom-call(s32[1,2]{1,0:T(1,128)S(1)} %copy-done.24, f32[1280,1792]{1,0:T(8,128)S(1)} %fusion.87.xzb_ref.tail_ref, f32[1280,1792]{1,0:T(8,128)S(1)} %fusion.87.xzb_ref.tail_ref, f32[8,896]{1,0:T(8,128)S(1)} %pad.141.conv_ref, ...), custom_call_target="tpu_custom_call" | custom-call | flops 20000000000 | bytes 16777216 | tf_op jit(solution)/shard_map/pallas_call | solution.py:734
  387.7 3.9 copy-done.29
  394.2 5.3 convolution_convert_fusion.5
  399.8 4.2 collective-permute-done.15
  409.9 21.1 %collective-permute-done.16 = bf16[320,1600]{1,0:T(8,128)(2,1)} collective-permute-done((bf16[320,1600]{1,0:T(8,128)(2,1)S(1)}, bf16[320,1600]{1,0:T(8,128)(2,1)}, u32[]{:S(2)}, u32[]{:S(2)}) %collective-permute-start.16) | collective-permute-done | bytes 1024032 | tf_op jit(solution)/shard_map/ppermute | solution.py:41
  436.4 13.1 %fusion.34 = f32[1280,1408]{1,0:T(8,128)} fusion(bf16[1600,1408]{1,0:T(8,128)(2,1)} %all-gather.3.cloned.1.call-done, bf16[320,1600]{1,0:T(8,128)(2,1)} %collective-permute-done.18, bf16[320,1600]{1,0:T(8,128)(2,1)} %collective-permute-done.8, bf16[320,1600]{1,0:T(8,128)(2,1)} %collective-permute-done.9, bf16[320,1600]{1,0:T(8,128)(2,1)} %fusion.16), kind=kOutput, calls=%fused_computation.128 | convolution fusion | flops 5783552000 | bytes 15810560 | tf_op jit(solution)/shard_map/dot_general | solution.py:440
  449.5 10.2 collective-permute-done.17
  466.5 22.3 %fusion.33 = f32[1280,2816]{1,0:T(8,128)} fusion(bf16[1600,2816]{1,0:T(8,128)(2,1)} %all-gather.5.cloned.1.call-done, bf16[320,1600]{1,0:T(8,128)(2,1)} %collective-permute-done.20, bf16[320,1600]{1,0:T(8,128)(2,1)} %collective-permute-done.17, bf16[320,1600]{1,0:T(8,128)(2,1)} %collective-permute-done.19, bf16[320,1600]{1,0:T(8,128)(2,1)S(1)} %multiply_convert_fusion.4), kind=kOutput, calls=%fused_computation.127 | convolution fusion | flops 11550720000 | bytes 27525120 | tf_op jit(solution)/shard_map/dot_general | solution.py:440
  488.8 9.2 multiply_convert_fusion.2
  499.9 17.5 %convolution_convert_fusion.4 = bf16[1280,1600]{1,0:T(8,128)(2,1)S(1)} fusion(bf16[1600,2816]{1,0:T(8,128)(2,1)} %all-gather.5.cloned.1.call-done, bf16[1280,1408]{1,0:T(8,128)(2,1)} %get-tuple-element.262, bf16[1280,1408]{1,0:T(8,128)(2,1)S(1)} %get-tuple-element.261), kind=kOutput, calls=%fused_computation.8 | convolution fusion | flops 11550801920 | bytes 20316160 | tf_op jit(solution)/shard_map/dot_general | solution.py:444
  521.0 4.0 copy.113
  525.0 12.1 %convolution_convert_fusion.3 = bf16[1600,1408]{1,0:T(8,128)(2,1)} fusion(bf16[1280,1408]{1,0:T(8,128)(2,1)} %get-tuple-element.263, bf16[320,1600]{1,0:T(8,128)(2,1)} %collective-permute-done.18, bf16[320,1600]{1,0:T(8,128)(2,1)} %collective-permute-done.8, bf16[320,1600]{1,0:T(8,128)(2,1)} %collective-permute-done.9, bf16[320,1600]{1,0:T(8,128)(2,1)} %fusion.16), kind=kOutput, calls=%fused_computation.7 | convolution fusion | flops 5785804800 | bytes 12206080 | tf_op jit(solution)/shard_map/dot_general | solution.py:448
  537.2 4.6 copy.114
  546.3 18.5 %convolution_convert_fusion = bf16[1600,2816]{1,0:T(8,128)(2,1)} fusion(bf16[1280,1408]{1,0:T(8,128)(2,1)} %get-tuple-element.262, bf16[1280,1408]{1,0:T(8,128)(2,1)} %copy-done.63, bf16[320,1600]{1,0:T(8,128)(2,1)} %collective-permute-done.20, bf16[320,1600]{1,0:T(8,128)(2,1)} %collective-permute-done.17, bf16[320,1600]{1,0:T(8,128)(2,1)} %collective-permute-done.19, ...), kind=kOutput, calls=%fused_computation | convolution fusion | flops 11569643520 | bytes 20316160 | tf_op jit(solution)/shard_map/dot_general | solution.py:448
  564.8 6.2 collective-permute-done.22
  573.9 3.9 multiply_reduce_fusion.4
  580.6 9.0 convolution_convert_fusion.2
  589.6 14.8 %collective-permute-done.23.refs_3_ = bf16[320,1600]{1,0:T(8,128)(2,1)} collective-permute-done((bf16[320,1600]{1,0:T(8,128)(2,1)S(1)}, bf16[320,1600]{1,0:T(8,128)(2,1)}, u32[]{:S(2)}, u32[]{:S(2)}) %collective-permute-start.23) | collective-permute-done | bytes 1024032 | tf_op jit(solution)/shard_map/ppermute | solution.py:41
  614.7 6.0 convolution_convert_fusion.7.d_gated_ref
  620.7 4.5 convolution_convert_fusion.8
  634.7 4.0 copy.117
  657.9 54.4 %shard_map.244 = (bf16[1280,1792]{1,0:T(8,128)(2,1)S(1)}, f32[8,896]{1,0:T(8,128)S(1)}, f32[8,128]{1,0:T(8,128)S(1)}) custom-call(s32[1,2]{1,0:T(1,128)S(1)} %copy-done.24, f32[1280,1792]{1,0:T(8,128)S(1)} %copy-done.30, f32[1280,1792]{1,0:T(8,128)S(1)} %copy-done.30, f32[8,896]{1,0:T(8,128)S(1)} %copy-done.19, f32[8,128]{1,0:T(8,128)S(1)} %broadcast_in_dim.19.rate_ref, ...), custom_call_target="tpu_custom_call" | custom-call | flops 60000002048 | bytes 25165824 | tf_op jit(solution)/shard_map/pallas_call | solution.py:755
  727.8 13.8 %convolution_convert_fusion.1 = bf16[1600,1792]{1,0:T(8,128)(2,1)} fusion(bf16[1280,1600]{1,0:T(8,128)(2,1)} %shard_map.239, bf16[1280,1792]{1,0:T(8,128)(2,1)} %copy-done.28), kind=kOutput, calls=%fused_computation.5 | convolution fusion | flops 7342899200 | bytes 14417920 | tf_op jit(solution)/shard_map/dot_general | solution.py:448
  754.3 4.0 convolution_convert_fusion.14
  765.5 4.2 add_convert_fusion
  777.4 112.8 %shard_map.247 = (bf16[1600,320]{1,0:T(8,128)(2,1)}, bf16[1280,256]{1,0:T(8,128)(2,1)}, f32[200,1792]{1,0:T(8,128)}, f32[400,400]{1,0:T(8,128)}) custom-call(s32[1,2]{1,0:T(1,128)} %refs_0_.1, bf16[1600,320]{1,0:T(8,128)(2,1)} %copy-done.9, bf16[1280,256]{1,0:T(8,128)(2,1)} %copy-done.14, bf16[1600,320]{1,0:T(8,128)(2,1)} %copy-done.16, ...), custom_call_target="tpu_custom_call" | custom-call | flops 99999997952 | bytes 8388608 | tf_op jit(solution)/shard_map/pallas_call | solution.py:925
  892.8 6.8 collective-permute-start.44
  903.1 8.8 fusion.17
  911.9 16.1 %multiply_reduce_fusion = (f32[1600]{0:T(1024)S(1)}, bf16[1280,1600]{1,0:T(8,128)(2,1)}, f32[1280,1600]{1,0:T(8,128)}) fusion(f32[1280]{0:T(1024)S(1)} %copy-done.101, bf16[4,320,1600]{2,1,0:T(8,128)(2,1)S(1)} %bitcast.175, f32[1280,1600]{1,0:T(8,128)} %fusion.17, bf16[1280,1792]{1,0:T(8,128)(2,1)} %copy-done.28, bf16[1600,1792]{1,0:T(8,128)(2,1)} %bitcast.186), kind=kOutput, calls=%fused_computation.2 | convolution fusion | flops 7352318464 | bytes 34909440 | tf_op jit(solution)/shard_map/dot_general | solution.py:444
  931.8 4.4 multiply_reduce_fusion.2
  936.2 5.1 convolution_convert_fusion.10
  945.8 5.4 copy.137
  956.5 4.9 fusion.12
  961.4 65.5 %shard_map.249 = (f32[200,896]{1,0:T(8,128)}, f32[200,400]{1,0:T(8,128)}, f32[16,512]{1,0:T(8,128)}) custom-call(bf16[8,200,896]{2,1,0:T(8,128)(2,1)} %bitcast.192, bf16[8,200,400]{2,1,0:T(8,128)(2,1)} %bitcast.208, f32[8,16,512]{2,1,0:T(8,128)} %fusion.43.refs_2_), custom_call_target="tpu_custom_call" | custom-call | bytes 4278272 | tf_op jit(solution)/shard_map/pallas_call | solution.py:401
  1031.5 4.7 collective-permute-done.42.refs_3_
  1046.6 4.0 concatenate.113
  1052.8 12.3 %collective-permute-done.38 = bf16[320,1600]{1,0:T(8,128)(2,1)} collective-permute-done((bf16[320,1600]{1,0:T(8,128)(2,1)}, bf16[320,1600]{1,0:T(8,128)(2,1)}, u32[]{:S(2)}, u32[]{:S(2)}) %collective-permute-start.38) | collective-permute-done | bytes 1024032 | tf_op jit(solution)/shard_map/ppermute | solution.py:41
  (544 shorter events, 280.0 us)
Async XLA Ops:
  7.2 429.2 %all-gather.3.cloned.1.call-start = ((), (), s32[]{:S(2)}) async-start(), calls=%async_computation.2 | async-start | bytes 5068800 | tf_op jit(solution)/shard_map/all_gather | solution.py:417
  7.3 27.6 %collective-permute-start.6 = (bf16[320,1600]{1,0:T(8,128)(2,1)}, bf16[320,1600]{1,0:T(8,128)(2,1)S(1)}, u32[]{:S(2)}, u32[]{:S(2)}) collective-permute-start(bf16[320,1600]{1,0:T(8,128)(2,1)} %refs_1_), channel_id=1, source_target_pairs={{0,2},{1,3},{2,0},{3,1},{4,6},{5,7},{6,4},{7,5},{8,10},{9,11},{10,... | collective-permute-start | bytes 3072008 | tf_op jit(solution)/shard_map/ppermute | solution.py:41
  10.3 106.6 %collective-permute-start.5 = (bf16[320,1600]{1,0:T(8,128)(2,1)}, bf16[320,1600]{1,0:T(8,128)(2,1)S(1)}, u32[]{:S(2)}, u32[]{:S(2)}) collective-permute-start(bf16[320,1600]{1,0:T(8,128)(2,1)} %refs_1_), channel_id=1, source_target_pairs={{0,1},{1,0},{2,3},{3,2},{4,5},{5,4},{6,7},{7,6},{8,9},{9,8},{10,11... | collective-permute-start | bytes 3072008 | tf_op jit(solution)/shard_map/ppermute | solution.py:41
  10.3 29.7 %collective-permute-start.1 = (bf16[200,560]{1,0:T(8,128)(2,1)}, bf16[200,560]{1,0:T(8,128)(2,1)}, u32[]{:S(2)}, u32[]{:S(2)}) collective-permute-start(bf16[200,560]{1,0:T(8,128)(2,1)} %param.19), channel_id=1, source_target_pairs={{0,2},{1,3},{2,0},{3,1},{4,6},{5,7},{6,4},{7,5},{8,10},{9,11},{10,... | collective-permute-start | bytes 672008 | tf_op jit(solution)/shard_map/ppermute | solution.py:41
  10.4 31.8 %collective-permute-start = (bf16[200,560]{1,0:T(8,128)(2,1)}, bf16[200,560]{1,0:T(8,128)(2,1)}, u32[]{:S(2)}, u32[]{:S(2)}) collective-permute-start(bf16[200,560]{1,0:T(8,128)(2,1)} %param.19), channel_id=1, source_target_pairs={{0,1},{1,0},{2,3},{3,2},{4,5},{5,4},{6,7},{7,6},{8,9},{9,8},{10,11... | collective-permute-start | bytes 672008 | tf_op jit(solution)/shard_map/ppermute | solution.py:41
  13.9 31.3 %collective-permute-start.3 = (bf16[200,832]{1,0:T(8,128)(2,1)}, bf16[200,832]{1,0:T(8,128)(2,1)}, u32[]{:S(2)}, u32[]{:S(2)}) collective-permute-start(bf16[200,832]{1,0:T(8,128)(2,1)} %get-tuple-element.325), channel_id=1, source_target_pairs={{0,1},{1,2},{2,0},{4,5},{5,6},{6,4},{8,9},{9,10},{10,8},{12,13},{1... | collective-permute-start | bytes 998408 | tf_op jit(solution)/shard_map/ppermute | solution.py:427
  34.8 82.1 %collective-permute-start.7 = (bf16[320,1600]{1,0:T(8,128)(2,1)S(1)}, bf16[320,1600]{1,0:T(8,128)(2,1)}, u32[]{:S(2)}, u32[]{:S(2)}) collective-permute-start(bf16[320,1600]{1,0:T(8,128)(2,1)S(1)} %collective-permute-done.6.refs_3_), channel_id=1, source_target_pairs={{0,1},{1,0},{2,3},{3,2},{4,5},{5,4},{6,7},{7,6},{8,9},{9,8},{10,11... | collective-permute-start | bytes 3072008 | tf_op jit(solution)/shard_map/ppermute | solution.py:41
  40.0 74.5 %collective-permute-start.4 = (bf16[200,832]{1,0:T(8,128)(2,1)}, bf16[200,832]{1,0:T(8,128)(2,1)}, u32[]{:S(2)}, u32[]{:S(2)}) collective-permute-start(bf16[200,832]{1,0:T(8,128)(2,1)} %get-tuple-element.324), channel_id=1, source_target_pairs={{1,3},{2,1},{3,2},{5,7},{6,5},{7,6},{9,11},{10,9},{11,10},{13,15},... | collective-permute-start | bytes 998408 | tf_op jit(solution)/shard_map/ppermute | solution.py:428
  42.3 189.1 %collective-permute-start.8 = (bf16[320,1600]{1,0:T(8,128)(2,1)}, bf16[320,1600]{1,0:T(8,128)(2,1)}, u32[]{:S(2)}, u32[]{:S(2)}) collective-permute-start(bf16[320,1600]{1,0:T(8,128)(2,1)} %fusion.16), channel_id=1, source_target_pairs={{0,2},{1,3},{2,0},{3,1},{4,6},{5,7},{6,4},{7,5},{8,10},{9,11},{10,... | collective-permute-start | bytes 3072008 | tf_op jit(solution)/shard_map/ppermute | solution.py:41
  45.3 186.1 %collective-permute-start.9 = (bf16[320,1600]{1,0:T(8,128)(2,1)}, bf16[320,1600]{1,0:T(8,128)(2,1)}, u32[]{:S(2)}, u32[]{:S(2)}) collective-permute-start(bf16[320,1600]{1,0:T(8,128)(2,1)} %fusion.16), channel_id=1, source_target_pairs={{0,1},{1,0},{2,3},{3,2},{4,5},{5,4},{6,7},{7,6},{8,9},{9,8},{10,11... | collective-permute-start | bytes 3072008 | tf_op jit(solution)/shard_map/ppermute | solution.py:41
  231.4 235.1 %all-gather.5.cloned.1.call-start = ((), (), s32[]{:S(2)}) async-start(), calls=%async_computation.3 | async-start | bytes 10137600 | tf_op jit(solution)/shard_map/all_gather | solution.py:417
  279.6 59.1 %collective-permute-start.12 = (bf16[1600,400]{0,1:T(8,128)(2,1)}, bf16[1600,400]{0,1:T(8,128)(2,1)}, u32[]{:S(2)}, u32[]{:S(2)}) collective-permute-start(bf16[1600,400]{0,1:T(8,128)(2,1)} %concatenate.97), channel_id=1, source_target_pairs={{0,3},{1,2},{2,1},{3,0},{4,7},{5,6},{6,5},{7,4},{8,11},{9,10},{10,... | collective-permute-start | bytes 3840008 | tf_op jit(solution)/shard_map/ppermute | solution.py:41
  284.7 54.0 %collective-permute-start.11 = (bf16[1600,400]{0,1:T(8,128)(2,1)}, bf16[1600,400]{0,1:T(8,128)(2,1)}, u32[]{:S(2)}, u32[]{:S(2)}) collective-permute-start(bf16[1600,400]{0,1:T(8,128)(2,1)} %concatenate.96), channel_id=1, source_target_pairs={{0,2},{1,3},{2,0},{3,1},{4,6},{5,7},{6,4},{7,5},{8,10},{9,11},{10,... | collective-permute-start | bytes 3840008 | tf_op jit(solution)/shard_map/ppermute | solution.py:41
  289.3 49.5 %collective-permute-start.10 = (bf16[1600,400]{0,1:T(8,128)(2,1)}, bf16[1600,400]{0,1:T(8,128)(2,1)}, u32[]{:S(2)}, u32[]{:S(2)}) collective-permute-start(bf16[1600,400]{0,1:T(8,128)(2,1)} %concatenate.95), channel_id=1, source_target_pairs={{0,1},{1,0},{2,3},{3,2},{4,5},{5,4},{6,7},{7,6},{8,9},{9,8},{10,11... | collective-permute-start | bytes 3840008 | tf_op jit(solution)/shard_map/ppermute | solution.py:41
  330.5 743.3 %reduce-scatter.7.cloned.1.call-start = ((), (), s32[]{:S(2)}) async-start(), calls=%async_computation.5 | async-start | bytes 5068800
  351.8 11.8 %collective-permute-start.13 = (bf16[2,320,1600]{2,1,0:T(8,128)(2,1)S(1)}, bf16[2,320,1600]{2,1,0:T(8,128)(2,1)S(1)}, u32[]{:S(2)}, u32[]{:S(2)}) collective-permute-start(bf16[2,320,1600]{2,1,0:T(8,128)(2,1)S(1)} %dynamic-slice_bitcast_fusion.2), channel_id=1, source_target_pairs={{0,1},{1,0},{2,3},{3,2},{4,5},{5,4},{6,7},{7,6},{8,9},{9,8},{10,11... | collective-permute-start | bytes 6144008 | tf_op jit(solution)/shard_map/ppermute | solution.py:41
  365.4 27.6 %collective-permute-start.14 = (bf16[320,1600]{1,0:T(8,128)(2,1)S(1)}, bf16[320,1600]{1,0:T(8,128)(2,1)S(1)}, u32[]{:S(2)}, u32[]{:S(2)}) collective-permute-start(bf16[320,1600]{1,0:T(8,128)(2,1)S(1)} %get-tuple-element.270), channel_id=1, source_target_pairs={{0,2},{1,3},{2,0},{3,1},{4,6},{5,7},{6,4},{7,5},{8,10},{9,11},{10,... | collective-permute-start | bytes 3072008 | tf_op jit(solution)/shard_map/ppermute | solution.py:41
  399.7 4.3 collective-permute-start.15
  405.3 25.7 %collective-permute-start.16 = (bf16[320,1600]{1,0:T(8,128)(2,1)S(1)}, bf16[320,1600]{1,0:T(8,128)(2,1)}, u32[]{:S(2)}, u32[]{:S(2)}) collective-permute-start(bf16[320,1600]{1,0:T(8,128)(2,1)S(1)} %fusion.13), channel_id=1, source_target_pairs={{0,2},{1,3},{2,0},{3,1},{4,6},{5,7},{6,4},{7,5},{8,10},{9,11},{10,... | collective-permute-start | bytes 3072008 | tf_op jit(solution)/shard_map/ppermute | solution.py:41
  406.8 29.5 %collective-permute-start.18 = (bf16[320,1600]{1,0:T(8,128)(2,1)}, bf16[320,1600]{1,0:T(8,128)(2,1)}, u32[]{:S(2)}, u32[]{:S(2)}) collective-permute-start(bf16[320,1600]{1,0:T(8,128)(2,1)} %collective-permute-done.8), channel_id=1, source_target_pairs={{0,1},{1,0},{2,3},{3,2},{4,5},{5,4},{6,7},{7,6},{8,9},{9,8},{10,11... | collective-permute-start | bytes 3072008 | tf_op jit(solution)/shard_map/ppermute | solution.py:41
  434.7 24.9 %collective-permute-start.17 = (bf16[320,1600]{1,0:T(8,128)(2,1)S(1)}, bf16[320,1600]{1,0:T(8,128)(2,1)}, u32[]{:S(2)}, u32[]{:S(2)}) collective-permute-start(bf16[320,1600]{1,0:T(8,128)(2,1)S(1)} %multiply_convert_fusion.4), channel_id=1, source_target_pairs={{0,2},{1,3},{2,0},{3,1},{4,6},{5,7},{6,4},{7,5},{8,10},{9,11},{10,... | collective-permute-start | bytes 3072008 | tf_op jit(solution)/shard_map/ppermute | solution.py:41
  436.4 23.3 %collective-permute-start.19 = (bf16[320,1600]{1,0:T(8,128)(2,1)S(1)}, bf16[320,1600]{1,0:T(8,128)(2,1)}, u32[]{:S(2)}, u32[]{:S(2)}) collective-permute-start(bf16[320,1600]{1,0:T(8,128)(2,1)S(1)} %multiply_convert_fusion.4), channel_id=1, source_target_pairs={{0,1},{1,0},{2,3},{3,2},{4,5},{5,4},{6,7},{7,6},{8,9},{9,8},{10,11... | collective-permute-start | bytes 3072008 | tf_op jit(solution)/shard_map/ppermute | solution.py:41
  459.6 3.0 collective-permute-start.20
  525.0 12.1 %collective-permute-start.21 = (bf16[640,1600]{0,1:T(8,128)(2,1)}, bf16[640,1600]{0,1:T(8,128)(2,1)}, u32[]{:S(2)}, u32[]{:S(2)}) collective-permute-start(bf16[640,1600]{0,1:T(8,128)(2,1)} %copy.113), channel_id=1, source_target_pairs={{0,1},{1,0},{2,3},{3,2},{4,5},{5,4},{6,7},{7,6},{8,9},{9,8},{10,11... | collective-permute-start | bytes 6144008 | tf_op jit(solution)/shard_map/ppermute | solution.py:41
  537.1 538.8 %reduce-scatter.5.cloned.1.call-start = ((), (), s32[]{:S(2)}) async-start(), calls=%async_computation.4 | async-start | bytes 10137600 | tf_op jit(solution)/shard_map/reduce_scatter | solution.py:421
  544.9 26.1 %collective-permute-start.22 = (bf16[320,1600]{1,0:T(8,128)(2,1)}, bf16[320,1600]{1,0:T(8,128)(2,1)S(1)}, u32[]{:S(2)}, u32[]{:S(2)}) collective-permute-start(bf16[320,1600]{1,0:T(8,128)(2,1)} %add_convert_fusion.1), channel_id=1, source_target_pairs={{0,2},{1,3},{2,0},{3,1},{4,6},{5,7},{6,4},{7,5},{8,10},{9,11},{10,... | collective-permute-start | bytes 3072008 | tf_op jit(solution)/shard_map/ppermute | solution.py:41
  579.1 25.2 %collective-permute-start.23 = (bf16[320,1600]{1,0:T(8,128)(2,1)S(1)}, bf16[320,1600]{1,0:T(8,128)(2,1)}, u32[]{:S(2)}, u32[]{:S(2)}) collective-permute-start(bf16[320,1600]{1,0:T(8,128)(2,1)S(1)} %get-tuple-element.312.refs_1_), channel_id=1, source_target_pairs={{0,2},{1,3},{2,0},{3,1},{4,6},{5,7},{6,4},{7,5},{8,10},{9,11},{10,... | collective-permute-start | bytes 3072008 | tf_op jit(solution)/shard_map/ppermute | solution.py:41
  589.6 22.4 %collective-permute-start.25 = (bf16[320,1600]{1,0:T(8,128)(2,1)S(1)}, bf16[320,1600]{1,0:T(8,128)(2,1)}, u32[]{:S(2)}, u32[]{:S(2)}) collective-permute-start(bf16[320,1600]{1,0:T(8,128)(2,1)S(1)} %get-tuple-element.312.refs_1_), channel_id=1, source_target_pairs={{0,1},{1,0},{2,3},{3,2},{4,5},{5,4},{6,7},{7,6},{8,9},{9,8},{10,11... | collective-permute-start | bytes 3072008 | tf_op jit(solution)/shard_map/ppermute | solution.py:41
  604.3 7.6 collective-permute-start.26
  606.7 42.9 %collective-permute-start.28 = (bf16[320,1600]{1,0:T(8,128)(2,1)S(1)}, bf16[320,1600]{1,0:T(8,128)(2,1)S(1)}, u32[]{:S(2)}, u32[]{:S(2)}) collective-permute-start(bf16[320,1600]{1,0:T(8,128)(2,1)S(1)} %get-tuple-element.158.refs_1_), channel_id=1, source_target_pairs={{0,1},{1,0},{2,3},{3,2},{4,5},{5,4},{6,7},{7,6},{8,9},{9,8},{10,11... | collective-permute-start | bytes 3072008 | tf_op jit(solution)/shard_map/ppermute | solution.py:41
  607.2 107.4 %collective-permute-start.31 = (bf16[320,1600]{1,0:T(8,128)(2,1)S(1)}, bf16[320,1600]{1,0:T(8,128)(2,1)}, u32[]{:S(2)}, u32[]{:S(2)}) collective-permute-start(bf16[320,1600]{1,0:T(8,128)(2,1)S(1)} %get-tuple-element.158.refs_1_), channel_id=1, source_target_pairs={{0,2},{1,3},{2,0},{3,1},{4,6},{5,7},{6,4},{7,5},{8,10},{9,11},{10,... | collective-permute-start | bytes 3072008 | tf_op jit(solution)/shard_map/ppermute | solution.py:41
  631.9 18.5 %collective-permute-start.27 = (bf16[896,400]{0,1:T(8,128)(2,1)}, bf16[896,400]{0,1:T(8,128)(2,1)}, u32[]{:S(2)}, u32[]{:S(2)}) collective-permute-start(bf16[896,400]{0,1:T(8,128)(2,1)} %copy.119), channel_id=1, source_target_pairs={{0,1},{1,0},{2,3},{3,2},{4,5},{5,4},{6,7},{7,6},{8,9},{9,8},{10,11... | collective-permute-start | bytes 2150408 | tf_op jit(solution)/shard_map/ppermute | solution.py:41
  638.8 123.6 %collective-permute-start.24 = (bf16[640,1600]{0,1:T(8,128)(2,1)}, bf16[640,1600]{0,1:T(8,128)(2,1)}, u32[]{:S(2)}, u32[]{:S(2)}) collective-permute-start(bf16[640,1600]{0,1:T(8,128)(2,1)} %copy.117), channel_id=1, source_target_pairs={{0,1},{1,0},{2,3},{3,2},{4,5},{5,4},{6,7},{7,6},{8,9},{9,8},{10,11... | collective-permute-start | bytes 6144008 | tf_op jit(solution)/shard_map/ppermute | solution.py:41
  646.9 67.7 %collective-permute-start.29 = (bf16[896,400]{0,1:T(8,128)(2,1)}, bf16[896,400]{0,1:T(8,128)(2,1)S(1)}, u32[]{:S(2)}, u32[]{:S(2)}) collective-permute-start(bf16[896,400]{0,1:T(8,128)(2,1)} %copy.120), channel_id=1, source_target_pairs={{0,2},{1,3},{2,0},{3,1},{4,6},{5,7},{6,4},{7,5},{8,10},{9,11},{10,... | collective-permute-start | bytes 2150408 | tf_op jit(solution)/shard_map/ppermute | solution.py:41
  649.6 65.0 %collective-permute-start.30 = (bf16[896,400]{0,1:T(8,128)(2,1)}, bf16[896,400]{0,1:T(8,128)(2,1)S(1)}, u32[]{:S(2)}, u32[]{:S(2)}) collective-permute-start(bf16[896,400]{0,1:T(8,128)(2,1)} %copy.121), channel_id=1, source_target_pairs={{0,3},{1,2},{2,1},{3,0},{4,7},{5,6},{6,5},{7,4},{8,11},{9,10},{10,... | collective-permute-start | bytes 2150408 | tf_op jit(solution)/shard_map/ppermute | solution.py:41
  741.6 4.2 collective-permute-start.32
  769.7 131.6 %collective-permute-start.36 = (bf16[320,1600]{1,0:T(8,128)(2,1)}, bf16[320,1600]{1,0:T(8,128)(2,1)}, u32[]{:S(2)}, u32[]{:S(2)}) collective-permute-start(bf16[320,1600]{1,0:T(8,128)(2,1)} %get-tuple-element.268), channel_id=1, source_target_pairs={{0,2},{1,3},{2,0},{3,1},{4,6},{5,7},{6,4},{7,5},{8,10},{9,11},{10,... | collective-permute-start | bytes 3072008 | tf_op jit(solution)/shard_map/ppermute | solution.py:41
  772.4 127.3 %collective-permute-start.33 = (bf16[640,400]{0,1:T(8,128)(2,1)}, bf16[640,400]{0,1:T(8,128)(2,1)S(1)}, u32[]{:S(2)}, u32[]{:S(2)}) collective-permute-start(bf16[640,400]{0,1:T(8,128)(2,1)} %copy.125), channel_id=1, source_target_pairs={{0,1},{1,0},{2,3},{3,2},{4,5},{5,4},{6,7},{7,6},{8,9},{9,8},{10,11... | collective-permute-start | bytes 1536008 | tf_op jit(solution)/shard_map/ppermute | solution.py:41
  774.5 126.8 %collective-permute-start.34 = (bf16[640,400]{0,1:T(8,128)(2,1)}, bf16[640,400]{0,1:T(8,128)(2,1)}, u32[]{:S(2)}, u32[]{:S(2)}) collective-permute-start(bf16[640,400]{0,1:T(8,128)(2,1)} %copy.126), channel_id=1, source_target_pairs={{0,2},{1,3},{2,0},{3,1},{4,6},{5,7},{6,4},{7,5},{8,10},{9,11},{10,... | collective-permute-start | bytes 1536008 | tf_op jit(solution)/shard_map/ppermute | solution.py:41
  777.0 124.3 %collective-permute-start.35 = (bf16[640,400]{0,1:T(8,128)(2,1)}, bf16[640,400]{0,1:T(8,128)(2,1)S(1)}, u32[]{:S(2)}, u32[]{:S(2)}) collective-permute-start(bf16[640,400]{0,1:T(8,128)(2,1)} %copy.127), channel_id=1, source_target_pairs={{0,3},{1,2},{2,1},{3,0},{4,7},{5,6},{6,5},{7,4},{8,11},{9,10},{10,... | collective-permute-start | bytes 1536008 | tf_op jit(solution)/shard_map/ppermute | solution.py:41
  892.8 135.9 %collective-permute-start.44 = (bf16[200,832]{1,0:T(8,128)(2,1)}, bf16[200,832]{1,0:T(8,128)(2,1)}, u32[]{:S(2)}, u32[]{:S(2)}) collective-permute-start(bf16[200,832]{1,0:T(8,128)(2,1)} %get-tuple-element.328), channel_id=1, source_target_pairs={{1,0},{2,1},{0,2},{5,4},{6,5},{4,6},{9,8},{10,9},{8,10},{13,12},{1... | collective-permute-start | bytes 998408 | tf_op jit(solution)/shard_map/ppermute | solution.py:434
  899.7 129.0 %collective-permute-start.45 = (bf16[200,832]{1,0:T(8,128)(2,1)}, bf16[200,832]{1,0:T(8,128)(2,1)}, u32[]{:S(2)}, u32[]{:S(2)}) collective-permute-start(bf16[200,832]{1,0:T(8,128)(2,1)} %get-tuple-element.329), channel_id=1, source_target_pairs={{3,1},{1,2},{2,3},{7,5},{5,6},{6,7},{11,9},{9,10},{10,11},{15,13},... | collective-permute-start | bytes 998408 | tf_op jit(solution)/shard_map/ppermute | solution.py:435
  931.1 25.3 %collective-permute-start.37 = (bf16[2,320,1600]{2,1,0:T(8,128)(2,1)}, bf16[2,320,1600]{2,1,0:T(8,128)(2,1)}, u32[]{:S(2)}, u32[]{:S(2)}) collective-permute-start(bf16[2,320,1600]{2,1,0:T(8,128)(2,1)} %dynamic-slice_bitcast_fusion), channel_id=1, source_target_pairs={{0,1},{1,0},{2,3},{3,2},{4,5},{5,4},{6,7},{7,6},{8,9},{9,8},{10,11... | collective-permute-start | bytes 6144008 | tf_op jit(solution)/shard_map/ppermute | solution.py:41
  1028.2 8.0 collective-permute-start.42
  1031.5 8.0 collective-permute-start.41
  1036.2 3.3 collective-permute-start.43
  1038.8 26.2 %collective-permute-start.38 = (bf16[320,1600]{1,0:T(8,128)(2,1)}, bf16[320,1600]{1,0:T(8,128)(2,1)}, u32[]{:S(2)}, u32[]{:S(2)}) collective-permute-start(bf16[320,1600]{1,0:T(8,128)(2,1)} %get-tuple-element.266), channel_id=1, source_target_pairs={{0,2},{1,3},{2,0},{3,1},{4,6},{5,7},{6,4},{7,5},{8,10},{9,11},{10,... | collective-permute-start | bytes 3072008 | tf_op jit(solution)/shard_map/ppermute | solution.py:41
  1067.9 4.1 collective-permute-start.40
  (126 other events, 1764.3 us)
Sparse Core Ops, SparseCore 0:
  231.5 75.3 all-gather.2
  330.6 135.8 all-gather.4
  537.2 109.4 reduce-scatter.6
  650.1 156.7 reduce-scatter.4

commit v5 on v4

--- a/solution.py
+++ b/solution.py
@@ -978,9 +978,84 @@
     return mm(w_bcdt, (shared | steps).astype(LOW)).astype(LOW)
 
 
+def rows_by_peer_kernel(mamba_ref, o_ref, *refs):
+    outs, held, load_sem, store_sem = refs[:SEQ], *refs[SEQ:]
+    me = lax.axis_index("seq")
+    shared = (KV_HEADS - 1) * QW
+
+    def loads(p):
+        own = HEAD_COUNT[p] * SSM_HEAD
+        parts = [
+            (mamba_ref, FIRST_HEAD[p] * SSM_HEAD, OUT_AT, own),
+            (o_ref, p * QW, O_AT, QW),
+            (o_ref, shared, O5_AT, QW),
+        ]
+        return [
+            pltpu.make_async_copy(
+                source.at[pl.ds(at, count)], held.at[p, pl.ds(to, count)], load_sem.at[p, k]
+            )
+            for k, (source, at, to, count) in enumerate(parts)
+        ]
+
+    for p in range(SEQ):
+        for load in loads(p):
+            load.start()
+        for start, end in ((HEAD_COUNT[p] * SSM_HEAD, O_AT), (O_AT + QW, O5_AT)):
+            held[p, start:end] = jnp.zeros((end - start, held.shape[2]), held.dtype)
+
+    def stores(act):
+        for p in range(SEQ):
+            if act == "start":
+                for load in loads(p):
+                    load.wait()
+            for k in range(SEQ):
+                copy = pltpu.make_async_copy(held.at[p], outs[k], store_sem.at[p])
+                pl.when(jnp.bitwise_xor(me, p) == k)(copy.start if act == "start" else copy.wait)
+
+    stores("start")
+    stores("wait")
+
+
+def rows_by_peer(mamba_cols, o_cols):
+    block = (OUT_WIDTH, o_cols.shape[1])
+    anywhere = pl.BlockSpec(memory_space=pl.ANY)
+    return pl.pallas_call(
+        rows_by_peer_kernel,
+        in_specs=[anywhere] * 2,
+        out_specs=[anywhere] * SEQ,
+        out_shape=[jax.ShapeDtypeStruct(block, LOW)] * SEQ,
+        scratch_shapes=[
+            pltpu.VMEM((SEQ,) + block, LOW),
+            pltpu.SemaphoreType.DMA((SEQ, 3)),
+            pltpu.SemaphoreType.DMA((SEQ,)),
+        ],
+        compiler_params=pltpu.CompilerParams(vmem_limit_bytes=32 << 20),
+        cost_estimate=pl.CostEstimate(flops=0, bytes_accessed=12 << 20, transcendentals=0),
+    )(mamba_cols, o_cols)
+
+
+def wide_kernel(*refs):
+    pieces, out = refs[:SEQ], refs[SEQ]
+    me, width = lax.axis_index("seq"), pieces[0].shape[1]
+    for j in range(SEQ):
+        for k in range(SEQ):
+
+            @pl.when(jnp.bitwise_xor(me, j) == k)
+            def _():
+                out[:, width * j : width * (j + 1)] = pieces[k][...]
+
+
 def wide_of(arrivals):
-    me = lax.axis_index("seq")
-    return jnp.concatenate([pick(arrivals, me ^ j) for j in range(SEQ)], axis=1)
+    rows, width = arrivals[0].shape
+    block = rows if rows < 400 else 400
+    return pl.pallas_call(
+        wide_kernel,
+        grid=(rows // block,),
+        in_specs=[pl.BlockSpec((block, width), lambda i: (i, 0))] * SEQ,
+        out_specs=pl.BlockSpec((block, SEQ * width), lambda i: (i, 0)),
+        out_shape=jax.ShapeDtypeStruct((rows, SEQ * width), arrivals[0].dtype),
+        cost_estimate=pl.CostEstimate(flops=0, bytes_accessed=16 * rows * width, transcendentals=0),
+    )(*arrivals)
 
 
 def on_device(
@@ -1019,16 +1094,17 @@
         ]
     )
     out_block = w_out.shape[0]
-    out_packet = jnp.concatenate([w_o, w_out], axis=0)
-    qkv_shards = seq_arrivals(w_qkv)
+    qkv_far, qkv_near = swap(w_qkv, "seq", 2), swap(w_qkv, "seq", 1)
     x_part, z_part = trade_halves(
         w_xz[:, :LOCAL_CH], jnp.pad(w_xz[:, LOCAL_CH:], ((0, 0), (0, 2 * LOCAL_CH - w_xz.shape[1])))
     )
-    token_blocks = seq_arrivals(tokens_in)
-    small, out_cols = gather_dp([small, out_packet], 0)
-    small, out_cols, qkv_shards, x_part, z_part, token_blocks = lax.optimization_barrier(
-        (small, out_cols, qkv_shards, x_part, z_part, token_blocks)
-    )
+    tokens_far, tokens_near = swap(tokens_in, "seq", 2), swap(tokens_in, "seq", 1)
+    small, o_cols, mamba_cols = gather_dp([small, w_o, w_out], 0)
+    small, o_cols, mamba_cols, qkv_far, qkv_near, x_part, z_part, tokens_far, tokens_near = lax.optimization_barrier(
+        (small, o_cols, mamba_cols, qkv_far, qkv_near, x_part, z_part, tokens_far, tokens_near)
+    )
+    qkv_shards = [w_qkv, qkv_near, qkv_far, swap(qkv_far, "seq", 1)]
+    token_blocks = [tokens_in, tokens_near, tokens_far, swap(tokens_far, "seq", 1)]
     full_conv = small[:, :4, :conv_block].transpose(1, 0, 2).reshape(4, INNER).astype(FULL)
     gains = small[:, 8:12, :gains_block].transpose(1, 0, 2).reshape(4, D).astype(FULL)
     tokens_group = place(list(zip(seq_order(), token_blocks))).reshape(group, D)
@@ -1047,8 +1123,10 @@
     d_total = cotangent.astype(FULL) * live
     d_ffn = d_total.astype(LOW)
     d_ffn_far, d_ffn_near = swap(d_ffn, "seq", 2), swap(d_ffn, "seq", 1)
-    full_qkv, full_xz, out_cols, gate_up_packet, down_packet, d_ffn_far, d_ffn_near = lax.optimization_barrier(
-        (full_qkv, full_xz, out_cols, gate_up_packet, down_packet, d_ffn_far, d_ffn_near)
+    full_qkv, full_xz, o_cols, mamba_cols, gate_up_packet, down_packet, d_ffn_far, d_ffn_near = (
+        lax.optimization_barrier(
+            (full_qkv, full_xz, o_cols, mamba_cols, gate_up_packet, down_packet, d_ffn_far, d_ffn_near)
+        )
     )
     d_ffn_group = jnp.concatenate([d_ffn, d_ffn_near, d_ffn_far, swap(d_ffn_far, "seq", 1)])
     full_qkv = full_qkv.reshape(D, -1)
@@ -1063,20 +1141,11 @@
     q_last = mm(normed_own, full_qkv[:, 256 + QW :]).astype(LOW)
     queries = jnp.concatenate([kvq[:, 256:], q_last])
     kv = kvq[:, :256]
+    out_blocks = list(rows_by_peer(mamba_cols.reshape(INNER, -1), o_cols.reshape(D, -1)))
+    out_blocks, queries = meet(out_blocks, queries)
     attended, logs = attention_forward(doc_lengths, queries, kv, rows)
-    o_cols = out_cols[:, :block_rows].reshape(D, -1)
-    mamba_cols = out_cols[:, block_rows:].reshape(INNER, -1)
-
-    def rows_for(peer):
-        cut = channel_cut(mamba_cols, peer, 0)
-        heads = lax.dynamic_slice_in_dim(o_cols, peer * QW, QW, 0)
-        spare = lambda n: jnp.zeros((n, cut.shape[1]), LOW)
-        return jnp.concatenate(
-            [cut, spare(O_AT - LOCAL_CH), heads, spare(O5_AT - O_AT - QW), o_cols[(KV_HEADS - 1) * QW :]]
-        )
-
-    out_pieces = [rows_for(s)] + [swap(rows_for(s ^ bit), "seq", bit) for bit in (1, 2, 3)]
-    out_rows = lax.optimization_barrier(wide_of(after(out_pieces, attended)))
+    out_pieces = out_blocks[:1] + [swap(out_blocks[bit], "seq", bit) for bit in (1, 2, 3)]
+    out_rows = wide_of(after(out_pieces, attended))
     w_out_rows = out_rows[:WIDE]
     w_o_rows = out_rows[O_AT : O_AT + QW]
     w_o5_rows = out_rows[O5_AT:]

time: 1100 us -> 1060 us (0.964)
  local copies, waits for them, and re-layouts: 164 us -> 144 us
  other arithmetic: 99.4 us -> 81.9 us
  Pallas kernels: 468 us -> 479 us
    concatenate x5 -> x0, local copies, waits for them, and re-layouts: 14.9 us -> none  [the longest x4 12.6 us: rows_for(): jnp.concatenate([cut, spare(O_AT - LOCAL_CH), heads, spare(O5_AT - O_AT -...]
    select_n x15 -> x11, other arithmetic: 24.4 us -> 12.1 us  [pick(): return lax.select_n(seq_index, *options)]
    pallas_call x0 -> x3, Pallas kernels: none -> 11.8 us  [the longest x2 9.59 us: wide_of(): pl.pallas_call(wide_kernel, grid=(rows // block,), in_specs=[pl.BlockSpec...]
    unnamed x261 -> x252, local copies, waits for them, and re-layouts: 59.3 us -> 52.1 us
    optimization_barrier x14 -> x17, local copies, waits for them, and re-layouts: 26 us -> 32.7 us  [meet(): return lax.optimization_barrier((one, two))]
  transfers between devices with their start and end apart: 50 -> 50, of which waited for: 12 -> 11; matrix products, arithmetic and copies ran while one was open for 33% -> 30% of each run, Pallas kernels for 43% -> 45%
where the time goes in v5:
time: 1060 us
  Pallas kernels  479 us (45%)
  matrix products  198 us (19%)
  local copies, waits for them, and re-layouts  144 us (14%)
  waiting for transfers between devices  93.6 us (9%)
  other arithmetic  81.9 us (8%)
  starting transfers between devices  41.3 us (4%)
  between operations  17.1 us (2%)
    pallas_call x2, Pallas kernels, gather_dp(): pl.pallas_call(lambda *refs: gather_kernel(pieces, line, *refs), out_shap...  161 us
    pallas_call x1, Pallas kernels, attention_backward(): pl.pallas_call(kernel, grid=(SEQ + 1, GROUP_HEADS), in_specs=[pl.BlockSpe...  113 us
    ppermute x42, waiting for transfers between devices, swap(): lax.ppermute(value, axis, [(i, i ^ bit) for i in range(lax.axis_size(axis...  93.5 us
    dot_general x8, matrix products, mm_nt(): lax.dot_general(left, right, (((1,), (1,)), ((), ())), preferred_element_...  69.6 us
    dot_general x9, matrix products, mm(): return jnp.dot(left, right, preferred_element_type=FULL)  66.3 us
    pallas_call x1, Pallas kernels, scatter_dp(): pl.pallas_call(lambda *refs: scatter_kernel(pieces, line, *refs), out_sha...  65.6 us
    dot_general x8, matrix products, mm_tn(): lax.dot_general(left, right, (((0,), (0,)), ((), ())), preferred_element_...  62.4 us
    pallas_call x1, Pallas kernels, mamba_backward(): pl.pallas_call(mamba_backward_kernel, grid=(chunks,), in_specs=mamba_spec...  54.6 us
  transfers between devices with their start and end apart: 50, of which 11 were waited for; matrix products, arithmetic and copies ran while one was open for 30% of the time, Pallas kernels for 45%

profile of v5, /device:TPU:0, one launch (start us, length us, event | category | flops | bytes accessed | tf_op | source)
XLA Modules:
  0.0 1055.3 jit_solution(10765287601555828188)
XLA Ops:
  27.0 64.0 %shard_map.237 = (bf16[8,16,512]{2,1,0:T(8,128)(2,1)S(1)}, bf16[8,200,400]{2,1,0:T(8,128)(2,1)S(1)}, bf16[8,400,400]{2,1,0:T(8,128)(2,1)S(1)}) custom-call(bf16[16,512]{1,0:T(8,128)(2,1)S(1)} %fusion.61.refs_0_, bf16[200,400]{1,0:T(8,128)(2,1)S(1)} %copy-done.24, bf16[400,400]{1,0:T(8,128)(2,1)S(1)} %copy-done.23), custom_call_target="tpu_custom_call" | custom-call | bytes 7942144 | tf_op jit(solution)/shard_map/pallas_call | solution.py:259
  103.9 96.9 %shard_map.241 = (bf16[8,200,896]{2,1,0:T(8,128)(2,1)S(1)}, bf16[8,200,1792]{2,1,0:T(8,128)(2,1)S(1)}) custom-call(bf16[200,896]{1,0:T(8,128)(2,1)S(1)} %concatenate.68.refs_0_, bf16[200,1792]{1,0:T(8,128)(2,1)S(1)} %concatenate.69.refs_1_), custom_call_target="tpu_custom_call" | custom-call | bytes 17203200 | tf_op jit(solution)/shard_map/pallas_call | solution.py:259
  221.4 5.5 shard_map.239
  226.9 6.6 convolution_convert_fusion.9
  240.3 3.7 copy.100
  249.9 35.7 %shard_map.243 = (bf16[1600,320]{1,0:T(8,128)(2,1)S(1)}, f32[1600,128]{1,0:T(8,128)S(1)}) custom-call(s32[1,2]{1,0:T(1,128)S(1)} %copy-done.31, bf16[1600,320]{1,0:T(8,128)(2,1)S(1)} %copy-done.16, bf16[1280,256]{1,0:T(8,128)(2,1)S(1)} %slice.458.kv_ref.refs_2_), custom_call_target="tpu_custom_call" | custom-call | flops 40000000000 | bytes 4194304 | tf_op jit(solution)/shard_map/pallas_call | solution.py:887
  286.5 17.5 %collective-permute-done.12 = bf16[1600,400]{0,1:T(8,128)(2,1)} collective-permute-done((bf16[1600,400]{0,1:T(8,128)(2,1)}, bf16[1600,400]{0,1:T(8,128)(2,1)}, u32[]{:S(2)}, u32[]{:S(2)}) %collective-permute-start.12) | collective-permute-done | bytes 1280032 | tf_op jit(solution)/shard_map/ppermute | solution.py:41
  307.5 3.5 copy.103.refs_2_
  314.4 6.8 shard_map.244
  321.2 3.7 convolution_convert_fusion.6
  325.8 11.9 %fusion.88.xzb_ref.tail_ref = f32[1280,1792]{1,0:T(8,128)S(1)} fusion(bf16[1280,1600]{1,0:T(8,128)(2,1)} %shard_map.239, bf16[1600,1792]{1,0:T(8,128)(2,1)} %bitcast.186), kind=kOutput, calls=%fused_computation.269 | convolution fusion | flops 7340032000 | bytes 19005440 | tf_op jit(solution)/shard_map/dot_general | solution.py:440
  341.3 18.3 %shard_map.245 = (bf16[1280,896]{1,0:T(8,128)(2,1)S(1)}, bf16[1280,896]{1,0:T(8,128)(2,1)S(1)}, f32[10,16,896]{2,1,0:T(8,128)S(1)}) custom-call(s32[1,2]{1,0:T(1,128)S(1)} %copy-done.31, f32[1280,1792]{1,0:T(8,128)S(1)} %fusion.88.xzb_ref.tail_ref, f32[1280,1792]{1,0:T(8,128)S(1)} %fusion.88.xzb_ref.tail_ref, f32[8,896]{1,0:T(8,128)S(1)} %pad.126.conv_ref, ...), custom_call_target="tpu_custom_call" | custom-call | flops 20000000000 | bytes 16777216 | tf_op jit(solution)/shard_map/pallas_call | solution.py:734
  359.7 3.6 copy-done.36
  366.0 5.4 convolution_convert_fusion.5
  371.8 4.2 collective-permute-done.15
  382.9 20.6 %collective-permute-done.16 = bf16[320,1600]{1,0:T(8,128)(2,1)} collective-permute-done((bf16[320,1600]{1,0:T(8,128)(2,1)}, bf16[320,1600]{1,0:T(8,128)(2,1)}, u32[]{:S(2)}, u32[]{:S(2)}) %collective-permute-start.16) | collective-permute-done | bytes 1024032 | tf_op jit(solution)/shard_map/ppermute | solution.py:41
  410.4 13.2 %fusion.36 = f32[1280,1408]{1,0:T(8,128)} fusion(bf16[1600,1408]{1,0:T(8,128)(2,1)} %all-gather.3.cloned.1.call-done, bf16[320,1600]{1,0:T(8,128)(2,1)} %collective-permute-done.18, bf16[320,1600]{1,0:T(8,128)(2,1)} %collective-permute-done.8, bf16[320,1600]{1,0:T(8,128)(2,1)} %collective-permute-done.9, bf16[320,1600]{1,0:T(8,128)(2,1)} %fusion.16), kind=kOutput, calls=%fused_computation.123 | convolution fusion | flops 5783552000 | bytes 15810560 | tf_op jit(solution)/shard_map/dot_general | solution.py:440
  423.5 9.8 collective-permute-done.17
  436.2 19.3 %fusion.35 = f32[1280,2816]{1,0:T(8,128)S(1)} fusion(bf16[1600,2816]{1,0:T(8,128)(2,1)} %all-gather.5.cloned.1.call-done, bf16[320,1600]{1,0:T(8,128)(2,1)} %collective-permute-done.20, bf16[320,1600]{1,0:T(8,128)(2,1)} %copy-done.108, bf16[320,1600]{1,0:T(8,128)(2,1)} %copy-done.110, bf16[320,1600]{1,0:T(8,128)(2,1)S(1)} %multiply_convert_fusion.4), kind=kOutput, calls=%fused_computation.122 | convolution fusion | flops 11550720000 | bytes 27525120 | tf_op jit(solution)/shard_map/dot_general | solution.py:440
  455.6 8.7 multiply_convert_fusion.2
  464.3 18.0 %convolution_convert_fusion.4 = bf16[1280,1600]{1,0:T(8,128)(2,1)S(1)} fusion(bf16[1600,2816]{1,0:T(8,128)(2,1)} %all-gather.5.cloned.1.call-done, bf16[1280,1408]{1,0:T(8,128)(2,1)} %get-tuple-element.276, bf16[1280,1408]{1,0:T(8,128)(2,1)} %get-tuple-element.275), kind=kOutput, calls=%fused_computation.8 | convolution fusion | flops 11550801920 | bytes 20316160 | tf_op jit(solution)/shard_map/dot_general | solution.py:444
  487.3 12.1 %convolution_convert_fusion.3 = bf16[1600,1408]{1,0:T(8,128)(2,1)} fusion(bf16[1280,1408]{1,0:T(8,128)(2,1)} %get-tuple-element.277, bf16[320,1600]{1,0:T(8,128)(2,1)} %collective-permute-done.18, bf16[320,1600]{1,0:T(8,128)(2,1)} %collective-permute-done.8, bf16[320,1600]{1,0:T(8,128)(2,1)} %collective-permute-done.9, bf16[320,1600]{1,0:T(8,128)(2,1)} %fusion.16), kind=kOutput, calls=%fused_computation.7 | convolution fusion | flops 5785804800 | bytes 12206080 | tf_op jit(solution)/shard_map/dot_general | solution.py:448
  509.8 18.1 %convolution_convert_fusion = bf16[1600,2816]{1,0:T(8,128)(2,1)} fusion(bf16[1280,1408]{1,0:T(8,128)(2,1)} %get-tuple-element.276, bf16[1280,1408]{1,0:T(8,128)(2,1)} %get-tuple-element.275, bf16[320,1600]{1,0:T(8,128)(2,1)} %collective-permute-done.20, bf16[320,1600]{1,0:T(8,128)(2,1)S(1)} %copy-done.109, bf16[320,1600]{1,0:T(8,128)(2,1)} %copy-done.110, ...), kind=kOutput, calls=%fused_computation | convolution fusion | flops 11569643520 | bytes 20316160 | tf_op jit(solution)/shard_map/dot_general | solution.py:448
  528.0 6.3 collective-permute-done.22
  537.4 4.2 multiply_reduce_fusion.4
  544.7 9.2 convolution_convert_fusion.2
  553.9 14.3 %collective-permute-done.23.refs_3_ = bf16[320,1600]{1,0:T(8,128)(2,1)} collective-permute-done((bf16[320,1600]{1,0:T(8,128)(2,1)S(1)}, bf16[320,1600]{1,0:T(8,128)(2,1)}, u32[]{:S(2)}, u32[]{:S(2)}) %collective-permute-start.23) | collective-permute-done | bytes 1024032 | tf_op jit(solution)/shard_map/ppermute | solution.py:41
  578.5 6.3 convolution_convert_fusion.7.d_gated_ref
  584.9 4.5 convolution_convert_fusion.8
  598.7 4.1 copy.111
  614.3 3.6 copy-done.37
  621.6 54.6 %shard_map.247 = (bf16[1280,1792]{1,0:T(8,128)(2,1)S(1)}, f32[8,896]{1,0:T(8,128)S(1)}, f32[8,128]{1,0:T(8,128)S(1)}) custom-call(s32[1,2]{1,0:T(1,128)S(1)} %copy-done.31, f32[1280,1792]{1,0:T(8,128)S(1)} %copy-done.37, f32[1280,1792]{1,0:T(8,128)S(1)} %copy-done.37, f32[8,896]{1,0:T(8,128)S(1)} %pad.126.conv_ref, f32[8,128]{1,0:T(8,128)S(1)} %broadcast_in_dim.19.rate_ref, ...), custom_call_target="tpu_custom_call" | custom-call | flops 60000002048 | bytes 25165824 | tf_op jit(solution)/shard_map/pallas_call | solution.py:755
  692.5 13.8 %convolution_convert_fusion.1 = bf16[1600,1792]{1,0:T(8,128)(2,1)} fusion(bf16[1280,1600]{1,0:T(8,128)(2,1)} %shard_map.239, bf16[1280,1792]{1,0:T(8,128)(2,1)} %copy-done.35), kind=kOutput, calls=%fused_computation.5 | convolution fusion | flops 7342899200 | bytes 14417920 | tf_op jit(solution)/shard_map/dot_general | solution.py:448
  715.0 3.9 convolution_convert_fusion.13
  720.7 4.0 convolution_convert_fusion.14
  732.6 3.8 add_convert_fusion
  743.2 112.7 %shard_map.250 = (bf16[1600,320]{1,0:T(8,128)(2,1)}, bf16[1280,256]{1,0:T(8,128)(2,1)}, f32[200,1792]{1,0:T(8,128)}, f32[400,400]{1,0:T(8,128)}) custom-call(s32[1,2]{1,0:T(1,128)} %refs_0_.3, bf16[1600,320]{1,0:T(8,128)(2,1)} %pad_maximum_fusion.10.q_ref.refs_1_, bf16[1280,256]{1,0:T(8,128)(2,1)} %copy-done.21, bf16[1600,320]{1,0:T(8,128)(2,1)} %copy-done.25, ...), custom_call_target="tpu_custom_call" | custom-call | flops 99999997952 | bytes 8388608 | tf_op jit(solution)/shard_map/pallas_call | solution.py:925
  858.5 6.9 collective-permute-start.44
  869.1 8.9 fusion.17
  878.0 16.3 %multiply_reduce_fusion = (f32[1600]{0:T(1024)S(1)}, bf16[1280,1600]{1,0:T(8,128)(2,1)}, f32[1280,1600]{1,0:T(8,128)}) fusion(f32[1280]{0:T(1024)S(1)} %copy-done.103, bf16[4,320,1600]{2,1,0:T(8,128)(2,1)S(1)} %bitcast.175, f32[1280,1600]{1,0:T(8,128)} %fusion.17, bf16[1280,1792]{1,0:T(8,128)(2,1)} %copy-done.35, bf16[1600,1792]{1,0:T(8,128)(2,1)} %bitcast.187), kind=kOutput, calls=%fused_computation.2 | convolution fusion | flops 7352318464 | bytes 34909440 | tf_op jit(solution)/shard_map/dot_general | solution.py:444
  898.1 4.3 multiply_reduce_fusion.2
  902.4 5.1 convolution_convert_fusion.10
  911.8 5.4 copy.131
  922.5 4.9 fusion.12
  927.4 65.6 %shard_map.252 = (f32[200,896]{1,0:T(8,128)}, f32[200,400]{1,0:T(8,128)}, f32[16,512]{1,0:T(8,128)}) custom-call(bf16[8,200,896]{2,1,0:T(8,128)(2,1)} %bitcast.188, bf16[8,200,400]{2,1,0:T(8,128)(2,1)} %bitcast.203, f32[8,16,512]{2,1,0:T(8,128)} %fusion.45.refs_2_), custom_call_target="tpu_custom_call" | custom-call | bytes 4278272 | tf_op jit(solution)/shard_map/pallas_call | solution.py:401
  997.7 4.7 collective-permute-done.42.refs_3_
  1012.8 4.0 concatenate.85
  1018.9 12.3 %collective-permute-done.38 = bf16[320,1600]{1,0:T(8,128)(2,1)} collective-permute-done((bf16[320,1600]{1,0:T(8,128)(2,1)}, bf16[320,1600]{1,0:T(8,128)(2,1)}, u32[]{:S(2)}, u32[]{:S(2)}) %collective-permute-start.38) | collective-permute-done | bytes 1024032 | tf_op jit(solution)/shard_map/ppermute | solution.py:41
  (521 shorter events, 247.2 us)
Async XLA Ops:
  7.2 403.1 %all-gather.3.cloned.1.call-start = ((), (), s32[]{:S(2)}) async-start(), calls=%async_computation.2 | async-start | bytes 5068800 | tf_op jit(solution)/shard_map/all_gather | solution.py:417
  7.3 88.7 %collective-permute-start.4 = (bf16[320,1600]{1,0:T(8,128)(2,1)}, bf16[320,1600]{1,0:T(8,128)(2,1)S(1)}, u32[]{:S(2)}, u32[]{:S(2)}) collective-permute-start(bf16[320,1600]{1,0:T(8,128)(2,1)} %refs_1_.3), channel_id=1, source_target_pairs={{0,2},{1,3},{2,0},{3,1},{4,6},{5,7},{6,4},{7,5},{8,10},{9,11},{10,... | collective-permute-start | bytes 3072008 | tf_op jit(solution)/shard_map/ppermute | solution.py:41
  10.3 85.7 %collective-permute-start.5 = (bf16[320,1600]{1,0:T(8,128)(2,1)}, bf16[320,1600]{1,0:T(8,128)(2,1)}, u32[]{:S(2)}, u32[]{:S(2)}) collective-permute-start(bf16[320,1600]{1,0:T(8,128)(2,1)} %refs_1_.3), channel_id=1, source_target_pairs={{0,1},{1,0},{2,3},{3,2},{4,5},{5,4},{6,7},{7,6},{8,9},{9,8},{10,11... | collective-permute-start | bytes 3072008 | tf_op jit(solution)/shard_map/ppermute | solution.py:41
  14.1 78.7 %collective-permute-start.2 = (bf16[200,832]{1,0:T(8,128)(2,1)}, bf16[200,832]{1,0:T(8,128)(2,1)}, u32[]{:S(2)}, u32[]{:S(2)}) collective-permute-start(bf16[200,832]{1,0:T(8,128)(2,1)} %get-tuple-element.319), channel_id=1, source_target_pairs={{0,1},{1,2},{2,0},{4,5},{5,6},{6,4},{8,9},{9,10},{10,8},{12,13},{1... | collective-permute-start | bytes 998408 | tf_op jit(solution)/shard_map/ppermute | solution.py:427
  16.5 76.4 %collective-permute-start.3 = (bf16[200,832]{1,0:T(8,128)(2,1)}, bf16[200,832]{1,0:T(8,128)(2,1)}, u32[]{:S(2)}, u32[]{:S(2)}) collective-permute-start(bf16[200,832]{1,0:T(8,128)(2,1)} %get-tuple-element.318), channel_id=1, source_target_pairs={{1,3},{2,1},{3,2},{5,7},{6,5},{7,6},{9,11},{10,9},{11,10},{13,15},... | collective-permute-start | bytes 998408 | tf_op jit(solution)/shard_map/ppermute | solution.py:428
  18.0 74.7 %collective-permute-start = (bf16[200,560]{1,0:T(8,128)(2,1)}, bf16[200,560]{1,0:T(8,128)(2,1)}, u32[]{:S(2)}, u32[]{:S(2)}) collective-permute-start(bf16[200,560]{1,0:T(8,128)(2,1)} %refs_0_.2), channel_id=1, source_target_pairs={{0,2},{1,3},{2,0},{3,1},{4,6},{5,7},{6,4},{7,5},{8,10},{9,11},{10,... | collective-permute-start | bytes 672008 | tf_op jit(solution)/shard_map/ppermute | solution.py:41
  92.7 112.1 %collective-permute-start.8 = (bf16[320,1600]{1,0:T(8,128)(2,1)}, bf16[320,1600]{1,0:T(8,128)(2,1)}, u32[]{:S(2)}, u32[]{:S(2)}) collective-permute-start(bf16[320,1600]{1,0:T(8,128)(2,1)} %fusion.16), channel_id=1, source_target_pairs={{0,2},{1,3},{2,0},{3,1},{4,6},{5,7},{6,4},{7,5},{8,10},{9,11},{10,... | collective-permute-start | bytes 3072008 | tf_op jit(solution)/shard_map/ppermute | solution.py:41
  92.8 112.0 %collective-permute-start.9 = (bf16[320,1600]{1,0:T(8,128)(2,1)}, bf16[320,1600]{1,0:T(8,128)(2,1)}, u32[]{:S(2)}, u32[]{:S(2)}) collective-permute-start(bf16[320,1600]{1,0:T(8,128)(2,1)} %fusion.16), channel_id=1, source_target_pairs={{0,1},{1,0},{2,3},{3,2},{4,5},{5,4},{6,7},{7,6},{8,9},{9,8},{10,11... | collective-permute-start | bytes 3072008 | tf_op jit(solution)/shard_map/ppermute | solution.py:41
  92.9 3.1 collective-permute-start.1
  204.8 231.4 %all-gather.5.cloned.1.call-start = ((), (), s32[]{:S(2)}) async-start(), calls=%async_computation.3 | async-start | bytes 10137600 | tf_op jit(solution)/shard_map/all_gather | solution.py:417
  205.2 9.9 collective-permute-start.6
  214.9 825.1 %reduce-scatter.7.cloned.1.call-start = ((), (), s32[]{:S(2)}) async-start(), calls=%async_computation.5 | async-start | bytes 5068800
  239.9 46.7 %collective-permute-start.10 = (bf16[1600,400]{0,1:T(8,128)(2,1)}, bf16[1600,400]{0,1:T(8,128)(2,1)}, u32[]{:S(2)}, u32[]{:S(2)}) collective-permute-start(bf16[1600,400]{0,1:T(8,128)(2,1)} %copy.99), channel_id=1, source_target_pairs={{0,1},{1,0},{2,3},{3,2},{4,5},{5,4},{6,7},{7,6},{8,9},{9,8},{10,11... | collective-permute-start | bytes 3840008 | tf_op jit(solution)/shard_map/ppermute | solution.py:41
  244.1 42.5 %collective-permute-start.11 = (bf16[1600,400]{0,1:T(8,128)(2,1)}, bf16[1600,400]{0,1:T(8,128)(2,1)}, u32[]{:S(2)}, u32[]{:S(2)}) collective-permute-start(bf16[1600,400]{0,1:T(8,128)(2,1)} %copy.100), channel_id=1, source_target_pairs={{0,2},{1,3},{2,0},{3,1},{4,6},{5,7},{6,4},{7,5},{8,10},{9,11},{10,... | collective-permute-start | bytes 3840008 | tf_op jit(solution)/shard_map/ppermute | solution.py:41
  248.6 55.4 %collective-permute-start.12 = (bf16[1600,400]{0,1:T(8,128)(2,1)}, bf16[1600,400]{0,1:T(8,128)(2,1)}, u32[]{:S(2)}, u32[]{:S(2)}) collective-permute-start(bf16[1600,400]{0,1:T(8,128)(2,1)} %copy.101), channel_id=1, source_target_pairs={{0,3},{1,2},{2,1},{3,0},{4,7},{5,6},{6,5},{7,4},{8,11},{9,10},{10,... | collective-permute-start | bytes 3840008 | tf_op jit(solution)/shard_map/ppermute | solution.py:41
  325.1 12.6 %collective-permute-start.13 = (bf16[2,320,1600]{2,1,0:T(8,128)(2,1)S(1)}, bf16[2,320,1600]{2,1,0:T(8,128)(2,1)S(1)}, u32[]{:S(2)}, u32[]{:S(2)}) collective-permute-start(bf16[2,320,1600]{2,1,0:T(8,128)(2,1)S(1)} %dynamic-slice_bitcast_fusion.2), channel_id=1, source_target_pairs={{0,1},{1,0},{2,3},{3,2},{4,5},{5,4},{6,7},{7,6},{8,9},{9,8},{10,11... | collective-permute-start | bytes 6144008 | tf_op jit(solution)/shard_map/ppermute | solution.py:41
  339.6 25.4 %collective-permute-start.14 = (bf16[320,1600]{1,0:T(8,128)(2,1)S(1)}, bf16[320,1600]{1,0:T(8,128)(2,1)S(1)}, u32[]{:S(2)}, u32[]{:S(2)}) collective-permute-start(bf16[320,1600]{1,0:T(8,128)(2,1)S(1)} %get-tuple-element.284), channel_id=1, source_target_pairs={{0,2},{1,3},{2,0},{3,1},{4,6},{5,7},{6,4},{7,5},{8,10},{9,11},{10,... | collective-permute-start | bytes 3072008 | tf_op jit(solution)/shard_map/ppermute | solution.py:41
  371.7 4.3 collective-permute-start.15
  377.6 25.9 %collective-permute-start.16 = (bf16[320,1600]{1,0:T(8,128)(2,1)}, bf16[320,1600]{1,0:T(8,128)(2,1)}, u32[]{:S(2)}, u32[]{:S(2)}) collective-permute-start(bf16[320,1600]{1,0:T(8,128)(2,1)} %fusion.13), channel_id=1, source_target_pairs={{0,2},{1,3},{2,0},{3,1},{4,6},{5,7},{6,4},{7,5},{8,10},{9,11},{10,... | collective-permute-start | bytes 3072008 | tf_op jit(solution)/shard_map/ppermute | solution.py:41
  379.6 30.7 %collective-permute-start.18 = (bf16[320,1600]{1,0:T(8,128)(2,1)}, bf16[320,1600]{1,0:T(8,128)(2,1)}, u32[]{:S(2)}, u32[]{:S(2)}) collective-permute-start(bf16[320,1600]{1,0:T(8,128)(2,1)} %collective-permute-done.8), channel_id=1, source_target_pairs={{0,1},{1,0},{2,3},{3,2},{4,5},{5,4},{6,7},{7,6},{8,9},{9,8},{10,11... | collective-permute-start | bytes 3072008 | tf_op jit(solution)/shard_map/ppermute | solution.py:41
  408.6 24.8 %collective-permute-start.17 = (bf16[320,1600]{1,0:T(8,128)(2,1)S(1)}, bf16[320,1600]{1,0:T(8,128)(2,1)S(1)}, u32[]{:S(2)}, u32[]{:S(2)}) collective-permute-start(bf16[320,1600]{1,0:T(8,128)(2,1)S(1)} %multiply_convert_fusion.4), channel_id=1, source_target_pairs={{0,2},{1,3},{2,0},{3,1},{4,6},{5,7},{6,4},{7,5},{8,10},{9,11},{10,... | collective-permute-start | bytes 3072008 | tf_op jit(solution)/shard_map/ppermute | solution.py:41
  423.5 9.9 collective-permute-start.19
  487.1 12.3 %collective-permute-start.21 = (bf16[640,1600]{0,1:T(8,128)(2,1)}, bf16[640,1600]{0,1:T(8,128)(2,1)S(1)}, u32[]{:S(2)}, u32[]{:S(2)}) collective-permute-start(bf16[640,1600]{0,1:T(8,128)(2,1)} %copy.107), channel_id=1, source_target_pairs={{0,1},{1,0},{2,3},{3,2},{4,5},{5,4},{6,7},{7,6},{8,9},{9,8},{10,11... | collective-permute-start | bytes 6144008 | tf_op jit(solution)/shard_map/ppermute | solution.py:41
  500.8 541.3 %reduce-scatter.5.cloned.1.call-start = ((), (), s32[]{:S(2)}) async-start(), calls=%async_computation.4 | async-start | bytes 10137600 | tf_op jit(solution)/shard_map/reduce_scatter | solution.py:421
  508.1 26.1 %collective-permute-start.22 = (bf16[320,1600]{1,0:T(8,128)(2,1)}, bf16[320,1600]{1,0:T(8,128)(2,1)}, u32[]{:S(2)}, u32[]{:S(2)}) collective-permute-start(bf16[320,1600]{1,0:T(8,128)(2,1)} %add_convert_fusion.1), channel_id=1, source_target_pairs={{0,2},{1,3},{2,0},{3,1},{4,6},{5,7},{6,4},{7,5},{8,10},{9,11},{10,... | collective-permute-start | bytes 3072008 | tf_op jit(solution)/shard_map/ppermute | solution.py:41
  543.0 25.2 %collective-permute-start.23 = (bf16[320,1600]{1,0:T(8,128)(2,1)S(1)}, bf16[320,1600]{1,0:T(8,128)(2,1)}, u32[]{:S(2)}, u32[]{:S(2)}) collective-permute-start(bf16[320,1600]{1,0:T(8,128)(2,1)S(1)} %get-tuple-element.315.refs_1_), channel_id=1, source_target_pairs={{0,2},{1,3},{2,0},{3,1},{4,6},{5,7},{6,4},{7,5},{8,10},{9,11},{10,... | collective-permute-start | bytes 3072008 | tf_op jit(solution)/shard_map/ppermute | solution.py:41
  553.9 21.9 %collective-permute-start.25 = (bf16[320,1600]{1,0:T(8,128)(2,1)S(1)}, bf16[320,1600]{1,0:T(8,128)(2,1)}, u32[]{:S(2)}, u32[]{:S(2)}) collective-permute-start(bf16[320,1600]{1,0:T(8,128)(2,1)S(1)} %get-tuple-element.315.refs_1_), channel_id=1, source_target_pairs={{0,1},{1,0},{2,3},{3,2},{4,5},{5,4},{6,7},{7,6},{8,9},{9,8},{10,11... | collective-permute-start | bytes 3072008 | tf_op jit(solution)/shard_map/ppermute | solution.py:41
  568.2 7.6 collective-permute-start.26
  570.5 42.9 %collective-permute-start.28 = (bf16[320,1600]{1,0:T(8,128)(2,1)S(1)}, bf16[320,1600]{1,0:T(8,128)(2,1)S(1)}, u32[]{:S(2)}, u32[]{:S(2)}) collective-permute-start(bf16[320,1600]{1,0:T(8,128)(2,1)S(1)} %get-tuple-element.174.refs_1_), channel_id=1, source_target_pairs={{0,1},{1,0},{2,3},{3,2},{4,5},{5,4},{6,7},{7,6},{8,9},{9,8},{10,11... | collective-permute-start | bytes 3072008 | tf_op jit(solution)/shard_map/ppermute | solution.py:41
  571.0 107.5 %collective-permute-start.31 = (bf16[320,1600]{1,0:T(8,128)(2,1)S(1)}, bf16[320,1600]{1,0:T(8,128)(2,1)}, u32[]{:S(2)}, u32[]{:S(2)}) collective-permute-start(bf16[320,1600]{1,0:T(8,128)(2,1)S(1)} %get-tuple-element.174.refs_1_), channel_id=1, source_target_pairs={{0,2},{1,3},{2,0},{3,1},{4,6},{5,7},{6,4},{7,5},{8,10},{9,11},{10,... | collective-permute-start | bytes 3072008 | tf_op jit(solution)/shard_map/ppermute | solution.py:41
  595.9 18.4 %collective-permute-start.27 = (bf16[896,400]{0,1:T(8,128)(2,1)}, bf16[896,400]{0,1:T(8,128)(2,1)}, u32[]{:S(2)}, u32[]{:S(2)}) collective-permute-start(bf16[896,400]{0,1:T(8,128)(2,1)} %copy.113), channel_id=1, source_target_pairs={{0,1},{1,0},{2,3},{3,2},{4,5},{5,4},{6,7},{7,6},{8,9},{9,8},{10,11... | collective-permute-start | bytes 2150408 | tf_op jit(solution)/shard_map/ppermute | solution.py:41
  602.7 126.6 %collective-permute-start.24 = (bf16[640,1600]{0,1:T(8,128)(2,1)}, bf16[640,1600]{0,1:T(8,128)(2,1)}, u32[]{:S(2)}, u32[]{:S(2)}) collective-permute-start(bf16[640,1600]{0,1:T(8,128)(2,1)} %copy.111), channel_id=1, source_target_pairs={{0,1},{1,0},{2,3},{3,2},{4,5},{5,4},{6,7},{7,6},{8,9},{9,8},{10,11... | collective-permute-start | bytes 6144008 | tf_op jit(solution)/shard_map/ppermute | solution.py:41
  610.8 67.8 %collective-permute-start.29 = (bf16[896,400]{0,1:T(8,128)(2,1)}, bf16[896,400]{0,1:T(8,128)(2,1)}, u32[]{:S(2)}, u32[]{:S(2)}) collective-permute-start(bf16[896,400]{0,1:T(8,128)(2,1)} %copy.114), channel_id=1, source_target_pairs={{0,2},{1,3},{2,0},{3,1},{4,6},{5,7},{6,4},{7,5},{8,10},{9,11},{10,... | collective-permute-start | bytes 2150408 | tf_op jit(solution)/shard_map/ppermute | solution.py:41
  613.4 65.1 %collective-permute-start.30 = (bf16[896,400]{0,1:T(8,128)(2,1)}, bf16[896,400]{0,1:T(8,128)(2,1)S(1)}, u32[]{:S(2)}, u32[]{:S(2)}) collective-permute-start(bf16[896,400]{0,1:T(8,128)(2,1)} %copy.115), channel_id=1, source_target_pairs={{0,3},{1,2},{2,1},{3,0},{4,7},{5,6},{6,5},{7,4},{8,11},{9,10},{10,... | collective-permute-start | bytes 2150408 | tf_op jit(solution)/shard_map/ppermute | solution.py:41
  706.2 4.5 collective-permute-start.32
  736.4 130.8 %collective-permute-start.36 = (bf16[320,1600]{1,0:T(8,128)(2,1)}, bf16[320,1600]{1,0:T(8,128)(2,1)}, u32[]{:S(2)}, u32[]{:S(2)}) collective-permute-start(bf16[320,1600]{1,0:T(8,128)(2,1)} %get-tuple-element.282), channel_id=1, source_target_pairs={{0,2},{1,3},{2,0},{3,1},{4,6},{5,7},{6,4},{7,5},{8,10},{9,11},{10,... | collective-permute-start | bytes 3072008 | tf_op jit(solution)/shard_map/ppermute | solution.py:41
  739.2 126.2 %collective-permute-start.33 = (bf16[640,400]{0,1:T(8,128)(2,1)}, bf16[640,400]{0,1:T(8,128)(2,1)S(1)}, u32[]{:S(2)}, u32[]{:S(2)}) collective-permute-start(bf16[640,400]{0,1:T(8,128)(2,1)} %copy.119), channel_id=1, source_target_pairs={{0,1},{1,0},{2,3},{3,2},{4,5},{5,4},{6,7},{7,6},{8,9},{9,8},{10,11... | collective-permute-start | bytes 1536008 | tf_op jit(solution)/shard_map/ppermute | solution.py:41
  740.5 126.7 %collective-permute-start.34 = (bf16[640,400]{0,1:T(8,128)(2,1)}, bf16[640,400]{0,1:T(8,128)(2,1)}, u32[]{:S(2)}, u32[]{:S(2)}) collective-permute-start(bf16[640,400]{0,1:T(8,128)(2,1)} %copy.120), channel_id=1, source_target_pairs={{0,2},{1,3},{2,0},{3,1},{4,6},{5,7},{6,4},{7,5},{8,10},{9,11},{10,... | collective-permute-start | bytes 1536008 | tf_op jit(solution)/shard_map/ppermute | solution.py:41
  742.6 124.6 %collective-permute-start.35 = (bf16[640,400]{0,1:T(8,128)(2,1)}, bf16[640,400]{0,1:T(8,128)(2,1)S(1)}, u32[]{:S(2)}, u32[]{:S(2)}) collective-permute-start(bf16[640,400]{0,1:T(8,128)(2,1)} %copy.121), channel_id=1, source_target_pairs={{0,3},{1,2},{2,1},{3,0},{4,7},{5,6},{6,5},{7,4},{8,11},{9,10},{10,... | collective-permute-start | bytes 1536008 | tf_op jit(solution)/shard_map/ppermute | solution.py:41
  858.5 136.4 %collective-permute-start.44 = (bf16[200,832]{1,0:T(8,128)(2,1)}, bf16[200,832]{1,0:T(8,128)(2,1)}, u32[]{:S(2)}, u32[]{:S(2)}) collective-permute-start(bf16[200,832]{1,0:T(8,128)(2,1)} %get-tuple-element.326), channel_id=1, source_target_pairs={{1,0},{2,1},{0,2},{5,4},{6,5},{4,6},{9,8},{10,9},{8,10},{13,12},{1... | collective-permute-start | bytes 998408 | tf_op jit(solution)/shard_map/ppermute | solution.py:434
  865.4 129.4 %collective-permute-start.45 = (bf16[200,832]{1,0:T(8,128)(2,1)}, bf16[200,832]{1,0:T(8,128)(2,1)}, u32[]{:S(2)}, u32[]{:S(2)}) collective-permute-start(bf16[200,832]{1,0:T(8,128)(2,1)} %get-tuple-element.327), channel_id=1, source_target_pairs={{3,1},{1,2},{2,3},{7,5},{5,6},{6,7},{11,9},{9,10},{10,11},{15,13},... | collective-permute-start | bytes 998408 | tf_op jit(solution)/shard_map/ppermute | solution.py:435
  897.4 25.1 %collective-permute-start.37 = (bf16[2,320,1600]{2,1,0:T(8,128)(2,1)}, bf16[2,320,1600]{2,1,0:T(8,128)(2,1)}, u32[]{:S(2)}, u32[]{:S(2)}) collective-permute-start(bf16[2,320,1600]{2,1,0:T(8,128)(2,1)} %dynamic-slice_bitcast_fusion), channel_id=1, source_target_pairs={{0,1},{1,0},{2,3},{3,2},{4,5},{5,4},{6,7},{7,6},{8,9},{9,8},{10,11... | collective-permute-start | bytes 6144008 | tf_op jit(solution)/shard_map/ppermute | solution.py:41
  994.3 8.0 collective-permute-start.42
  997.7 8.0 collective-permute-start.41
  1002.4 3.4 collective-permute-start.43
  1004.9 26.2 %collective-permute-start.38 = (bf16[320,1600]{1,0:T(8,128)(2,1)}, bf16[320,1600]{1,0:T(8,128)(2,1)}, u32[]{:S(2)}, u32[]{:S(2)}) collective-permute-start(bf16[320,1600]{1,0:T(8,128)(2,1)} %get-tuple-element.280), channel_id=1, source_target_pairs={{0,2},{1,3},{2,0},{3,1},{4,6},{5,7},{6,4},{7,5},{8,10},{9,11},{10,... | collective-permute-start | bytes 3072008 | tf_op jit(solution)/shard_map/ppermute | solution.py:41
  1031.2 2.9 collective-permute-start.39
  1034.1 4.1 collective-permute-start.40
  (125 other events, 1345.6 us)
Sparse Core Ops, SparseCore 0:
  204.9 77.1 all-gather.2
  284.9 130.9 all-gather.4
  499.6 110.6 reduce-scatter.6
  613.6 156.7 reduce-scatter.4

commit v6 on v5

--- a/solution.py
+++ b/solution.py
@@ -408,7 +408,7 @@
             collective_id=collective_id, has_side_effects=True, vmem_limit_bytes=56 << 20
         ),
         cost_estimate=pl.CostEstimate(
-            flops=0, bytes_accessed=sum(p.size * 2 for p in parts), transcendentals=0
+            flops=6 * 10**10, bytes_accessed=sum(p.size * 2 for p in parts), transcendentals=0
         ),
     )(*parts)
 

time: 1060 us -> 1060 us (level)
  no operation moved by 1% of the time
where the time goes in v6:
time: 1060 us
  Pallas kernels  479 us (45%)
  matrix products  198 us (19%)
  local copies, waits for them, and re-layouts  144 us (14%)
  waiting for transfers between devices  93.6 us (9%)
  other arithmetic  81.9 us (8%)
  starting transfers between devices  41.3 us (4%)
  between operations  17.1 us (2%)
    pallas_call x2, Pallas kernels, gather_dp(): pl.pallas_call(lambda *refs: gather_kernel(pieces, line, *refs), out_shap...  161 us
    pallas_call x1, Pallas kernels, attention_backward(): pl.pallas_call(kernel, grid=(SEQ + 1, GROUP_HEADS), in_specs=[pl.BlockSpe...  113 us
    ppermute x42, waiting for transfers between devices, swap(): lax.ppermute(value, axis, [(i, i ^ bit) for i in range(lax.axis_size(axis...  93.5 us
    dot_general x8, matrix products, mm_nt(): lax.dot_general(left, right, (((1,), (1,)), ((), ())), preferred_element_...  69.6 us
    dot_general x9, matrix products, mm(): return jnp.dot(left, right, preferred_element_type=FULL)  66.3 us
    pallas_call x1, Pallas kernels, scatter_dp(): pl.pallas_call(lambda *refs: scatter_kernel(pieces, line, *refs), out_sha...  65.6 us
    dot_general x8, matrix products, mm_tn(): lax.dot_general(left, right, (((0,), (0,)), ((), ())), preferred_element_...  62.4 us
    pallas_call x1, Pallas kernels, mamba_backward(): pl.pallas_call(mamba_backward_kernel, grid=(chunks,), in_specs=mamba_spec...  54.6 us
  transfers between devices with their start and end apart: 50, of which 11 were waited for; matrix products, arithmetic and copies ran while one was open for 30% of the time, Pallas kernels for 45%

profile of v6, /device:TPU:0, one launch (start us, length us, event | category | flops | bytes accessed | tf_op | source)
XLA Modules:
  0.0 1055.3 jit_solution(10765287601555828188)
XLA Ops:
  27.0 64.0 %shard_map.237 = (bf16[8,16,512]{2,1,0:T(8,128)(2,1)S(1)}, bf16[8,200,400]{2,1,0:T(8,128)(2,1)S(1)}, bf16[8,400,400]{2,1,0:T(8,128)(2,1)S(1)}) custom-call(bf16[16,512]{1,0:T(8,128)(2,1)S(1)} %fusion.61.refs_0_, bf16[200,400]{1,0:T(8,128)(2,1)S(1)} %copy-done.24, bf16[400,400]{1,0:T(8,128)(2,1)S(1)} %copy-done.23), custom_call_target="tpu_custom_call" | custom-call | bytes 7942144 | tf_op jit(solution)/shard_map/pallas_call | solution.py:259
  103.9 96.9 %shard_map.241 = (bf16[8,200,896]{2,1,0:T(8,128)(2,1)S(1)}, bf16[8,200,1792]{2,1,0:T(8,128)(2,1)S(1)}) custom-call(bf16[200,896]{1,0:T(8,128)(2,1)S(1)} %concatenate.68.refs_0_, bf16[200,1792]{1,0:T(8,128)(2,1)S(1)} %concatenate.69.refs_1_), custom_call_target="tpu_custom_call" | custom-call | bytes 17203200 | tf_op jit(solution)/shard_map/pallas_call | solution.py:259
  221.4 5.5 shard_map.239
  226.9 6.6 convolution_convert_fusion.9
  240.3 3.7 copy.100
  249.9 35.7 %shard_map.243 = (bf16[1600,320]{1,0:T(8,128)(2,1)S(1)}, f32[1600,128]{1,0:T(8,128)S(1)}) custom-call(s32[1,2]{1,0:T(1,128)S(1)} %copy-done.31, bf16[1600,320]{1,0:T(8,128)(2,1)S(1)} %copy-done.16, bf16[1280,256]{1,0:T(8,128)(2,1)S(1)} %slice.458.kv_ref.refs_2_), custom_call_target="tpu_custom_call" | custom-call | flops 40000000000 | bytes 4194304 | tf_op jit(solution)/shard_map/pallas_call | solution.py:887
  286.5 17.5 %collective-permute-done.12 = bf16[1600,400]{0,1:T(8,128)(2,1)} collective-permute-done((bf16[1600,400]{0,1:T(8,128)(2,1)}, bf16[1600,400]{0,1:T(8,128)(2,1)}, u32[]{:S(2)}, u32[]{:S(2)}) %collective-permute-start.12) | collective-permute-done | bytes 1280032 | tf_op jit(solution)/shard_map/ppermute | solution.py:41
  307.5 3.5 copy.103.refs_2_
  314.4 6.8 shard_map.244
  321.2 3.7 convolution_convert_fusion.6
  325.8 11.9 %fusion.88.xzb_ref.tail_ref = f32[1280,1792]{1,0:T(8,128)S(1)} fusion(bf16[1280,1600]{1,0:T(8,128)(2,1)} %shard_map.239, bf16[1600,1792]{1,0:T(8,128)(2,1)} %bitcast.186), kind=kOutput, calls=%fused_computation.269 | convolution fusion | flops 7340032000 | bytes 19005440 | tf_op jit(solution)/shard_map/dot_general | solution.py:440
  341.3 18.3 %shard_map.245 = (bf16[1280,896]{1,0:T(8,128)(2,1)S(1)}, bf16[1280,896]{1,0:T(8,128)(2,1)S(1)}, f32[10,16,896]{2,1,0:T(8,128)S(1)}) custom-call(s32[1,2]{1,0:T(1,128)S(1)} %copy-done.31, f32[1280,1792]{1,0:T(8,128)S(1)} %fusion.88.xzb_ref.tail_ref, f32[1280,1792]{1,0:T(8,128)S(1)} %fusion.88.xzb_ref.tail_ref, f32[8,896]{1,0:T(8,128)S(1)} %pad.126.conv_ref, ...), custom_call_target="tpu_custom_call" | custom-call | flops 20000000000 | bytes 16777216 | tf_op jit(solution)/shard_map/pallas_call | solution.py:734
  359.7 3.6 copy-done.36
  366.0 5.4 convolution_convert_fusion.5
  371.8 4.2 collective-permute-done.15
  382.9 20.6 %collective-permute-done.16 = bf16[320,1600]{1,0:T(8,128)(2,1)} collective-permute-done((bf16[320,1600]{1,0:T(8,128)(2,1)}, bf16[320,1600]{1,0:T(8,128)(2,1)}, u32[]{:S(2)}, u32[]{:S(2)}) %collective-permute-start.16) | collective-permute-done | bytes 1024032 | tf_op jit(solution)/shard_map/ppermute | solution.py:41
  410.4 13.2 %fusion.36 = f32[1280,1408]{1,0:T(8,128)} fusion(bf16[1600,1408]{1,0:T(8,128)(2,1)} %all-gather.3.cloned.1.call-done, bf16[320,1600]{1,0:T(8,128)(2,1)} %collective-permute-done.18, bf16[320,1600]{1,0:T(8,128)(2,1)} %collective-permute-done.8, bf16[320,1600]{1,0:T(8,128)(2,1)} %collective-permute-done.9, bf16[320,1600]{1,0:T(8,128)(2,1)} %fusion.16), kind=kOutput, calls=%fused_computation.123 | convolution fusion | flops 5783552000 | bytes 15810560 | tf_op jit(solution)/shard_map/dot_general | solution.py:440
  423.5 9.8 collective-permute-done.17
  436.2 19.3 %fusion.35 = f32[1280,2816]{1,0:T(8,128)S(1)} fusion(bf16[1600,2816]{1,0:T(8,128)(2,1)} %all-gather.5.cloned.1.call-done, bf16[320,1600]{1,0:T(8,128)(2,1)} %collective-permute-done.20, bf16[320,1600]{1,0:T(8,128)(2,1)} %copy-done.108, bf16[320,1600]{1,0:T(8,128)(2,1)} %copy-done.110, bf16[320,1600]{1,0:T(8,128)(2,1)S(1)} %multiply_convert_fusion.4), kind=kOutput, calls=%fused_computation.122 | convolution fusion | flops 11550720000 | bytes 27525120 | tf_op jit(solution)/shard_map/dot_general | solution.py:440
  455.6 8.7 multiply_convert_fusion.2
  464.3 18.0 %convolution_convert_fusion.4 = bf16[1280,1600]{1,0:T(8,128)(2,1)S(1)} fusion(bf16[1600,2816]{1,0:T(8,128)(2,1)} %all-gather.5.cloned.1.call-done, bf16[1280,1408]{1,0:T(8,128)(2,1)} %get-tuple-element.276, bf16[1280,1408]{1,0:T(8,128)(2,1)} %get-tuple-element.275), kind=kOutput, calls=%fused_computation.8 | convolution fusion | flops 11550801920 | bytes 20316160 | tf_op jit(solution)/shard_map/dot_general | solution.py:444
  487.3 12.1 %convolution_convert_fusion.3 = bf16[1600,1408]{1,0:T(8,128)(2,1)} fusion(bf16[1280,1408]{1,0:T(8,128)(2,1)} %get-tuple-element.277, bf16[320,1600]{1,0:T(8,128)(2,1)} %collective-permute-done.18, bf16[320,1600]{1,0:T(8,128)(2,1)} %collective-permute-done.8, bf16[320,1600]{1,0:T(8,128)(2,1)} %collective-permute-done.9, bf16[320,1600]{1,0:T(8,128)(2,1)} %fusion.16), kind=kOutput, calls=%fused_computation.7 | convolution fusion | flops 5785804800 | bytes 12206080 | tf_op jit(solution)/shard_map/dot_general | solution.py:448
  509.8 18.1 %convolution_convert_fusion = bf16[1600,2816]{1,0:T(8,128)(2,1)} fusion(bf16[1280,1408]{1,0:T(8,128)(2,1)} %get-tuple-element.276, bf16[1280,1408]{1,0:T(8,128)(2,1)} %get-tuple-element.275, bf16[320,1600]{1,0:T(8,128)(2,1)} %collective-permute-done.20, bf16[320,1600]{1,0:T(8,128)(2,1)S(1)} %copy-done.109, bf16[320,1600]{1,0:T(8,128)(2,1)} %copy-done.110, ...), kind=kOutput, calls=%fused_computation | convolution fusion | flops 11569643520 | bytes 20316160 | tf_op jit(solution)/shard_map/dot_general | solution.py:448
  528.0 6.3 collective-permute-done.22
  537.4 4.2 multiply_reduce_fusion.4
  544.7 9.2 convolution_convert_fusion.2
  553.9 14.3 %collective-permute-done.23.refs_3_ = bf16[320,1600]{1,0:T(8,128)(2,1)} collective-permute-done((bf16[320,1600]{1,0:T(8,128)(2,1)S(1)}, bf16[320,1600]{1,0:T(8,128)(2,1)}, u32[]{:S(2)}, u32[]{:S(2)}) %collective-permute-start.23) | collective-permute-done | bytes 1024032 | tf_op jit(solution)/shard_map/ppermute | solution.py:41
  578.5 6.3 convolution_convert_fusion.7.d_gated_ref
  584.9 4.5 convolution_convert_fusion.8
  598.7 4.1 copy.111
  614.3 3.6 copy-done.37
  621.6 54.6 %shard_map.247 = (bf16[1280,1792]{1,0:T(8,128)(2,1)S(1)}, f32[8,896]{1,0:T(8,128)S(1)}, f32[8,128]{1,0:T(8,128)S(1)}) custom-call(s32[1,2]{1,0:T(1,128)S(1)} %copy-done.31, f32[1280,1792]{1,0:T(8,128)S(1)} %copy-done.37, f32[1280,1792]{1,0:T(8,128)S(1)} %copy-done.37, f32[8,896]{1,0:T(8,128)S(1)} %pad.126.conv_ref, f32[8,128]{1,0:T(8,128)S(1)} %broadcast_in_dim.19.rate_ref, ...), custom_call_target="tpu_custom_call" | custom-call | flops 60000002048 | bytes 25165824 | tf_op jit(solution)/shard_map/pallas_call | solution.py:755
  692.5 13.8 %convolution_convert_fusion.1 = bf16[1600,1792]{1,0:T(8,128)(2,1)} fusion(bf16[1280,1600]{1,0:T(8,128)(2,1)} %shard_map.239, bf16[1280,1792]{1,0:T(8,128)(2,1)} %copy-done.35), kind=kOutput, calls=%fused_computation.5 | convolution fusion | flops 7342899200 | bytes 14417920 | tf_op jit(solution)/shard_map/dot_general | solution.py:448
  715.0 3.9 convolution_convert_fusion.13
  720.7 4.0 convolution_convert_fusion.14
  732.6 3.8 add_convert_fusion
  743.2 112.7 %shard_map.250 = (bf16[1600,320]{1,0:T(8,128)(2,1)}, bf16[1280,256]{1,0:T(8,128)(2,1)}, f32[200,1792]{1,0:T(8,128)}, f32[400,400]{1,0:T(8,128)}) custom-call(s32[1,2]{1,0:T(1,128)} %refs_0_.3, bf16[1600,320]{1,0:T(8,128)(2,1)} %pad_maximum_fusion.10.q_ref.refs_1_, bf16[1280,256]{1,0:T(8,128)(2,1)} %copy-done.21, bf16[1600,320]{1,0:T(8,128)(2,1)} %copy-done.25, ...), custom_call_target="tpu_custom_call" | custom-call | flops 99999997952 | bytes 8388608 | tf_op jit(solution)/shard_map/pallas_call | solution.py:925
  858.5 6.9 collective-permute-start.44
  869.1 8.9 fusion.17
  878.0 16.3 %multiply_reduce_fusion = (f32[1600]{0:T(1024)S(1)}, bf16[1280,1600]{1,0:T(8,128)(2,1)}, f32[1280,1600]{1,0:T(8,128)}) fusion(f32[1280]{0:T(1024)S(1)} %copy-done.103, bf16[4,320,1600]{2,1,0:T(8,128)(2,1)S(1)} %bitcast.175, f32[1280,1600]{1,0:T(8,128)} %fusion.17, bf16[1280,1792]{1,0:T(8,128)(2,1)} %copy-done.35, bf16[1600,1792]{1,0:T(8,128)(2,1)} %bitcast.187), kind=kOutput, calls=%fused_computation.2 | convolution fusion | flops 7352318464 | bytes 34909440 | tf_op jit(solution)/shard_map/dot_general | solution.py:444
  898.1 4.3 multiply_reduce_fusion.2
  902.4 5.1 convolution_convert_fusion.10
  911.8 5.4 copy.131
  922.5 4.9 fusion.12
  927.4 65.6 %shard_map.252 = (f32[200,896]{1,0:T(8,128)}, f32[200,400]{1,0:T(8,128)}, f32[16,512]{1,0:T(8,128)}) custom-call(bf16[8,200,896]{2,1,0:T(8,128)(2,1)} %bitcast.202, bf16[8,200,400]{2,1,0:T(8,128)(2,1)} %bitcast.205, f32[8,16,512]{2,1,0:T(8,128)} %fusion.45.refs_2_), custom_call_target="tpu_custom_call" | custom-call | flops 60000002048 | bytes 4278272 | tf_op jit(solution)/shard_map/pallas_call | solution.py:401
  997.7 4.7 collective-permute-done.42.refs_3_
  1012.8 4.0 concatenate.85
  1018.9 12.3 %collective-permute-done.38 = bf16[320,1600]{1,0:T(8,128)(2,1)} collective-permute-done((bf16[320,1600]{1,0:T(8,128)(2,1)}, bf16[320,1600]{1,0:T(8,128)(2,1)}, u32[]{:S(2)}, u32[]{:S(2)}) %collective-permute-start.38) | collective-permute-done | bytes 1024032 | tf_op jit(solution)/shard_map/ppermute | solution.py:41
  (521 shorter events, 247.2 us)
Async XLA Ops:
  7.2 403.1 %all-gather.3.cloned.1.call-start = ((), (), s32[]{:S(2)}) async-start(), calls=%async_computation.2 | async-start | bytes 5068800 | tf_op jit(solution)/shard_map/all_gather | solution.py:417
  7.3 88.7 %collective-permute-start.4 = (bf16[320,1600]{1,0:T(8,128)(2,1)}, bf16[320,1600]{1,0:T(8,128)(2,1)S(1)}, u32[]{:S(2)}, u32[]{:S(2)}) collective-permute-start(bf16[320,1600]{1,0:T(8,128)(2,1)} %refs_1_.3), channel_id=1, source_target_pairs={{0,2},{1,3},{2,0},{3,1},{4,6},{5,7},{6,4},{7,5},{8,10},{9,11},{10,... | collective-permute-start | bytes 3072008 | tf_op jit(solution)/shard_map/ppermute | solution.py:41
  10.3 85.7 %collective-permute-start.5 = (bf16[320,1600]{1,0:T(8,128)(2,1)}, bf16[320,1600]{1,0:T(8,128)(2,1)}, u32[]{:S(2)}, u32[]{:S(2)}) collective-permute-start(bf16[320,1600]{1,0:T(8,128)(2,1)} %refs_1_.3), channel_id=1, source_target_pairs={{0,1},{1,0},{2,3},{3,2},{4,5},{5,4},{6,7},{7,6},{8,9},{9,8},{10,11... | collective-permute-start | bytes 3072008 | tf_op jit(solution)/shard_map/ppermute | solution.py:41
  14.1 78.7 %collective-permute-start.2 = (bf16[200,832]{1,0:T(8,128)(2,1)}, bf16[200,832]{1,0:T(8,128)(2,1)}, u32[]{:S(2)}, u32[]{:S(2)}) collective-permute-start(bf16[200,832]{1,0:T(8,128)(2,1)} %get-tuple-element.319), channel_id=1, source_target_pairs={{0,1},{1,2},{2,0},{4,5},{5,6},{6,4},{8,9},{9,10},{10,8},{12,13},{1... | collective-permute-start | bytes 998408 | tf_op jit(solution)/shard_map/ppermute | solution.py:427
  16.5 76.4 %collective-permute-start.3 = (bf16[200,832]{1,0:T(8,128)(2,1)}, bf16[200,832]{1,0:T(8,128)(2,1)}, u32[]{:S(2)}, u32[]{:S(2)}) collective-permute-start(bf16[200,832]{1,0:T(8,128)(2,1)} %get-tuple-element.318), channel_id=1, source_target_pairs={{1,3},{2,1},{3,2},{5,7},{6,5},{7,6},{9,11},{10,9},{11,10},{13,15},... | collective-permute-start | bytes 998408 | tf_op jit(solution)/shard_map/ppermute | solution.py:428
  18.0 74.7 %collective-permute-start = (bf16[200,560]{1,0:T(8,128)(2,1)}, bf16[200,560]{1,0:T(8,128)(2,1)}, u32[]{:S(2)}, u32[]{:S(2)}) collective-permute-start(bf16[200,560]{1,0:T(8,128)(2,1)} %refs_0_.2), channel_id=1, source_target_pairs={{0,2},{1,3},{2,0},{3,1},{4,6},{5,7},{6,4},{7,5},{8,10},{9,11},{10,... | collective-permute-start | bytes 672008 | tf_op jit(solution)/shard_map/ppermute | solution.py:41
  92.7 112.1 %collective-permute-start.8 = (bf16[320,1600]{1,0:T(8,128)(2,1)}, bf16[320,1600]{1,0:T(8,128)(2,1)}, u32[]{:S(2)}, u32[]{:S(2)}) collective-permute-start(bf16[320,1600]{1,0:T(8,128)(2,1)} %fusion.16), channel_id=1, source_target_pairs={{0,2},{1,3},{2,0},{3,1},{4,6},{5,7},{6,4},{7,5},{8,10},{9,11},{10,... | collective-permute-start | bytes 3072008 | tf_op jit(solution)/shard_map/ppermute | solution.py:41
  92.8 112.0 %collective-permute-start.9 = (bf16[320,1600]{1,0:T(8,128)(2,1)}, bf16[320,1600]{1,0:T(8,128)(2,1)}, u32[]{:S(2)}, u32[]{:S(2)}) collective-permute-start(bf16[320,1600]{1,0:T(8,128)(2,1)} %fusion.16), channel_id=1, source_target_pairs={{0,1},{1,0},{2,3},{3,2},{4,5},{5,4},{6,7},{7,6},{8,9},{9,8},{10,11... | collective-permute-start | bytes 3072008 | tf_op jit(solution)/shard_map/ppermute | solution.py:41
  92.9 3.1 collective-permute-start.1
  204.8 231.4 %all-gather.5.cloned.1.call-start = ((), (), s32[]{:S(2)}) async-start(), calls=%async_computation.3 | async-start | bytes 10137600 | tf_op jit(solution)/shard_map/all_gather | solution.py:417
  205.2 9.9 collective-permute-start.6
  214.9 825.1 %reduce-scatter.7.cloned.1.call-start = ((), (), s32[]{:S(2)}) async-start(), calls=%async_computation.5 | async-start | bytes 5068800
  239.9 46.7 %collective-permute-start.10 = (bf16[1600,400]{0,1:T(8,128)(2,1)}, bf16[1600,400]{0,1:T(8,128)(2,1)}, u32[]{:S(2)}, u32[]{:S(2)}) collective-permute-start(bf16[1600,400]{0,1:T(8,128)(2,1)} %copy.99), channel_id=1, source_target_pairs={{0,1},{1,0},{2,3},{3,2},{4,5},{5,4},{6,7},{7,6},{8,9},{9,8},{10,11... | collective-permute-start | bytes 3840008 | tf_op jit(solution)/shard_map/ppermute | solution.py:41
  244.1 42.5 %collective-permute-start.11 = (bf16[1600,400]{0,1:T(8,128)(2,1)}, bf16[1600,400]{0,1:T(8,128)(2,1)}, u32[]{:S(2)}, u32[]{:S(2)}) collective-permute-start(bf16[1600,400]{0,1:T(8,128)(2,1)} %copy.100), channel_id=1, source_target_pairs={{0,2},{1,3},{2,0},{3,1},{4,6},{5,7},{6,4},{7,5},{8,10},{9,11},{10,... | collective-permute-start | bytes 3840008 | tf_op jit(solution)/shard_map/ppermute | solution.py:41
  248.6 55.4 %collective-permute-start.12 = (bf16[1600,400]{0,1:T(8,128)(2,1)}, bf16[1600,400]{0,1:T(8,128)(2,1)}, u32[]{:S(2)}, u32[]{:S(2)}) collective-permute-start(bf16[1600,400]{0,1:T(8,128)(2,1)} %copy.101), channel_id=1, source_target_pairs={{0,3},{1,2},{2,1},{3,0},{4,7},{5,6},{6,5},{7,4},{8,11},{9,10},{10,... | collective-permute-start | bytes 3840008 | tf_op jit(solution)/shard_map/ppermute | solution.py:41
  325.1 12.6 %collective-permute-start.13 = (bf16[2,320,1600]{2,1,0:T(8,128)(2,1)S(1)}, bf16[2,320,1600]{2,1,0:T(8,128)(2,1)S(1)}, u32[]{:S(2)}, u32[]{:S(2)}) collective-permute-start(bf16[2,320,1600]{2,1,0:T(8,128)(2,1)S(1)} %dynamic-slice_bitcast_fusion.2), channel_id=1, source_target_pairs={{0,1},{1,0},{2,3},{3,2},{4,5},{5,4},{6,7},{7,6},{8,9},{9,8},{10,11... | collective-permute-start | bytes 6144008 | tf_op jit(solution)/shard_map/ppermute | solution.py:41
  339.6 25.4 %collective-permute-start.14 = (bf16[320,1600]{1,0:T(8,128)(2,1)S(1)}, bf16[320,1600]{1,0:T(8,128)(2,1)S(1)}, u32[]{:S(2)}, u32[]{:S(2)}) collective-permute-start(bf16[320,1600]{1,0:T(8,128)(2,1)S(1)} %get-tuple-element.284), channel_id=1, source_target_pairs={{0,2},{1,3},{2,0},{3,1},{4,6},{5,7},{6,4},{7,5},{8,10},{9,11},{10,... | collective-permute-start | bytes 3072008 | tf_op jit(solution)/shard_map/ppermute | solution.py:41
  371.7 4.3 collective-permute-start.15
  377.6 25.9 %collective-permute-start.16 = (bf16[320,1600]{1,0:T(8,128)(2,1)}, bf16[320,1600]{1,0:T(8,128)(2,1)}, u32[]{:S(2)}, u32[]{:S(2)}) collective-permute-start(bf16[320,1600]{1,0:T(8,128)(2,1)} %fusion.13), channel_id=1, source_target_pairs={{0,2},{1,3},{2,0},{3,1},{4,6},{5,7},{6,4},{7,5},{8,10},{9,11},{10,... | collective-permute-start | bytes 3072008 | tf_op jit(solution)/shard_map/ppermute | solution.py:41
  379.6 30.7 %collective-permute-start.18 = (bf16[320,1600]{1,0:T(8,128)(2,1)}, bf16[320,1600]{1,0:T(8,128)(2,1)}, u32[]{:S(2)}, u32[]{:S(2)}) collective-permute-start(bf16[320,1600]{1,0:T(8,128)(2,1)} %collective-permute-done.8), channel_id=1, source_target_pairs={{0,1},{1,0},{2,3},{3,2},{4,5},{5,4},{6,7},{7,6},{8,9},{9,8},{10,11... | collective-permute-start | bytes 3072008 | tf_op jit(solution)/shard_map/ppermute | solution.py:41
  408.6 24.8 %collective-permute-start.17 = (bf16[320,1600]{1,0:T(8,128)(2,1)S(1)}, bf16[320,1600]{1,0:T(8,128)(2,1)S(1)}, u32[]{:S(2)}, u32[]{:S(2)}) collective-permute-start(bf16[320,1600]{1,0:T(8,128)(2,1)S(1)} %multiply_convert_fusion.4), channel_id=1, source_target_pairs={{0,2},{1,3},{2,0},{3,1},{4,6},{5,7},{6,4},{7,5},{8,10},{9,11},{10,... | collective-permute-start | bytes 3072008 | tf_op jit(solution)/shard_map/ppermute | solution.py:41
  423.5 9.9 collective-permute-start.19
  487.1 12.3 %collective-permute-start.21 = (bf16[640,1600]{0,1:T(8,128)(2,1)}, bf16[640,1600]{0,1:T(8,128)(2,1)S(1)}, u32[]{:S(2)}, u32[]{:S(2)}) collective-permute-start(bf16[640,1600]{0,1:T(8,128)(2,1)} %copy.107), channel_id=1, source_target_pairs={{0,1},{1,0},{2,3},{3,2},{4,5},{5,4},{6,7},{7,6},{8,9},{9,8},{10,11... | collective-permute-start | bytes 6144008 | tf_op jit(solution)/shard_map/ppermute | solution.py:41
  500.8 541.3 %reduce-scatter.5.cloned.1.call-start = ((), (), s32[]{:S(2)}) async-start(), calls=%async_computation.4 | async-start | bytes 10137600 | tf_op jit(solution)/shard_map/reduce_scatter | solution.py:421
  508.1 26.1 %collective-permute-start.22 = (bf16[320,1600]{1,0:T(8,128)(2,1)}, bf16[320,1600]{1,0:T(8,128)(2,1)}, u32[]{:S(2)}, u32[]{:S(2)}) collective-permute-start(bf16[320,1600]{1,0:T(8,128)(2,1)} %add_convert_fusion.1), channel_id=1, source_target_pairs={{0,2},{1,3},{2,0},{3,1},{4,6},{5,7},{6,4},{7,5},{8,10},{9,11},{10,... | collective-permute-start | bytes 3072008 | tf_op jit(solution)/shard_map/ppermute | solution.py:41
  543.0 25.2 %collective-permute-start.23 = (bf16[320,1600]{1,0:T(8,128)(2,1)S(1)}, bf16[320,1600]{1,0:T(8,128)(2,1)}, u32[]{:S(2)}, u32[]{:S(2)}) collective-permute-start(bf16[320,1600]{1,0:T(8,128)(2,1)S(1)} %get-tuple-element.315.refs_1_), channel_id=1, source_target_pairs={{0,2},{1,3},{2,0},{3,1},{4,6},{5,7},{6,4},{7,5},{8,10},{9,11},{10,... | collective-permute-start | bytes 3072008 | tf_op jit(solution)/shard_map/ppermute | solution.py:41
  553.9 21.9 %collective-permute-start.25 = (bf16[320,1600]{1,0:T(8,128)(2,1)S(1)}, bf16[320,1600]{1,0:T(8,128)(2,1)}, u32[]{:S(2)}, u32[]{:S(2)}) collective-permute-start(bf16[320,1600]{1,0:T(8,128)(2,1)S(1)} %get-tuple-element.315.refs_1_), channel_id=1, source_target_pairs={{0,1},{1,0},{2,3},{3,2},{4,5},{5,4},{6,7},{7,6},{8,9},{9,8},{10,11... | collective-permute-start | bytes 3072008 | tf_op jit(solution)/shard_map/ppermute | solution.py:41
  568.2 7.6 collective-permute-start.26
  570.5 42.9 %collective-permute-start.28 = (bf16[320,1600]{1,0:T(8,128)(2,1)S(1)}, bf16[320,1600]{1,0:T(8,128)(2,1)S(1)}, u32[]{:S(2)}, u32[]{:S(2)}) collective-permute-start(bf16[320,1600]{1,0:T(8,128)(2,1)S(1)} %get-tuple-element.174.refs_1_), channel_id=1, source_target_pairs={{0,1},{1,0},{2,3},{3,2},{4,5},{5,4},{6,7},{7,6},{8,9},{9,8},{10,11... | collective-permute-start | bytes 3072008 | tf_op jit(solution)/shard_map/ppermute | solution.py:41
  571.0 107.5 %collective-permute-start.31 = (bf16[320,1600]{1,0:T(8,128)(2,1)S(1)}, bf16[320,1600]{1,0:T(8,128)(2,1)}, u32[]{:S(2)}, u32[]{:S(2)}) collective-permute-start(bf16[320,1600]{1,0:T(8,128)(2,1)S(1)} %get-tuple-element.174.refs_1_), channel_id=1, source_target_pairs={{0,2},{1,3},{2,0},{3,1},{4,6},{5,7},{6,4},{7,5},{8,10},{9,11},{10,... | collective-permute-start | bytes 3072008 | tf_op jit(solution)/shard_map/ppermute | solution.py:41
  595.9 18.4 %collective-permute-start.27 = (bf16[896,400]{0,1:T(8,128)(2,1)}, bf16[896,400]{0,1:T(8,128)(2,1)}, u32[]{:S(2)}, u32[]{:S(2)}) collective-permute-start(bf16[896,400]{0,1:T(8,128)(2,1)} %copy.113), channel_id=1, source_target_pairs={{0,1},{1,0},{2,3},{3,2},{4,5},{5,4},{6,7},{7,6},{8,9},{9,8},{10,11... | collective-permute-start | bytes 2150408 | tf_op jit(solution)/shard_map/ppermute | solution.py:41
  602.7 126.6 %collective-permute-start.24 = (bf16[640,1600]{0,1:T(8,128)(2,1)}, bf16[640,1600]{0,1:T(8,128)(2,1)}, u32[]{:S(2)}, u32[]{:S(2)}) collective-permute-start(bf16[640,1600]{0,1:T(8,128)(2,1)} %copy.111), channel_id=1, source_target_pairs={{0,1},{1,0},{2,3},{3,2},{4,5},{5,4},{6,7},{7,6},{8,9},{9,8},{10,11... | collective-permute-start | bytes 6144008 | tf_op jit(solution)/shard_map/ppermute | solution.py:41
  610.8 67.8 %collective-permute-start.29 = (bf16[896,400]{0,1:T(8,128)(2,1)}, bf16[896,400]{0,1:T(8,128)(2,1)}, u32[]{:S(2)}, u32[]{:S(2)}) collective-permute-start(bf16[896,400]{0,1:T(8,128)(2,1)} %copy.114), channel_id=1, source_target_pairs={{0,2},{1,3},{2,0},{3,1},{4,6},{5,7},{6,4},{7,5},{8,10},{9,11},{10,... | collective-permute-start | bytes 2150408 | tf_op jit(solution)/shard_map/ppermute | solution.py:41
  613.4 65.1 %collective-permute-start.30 = (bf16[896,400]{0,1:T(8,128)(2,1)}, bf16[896,400]{0,1:T(8,128)(2,1)S(1)}, u32[]{:S(2)}, u32[]{:S(2)}) collective-permute-start(bf16[896,400]{0,1:T(8,128)(2,1)} %copy.115), channel_id=1, source_target_pairs={{0,3},{1,2},{2,1},{3,0},{4,7},{5,6},{6,5},{7,4},{8,11},{9,10},{10,... | collective-permute-start | bytes 2150408 | tf_op jit(solution)/shard_map/ppermute | solution.py:41
  706.2 4.5 collective-permute-start.32
  736.4 130.8 %collective-permute-start.36 = (bf16[320,1600]{1,0:T(8,128)(2,1)}, bf16[320,1600]{1,0:T(8,128)(2,1)}, u32[]{:S(2)}, u32[]{:S(2)}) collective-permute-start(bf16[320,1600]{1,0:T(8,128)(2,1)} %get-tuple-element.282), channel_id=1, source_target_pairs={{0,2},{1,3},{2,0},{3,1},{4,6},{5,7},{6,4},{7,5},{8,10},{9,11},{10,... | collective-permute-start | bytes 3072008 | tf_op jit(solution)/shard_map/ppermute | solution.py:41
  739.2 126.2 %collective-permute-start.33 = (bf16[640,400]{0,1:T(8,128)(2,1)}, bf16[640,400]{0,1:T(8,128)(2,1)S(1)}, u32[]{:S(2)}, u32[]{:S(2)}) collective-permute-start(bf16[640,400]{0,1:T(8,128)(2,1)} %copy.119), channel_id=1, source_target_pairs={{0,1},{1,0},{2,3},{3,2},{4,5},{5,4},{6,7},{7,6},{8,9},{9,8},{10,11... | collective-permute-start | bytes 1536008 | tf_op jit(solution)/shard_map/ppermute | solution.py:41
  740.5 126.7 %collective-permute-start.34 = (bf16[640,400]{0,1:T(8,128)(2,1)}, bf16[640,400]{0,1:T(8,128)(2,1)}, u32[]{:S(2)}, u32[]{:S(2)}) collective-permute-start(bf16[640,400]{0,1:T(8,128)(2,1)} %copy.120), channel_id=1, source_target_pairs={{0,2},{1,3},{2,0},{3,1},{4,6},{5,7},{6,4},{7,5},{8,10},{9,11},{10,... | collective-permute-start | bytes 1536008 | tf_op jit(solution)/shard_map/ppermute | solution.py:41
  742.6 124.6 %collective-permute-start.35 = (bf16[640,400]{0,1:T(8,128)(2,1)}, bf16[640,400]{0,1:T(8,128)(2,1)S(1)}, u32[]{:S(2)}, u32[]{:S(2)}) collective-permute-start(bf16[640,400]{0,1:T(8,128)(2,1)} %copy.121), channel_id=1, source_target_pairs={{0,3},{1,2},{2,1},{3,0},{4,7},{5,6},{6,5},{7,4},{8,11},{9,10},{10,... | collective-permute-start | bytes 1536008 | tf_op jit(solution)/shard_map/ppermute | solution.py:41
  858.5 136.4 %collective-permute-start.44 = (bf16[200,832]{1,0:T(8,128)(2,1)}, bf16[200,832]{1,0:T(8,128)(2,1)}, u32[]{:S(2)}, u32[]{:S(2)}) collective-permute-start(bf16[200,832]{1,0:T(8,128)(2,1)} %get-tuple-element.326), channel_id=1, source_target_pairs={{1,0},{2,1},{0,2},{5,4},{6,5},{4,6},{9,8},{10,9},{8,10},{13,12},{1... | collective-permute-start | bytes 998408 | tf_op jit(solution)/shard_map/ppermute | solution.py:434
  865.4 129.4 %collective-permute-start.45 = (bf16[200,832]{1,0:T(8,128)(2,1)}, bf16[200,832]{1,0:T(8,128)(2,1)}, u32[]{:S(2)}, u32[]{:S(2)}) collective-permute-start(bf16[200,832]{1,0:T(8,128)(2,1)} %get-tuple-element.327), channel_id=1, source_target_pairs={{3,1},{1,2},{2,3},{7,5},{5,6},{6,7},{11,9},{9,10},{10,11},{15,13},... | collective-permute-start | bytes 998408 | tf_op jit(solution)/shard_map/ppermute | solution.py:435
  897.4 25.1 %collective-permute-start.37 = (bf16[2,320,1600]{2,1,0:T(8,128)(2,1)}, bf16[2,320,1600]{2,1,0:T(8,128)(2,1)}, u32[]{:S(2)}, u32[]{:S(2)}) collective-permute-start(bf16[2,320,1600]{2,1,0:T(8,128)(2,1)} %dynamic-slice_bitcast_fusion), channel_id=1, source_target_pairs={{0,1},{1,0},{2,3},{3,2},{4,5},{5,4},{6,7},{7,6},{8,9},{9,8},{10,11... | collective-permute-start | bytes 6144008 | tf_op jit(solution)/shard_map/ppermute | solution.py:41
  994.3 8.0 collective-permute-start.42
  997.7 8.0 collective-permute-start.41
  1002.4 3.4 collective-permute-start.43
  1004.9 26.2 %collective-permute-start.38 = (bf16[320,1600]{1,0:T(8,128)(2,1)}, bf16[320,1600]{1,0:T(8,128)(2,1)}, u32[]{:S(2)}, u32[]{:S(2)}) collective-permute-start(bf16[320,1600]{1,0:T(8,128)(2,1)} %get-tuple-element.280), channel_id=1, source_target_pairs={{0,2},{1,3},{2,0},{3,1},{4,6},{5,7},{6,4},{7,5},{8,10},{9,11},{10,... | collective-permute-start | bytes 3072008 | tf_op jit(solution)/shard_map/ppermute | solution.py:41
  1031.2 2.9 collective-permute-start.39
  1034.1 4.1 collective-permute-start.40
  (125 other events, 1345.6 us)
Sparse Core Ops, SparseCore 0:
  204.9 77.1 all-gather.2
  284.9 130.9 all-gather.4
  499.6 110.6 reduce-scatter.6
  613.6 156.7 reduce-scatter.4

commit v7 on v6

--- a/solution.py
+++ b/solution.py
@@ -1270,7 +1270,7 @@
     normed_held, normed_far = scatter_far(normed_keep, normed_got)
     grad_o_part, normed_held = meet(grad_o_part, normed_held)
     grad_qkv_sum, grad_o, small_sum = scatter_dp([grad_qkv_part, grad_o_part, small_part], 2)
-    normed_far, small_sum = meet(normed_far, small_sum)
+    normed_far, (grad_qkv_sum, grad_o, small_sum) = meet(normed_far, (grad_qkv_sum, grad_o, small_sum))
     small_sum = small_sum + swap(small_sum, "seq", 1)
     small_sum = small_sum + swap(small_sum, "seq", 2)
     grad_xz_sum = grad_xz_sum.astype(LOW)

time: 1060 us -> 1060 us (level)
    unnamed x252 -> x240, local copies, waits for them, and re-layouts: 52.1 us -> 52.9 us
  transfers between devices with their start and end apart: 50 -> 50, of which waited for: 11 -> 14; matrix products, arithmetic and copies ran while one was open for 30% -> 29% of each run, Pallas kernels for 45% -> 46%
where the time goes in v7:
time: 1060 us; the launch traced here: 1050 us
  Pallas kernels  483 us (46%)
  matrix products  193 us (18%)
  local copies, waits for them, and re-layouts  138 us (13%)
  waiting for transfers between devices  102 us (10%)
  other arithmetic  77 us (7%)
  starting transfers between devices  44 us (4%)
  between operations  17.3 us (2%)
    pallas_call x2, Pallas kernels, gather_dp(): pl.pallas_call(lambda *refs: gather_kernel(pieces, line, *refs), out_shap...  161 us
    pallas_call x1, Pallas kernels, attention_backward(): pl.pallas_call(kernel, grid=(SEQ + 1, GROUP_HEADS), in_specs=[pl.BlockSpe...  117 us
    ppermute x42, waiting for transfers between devices, swap(): lax.ppermute(value, axis, [(i, i ^ bit) for i in range(lax.axis_size(axis...  99.6 us
    dot_general x8, matrix products, mm_nt(): lax.dot_general(left, right, (((1,), (1,)), ((), ())), preferred_element_...  66.8 us
    dot_general x9, matrix products, mm(): return jnp.dot(left, right, preferred_element_type=FULL)  66.1 us
    pallas_call x1, Pallas kernels, scatter_dp(): pl.pallas_call(lambda *refs: scatter_kernel(pieces, line, *refs), out_sha...  64.2 us
    dot_general x8, matrix products, mm_tn(): lax.dot_general(left, right, (((0,), (0,)), ((), ())), preferred_element_...  60.3 us
    pallas_call x1, Pallas kernels, mamba_backward(): pl.pallas_call(mamba_backward_kernel, grid=(chunks,), in_specs=mamba_spec...  54.7 us
  transfers between devices with their start and end apart: 50, of which 14 were waited for; matrix products, arithmetic and copies ran while one was open for 29% of the time, Pallas kernels for 46%

profile of v7, /device:TPU:0, one launch (start us, length us, event | category | flops | bytes accessed | tf_op | source)
XLA Modules:
  0.0 1054.4 jit_solution(9629277198114747063)
XLA Ops:
  27.0 64.0 %shard_map.237 = (bf16[8,16,512]{2,1,0:T(8,128)(2,1)S(1)}, bf16[8,200,400]{2,1,0:T(8,128)(2,1)S(1)}, bf16[8,400,400]{2,1,0:T(8,128)(2,1)S(1)}) custom-call(bf16[16,512]{1,0:T(8,128)(2,1)S(1)} %fusion.61.refs_0_, bf16[200,400]{1,0:T(8,128)(2,1)S(1)} %copy-done.25, bf16[400,400]{1,0:T(8,128)(2,1)S(1)} %copy-done.24), custom_call_target="tpu_custom_call" | custom-call | bytes 7942144 | tf_op jit(solution)/shard_map/pallas_call | solution.py:259
  103.8 96.9 %shard_map.241 = (bf16[8,200,896]{2,1,0:T(8,128)(2,1)S(1)}, bf16[8,200,1792]{2,1,0:T(8,128)(2,1)S(1)}) custom-call(bf16[200,896]{1,0:T(8,128)(2,1)S(1)} %concatenate.68.refs_0_, bf16[200,1792]{1,0:T(8,128)(2,1)S(1)} %concatenate.69.refs_1_), custom_call_target="tpu_custom_call" | custom-call | bytes 17203200 | tf_op jit(solution)/shard_map/pallas_call | solution.py:259
  221.4 5.5 shard_map.239
  227.0 6.6 convolution_convert_fusion.9
  240.4 3.7 copy.100
  249.9 35.7 %shard_map.243 = (bf16[1600,320]{1,0:T(8,128)(2,1)S(1)}, f32[1600,128]{1,0:T(8,128)S(1)}) custom-call(s32[1,2]{1,0:T(1,128)S(1)} %copy-done.32, bf16[1600,320]{1,0:T(8,128)(2,1)S(1)} %copy-done.16, bf16[1280,256]{1,0:T(8,128)(2,1)S(1)} %slice.458.kv_ref.refs_2_), custom_call_target="tpu_custom_call" | custom-call | flops 40000000000 | bytes 4194304 | tf_op jit(solution)/shard_map/pallas_call | solution.py:887
  286.5 17.5 %collective-permute-done.12 = bf16[1600,400]{0,1:T(8,128)(2,1)} collective-permute-done((bf16[1600,400]{0,1:T(8,128)(2,1)}, bf16[1600,400]{0,1:T(8,128)(2,1)}, u32[]{:S(2)}, u32[]{:S(2)}) %collective-permute-start.12) | collective-permute-done | bytes 1280032 | tf_op jit(solution)/shard_map/ppermute | solution.py:41
  304.0 3.5 copy.102.refs_1_
  307.5 3.4 copy.103.refs_2_
  310.9 3.4 copy.104.refs_3_
  314.4 7.0 shard_map.244
  321.4 3.7 convolution_convert_fusion.6
  325.9 11.9 %fusion.88.xzb_ref.tail_ref = f32[1280,1792]{1,0:T(8,128)S(1)} fusion(bf16[1280,1600]{1,0:T(8,128)(2,1)} %shard_map.239, bf16[1600,1792]{1,0:T(8,128)(2,1)} %bitcast.186), kind=kOutput, calls=%fused_computation.269 | convolution fusion | flops 7340032000 | bytes 19005440 | tf_op jit(solution)/shard_map/dot_general | solution.py:440
  341.5 18.3 %shard_map.245 = (bf16[1280,896]{1,0:T(8,128)(2,1)S(1)}, bf16[1280,896]{1,0:T(8,128)(2,1)S(1)}, f32[10,16,896]{2,1,0:T(8,128)S(1)}) custom-call(s32[1,2]{1,0:T(1,128)S(1)} %copy-done.32, f32[1280,1792]{1,0:T(8,128)S(1)} %fusion.88.xzb_ref.tail_ref, f32[1280,1792]{1,0:T(8,128)S(1)} %fusion.88.xzb_ref.tail_ref, f32[8,896]{1,0:T(8,128)S(1)} %pad.126.conv_ref, ...), custom_call_target="tpu_custom_call" | custom-call | flops 20000000000 | bytes 16777216 | tf_op jit(solution)/shard_map/pallas_call | solution.py:734
  359.8 3.6 copy-done.37
  366.1 5.2 convolution_convert_fusion.5
  371.7 4.2 collective-permute-done.15
  382.8 20.6 %collective-permute-done.16 = bf16[320,1600]{1,0:T(8,128)(2,1)} collective-permute-done((bf16[320,1600]{1,0:T(8,128)(2,1)}, bf16[320,1600]{1,0:T(8,128)(2,1)}, u32[]{:S(2)}, u32[]{:S(2)}) %collective-permute-start.16) | collective-permute-done | bytes 1024032 | tf_op jit(solution)/shard_map/ppermute | solution.py:41
  410.3 13.2 %fusion.36 = f32[1280,1408]{1,0:T(8,128)} fusion(bf16[1600,1408]{1,0:T(8,128)(2,1)} %all-gather.3.cloned.1.call-done, bf16[320,1600]{1,0:T(8,128)(2,1)} %collective-permute-done.18, bf16[320,1600]{1,0:T(8,128)(2,1)} %collective-permute-done.8, bf16[320,1600]{1,0:T(8,128)(2,1)} %collective-permute-done.9, bf16[320,1600]{1,0:T(8,128)(2,1)} %fusion.16), kind=kOutput, calls=%fused_computation.123 | convolution fusion | flops 5783552000 | bytes 15810560 | tf_op jit(solution)/shard_map/dot_general | solution.py:440
  423.4 9.8 collective-permute-done.17
  436.1 19.4 %fusion.35 = f32[1280,2816]{1,0:T(8,128)S(1)} fusion(bf16[1600,2816]{1,0:T(8,128)(2,1)} %all-gather.5.cloned.1.call-done, bf16[320,1600]{1,0:T(8,128)(2,1)} %collective-permute-done.20, bf16[320,1600]{1,0:T(8,128)(2,1)} %copy-done.99, bf16[320,1600]{1,0:T(8,128)(2,1)} %copy-done.101, bf16[320,1600]{1,0:T(8,128)(2,1)S(1)} %multiply_convert_fusion.4), kind=kOutput, calls=%fused_computation.122 | convolution fusion | flops 11550720000 | bytes 27525120 | tf_op jit(solution)/shard_map/dot_general | solution.py:440
  455.5 8.7 multiply_convert_fusion.2
  464.2 18.0 %convolution_convert_fusion.4 = bf16[1280,1600]{1,0:T(8,128)(2,1)S(1)} fusion(bf16[1600,2816]{1,0:T(8,128)(2,1)} %all-gather.5.cloned.1.call-done, bf16[1280,1408]{1,0:T(8,128)(2,1)} %get-tuple-element.280, bf16[1280,1408]{1,0:T(8,128)(2,1)} %get-tuple-element.279), kind=kOutput, calls=%fused_computation.8 | convolution fusion | flops 11550801920 | bytes 20316160 | tf_op jit(solution)/shard_map/dot_general | solution.py:444
  487.4 12.1 %convolution_convert_fusion.3 = bf16[1600,1408]{1,0:T(8,128)(2,1)} fusion(bf16[1280,1408]{1,0:T(8,128)(2,1)} %get-tuple-element.281, bf16[320,1600]{1,0:T(8,128)(2,1)} %collective-permute-done.18, bf16[320,1600]{1,0:T(8,128)(2,1)} %collective-permute-done.8, bf16[320,1600]{1,0:T(8,128)(2,1)} %collective-permute-done.9, bf16[320,1600]{1,0:T(8,128)(2,1)} %fusion.16), kind=kOutput, calls=%fused_computation.7 | convolution fusion | flops 5785804800 | bytes 12206080 | tf_op jit(solution)/shard_map/dot_general | solution.py:448
  510.0 18.1 %convolution_convert_fusion = bf16[1600,2816]{1,0:T(8,128)(2,1)} fusion(bf16[1280,1408]{1,0:T(8,128)(2,1)} %get-tuple-element.280, bf16[1280,1408]{1,0:T(8,128)(2,1)} %get-tuple-element.279, bf16[320,1600]{1,0:T(8,128)(2,1)} %collective-permute-done.20, bf16[320,1600]{1,0:T(8,128)(2,1)S(1)} %copy-done.100, bf16[320,1600]{1,0:T(8,128)(2,1)} %copy-done.101, ...), kind=kOutput, calls=%fused_computation | convolution fusion | flops 11569643520 | bytes 20316160 | tf_op jit(solution)/shard_map/dot_general | solution.py:448
  528.1 6.2 collective-permute-done.22
  537.5 4.2 multiply_reduce_fusion.4
  544.8 9.0 convolution_convert_fusion.2
  553.8 14.5 %collective-permute-done.23.refs_3_ = bf16[320,1600]{1,0:T(8,128)(2,1)} collective-permute-done((bf16[320,1600]{1,0:T(8,128)(2,1)S(1)}, bf16[320,1600]{1,0:T(8,128)(2,1)}, u32[]{:S(2)}, u32[]{:S(2)}) %collective-permute-start.23) | collective-permute-done | bytes 1024032 | tf_op jit(solution)/shard_map/ppermute | solution.py:41
  578.7 6.3 convolution_convert_fusion.7.d_gated_ref
  585.0 4.5 convolution_convert_fusion.8
  598.9 4.1 copy.111
  614.6 3.6 copy-done.38
  621.9 54.7 %shard_map.247 = (bf16[1280,1792]{1,0:T(8,128)(2,1)S(1)}, f32[8,896]{1,0:T(8,128)S(1)}, f32[8,128]{1,0:T(8,128)S(1)}) custom-call(s32[1,2]{1,0:T(1,128)S(1)} %copy-done.32, f32[1280,1792]{1,0:T(8,128)S(1)} %copy-done.38, f32[1280,1792]{1,0:T(8,128)S(1)} %copy-done.38, f32[8,896]{1,0:T(8,128)S(1)} %pad.126.conv_ref, f32[8,128]{1,0:T(8,128)S(1)} %broadcast_in_dim.19.rate_ref, ...), custom_call_target="tpu_custom_call" | custom-call | flops 60000002048 | bytes 25165824 | tf_op jit(solution)/shard_map/pallas_call | solution.py:755
  690.1 13.8 %convolution_convert_fusion.1 = bf16[1600,1792]{1,0:T(8,128)(2,1)} fusion(bf16[1280,1600]{1,0:T(8,128)(2,1)} %shard_map.239, bf16[1280,1792]{1,0:T(8,128)(2,1)} %copy-done.36), kind=kOutput, calls=%fused_computation.5 | convolution fusion | flops 7342899200 | bytes 14417920 | tf_op jit(solution)/shard_map/dot_general | solution.py:448
  712.2 3.9 convolution_convert_fusion.13
  717.7 4.0 convolution_convert_fusion.14
  729.8 3.8 add_convert_fusion
  734.5 117.1 %shard_map.250 = (bf16[1600,320]{1,0:T(8,128)(2,1)}, bf16[1280,256]{1,0:T(8,128)(2,1)}, f32[200,1792]{1,0:T(8,128)}, f32[400,400]{1,0:T(8,128)}) custom-call(s32[1,2]{1,0:T(1,128)} %refs_0_.3, bf16[1600,320]{1,0:T(8,128)(2,1)} %pad_maximum_fusion.10.q_ref.refs_1_, bf16[1280,256]{1,0:T(8,128)(2,1)} %copy-done.21, bf16[1600,320]{1,0:T(8,128)(2,1)} %copy-done.26, ...), custom_call_target="tpu_custom_call" | custom-call | flops 99999997952 | bytes 8388608 | tf_op jit(solution)/shard_map/pallas_call | solution.py:925
  854.2 7.1 collective-permute-start.44
  871.7 9.8 collective-permute-done.34
  881.5 9.4 collective-permute-done.35
  891.8 6.3 fusion.17
  898.2 16.2 %multiply_reduce_fusion = (f32[1600]{0:T(1024)S(1)}, bf16[1280,1600]{1,0:T(8,128)(2,1)}, f32[1280,1600]{1,0:T(8,128)}) fusion(f32[1280]{0:T(1024)S(1)} %copy-done.94, bf16[4,320,1600]{2,1,0:T(8,128)(2,1)S(1)} %bitcast.175, f32[1280,1600]{1,0:T(8,128)} %fusion.17, bf16[1280,1792]{1,0:T(8,128)(2,1)} %copy-done.36, bf16[1600,1792]{1,0:T(8,128)(2,1)} %bitcast.187), kind=kOutput, calls=%fused_computation.2 | convolution fusion | flops 7352318464 | bytes 34909440 | tf_op jit(solution)/shard_map/dot_general | solution.py:444
  919.1 4.3 multiply_reduce_fusion.2
  930.7 5.6 copy.131
  952.6 64.2 %shard_map.252 = (f32[200,896]{1,0:T(8,128)}, f32[200,400]{1,0:T(8,128)}, f32[16,512]{1,0:T(8,128)}) custom-call(bf16[8,200,896]{2,1,0:T(8,128)(2,1)} %bitcast.204, bf16[8,200,400]{2,1,0:T(8,128)(2,1)} %bitcast.207, f32[8,16,512]{2,1,0:T(8,128)} %fusion.45.refs_2_), custom_call_target="tpu_custom_call" | custom-call | flops 60000002048 | bytes 4278272 | tf_op jit(solution)/shard_map/pallas_call | solution.py:401
  1023.8 3.5 collective-permute-done.40
  (510 shorter events, 246.9 us)
Async XLA Ops:
  7.2 403.1 %all-gather.3.cloned.1.call-start = ((), (), s32[]{:S(2)}) async-start(), calls=%async_computation.2 | async-start | bytes 5068800 | tf_op jit(solution)/shard_map/all_gather | solution.py:417
  7.3 88.7 %collective-permute-start.4 = (bf16[320,1600]{1,0:T(8,128)(2,1)}, bf16[320,1600]{1,0:T(8,128)(2,1)S(1)}, u32[]{:S(2)}, u32[]{:S(2)}) collective-permute-start(bf16[320,1600]{1,0:T(8,128)(2,1)} %refs_1_.3), channel_id=1, source_target_pairs={{0,2},{1,3},{2,0},{3,1},{4,6},{5,7},{6,4},{7,5},{8,10},{9,11},{10,... | collective-permute-start | bytes 3072008 | tf_op jit(solution)/shard_map/ppermute | solution.py:41
  10.3 85.7 %collective-permute-start.5 = (bf16[320,1600]{1,0:T(8,128)(2,1)}, bf16[320,1600]{1,0:T(8,128)(2,1)}, u32[]{:S(2)}, u32[]{:S(2)}) collective-permute-start(bf16[320,1600]{1,0:T(8,128)(2,1)} %refs_1_.3), channel_id=1, source_target_pairs={{0,1},{1,0},{2,3},{3,2},{4,5},{5,4},{6,7},{7,6},{8,9},{9,8},{10,11... | collective-permute-start | bytes 3072008 | tf_op jit(solution)/shard_map/ppermute | solution.py:41
  14.1 78.6 %collective-permute-start.2 = (bf16[200,832]{1,0:T(8,128)(2,1)}, bf16[200,832]{1,0:T(8,128)(2,1)}, u32[]{:S(2)}, u32[]{:S(2)}) collective-permute-start(bf16[200,832]{1,0:T(8,128)(2,1)} %get-tuple-element.323), channel_id=1, source_target_pairs={{0,1},{1,2},{2,0},{4,5},{5,6},{6,4},{8,9},{9,10},{10,8},{12,13},{1... | collective-permute-start | bytes 998408 | tf_op jit(solution)/shard_map/ppermute | solution.py:427
  16.5 76.3 %collective-permute-start.3 = (bf16[200,832]{1,0:T(8,128)(2,1)}, bf16[200,832]{1,0:T(8,128)(2,1)}, u32[]{:S(2)}, u32[]{:S(2)}) collective-permute-start(bf16[200,832]{1,0:T(8,128)(2,1)} %get-tuple-element.322), channel_id=1, source_target_pairs={{1,3},{2,1},{3,2},{5,7},{6,5},{7,6},{9,11},{10,9},{11,10},{13,15},... | collective-permute-start | bytes 998408 | tf_op jit(solution)/shard_map/ppermute | solution.py:428
  17.9 74.7 %collective-permute-start = (bf16[200,560]{1,0:T(8,128)(2,1)}, bf16[200,560]{1,0:T(8,128)(2,1)}, u32[]{:S(2)}, u32[]{:S(2)}) collective-permute-start(bf16[200,560]{1,0:T(8,128)(2,1)} %refs_0_.2), channel_id=1, source_target_pairs={{0,2},{1,3},{2,0},{3,1},{4,6},{5,7},{6,4},{7,5},{8,10},{9,11},{10,... | collective-permute-start | bytes 672008 | tf_op jit(solution)/shard_map/ppermute | solution.py:41
  92.7 112.1 %collective-permute-start.8 = (bf16[320,1600]{1,0:T(8,128)(2,1)}, bf16[320,1600]{1,0:T(8,128)(2,1)}, u32[]{:S(2)}, u32[]{:S(2)}) collective-permute-start(bf16[320,1600]{1,0:T(8,128)(2,1)} %fusion.16), channel_id=1, source_target_pairs={{0,2},{1,3},{2,0},{3,1},{4,6},{5,7},{6,4},{7,5},{8,10},{9,11},{10,... | collective-permute-start | bytes 3072008 | tf_op jit(solution)/shard_map/ppermute | solution.py:41
  92.8 112.0 %collective-permute-start.9 = (bf16[320,1600]{1,0:T(8,128)(2,1)}, bf16[320,1600]{1,0:T(8,128)(2,1)}, u32[]{:S(2)}, u32[]{:S(2)}) collective-permute-start(bf16[320,1600]{1,0:T(8,128)(2,1)} %fusion.16), channel_id=1, source_target_pairs={{0,1},{1,0},{2,3},{3,2},{4,5},{5,4},{6,7},{7,6},{8,9},{9,8},{10,11... | collective-permute-start | bytes 3072008 | tf_op jit(solution)/shard_map/ppermute | solution.py:41
  92.9 3.1 collective-permute-start.1
  96.0 2.7 collective-permute-start.7
  204.8 231.3 %all-gather.5.cloned.1.call-start = ((), (), s32[]{:S(2)}) async-start(), calls=%async_computation.3 | async-start | bytes 10137600 | tf_op jit(solution)/shard_map/all_gather | solution.py:417
  205.2 10.0 collective-permute-start.6
  214.9 814.2 %reduce-scatter.7.cloned.1.call-start = ((), (), s32[]{:S(2)}) async-start(), calls=%async_computation.5 | async-start | bytes 5068800
  239.9 46.6 %collective-permute-start.10 = (bf16[1600,400]{0,1:T(8,128)(2,1)}, bf16[1600,400]{0,1:T(8,128)(2,1)}, u32[]{:S(2)}, u32[]{:S(2)}) collective-permute-start(bf16[1600,400]{0,1:T(8,128)(2,1)} %copy.99), channel_id=1, source_target_pairs={{0,1},{1,0},{2,3},{3,2},{4,5},{5,4},{6,7},{7,6},{8,9},{9,8},{10,11... | collective-permute-start | bytes 3840008 | tf_op jit(solution)/shard_map/ppermute | solution.py:41
  244.0 42.5 %collective-permute-start.11 = (bf16[1600,400]{0,1:T(8,128)(2,1)}, bf16[1600,400]{0,1:T(8,128)(2,1)}, u32[]{:S(2)}, u32[]{:S(2)}) collective-permute-start(bf16[1600,400]{0,1:T(8,128)(2,1)} %copy.100), channel_id=1, source_target_pairs={{0,2},{1,3},{2,0},{3,1},{4,6},{5,7},{6,4},{7,5},{8,10},{9,11},{10,... | collective-permute-start | bytes 3840008 | tf_op jit(solution)/shard_map/ppermute | solution.py:41
  248.6 55.4 %collective-permute-start.12 = (bf16[1600,400]{0,1:T(8,128)(2,1)}, bf16[1600,400]{0,1:T(8,128)(2,1)}, u32[]{:S(2)}, u32[]{:S(2)}) collective-permute-start(bf16[1600,400]{0,1:T(8,128)(2,1)} %copy.101), channel_id=1, source_target_pairs={{0,3},{1,2},{2,1},{3,0},{4,7},{5,6},{6,5},{7,4},{8,11},{9,10},{10,... | collective-permute-start | bytes 3840008 | tf_op jit(solution)/shard_map/ppermute | solution.py:41
  325.2 12.6 %collective-permute-start.13 = (bf16[2,320,1600]{2,1,0:T(8,128)(2,1)S(1)}, bf16[2,320,1600]{2,1,0:T(8,128)(2,1)S(1)}, u32[]{:S(2)}, u32[]{:S(2)}) collective-permute-start(bf16[2,320,1600]{2,1,0:T(8,128)(2,1)S(1)} %dynamic-slice_bitcast_fusion.2), channel_id=1, source_target_pairs={{0,1},{1,0},{2,3},{3,2},{4,5},{5,4},{6,7},{7,6},{8,9},{9,8},{10,11... | collective-permute-start | bytes 6144008 | tf_op jit(solution)/shard_map/ppermute | solution.py:41
  339.7 25.4 %collective-permute-start.14 = (bf16[320,1600]{1,0:T(8,128)(2,1)S(1)}, bf16[320,1600]{1,0:T(8,128)(2,1)S(1)}, u32[]{:S(2)}, u32[]{:S(2)}) collective-permute-start(bf16[320,1600]{1,0:T(8,128)(2,1)S(1)} %get-tuple-element.288), channel_id=1, source_target_pairs={{0,2},{1,3},{2,0},{3,1},{4,6},{5,7},{6,4},{7,5},{8,10},{9,11},{10,... | collective-permute-start | bytes 3072008 | tf_op jit(solution)/shard_map/ppermute | solution.py:41
  371.6 4.3 collective-permute-start.15
  377.5 25.9 %collective-permute-start.16 = (bf16[320,1600]{1,0:T(8,128)(2,1)}, bf16[320,1600]{1,0:T(8,128)(2,1)}, u32[]{:S(2)}, u32[]{:S(2)}) collective-permute-start(bf16[320,1600]{1,0:T(8,128)(2,1)} %fusion.13), channel_id=1, source_target_pairs={{0,2},{1,3},{2,0},{3,1},{4,6},{5,7},{6,4},{7,5},{8,10},{9,11},{10,... | collective-permute-start | bytes 3072008 | tf_op jit(solution)/shard_map/ppermute | solution.py:41
  379.5 30.7 %collective-permute-start.18 = (bf16[320,1600]{1,0:T(8,128)(2,1)}, bf16[320,1600]{1,0:T(8,128)(2,1)}, u32[]{:S(2)}, u32[]{:S(2)}) collective-permute-start(bf16[320,1600]{1,0:T(8,128)(2,1)} %collective-permute-done.8), channel_id=1, source_target_pairs={{0,1},{1,0},{2,3},{3,2},{4,5},{5,4},{6,7},{7,6},{8,9},{9,8},{10,11... | collective-permute-start | bytes 3072008 | tf_op jit(solution)/shard_map/ppermute | solution.py:41
  408.5 24.8 %collective-permute-start.17 = (bf16[320,1600]{1,0:T(8,128)(2,1)S(1)}, bf16[320,1600]{1,0:T(8,128)(2,1)S(1)}, u32[]{:S(2)}, u32[]{:S(2)}) collective-permute-start(bf16[320,1600]{1,0:T(8,128)(2,1)S(1)} %multiply_convert_fusion.4), channel_id=1, source_target_pairs={{0,2},{1,3},{2,0},{3,1},{4,6},{5,7},{6,4},{7,5},{8,10},{9,11},{10,... | collective-permute-start | bytes 3072008 | tf_op jit(solution)/shard_map/ppermute | solution.py:41
  423.4 9.8 collective-permute-start.19
  433.3 2.8 collective-permute-start.20
  487.2 12.3 %collective-permute-start.21 = (bf16[640,1600]{0,1:T(8,128)(2,1)}, bf16[640,1600]{0,1:T(8,128)(2,1)S(1)}, u32[]{:S(2)}, u32[]{:S(2)}) collective-permute-start(bf16[640,1600]{0,1:T(8,128)(2,1)} %copy.107), channel_id=1, source_target_pairs={{0,1},{1,0},{2,3},{3,2},{4,5},{5,4},{6,7},{7,6},{8,9},{9,8},{10,11... | collective-permute-start | bytes 6144008 | tf_op jit(solution)/shard_map/ppermute | solution.py:41
  500.9 540.1 %reduce-scatter.5.cloned.1.call-start = ((), (), s32[]{:S(2)}) async-start(), calls=%async_computation.4 | async-start | bytes 10137600 | tf_op jit(solution)/shard_map/reduce_scatter | solution.py:421
  508.2 26.1 %collective-permute-start.22 = (bf16[320,1600]{1,0:T(8,128)(2,1)}, bf16[320,1600]{1,0:T(8,128)(2,1)}, u32[]{:S(2)}, u32[]{:S(2)}) collective-permute-start(bf16[320,1600]{1,0:T(8,128)(2,1)} %add_convert_fusion.1), channel_id=1, source_target_pairs={{0,2},{1,3},{2,0},{3,1},{4,6},{5,7},{6,4},{7,5},{8,10},{9,11},{10,... | collective-permute-start | bytes 3072008 | tf_op jit(solution)/shard_map/ppermute | solution.py:41
  543.1 25.2 %collective-permute-start.23 = (bf16[320,1600]{1,0:T(8,128)(2,1)S(1)}, bf16[320,1600]{1,0:T(8,128)(2,1)}, u32[]{:S(2)}, u32[]{:S(2)}) collective-permute-start(bf16[320,1600]{1,0:T(8,128)(2,1)S(1)} %get-tuple-element.319.refs_1_), channel_id=1, source_target_pairs={{0,2},{1,3},{2,0},{3,1},{4,6},{5,7},{6,4},{7,5},{8,10},{9,11},{10,... | collective-permute-start | bytes 3072008 | tf_op jit(solution)/shard_map/ppermute | solution.py:41
  553.8 22.2 %collective-permute-start.25 = (bf16[320,1600]{1,0:T(8,128)(2,1)S(1)}, bf16[320,1600]{1,0:T(8,128)(2,1)}, u32[]{:S(2)}, u32[]{:S(2)}) collective-permute-start(bf16[320,1600]{1,0:T(8,128)(2,1)S(1)} %get-tuple-element.319.refs_1_), channel_id=1, source_target_pairs={{0,1},{1,0},{2,3},{3,2},{4,5},{5,4},{6,7},{7,6},{8,9},{9,8},{10,11... | collective-permute-start | bytes 3072008 | tf_op jit(solution)/shard_map/ppermute | solution.py:41
  568.3 7.7 collective-permute-start.26
  570.6 43.0 %collective-permute-start.28 = (bf16[320,1600]{1,0:T(8,128)(2,1)S(1)}, bf16[320,1600]{1,0:T(8,128)(2,1)S(1)}, u32[]{:S(2)}, u32[]{:S(2)}) collective-permute-start(bf16[320,1600]{1,0:T(8,128)(2,1)S(1)} %get-tuple-element.176.refs_1_), channel_id=1, source_target_pairs={{0,1},{1,0},{2,3},{3,2},{4,5},{5,4},{6,7},{7,6},{8,9},{9,8},{10,11... | collective-permute-start | bytes 3072008 | tf_op jit(solution)/shard_map/ppermute | solution.py:41
  571.1 107.6 %collective-permute-start.31 = (bf16[320,1600]{1,0:T(8,128)(2,1)S(1)}, bf16[320,1600]{1,0:T(8,128)(2,1)}, u32[]{:S(2)}, u32[]{:S(2)}) collective-permute-start(bf16[320,1600]{1,0:T(8,128)(2,1)S(1)} %get-tuple-element.176.refs_1_), channel_id=1, source_target_pairs={{0,2},{1,3},{2,0},{3,1},{4,6},{5,7},{6,4},{7,5},{8,10},{9,11},{10,... | collective-permute-start | bytes 3072008 | tf_op jit(solution)/shard_map/ppermute | solution.py:41
  596.1 18.4 %collective-permute-start.27 = (bf16[896,400]{0,1:T(8,128)(2,1)}, bf16[896,400]{0,1:T(8,128)(2,1)}, u32[]{:S(2)}, u32[]{:S(2)}) collective-permute-start(bf16[896,400]{0,1:T(8,128)(2,1)} %copy.113), channel_id=1, source_target_pairs={{0,1},{1,0},{2,3},{3,2},{4,5},{5,4},{6,7},{7,6},{8,9},{9,8},{10,11... | collective-permute-start | bytes 2150408 | tf_op jit(solution)/shard_map/ppermute | solution.py:41
  603.0 123.6 %collective-permute-start.24 = (bf16[640,1600]{0,1:T(8,128)(2,1)}, bf16[640,1600]{0,1:T(8,128)(2,1)}, u32[]{:S(2)}, u32[]{:S(2)}) collective-permute-start(bf16[640,1600]{0,1:T(8,128)(2,1)} %copy.111), channel_id=1, source_target_pairs={{0,1},{1,0},{2,3},{3,2},{4,5},{5,4},{6,7},{7,6},{8,9},{9,8},{10,11... | collective-permute-start | bytes 6144008 | tf_op jit(solution)/shard_map/ppermute | solution.py:41
  611.0 67.7 %collective-permute-start.29 = (bf16[896,400]{0,1:T(8,128)(2,1)}, bf16[896,400]{0,1:T(8,128)(2,1)}, u32[]{:S(2)}, u32[]{:S(2)}) collective-permute-start(bf16[896,400]{0,1:T(8,128)(2,1)} %copy.114), channel_id=1, source_target_pairs={{0,2},{1,3},{2,0},{3,1},{4,6},{5,7},{6,4},{7,5},{8,10},{9,11},{10,... | collective-permute-start | bytes 2150408 | tf_op jit(solution)/shard_map/ppermute | solution.py:41
  613.6 65.2 %collective-permute-start.30 = (bf16[896,400]{0,1:T(8,128)(2,1)}, bf16[896,400]{0,1:T(8,128)(2,1)S(1)}, u32[]{:S(2)}, u32[]{:S(2)}) collective-permute-start(bf16[896,400]{0,1:T(8,128)(2,1)} %copy.115), channel_id=1, source_target_pairs={{0,3},{1,2},{2,1},{3,0},{4,7},{5,6},{6,5},{7,4},{8,11},{9,10},{10,... | collective-permute-start | bytes 2150408 | tf_op jit(solution)/shard_map/ppermute | solution.py:41
  703.9 3.9 collective-permute-start.32
  733.7 157.3 %collective-permute-start.36 = (bf16[320,1600]{1,0:T(8,128)(2,1)}, bf16[320,1600]{1,0:T(8,128)(2,1)}, u32[]{:S(2)}, u32[]{:S(2)}) collective-permute-start(bf16[320,1600]{1,0:T(8,128)(2,1)} %get-tuple-element.286), channel_id=1, source_target_pairs={{0,2},{1,3},{2,0},{3,1},{4,6},{5,7},{6,4},{7,5},{8,10},{9,11},{10,... | collective-permute-start | bytes 3072008 | tf_op jit(solution)/shard_map/ppermute | solution.py:41
  854.2 14.8 %collective-permute-start.44 = (bf16[200,832]{1,0:T(8,128)(2,1)}, bf16[200,832]{1,0:T(8,128)(2,1)}, u32[]{:S(2)}, u32[]{:S(2)}) collective-permute-start(bf16[200,832]{1,0:T(8,128)(2,1)} %get-tuple-element.330), channel_id=1, source_target_pairs={{1,0},{2,1},{0,2},{5,4},{6,5},{4,6},{9,8},{10,9},{8,10},{13,12},{1... | collective-permute-start | bytes 998408 | tf_op jit(solution)/shard_map/ppermute | solution.py:434
  861.3 7.7 collective-permute-start.45
  864.1 7.6 collective-permute-start.33
  865.7 15.8 %collective-permute-start.34 = (bf16[640,400]{0,1:T(8,128)(2,1)}, bf16[640,400]{0,1:T(8,128)(2,1)}, u32[]{:S(2)}, u32[]{:S(2)}) collective-permute-start(bf16[640,400]{0,1:T(8,128)(2,1)} %copy.120), channel_id=1, source_target_pairs={{0,2},{1,3},{2,0},{3,1},{4,6},{5,7},{6,4},{7,5},{8,10},{9,11},{10,... | collective-permute-start | bytes 1536008 | tf_op jit(solution)/shard_map/ppermute | solution.py:41
  869.0 21.9 %collective-permute-start.35 = (bf16[640,400]{0,1:T(8,128)(2,1)}, bf16[640,400]{0,1:T(8,128)(2,1)S(1)}, u32[]{:S(2)}, u32[]{:S(2)}) collective-permute-start(bf16[640,400]{0,1:T(8,128)(2,1)} %copy.121), channel_id=1, source_target_pairs={{0,3},{1,2},{2,1},{3,0},{4,7},{5,6},{6,5},{7,4},{8,11},{9,10},{10,... | collective-permute-start | bytes 1536008 | tf_op jit(solution)/shard_map/ppermute | solution.py:41
  917.5 30.0 %collective-permute-start.37 = (bf16[2,320,1600]{2,1,0:T(8,128)(2,1)}, bf16[2,320,1600]{2,1,0:T(8,128)(2,1)}, u32[]{:S(2)}, u32[]{:S(2)}) collective-permute-start(bf16[2,320,1600]{2,1,0:T(8,128)(2,1)} %dynamic-slice_bitcast_fusion), channel_id=1, source_target_pairs={{0,1},{1,0},{2,3},{3,2},{4,5},{5,4},{6,7},{7,6},{8,9},{9,8},{10,11... | collective-permute-start | bytes 6144008 | tf_op jit(solution)/shard_map/ppermute | solution.py:41
  950.2 66.5 %collective-permute-start.38 = (bf16[320,1600]{1,0:T(8,128)(2,1)S(1)}, bf16[320,1600]{1,0:T(8,128)(2,1)S(1)}, u32[]{:S(2)}, u32[]{:S(2)}) collective-permute-start(bf16[320,1600]{1,0:T(8,128)(2,1)S(1)} %get-tuple-element.284), channel_id=1, source_target_pairs={{0,2},{1,3},{2,0},{3,1},{4,6},{5,7},{6,4},{7,5},{8,10},{9,11},{10,... | collective-permute-start | bytes 3072008 | tf_op jit(solution)/shard_map/ppermute | solution.py:41
  1018.1 11.0 %collective-permute-start.42 = (bf16[200,1024]{1,0:T(8,128)(2,1)S(1)}, bf16[200,1024]{1,0:T(8,128)(2,1)S(1)}, u32[]{:S(2)}, u32[]{:S(2)}) collective-permute-start(bf16[200,1024]{1,0:T(8,128)(2,1)S(1)} %pad_maximum_fusion.20.refs_1_), channel_id=1, source_target_pairs={{0,2},{1,3},{2,0},{3,1},{4,6},{5,7},{6,4},{7,5},{8,10},{9,11},{10,... | collective-permute-start | bytes 1228808 | tf_op jit(solution)/shard_map/ppermute | solution.py:41
  1018.7 12.5 %collective-permute-start.41 = (bf16[200,1024]{1,0:T(8,128)(2,1)S(1)}, bf16[200,1024]{1,0:T(8,128)(2,1)S(1)}, u32[]{:S(2)}, u32[]{:S(2)}) collective-permute-start(bf16[200,1024]{1,0:T(8,128)(2,1)S(1)} %pad_maximum_fusion.20.refs_1_), channel_id=1, source_target_pairs={{0,1},{1,0},{2,3},{3,2},{4,5},{5,4},{6,7},{7,6},{8,9},{9,8},{10,11... | collective-permute-start | bytes 1228808 | tf_op jit(solution)/shard_map/ppermute | solution.py:41
  1020.4 6.9 collective-permute-start.40
  (119 other events, 1389.8 us)
Sparse Core Ops, SparseCore 0:
  204.9 77.1 all-gather.2
  284.8 131.0 all-gather.4
  499.7 110.2 reduce-scatter.6
  613.3 163.3 reduce-scatter.4
